TPU v7x, 32 devices: a whole 2x2x4 slice. The times are simulated.
32 devices in a mesh: row: 8 (over z, core), col: 4 (over y, x).
Axes of the slice: x: 2, y: 2, z: 4, core: 2. Of those that a mesh axis runs over, the one named last changes fastest.
Arguments:
- tensor_slab: float32 [1024, 65536], P(None, ('row', 'col')), may hold values from 0.25 to 1500, as said below
- left_init: float32 [1024, 128], replicated, may hold values from 0.15 to 1.5
- right_init: float32 [128, 65536], P(None, ('row', 'col')), may hold values from 0.1 to 1
- second_left_init: float32 [16384, 128], P('row'), may hold values from 0.1 to 1
- second_right_init: float32 [128, 512], P(None, 'col'), may hold values from 0.003 to 0.03
Outputs:
- left_out: float32 [1024, 128], replicated
- second_left_out: float32 [16384, 128], P(('row', 'col'))
Inputs may be any that keep to these rules, and one draw needn't show every extreme that they name: `tensor_slab`: every entry is positive.
All inputs are finite; a program needn't handle non-finite values.
Results may differ from a plain program's by a relative error of at most 0.0003.
Values sent between devices are 32-bit elements; how exact they have to be, the bound alone decides.
No kernel may reach another device: no remote copies, remote signals or barrier semaphores. Data moves between devices by JAX's collectives and lax.ppermute only.
A program may use at most 128 MiB of HBM per device.

v0:
```python
import functools

import jax
import jax.numpy as jnp
from jax import lax
from jax.experimental import pallas as pl
from jax.experimental.pallas import tpu as pltpu
from jax.sharding import PartitionSpec as P

AXES = ("row", "col")
F32, BF16 = jnp.float32, jnp.bfloat16
PAD = 8
VMEM_BYTES = 40 * 1024 * 1024


def exchange(parts):
    return lax.all_to_all(parts, AXES, split_axis=0, concat_axis=0, tiled=True)


def send(values, row_flip, col_flip):
    rows, cols = lax.axis_size("row"), lax.axis_size("col")
    pairs = [
        (r * cols + c, (r ^ row_flip) * cols + (c ^ col_flip))
        for r in range(rows)
        for c in range(cols)
    ]
    return lax.ppermute(values, AXES, pairs)


def pick(values, index):
    return lax.dynamic_index_in_dim(values, index, 0, keepdims=False)


def tree_sum(terms):
    while len(terms) > 1:
        terms = [a + b for a, b in zip(terms[::2], terms[1::2])]
    return terms[0]


def reduce_parts(parts):
    core, col = lax.axis_index("row") % 2, lax.axis_index("col")
    cols = lax.axis_size("col")
    own = pick(parts, core) + send(pick(parts, 1 - core), 1, 0)
    own = tree_sum(
        [pick(own, col)] + [send(pick(own, col ^ flip), 0, flip) for flip in range(1, cols)]
    )
    return tree_sum([own] + [send(own, flip, 0) for flip in range(2, lax.axis_size("row"), 2)])


def spread_parts(part):
    core, col = lax.axis_index("row") % 2, lax.axis_index("col")
    cols = lax.axis_size("col")
    near = jnp.stack([part] + [send(part, 0, flip) for flip in range(1, cols)])
    near = jnp.stack([pick(near, index ^ col) for index in range(cols)])
    both = jnp.stack([near, send(near, 1, 0)])
    return jnp.stack([pick(both, core), pick(both, 1 - core)])


def split(x):
    high = x.astype(BF16)
    return high, (x - high.astype(F32)).astype(BF16)


def dot(a, b):
    return jnp.dot(a, b, preferred_element_type=F32)


def dot_nt(a, b):
    return lax.dot_general(a, b, (((1,), (1,)), ((), ())), preferred_element_type=F32)


def divide(x, y):
    guess = pl.reciprocal(y, approx=True)
    return x * (guess * (2.0 - y * guess))


def prepare_left(left_ref, pair_ref):
    rank = left_ref.shape[1]
    high, low = split(left_ref[...])
    pair_ref[:, :rank] = high
    pair_ref[:, rank:] = low


def prepare_left_t(left_ref, pair_t_ref, sums_ref):
    rank = left_ref.shape[1]
    turned = left_ref[...].T
    high, low = split(turned)
    pair_t_ref[:rank, :] = high
    pair_t_ref[rank:, :] = low
    sums_ref[...] = jnp.broadcast_to(jnp.sum(turned, axis=1, keepdims=True), sums_ref.shape)


def row_chunks(m):
    size = min(256, m)
    return [pl.ds(start, size) for start in range(0, m, size)]


def quotients(slab_ref, pair_ref, right, rows):
    rank = right.shape[0]
    high, low = split(right)
    twice = jnp.concatenate([high, high], axis=0)
    product = dot(pair_ref[rows, :], twice) + dot(pair_ref[rows, :rank], low)
    return split(divide(slab_ref[rows, :], product))


def right_update(slab_ref, pair_ref, pair_t_ref, sums_ref, right, high_ref, low_ref):
    rank = right.shape[0]
    for rows in row_chunks(slab_ref.shape[0]):
        high, low = quotients(slab_ref, pair_ref, right, rows)
        high_ref[rows, :] = high
        low_ref[rows, :] = low
    both = dot(pair_t_ref[...], high_ref[...])
    numerator = both[:rank] + both[rank:] + dot(pair_t_ref[:rank, :], low_ref[...])
    return right * numerator / sums_ref[:, :1]


def left_numerator(slab_ref, pair_ref, right, total_ref, sums_ref, first):
    rank = right.shape[0]
    right_high, right_low = split(right)
    right_both = jnp.concatenate([right_high, right_low], axis=0)
    ones = jnp.ones((16, right.shape[1]), BF16)
    row_sums = dot_nt(ones, right_both)[:PAD]
    row_sums = row_sums[:, :rank] + row_sums[:, rank:]
    sums_ref[...] = jnp.where(first, row_sums, sums_ref[...] + row_sums)
    for rows in row_chunks(slab_ref.shape[0]):
        high, low = quotients(slab_ref, pair_ref, right, rows)
        both = dot_nt(high, right_both)
        term = both[:, :rank] + both[:, rank:] + dot_nt(low, right_high)
        total_ref[rows, :] = jnp.where(first, term, total_ref[rows, :] + term)


def write_left(total_ref, row_sums_ref, extra_ref, out_ref):
    parts, tall, rank = out_ref.shape
    height = tall - PAD
    first = lax.broadcasted_iota(jnp.int32, (PAD, rank), 0) == 0
    stats = jnp.where(first, row_sums_ref[...], extra_ref[...])
    for part in range(parts):
        out_ref[part, :height, :] = total_ref[pl.ds(part * height, height), :]
        out_ref[part, height:, :] = stats


def turn_kernel(
    slab_ref, left_ref, right_ref, extra_ref, right_out, left_out,
    pair_ref, pair_t_ref, sums_ref, high_ref, low_ref, total_ref, row_sums_ref,
):
    step = pl.program_id(0)

    @pl.when(step == 0)
    def _():
        prepare_left(left_ref, pair_ref)
        prepare_left_t(left_ref, pair_t_ref, sums_ref)

    right = right_update(
        slab_ref, pair_ref, pair_t_ref, sums_ref, right_ref[...], high_ref, low_ref
    )
    right_out[...] = right
    left_numerator(slab_ref, pair_ref, right, total_ref, row_sums_ref, step == 0)

    @pl.when(step == pl.num_programs(0) - 1)
    def _():
        write_left(total_ref, row_sums_ref, extra_ref, left_out)


def second_quotient(block, second_left, pairs):
    high, low = split(second_left)
    right_high, right_low = pairs
    product = dot(high, right_high) + (dot(low, right_high) + dot(high, right_low))
    return split(divide(block, product)), (high, low)


def right_kernel(
    slices, slab_ref, left_ref, right_ref, second_left_ref, second_right_ref, right_out, numer_out,
    pair_ref, pair_t_ref, sums_ref, high_ref, low_ref, numer_ref,
):
    step = pl.program_id(0)

    @pl.when(step == 0)
    def _():
        prepare_left(left_ref, pair_ref)
        prepare_left_t(left_ref, pair_t_ref, sums_ref)

    right = right_update(
        slab_ref, pair_ref, pair_t_ref, sums_ref, right_ref[...], high_ref, low_ref
    )
    right_out[...] = right
    rank, k = right.shape
    second_left = second_left_ref[pl.ds(step, rank, stride=slices), :]
    second_right = jnp.concatenate(
        [second_right_ref[block] for block in range(k // rank)], axis=1
    )
    (high, low), _ = second_quotient(right, second_left, split(second_right))
    left_high, left_low = split(second_left.T)
    term = dot(left_high, high) + (dot(left_low, high) + dot(left_high, low))
    numer_ref[...] = jnp.where(step == 0, term, numer_ref[...] + term)

    @pl.when(step == pl.num_programs(0) - 1)
    def _():
        for block in range(k // rank):
            numer_out[block] = numer_ref[:, pl.ds(block * rank, rank)]


def left_kernel(slab_ref, left_ref, right_ref, left_out, pair_ref, total_ref, row_sums_ref):
    step = pl.program_id(0)

    @pl.when(step == 0)
    def _():
        prepare_left(left_ref, pair_ref)

    left_numerator(slab_ref, pair_ref, right_ref[...], total_ref, row_sums_ref, step == 0)

    @pl.when(step == pl.num_programs(0) - 1)
    def _():
        write_left(total_ref, row_sums_ref, row_sums_ref, left_out)


def second_kernel(slices, right_ref, second_left_ref, second_right_ref, out_ref):
    rank = right_ref.shape[0]
    k = right_ref.shape[1] // slices
    second_right = jnp.concatenate(
        [second_right_ref[block] for block in range(k // rank)], axis=1
    )
    right_high, right_low = split(second_right)
    right_both = jnp.concatenate([right_high, right_low], axis=0)
    sums = dot_nt(jnp.ones((16, k), BF16), right_both)[:1]
    scale = 1.0 / (sums[:, :rank] + sums[:, rank:])
    for index in range(slices):
        rows = pl.ds(index, rank, stride=slices)
        second_left = second_left_ref[rows, :]
        (high, low), _ = second_quotient(
            right_ref[:, pl.ds(index * k, k)], second_left, (right_high, right_low)
        )
        both = dot_nt(high, right_both)
        numer = both[:, :rank] + both[:, rank:] + dot_nt(low, right_high)
        out_ref[rows, :] = second_left * numer * scale


def full(shape):
    return pl.BlockSpec(shape, lambda step: (0,) * len(shape))


def params():
    return pltpu.CompilerParams(
        dimension_semantics=("arbitrary",), vmem_limit_bytes=VMEM_BYTES
    )


def left_scratch(m, rank):
    return [pltpu.VMEM((m, 2 * rank), BF16)]


def right_scratch(m, rank, block):
    return [
        pltpu.VMEM((2 * rank, m), BF16),
        pltpu.VMEM((rank, rank), F32),
        pltpu.VMEM((m, block), BF16),
        pltpu.VMEM((m, block), BF16),
    ]


def total_scratch(m, rank):
    return [pltpu.VMEM((m, rank), F32), pltpu.VMEM((PAD, rank), F32)]


def cost(m, rank, columns, dots):
    return pl.CostEstimate(
        flops=6 * dots * m * rank * columns, bytes_accessed=4 * m * columns, transcendentals=0
    )


def full_turn(slab, left, right, extra, block, parts):
    (m, columns), rank = slab.shape, left.shape[1]
    columns_spec = lambda height: pl.BlockSpec((height, block), lambda step: (0, step))
    tall = m // parts + PAD
    return pl.pallas_call(
        turn_kernel,
        grid=(columns // block,),
        in_specs=[columns_spec(m), full((m, rank)), columns_spec(rank), full((PAD, rank))],
        out_specs=[columns_spec(rank), full((parts, tall, rank))],
        out_shape=[
            jax.ShapeDtypeStruct((rank, columns), F32),
            jax.ShapeDtypeStruct((parts, tall, rank), F32),
        ],
        scratch_shapes=left_scratch(m, rank)
        + right_scratch(m, rank, block)
        + total_scratch(m, rank),
        compiler_params=params(),
        cost_estimate=cost(m, rank, columns, 4),
        name="turn",
    )(slab, left, right, extra)


def right_half(slab, left, right, second_left, second_right, block):
    (m, columns), rank = slab.shape, left.shape[1]
    slices = columns // block
    columns_spec = lambda height: pl.BlockSpec((height, block), lambda step: (0, step))
    return pl.pallas_call(
        functools.partial(right_kernel, slices),
        grid=(slices,),
        in_specs=[
            columns_spec(m), full((m, rank)), columns_spec(rank),
            full(second_left.shape), full(second_right.shape),
        ],
        out_specs=[columns_spec(rank), full(second_right.shape)],
        out_shape=[
            jax.ShapeDtypeStruct((rank, columns), F32),
            jax.ShapeDtypeStruct(second_right.shape, F32),
        ],
        scratch_shapes=left_scratch(m, rank)
        + right_scratch(m, rank, block)
        + [pltpu.VMEM((rank, block), F32)],
        compiler_params=params(),
        cost_estimate=cost(m, rank, columns, 2),
        name="right_half",
    )(slab, left, right, second_left, second_right)


def left_half(slab, left, right, block, parts):
    (m, columns), rank = slab.shape, left.shape[1]
    columns_spec = lambda height: pl.BlockSpec((height, block), lambda step: (0, step))
    tall = m // parts + PAD
    return pl.pallas_call(
        left_kernel,
        grid=(columns // block,),
        in_specs=[columns_spec(m), full((m, rank)), columns_spec(rank)],
        out_specs=full((parts, tall, rank)),
        out_shape=jax.ShapeDtypeStruct((parts, tall, rank), F32),
        scratch_shapes=left_scratch(m, rank) + total_scratch(m, rank),
        compiler_params=params(),
        cost_estimate=cost(m, rank, columns, 2),
        name="left_half",
    )(slab, left, right)


def second_rows_out(right, second_left, second_right, slices):
    return pl.pallas_call(
        functools.partial(second_kernel, slices),
        out_shape=jax.ShapeDtypeStruct(second_left.shape, F32),
        compiler_params=pltpu.CompilerParams(vmem_limit_bytes=VMEM_BYTES),
        cost_estimate=cost(right.shape[0], right.shape[0], right.shape[1], 2),
        name="second_rows",
    )(right, second_left, second_right)


def body(tensor_slab, left_init, right_init, second_left_init, second_right_init):
    row_devices = lax.axis_size("row")
    col_devices = lax.axis_size("col")
    devices = row_devices * col_devices
    own_part = (lax.axis_index("row") % 2) * col_devices + lax.axis_index("col")
    parts = 2 * col_devices
    m, rank = left_init.shape
    k = second_right_init.shape[1] * col_devices
    slices = right_init.shape[1] // k
    per_owner = rank // devices
    rows_own = m // parts

    second_rows = second_left_init.shape[0] // col_devices
    own_left = lax.dynamic_slice_in_dim(
        second_left_init, lax.axis_index("col") * second_rows, second_rows, 0
    )
    col_part = jnp.broadcast_to(jnp.sum(own_left, axis=0)[None], (PAD, rank))
    own_left = own_left.reshape(per_owner, devices, slices, rank).transpose(1, 0, 2, 3)
    second_left = exchange(own_left.reshape(devices, per_owner * slices, rank))
    second_left = second_left.reshape(rank * slices, rank)
    whole = lax.all_to_all(
        jnp.broadcast_to(second_right_init[None], (col_devices,) + second_right_init.shape),
        "col", split_axis=0, concat_axis=0, tiled=True,
    )
    whole = whole.transpose(1, 0, 2).reshape(rank, k // rank, rank).transpose(1, 0, 2)

    def new_left(left, summed):
        total = reduce_parts(summed.reshape(2, col_devices, rows_own + PAD, rank))
        own = lax.dynamic_slice_in_dim(left, own_part * rows_own, rows_own, 0)
        own = own * total[:rows_own] / total[rows_own][None, :]
        return spread_parts(own).reshape(m, rank), total[rows_own + 1]

    right, summed = full_turn(tensor_slab, left_init, right_init, col_part, k, parts)
    left, col_totals = new_left(left_init, summed)
    right, numerator = right_half(tensor_slab, left, right, second_left, whole, k)
    summed = left_half(tensor_slab, left, right, k, parts)

    rows_part = k // parts
    part = reduce_parts(numerator.reshape(2, col_devices, rows_part, rank))
    init_over = (whole / col_totals[None, :, None]).reshape(k, rank)
    part = part * lax.dynamic_slice_in_dim(init_over, own_part * rows_part, rows_part, 0)
    second_right = spread_parts(part).reshape(k // rank, rank, rank)
    rows_out = second_rows_out(right, second_left, second_right, slices)
    returned = exchange(rows_out.reshape(devices, per_owner * slices, rank))
    returned = returned.reshape(devices, per_owner, slices, rank).transpose(1, 0, 2, 3)
    left_out, _ = new_left(left, summed)
    return (left_out, returned.reshape(second_rows, rank))


def solution(mesh):
    placed = (P(None, AXES), P(), P(None, AXES), P("row", None), P(None, "col"))
    return jax.shard_map(
        body, mesh=mesh, in_specs=placed, out_specs=(P(), P(AXES, None)), check_vma=False
    )
```

profile of v0, /device:TPU:0, one launch (start us, length us, event | category | flops | bytes accessed | tf_op | source)
XLA Modules:
  0.0 148.3 jit_solution(9240175540331304876)
XLA Ops:
  0.6 1.0 fusion.14
  1.7 1.0 copy-done
  2.7 3.4 %copy-done.1 = f32[1024,2048]{1,0:T(8,128)S(1)} copy-done((f32[1024,2048]{1,0:T(8,128)S(1)}, f32[1024,2048]{1,0:T(8,128)}, u32[]{:S(2)}) %copy-start.1) | copy-done | bytes 8388632
  6.1 1.2 copy-done.3
  7.3 12.5 %turn.1 = (f32[128,2048]{1,0:T(8,128)S(1)}, f32[8,136,128]{2,1,0:T(8,128)S(1)}) custom-call(f32[1024,2048]{1,0:T(8,128)S(1)} %copy-done.1, f32[1024,128]{1,0:T(8,128)S(1)} %copy-done, f32[128,2048]{1,0:T(8,128)S(1)} %copy-done.3, f32[8,128]{1,0:T(8,128)S(1)} %broadcast_in_dim.4.extra_ref), custom_call_target="tpu_custom_call" | custom-call | flops 6442450944 | bytes 8388608 | tf_op jit(solution)/shard_map/turn/pallas_call | solution.py:274
  19.9 0.5 collective-permute-start
  20.4 1.2 collective-permute-done
  21.7 2.9 %collective-permute-start.1 = (f32[136,128]{1,0:T(8,128)S(1)}, f32[136,128]{1,0:T(8,128)S(1)}, u32[]{:S(2)}, u32[]{:S(2)}) collective-permute-start(f32[136,128]{1,0:T(8,128)S(1)} %get-tuple-element.21), channel_id=1, source_target_pairs={{0,1},{1,0},{2,3},{3,2},{4,5},{5,4},{6,7},{7,6},{8,9},{9,8},{10,11... | collective-permute-start | bytes 208904 | tf_op jit(solution)/shard_map/ppermute | solution.py:27
  24.6 1.5 %collective-permute-start.2 = (f32[136,128]{1,0:T(8,128)S(1)}, f32[136,128]{1,0:T(8,128)S(1)}, u32[]{:S(2)}, u32[]{:S(2)}) collective-permute-start(f32[136,128]{1,0:T(8,128)S(1)} %get-tuple-element.20), channel_id=1, source_target_pairs={{0,2},{1,3},{2,0},{3,1},{4,6},{5,7},{6,4},{7,5},{8,10},{9,11},{10,... | collective-permute-start | bytes 208904 | tf_op jit(solution)/shard_map/ppermute | solution.py:27
  26.1 0.9 collective-permute-done.1
  27.1 1.8 %collective-permute-done.2 = f32[136,128]{1,0:T(8,128)S(1)} collective-permute-done((f32[136,128]{1,0:T(8,128)S(1)}, f32[136,128]{1,0:T(8,128)S(1)}, u32[]{:S(2)}, u32[]{:S(2)}) %collective-permute-start.2) | collective-permute-done | bytes 69664 | tf_op jit(solution)/shard_map/ppermute | solution.py:27
  28.9 2.4 %collective-permute-done.3 = f32[136,128]{1,0:T(8,128)S(1)} collective-permute-done((f32[136,128]{1,0:T(8,128)S(1)}, f32[136,128]{1,0:T(8,128)S(1)}, u32[]{:S(2)}, u32[]{:S(2)}) %collective-permute-start.3) | collective-permute-done | bytes 69664 | tf_op jit(solution)/shard_map/ppermute | solution.py:27
  31.3 1.6 %collective-permute-start.4 = (f32[136,128]{1,0:T(8,128)S(1)}, f32[136,128]{1,0:T(8,128)S(1)}, u32[]{:S(2)}, u32[]{:S(2)}) collective-permute-start(f32[136,128]{1,0:T(8,128)S(1)} %fusion.7), channel_id=1, source_target_pairs={{0,8},{1,9},{2,10},{3,11},{4,12},{5,13},{6,14},{7,15},{8,0},{9,1},... | collective-permute-start | bytes 208904 | tf_op jit(solution)/shard_map/ppermute | solution.py:27
  33.0 2.6 %collective-permute-start.5 = (f32[136,128]{1,0:T(8,128)S(1)}, f32[136,128]{1,0:T(8,128)S(1)}, u32[]{:S(2)}, u32[]{:S(2)}) collective-permute-start(f32[136,128]{1,0:T(8,128)S(1)} %fusion.7), channel_id=1, source_target_pairs={{0,16},{1,17},{2,18},{3,19},{4,20},{5,21},{6,22},{7,23},{8,24},{9,... | collective-permute-start | bytes 208904 | tf_op jit(solution)/shard_map/ppermute | solution.py:27
  35.6 0.2 collective-permute-start.6
  35.8 0.3 collective-permute-done.4
  36.0 3.6 %collective-permute-done.5 = f32[136,128]{1,0:T(8,128)S(1)} collective-permute-done((f32[136,128]{1,0:T(8,128)S(1)}, f32[136,128]{1,0:T(8,128)S(1)}, u32[]{:S(2)}, u32[]{:S(2)}) %collective-permute-start.5) | collective-permute-done | bytes 69664 | tf_op jit(solution)/shard_map/ppermute | solution.py:27
  39.7 2.0 %collective-permute-done.6 = f32[136,128]{1,0:T(8,128)S(1)} collective-permute-done((f32[136,128]{1,0:T(8,128)S(1)}, f32[136,128]{1,0:T(8,128)S(1)}, u32[]{:S(2)}, u32[]{:S(2)}) %collective-permute-start.6) | collective-permute-done | bytes 69664 | tf_op jit(solution)/shard_map/ppermute | solution.py:27
  41.7 0.9 fusion.9
  42.6 0.7 collective-permute-start.8
  43.2 1.4 collective-permute-start.9
  44.6 1.5 %collective-permute-start.7 = (f32[128,128]{1,0:T(8,128)S(1)}, f32[128,128]{1,0:T(8,128)S(1)}, u32[]{:S(2)}, u32[]{:S(2)}) collective-permute-start(f32[128,128]{1,0:T(8,128)S(1)} %fusion.9), channel_id=1, source_target_pairs={{0,1},{1,0},{2,3},{3,2},{4,5},{5,4},{6,7},{7,6},{8,9},{9,8},{10,11... | collective-permute-start | bytes 196616 | tf_op jit(solution)/shard_map/ppermute | solution.py:27
  46.1 0.7 broadcast_in_dim.5
  46.9 3.4 %all-to-all-start.1 = ((f32[4,128,128]{2,1,0:T(8,128)}), f32[4,128,128]{2,1,0:T(8,128)S(1)}, u32[]{:S(2)}, u32[]{:S(2)}) async-start(f32[4,128,128]{2,1,0:T(8,128)} %broadcast_in_dim.5), calls=%async_computation.1 | async-start | bytes 524288 | tf_op jit(solution)/shard_map/all_to_all | solution.py:364
  50.5 0.9 copy.13
  51.4 4.2 %all-to-all-done.1.second_right_ref = f32[4,128,128]{2,1,0:T(8,128)S(1)} async-done(((f32[4,128,128]{2,1,0:T(8,128)}), f32[4,128,128]{2,1,0:T(8,128)S(1)}, u32[]{:S(2)}, u32[]{:S(2)}) %all-to-all-start.1) | async-done | bytes 262176 | tf_op jit(solution)/shard_map/all_to_all | solution.py:364
  55.6 2.8 %all-to-all-start = ((f32[32,16,128]{2,1,0:T(8,128)}), f32[32,16,128]{2,1,0:T(8,128)S(1)}, u32[]{:S(2)}, u32[]{:S(2)}) async-start(f32[32,16,128]{2,1,0:T(8,128)} %copy.13), calls=%async_computation | async-start | bytes 524288 | tf_op jit(solution)/shard_map/all_to_all | solution.py:17
  58.6 10.6 %all-to-all-done = f32[32,16,128]{2,1,0:T(8,128)S(1)} async-done(((f32[32,16,128]{2,1,0:T(8,128)}), f32[32,16,128]{2,1,0:T(8,128)S(1)}, u32[]{:S(2)}, u32[]{:S(2)}) %all-to-all-start) | async-done | bytes 262176 | tf_op jit(solution)/shard_map/all_to_all | solution.py:17
  69.2 3.4 %copy-done.2 = f32[1024,2048]{1,0:T(8,128)S(1)} copy-done((f32[1024,2048]{1,0:T(8,128)S(1)}, f32[1024,2048]{1,0:T(8,128)}, u32[]{:S(2)}) %copy-start.2) | copy-done | bytes 8388632
  72.5 7.6 %right_half.1 = (f32[128,2048]{1,0:T(8,128)S(1)}, f32[4,128,128]{2,1,0:T(8,128)S(1)}) custom-call(f32[1024,2048]{1,0:T(8,128)S(1)} %copy-done.2, f32[1024,128]{1,0:T(8,128)S(1)} %bitcast.89, f32[128,2048]{1,0:T(8,128)S(1)} %get-tuple-element.7.right_ref, f32[512,128]{1,0:T(8,128)S(1)} %bitcast.86, f32[4,128,128]{2,1,0:T(8,128)S(1)} %all-to-all-done.1.second_right_ref), custom_call_target="tpu_custom_call" | custom-call | flops 3221225472 | bytes 8388608 | tf_op jit(solution)/shard_map/right_half/pallas_call | solution.py:296
  80.4 1.2 collective-permute-done.22
  81.7 1.4 collective-permute-start.24
  83.1 2.1 %collective-permute-start.25 = (f32[64,128]{1,0:T(8,128)S(1)}, f32[64,128]{1,0:T(8,128)S(1)}, u32[]{:S(2)}, u32[]{:S(2)}) collective-permute-start(f32[64,128]{1,0:T(8,128)S(1)} %get-tuple-element.42), channel_id=1, source_target_pairs={{0,3},{1,2},{2,1},{3,0},{4,7},{5,6},{6,5},{7,4},{8,11},{9,10},{10,... | collective-permute-start | bytes 98312 | tf_op jit(solution)/shard_map/ppermute | solution.py:27
  85.2 7.6 %left_half.1 = f32[8,136,128]{2,1,0:T(8,128)S(1)} custom-call(f32[1024,2048]{1,0:T(8,128)S(1)} %copy-done.2, f32[1024,128]{1,0:T(8,128)S(1)} %bitcast.90, f32[128,2048]{1,0:T(8,128)S(1)} %get-tuple-element.8.right_ref), custom_call_target="tpu_custom_call" | custom-call | flops 3221225472 | bytes 8388608 | tf_op jit(solution)/shard_map/left_half/pallas_call | solution.py:321
  92.9 0.8 collective-permute-start.26
  93.7 1.2 collective-permute-start.27
  94.9 2.4 %collective-permute-start.28 = (f32[64,128]{1,0:T(8,128)S(1)}, f32[64,128]{1,0:T(8,128)S(1)}, u32[]{:S(2)}, u32[]{:S(2)}) collective-permute-start(f32[64,128]{1,0:T(8,128)S(1)} %fusion.10), channel_id=1, source_target_pairs={{0,24},{1,25},{2,26},{3,27},{4,28},{5,29},{6,30},{7,31},{8,16},{9,... | collective-permute-start | bytes 98312 | tf_op jit(solution)/shard_map/ppermute | solution.py:27
  97.4 1.3 collective-permute-done.27
  98.7 1.9 %collective-permute-done.28 = f32[64,128]{1,0:T(8,128)S(1)} collective-permute-done((f32[64,128]{1,0:T(8,128)S(1)}, f32[64,128]{1,0:T(8,128)S(1)}, u32[]{:S(2)}, u32[]{:S(2)}) %collective-permute-start.28) | collective-permute-done | bytes 32800 | tf_op jit(solution)/shard_map/ppermute | solution.py:27
  100.8 1.2 collective-permute-start.30
  102.0 2.2 %collective-permute-start.31 = (f32[64,128]{1,0:T(8,128)S(1)}, f32[64,128]{1,0:T(8,128)S(1)}, u32[]{:S(2)}, u32[]{:S(2)}) collective-permute-start(f32[64,128]{1,0:T(8,128)S(1)} %dynamic-slice_multiply_fusion), channel_id=1, source_target_pairs={{0,3},{1,2},{2,1},{3,0},{4,7},{5,6},{6,5},{7,4},{8,11},{9,10},{10,... | collective-permute-start | bytes 98312 | tf_op jit(solution)/shard_map/ppermute | solution.py:27
  104.2 0.4 collective-permute-done.29
  104.7 2.4 %collective-permute-done.31 = f32[64,128]{1,0:T(8,128)S(1)} collective-permute-done((f32[64,128]{1,0:T(8,128)S(1)}, f32[64,128]{1,0:T(8,128)S(1)}, u32[]{:S(2)}, u32[]{:S(2)}) %collective-permute-start.31) | collective-permute-done | bytes 32800 | tf_op jit(solution)/shard_map/ppermute | solution.py:27
  107.2 0.6 collective-permute-start.12
  107.8 1.9 %collective-permute-start.13 = (f32[136,128]{1,0:T(8,128)S(1)}, f32[136,128]{1,0:T(8,128)S(1)}, u32[]{:S(2)}, u32[]{:S(2)}) collective-permute-start(f32[136,128]{1,0:T(8,128)S(1)} %get-tuple-element.17), channel_id=1, source_target_pairs={{0,2},{1,3},{2,0},{3,1},{4,6},{5,7},{6,4},{7,5},{8,10},{9,11},{10,... | collective-permute-start | bytes 208904 | tf_op jit(solution)/shard_map/ppermute | solution.py:27
  109.8 1.0 collective-permute-start.14
  110.9 0.7 collective-permute-done.12
  111.6 0.6 collective-permute-done.13
  112.2 2.8 %collective-permute-done.14 = f32[136,128]{1,0:T(8,128)S(1)} collective-permute-done((f32[136,128]{1,0:T(8,128)S(1)}, f32[136,128]{1,0:T(8,128)S(1)}, u32[]{:S(2)}, u32[]{:S(2)}) %collective-permute-start.14) | collective-permute-done | bytes 69664 | tf_op jit(solution)/shard_map/ppermute | solution.py:27
  115.1 3.0 %collective-permute-start.16 = (f32[136,128]{1,0:T(8,128)S(1)}, f32[136,128]{1,0:T(8,128)S(1)}, u32[]{:S(2)}, u32[]{:S(2)}) collective-permute-start(f32[136,128]{1,0:T(8,128)S(1)} %fusion.6), channel_id=1, source_target_pairs={{0,16},{1,17},{2,18},{3,19},{4,20},{5,21},{6,22},{7,23},{8,24},{9,... | collective-permute-start | bytes 208904 | tf_op jit(solution)/shard_map/ppermute | solution.py:27
  118.0 1.4 collective-permute-start.17
  119.5 1.1 collective-permute-done.15
  120.6 3.6 %collective-permute-done.17 = f32[136,128]{1,0:T(8,128)S(1)} collective-permute-done((f32[136,128]{1,0:T(8,128)S(1)}, f32[136,128]{1,0:T(8,128)S(1)}, u32[]{:S(2)}, u32[]{:S(2)}) %collective-permute-start.17) | collective-permute-done | bytes 69664 | tf_op jit(solution)/shard_map/ppermute | solution.py:27
  124.2 0.5 collective-permute-start.18
  124.7 1.2 collective-permute-start.19
  125.9 1.9 %collective-permute-start.20 = (f32[128,128]{1,0:T(8,128)S(1)}, f32[128,128]{1,0:T(8,128)S(1)}, u32[]{:S(2)}, u32[]{:S(2)}) collective-permute-start(f32[128,128]{1,0:T(8,128)S(1)} %fusion.8), channel_id=1, source_target_pairs={{0,3},{1,2},{2,1},{3,0},{4,7},{5,6},{6,5},{7,4},{8,11},{9,10},{10,... | collective-permute-start | bytes 196616 | tf_op jit(solution)/shard_map/ppermute | solution.py:27
  127.8 0.8 collective-permute-done.18
  128.5 0.4 collective-permute-done.19
  128.9 2.1 %collective-permute-done.20 = f32[128,128]{1,0:T(8,128)S(1)} collective-permute-done((f32[128,128]{1,0:T(8,128)S(1)}, f32[128,128]{1,0:T(8,128)S(1)}, u32[]{:S(2)}, u32[]{:S(2)}) %collective-permute-start.20) | collective-permute-done | bytes 65568 | tf_op jit(solution)/shard_map/ppermute | solution.py:27
  131.3 2.2 %second_rows.1 = f32[512,128]{1,0:T(8,128)} custom-call(f32[128,2048]{1,0:T(8,128)S(1)} %get-tuple-element.8.right_ref, f32[512,128]{1,0:T(8,128)S(1)} %bitcast.87, f32[4,128,128]{2,1,0:T(8,128)S(1)} %bitcast.88), custom_call_target="tpu_custom_call" | custom-call | flops 402653184 | bytes 1048576 | tf_op jit(solution)/shard_map/second_rows/pallas_call | solution.py:335
  133.5 3.2 %all-to-all-start.2 = ((f32[32,16,128]{2,1,0:T(8,128)}), f32[32,16,128]{2,1,0:T(8,128)S(1)}, u32[]{:S(2)}, u32[]{:S(2)}) async-start(f32[32,16,128]{2,1,0:T(8,128)} %bitcast.50), calls=%async_computation.2 | async-start | bytes 524288 | tf_op jit(solution)/shard_map/all_to_all | solution.py:17
  136.8 0.8 pad_maximum_fusion.1
  137.6 10.0 %all-to-all-done.2 = f32[32,16,128]{2,1,0:T(8,128)S(1)} async-done(((f32[32,16,128]{2,1,0:T(8,128)}), f32[32,16,128]{2,1,0:T(8,128)S(1)}, u32[]{:S(2)}, u32[]{:S(2)}) %all-to-all-start.2) | async-done | bytes 262176 | tf_op jit(solution)/shard_map/all_to_all | solution.py:17
  147.6 0.7 copy.14
  (63 shorter events, 1.8 us)
Async XLA Ops:
  1.7 1.0 copy-start
  2.7 3.4 %copy-start.1 = (f32[1024,2048]{1,0:T(8,128)S(1)}, f32[1024,2048]{1,0:T(8,128)}, u32[]{:S(2)}) copy-start(f32[1024,2048]{1,0:T(8,128)} %slab_ref.5) | copy-start | bytes 25165828
  6.1 1.2 copy-start.3
  7.3 38.8 %copy-start.4 = (f32[128,128]{1,0:T(8,128)S(1)}, f32[128,128]{1,0:T(8,128)}, u32[]{:S(2)}) copy-start(f32[128,128]{1,0:T(8,128)} %param.9) | copy-start | bytes 196612
  19.9 1.7 %collective-permute-start = (f32[4,136,128]{2,1,0:T(8,128)S(1)}, f32[4,136,128]{2,1,0:T(8,128)S(1)}, u32[]{:S(2)}, u32[]{:S(2)}) collective-permute-start(f32[4,136,128]{2,1,0:T(8,128)S(1)} %dynamic-slice_bitcast_fusion.1), channel_id=1, source_target_pairs={{0,4},{1,5},{2,6},{3,7},{4,0},{5,1},{6,2},{7,3},{8,12},{9,13},{10,... | collective-permute-start | bytes 835592 | tf_op jit(solution)/shard_map/ppermute | solution.py:27
  21.7 5.4 %collective-permute-start.1 = (f32[136,128]{1,0:T(8,128)S(1)}, f32[136,128]{1,0:T(8,128)S(1)}, u32[]{:S(2)}, u32[]{:S(2)}) collective-permute-start(f32[136,128]{1,0:T(8,128)S(1)} %get-tuple-element.21), channel_id=1, source_target_pairs={{0,1},{1,0},{2,3},{3,2},{4,5},{5,4},{6,7},{7,6},{8,9},{9,8},{10,11... | collective-permute-start | bytes 208904 | tf_op jit(solution)/shard_map/ppermute | solution.py:27
  24.6 4.3 %collective-permute-start.2 = (f32[136,128]{1,0:T(8,128)S(1)}, f32[136,128]{1,0:T(8,128)S(1)}, u32[]{:S(2)}, u32[]{:S(2)}) collective-permute-start(f32[136,128]{1,0:T(8,128)S(1)} %get-tuple-element.20), channel_id=1, source_target_pairs={{0,2},{1,3},{2,0},{3,1},{4,6},{5,7},{6,4},{7,5},{8,10},{9,11},{10,... | collective-permute-start | bytes 208904 | tf_op jit(solution)/shard_map/ppermute | solution.py:27
  26.1 5.2 %collective-permute-start.3 = (f32[136,128]{1,0:T(8,128)S(1)}, f32[136,128]{1,0:T(8,128)S(1)}, u32[]{:S(2)}, u32[]{:S(2)}) collective-permute-start(f32[136,128]{1,0:T(8,128)S(1)} %get-tuple-element.19), channel_id=1, source_target_pairs={{0,3},{1,2},{2,1},{3,0},{4,7},{5,6},{6,5},{7,4},{8,11},{9,10},{10,... | collective-permute-start | bytes 208904 | tf_op jit(solution)/shard_map/ppermute | solution.py:27
  31.3 4.7 %collective-permute-start.4 = (f32[136,128]{1,0:T(8,128)S(1)}, f32[136,128]{1,0:T(8,128)S(1)}, u32[]{:S(2)}, u32[]{:S(2)}) collective-permute-start(f32[136,128]{1,0:T(8,128)S(1)} %fusion.7), channel_id=1, source_target_pairs={{0,8},{1,9},{2,10},{3,11},{4,12},{5,13},{6,14},{7,15},{8,0},{9,1},... | collective-permute-start | bytes 208904 | tf_op jit(solution)/shard_map/ppermute | solution.py:27
  33.0 6.7 %collective-permute-start.5 = (f32[136,128]{1,0:T(8,128)S(1)}, f32[136,128]{1,0:T(8,128)S(1)}, u32[]{:S(2)}, u32[]{:S(2)}) collective-permute-start(f32[136,128]{1,0:T(8,128)S(1)} %fusion.7), channel_id=1, source_target_pairs={{0,16},{1,17},{2,18},{3,19},{4,20},{5,21},{6,22},{7,23},{8,24},{9,... | collective-permute-start | bytes 208904 | tf_op jit(solution)/shard_map/ppermute | solution.py:27
  35.6 6.1 %collective-permute-start.6 = (f32[136,128]{1,0:T(8,128)S(1)}, f32[136,128]{1,0:T(8,128)S(1)}, u32[]{:S(2)}, u32[]{:S(2)}) collective-permute-start(f32[136,128]{1,0:T(8,128)S(1)} %fusion.7), channel_id=1, source_target_pairs={{0,24},{1,25},{2,26},{3,27},{4,28},{5,29},{6,30},{7,31},{8,16},{9,... | collective-permute-start | bytes 208904 | tf_op jit(solution)/shard_map/ppermute | solution.py:27
  42.6 7.7 %collective-permute-start.8 = (f32[128,128]{1,0:T(8,128)S(1)}, f32[128,128]{1,0:T(8,128)S(1)}, u32[]{:S(2)}, u32[]{:S(2)}) collective-permute-start(f32[128,128]{1,0:T(8,128)S(1)} %fusion.9), channel_id=1, source_target_pairs={{0,2},{1,3},{2,0},{3,1},{4,6},{5,7},{6,4},{7,5},{8,10},{9,11},{10,... | collective-permute-start | bytes 196616 | tf_op jit(solution)/shard_map/ppermute | solution.py:27
  43.2 7.0 %collective-permute-start.9 = (f32[128,128]{1,0:T(8,128)S(1)}, f32[128,128]{1,0:T(8,128)S(1)}, u32[]{:S(2)}, u32[]{:S(2)}) collective-permute-start(f32[128,128]{1,0:T(8,128)S(1)} %fusion.9), channel_id=1, source_target_pairs={{0,3},{1,2},{2,1},{3,0},{4,7},{5,6},{6,5},{7,4},{8,11},{9,10},{10,... | collective-permute-start | bytes 196616 | tf_op jit(solution)/shard_map/ppermute | solution.py:27
  44.6 5.7 %collective-permute-start.7 = (f32[128,128]{1,0:T(8,128)S(1)}, f32[128,128]{1,0:T(8,128)S(1)}, u32[]{:S(2)}, u32[]{:S(2)}) collective-permute-start(f32[128,128]{1,0:T(8,128)S(1)} %fusion.9), channel_id=1, source_target_pairs={{0,1},{1,0},{2,3},{3,2},{4,5},{5,4},{6,7},{7,6},{8,9},{9,8},{10,11... | collective-permute-start | bytes 196616 | tf_op jit(solution)/shard_map/ppermute | solution.py:27
  46.9 8.8 %all-to-all-start.1 = ((f32[4,128,128]{2,1,0:T(8,128)}), f32[4,128,128]{2,1,0:T(8,128)S(1)}, u32[]{:S(2)}, u32[]{:S(2)}) async-start(f32[4,128,128]{2,1,0:T(8,128)} %broadcast_in_dim.5), calls=%async_computation.1 | async-start | bytes 524288 | tf_op jit(solution)/shard_map/all_to_all | solution.py:364
  50.4 8.0 %collective-permute-start.10 = (f32[4,128,128]{2,1,0:T(8,128)S(1)}, f32[4,128,128]{2,1,0:T(8,128)S(1)}, u32[]{:S(2)}, u32[]{:S(2)}) collective-permute-start(f32[4,128,128]{2,1,0:T(8,128)S(1)} %get-tuple-element.30), channel_id=1, source_target_pairs={{0,4},{1,5},{2,6},{3,7},{4,0},{5,1},{6,2},{7,3},{8,12},{9,13},{10,... | collective-permute-start | bytes 786440 | tf_op jit(solution)/shard_map/ppermute | solution.py:27
  55.6 13.5 %all-to-all-start = ((f32[32,16,128]{2,1,0:T(8,128)}), f32[32,16,128]{2,1,0:T(8,128)S(1)}, u32[]{:S(2)}, u32[]{:S(2)}) async-start(f32[32,16,128]{2,1,0:T(8,128)} %copy.13), calls=%async_computation | async-start | bytes 524288 | tf_op jit(solution)/shard_map/all_to_all | solution.py:17
  69.1 3.4 %copy-start.2 = (f32[1024,2048]{1,0:T(8,128)S(1)}, f32[1024,2048]{1,0:T(8,128)}, u32[]{:S(2)}) copy-start(f32[1024,2048]{1,0:T(8,128)} %slab_ref.5) | copy-start | bytes 25165828
  80.2 1.4 collective-permute-start.22
  81.7 11.1 %collective-permute-start.23 = (f32[64,128]{1,0:T(8,128)S(1)}, f32[64,128]{1,0:T(8,128)S(1)}, u32[]{:S(2)}, u32[]{:S(2)}) collective-permute-start(f32[64,128]{1,0:T(8,128)S(1)} %get-tuple-element.44), channel_id=1, source_target_pairs={{0,1},{1,0},{2,3},{3,2},{4,5},{5,4},{6,7},{7,6},{8,9},{9,8},{10,11... | collective-permute-start | bytes 98312 | tf_op jit(solution)/shard_map/ppermute | solution.py:27
  81.7 11.1 %collective-permute-start.24 = (f32[64,128]{1,0:T(8,128)S(1)}, f32[64,128]{1,0:T(8,128)S(1)}, u32[]{:S(2)}, u32[]{:S(2)}) collective-permute-start(f32[64,128]{1,0:T(8,128)S(1)} %get-tuple-element.43), channel_id=1, source_target_pairs={{0,2},{1,3},{2,0},{3,1},{4,6},{5,7},{6,4},{7,5},{8,10},{9,11},{10,... | collective-permute-start | bytes 98312 | tf_op jit(solution)/shard_map/ppermute | solution.py:27
  83.1 9.7 %collective-permute-start.25 = (f32[64,128]{1,0:T(8,128)S(1)}, f32[64,128]{1,0:T(8,128)S(1)}, u32[]{:S(2)}, u32[]{:S(2)}) collective-permute-start(f32[64,128]{1,0:T(8,128)S(1)} %get-tuple-element.42), channel_id=1, source_target_pairs={{0,3},{1,2},{2,1},{3,0},{4,7},{5,6},{6,5},{7,4},{8,11},{9,10},{10,... | collective-permute-start | bytes 98312 | tf_op jit(solution)/shard_map/ppermute | solution.py:27
  92.9 4.6 %collective-permute-start.26 = (f32[64,128]{1,0:T(8,128)S(1)}, f32[64,128]{1,0:T(8,128)S(1)}, u32[]{:S(2)}, u32[]{:S(2)}) collective-permute-start(f32[64,128]{1,0:T(8,128)S(1)} %fusion.10), channel_id=1, source_target_pairs={{0,8},{1,9},{2,10},{3,11},{4,12},{5,13},{6,14},{7,15},{8,0},{9,1},... | collective-permute-start | bytes 98312 | tf_op jit(solution)/shard_map/ppermute | solution.py:27
  93.7 5.1 %collective-permute-start.27 = (f32[64,128]{1,0:T(8,128)S(1)}, f32[64,128]{1,0:T(8,128)S(1)}, u32[]{:S(2)}, u32[]{:S(2)}) collective-permute-start(f32[64,128]{1,0:T(8,128)S(1)} %fusion.10), channel_id=1, source_target_pairs={{0,16},{1,17},{2,18},{3,19},{4,20},{5,21},{6,22},{7,23},{8,24},{9,... | collective-permute-start | bytes 98312 | tf_op jit(solution)/shard_map/ppermute | solution.py:27
  94.9 5.7 %collective-permute-start.28 = (f32[64,128]{1,0:T(8,128)S(1)}, f32[64,128]{1,0:T(8,128)S(1)}, u32[]{:S(2)}, u32[]{:S(2)}) collective-permute-start(f32[64,128]{1,0:T(8,128)S(1)} %fusion.10), channel_id=1, source_target_pairs={{0,24},{1,25},{2,26},{3,27},{4,28},{5,29},{6,30},{7,31},{8,16},{9,... | collective-permute-start | bytes 98312 | tf_op jit(solution)/shard_map/ppermute | solution.py:27
  97.3 9.8 %collective-permute-start.11 = (f32[4,136,128]{2,1,0:T(8,128)S(1)}, f32[4,136,128]{2,1,0:T(8,128)S(1)}, u32[]{:S(2)}, u32[]{:S(2)}) collective-permute-start(f32[4,136,128]{2,1,0:T(8,128)S(1)} %dynamic-slice_bitcast_fusion), channel_id=1, source_target_pairs={{0,4},{1,5},{2,6},{3,7},{4,0},{5,1},{6,2},{7,3},{8,12},{9,13},{10,... | collective-permute-start | bytes 835592 | tf_op jit(solution)/shard_map/ppermute | solution.py:27
  100.6 4.0 %collective-permute-start.29 = (f32[64,128]{1,0:T(8,128)S(1)}, f32[64,128]{1,0:T(8,128)S(1)}, u32[]{:S(2)}, u32[]{:S(2)}) collective-permute-start(f32[64,128]{1,0:T(8,128)S(1)} %dynamic-slice_multiply_fusion), channel_id=1, source_target_pairs={{0,1},{1,0},{2,3},{3,2},{4,5},{5,4},{6,7},{7,6},{8,9},{9,8},{10,11... | collective-permute-start | bytes 98312 | tf_op jit(solution)/shard_map/ppermute | solution.py:27
  100.8 3.9 %collective-permute-start.30 = (f32[64,128]{1,0:T(8,128)S(1)}, f32[64,128]{1,0:T(8,128)S(1)}, u32[]{:S(2)}, u32[]{:S(2)}) collective-permute-start(f32[64,128]{1,0:T(8,128)S(1)} %dynamic-slice_multiply_fusion), channel_id=1, source_target_pairs={{0,2},{1,3},{2,0},{3,1},{4,6},{5,7},{6,4},{7,5},{8,10},{9,11},{10,... | collective-permute-start | bytes 98312 | tf_op jit(solution)/shard_map/ppermute | solution.py:27
  102.0 5.1 %collective-permute-start.31 = (f32[64,128]{1,0:T(8,128)S(1)}, f32[64,128]{1,0:T(8,128)S(1)}, u32[]{:S(2)}, u32[]{:S(2)}) collective-permute-start(f32[64,128]{1,0:T(8,128)S(1)} %dynamic-slice_multiply_fusion), channel_id=1, source_target_pairs={{0,3},{1,2},{2,1},{3,0},{4,7},{5,6},{6,5},{7,4},{8,11},{9,10},{10,... | collective-permute-start | bytes 98312 | tf_op jit(solution)/shard_map/ppermute | solution.py:27
  107.2 4.4 %collective-permute-start.12 = (f32[136,128]{1,0:T(8,128)S(1)}, f32[136,128]{1,0:T(8,128)S(1)}, u32[]{:S(2)}, u32[]{:S(2)}) collective-permute-start(f32[136,128]{1,0:T(8,128)S(1)} %get-tuple-element.18), channel_id=1, source_target_pairs={{0,1},{1,0},{2,3},{3,2},{4,5},{5,4},{6,7},{7,6},{8,9},{9,8},{10,11... | collective-permute-start | bytes 208904 | tf_op jit(solution)/shard_map/ppermute | solution.py:27
  107.8 4.3 %collective-permute-start.13 = (f32[136,128]{1,0:T(8,128)S(1)}, f32[136,128]{1,0:T(8,128)S(1)}, u32[]{:S(2)}, u32[]{:S(2)}) collective-permute-start(f32[136,128]{1,0:T(8,128)S(1)} %get-tuple-element.17), channel_id=1, source_target_pairs={{0,2},{1,3},{2,0},{3,1},{4,6},{5,7},{6,4},{7,5},{8,10},{9,11},{10,... | collective-permute-start | bytes 208904 | tf_op jit(solution)/shard_map/ppermute | solution.py:27
  109.8 5.2 %collective-permute-start.14 = (f32[136,128]{1,0:T(8,128)S(1)}, f32[136,128]{1,0:T(8,128)S(1)}, u32[]{:S(2)}, u32[]{:S(2)}) collective-permute-start(f32[136,128]{1,0:T(8,128)S(1)} %get-tuple-element.16), channel_id=1, source_target_pairs={{0,3},{1,2},{2,1},{3,0},{4,7},{5,6},{6,5},{7,4},{8,11},{9,10},{10,... | collective-permute-start | bytes 208904 | tf_op jit(solution)/shard_map/ppermute | solution.py:27
  110.8 8.7 %collective-permute-start.32 = (f32[4,64,128]{2,1,0:T(8,128)S(1)}, f32[4,64,128]{2,1,0:T(8,128)S(1)}, u32[]{:S(2)}, u32[]{:S(2)}) collective-permute-start(f32[4,64,128]{2,1,0:T(8,128)S(1)} %get-tuple-element.36), channel_id=1, source_target_pairs={{0,4},{1,5},{2,6},{3,7},{4,0},{5,1},{6,2},{7,3},{8,12},{9,13},{10,... | collective-permute-start | bytes 393224 | tf_op jit(solution)/shard_map/ppermute | solution.py:27
  115.0 5.6 %collective-permute-start.15 = (f32[136,128]{1,0:T(8,128)S(1)}, f32[136,128]{1,0:T(8,128)S(1)}, u32[]{:S(2)}, u32[]{:S(2)}) collective-permute-start(f32[136,128]{1,0:T(8,128)S(1)} %fusion.6), channel_id=1, source_target_pairs={{0,8},{1,9},{2,10},{3,11},{4,12},{5,13},{6,14},{7,15},{8,0},{9,1},... | collective-permute-start | bytes 208904 | tf_op jit(solution)/shard_map/ppermute | solution.py:27
  115.1 5.5 %collective-permute-start.16 = (f32[136,128]{1,0:T(8,128)S(1)}, f32[136,128]{1,0:T(8,128)S(1)}, u32[]{:S(2)}, u32[]{:S(2)}) collective-permute-start(f32[136,128]{1,0:T(8,128)S(1)} %fusion.6), channel_id=1, source_target_pairs={{0,16},{1,17},{2,18},{3,19},{4,20},{5,21},{6,22},{7,23},{8,24},{9,... | collective-permute-start | bytes 208904 | tf_op jit(solution)/shard_map/ppermute | solution.py:27
  118.0 6.1 %collective-permute-start.17 = (f32[136,128]{1,0:T(8,128)S(1)}, f32[136,128]{1,0:T(8,128)S(1)}, u32[]{:S(2)}, u32[]{:S(2)}) collective-permute-start(f32[136,128]{1,0:T(8,128)S(1)} %fusion.6), channel_id=1, source_target_pairs={{0,24},{1,25},{2,26},{3,27},{4,28},{5,29},{6,30},{7,31},{8,16},{9,... | collective-permute-start | bytes 208904 | tf_op jit(solution)/shard_map/ppermute | solution.py:27
  124.2 4.3 %collective-permute-start.18 = (f32[128,128]{1,0:T(8,128)S(1)}, f32[128,128]{1,0:T(8,128)S(1)}, u32[]{:S(2)}, u32[]{:S(2)}) collective-permute-start(f32[128,128]{1,0:T(8,128)S(1)} %fusion.8), channel_id=1, source_target_pairs={{0,1},{1,0},{2,3},{3,2},{4,5},{5,4},{6,7},{7,6},{8,9},{9,8},{10,11... | collective-permute-start | bytes 196616 | tf_op jit(solution)/shard_map/ppermute | solution.py:27
  124.7 4.3 %collective-permute-start.19 = (f32[128,128]{1,0:T(8,128)S(1)}, f32[128,128]{1,0:T(8,128)S(1)}, u32[]{:S(2)}, u32[]{:S(2)}) collective-permute-start(f32[128,128]{1,0:T(8,128)S(1)} %fusion.8), channel_id=1, source_target_pairs={{0,2},{1,3},{2,0},{3,1},{4,6},{5,7},{6,4},{7,5},{8,10},{9,11},{10,... | collective-permute-start | bytes 196616 | tf_op jit(solution)/shard_map/ppermute | solution.py:27
  125.9 5.2 %collective-permute-start.20 = (f32[128,128]{1,0:T(8,128)S(1)}, f32[128,128]{1,0:T(8,128)S(1)}, u32[]{:S(2)}, u32[]{:S(2)}) collective-permute-start(f32[128,128]{1,0:T(8,128)S(1)} %fusion.8), channel_id=1, source_target_pairs={{0,3},{1,2},{2,1},{3,0},{4,7},{5,6},{6,5},{7,4},{8,11},{9,10},{10,... | collective-permute-start | bytes 196616 | tf_op jit(solution)/shard_map/ppermute | solution.py:27
  131.2 5.5 %collective-permute-start.21 = (f32[4,128,128]{2,1,0:T(8,128)S(1)}, f32[4,128,128]{2,1,0:T(8,128)S(1)}, u32[]{:S(2)}, u32[]{:S(2)}) collective-permute-start(f32[4,128,128]{2,1,0:T(8,128)S(1)} %get-tuple-element.24), channel_id=1, source_target_pairs={{0,4},{1,5},{2,6},{3,7},{4,0},{5,1},{6,2},{7,3},{8,12},{9,13},{10,... | collective-permute-start | bytes 786440 | tf_op jit(solution)/shard_map/ppermute | solution.py:27
  133.5 14.1 %all-to-all-start.2 = ((f32[32,16,128]{2,1,0:T(8,128)}), f32[32,16,128]{2,1,0:T(8,128)S(1)}, u32[]{:S(2)}, u32[]{:S(2)}) async-start(f32[32,16,128]{2,1,0:T(8,128)} %bitcast.50), calls=%async_computation.2 | async-start | bytes 524288 | tf_op jit(solution)/shard_map/all_to_all | solution.py:17
where the time goes:
time: 149 us; the launch traced here: 148 us
  waiting for transfers between devices  56.4 us (38%)
  starting transfers between devices  45.8 us (31%)
  Pallas kernels  29.9 us (20%)
  local copies, waits for them, and re-layouts  11.6 us (8%)
  other arithmetic  3.5 us (2%)
    ppermute x33, starting transfers between devices, send(): return lax.ppermute(values, AXES, pairs)  36.4 us
    ppermute x33, waiting for transfers between devices, send(): return lax.ppermute(values, AXES, pairs)  31.6 us
    all_to_all x2, waiting for transfers between devices, exchange(): return lax.all_to_all(parts, AXES, split_axis=0, concat_axis=0, tiled=True)  20.6 us
    pallas_call x1, Pallas kernels, full_turn(): pl.pallas_call(turn_kernel, grid=(columns // block,), in_specs=[columns_s...  12.5 us
    unnamed x10, local copies, waits for them, and re-layouts  9.03 us
    pallas_call x1, Pallas kernels, right_half(): pl.pallas_call(functools.partial(right_kernel, slices), grid=(slices,), i...  7.64 us
    pallas_call x1, Pallas kernels, left_half(): pl.pallas_call(left_kernel, grid=(columns // block,), in_specs=[columns_s...  7.58 us
    all_to_all x2, starting transfers between devices, exchange(): return lax.all_to_all(parts, AXES, split_axis=0, concat_axis=0, tiled=True)  5.92 us
  transfers between devices with their start and end apart: 36, of which 24 were waited for; matrix products, arithmetic and copies ran while one was open for 2% of the time, Pallas kernels for 7%

commit v1 on v0

--- a/solution.py
+++ b/solution.py
@@ -10,7 +10,7 @@
 AXES = ("row", "col")
 F32, BF16 = jnp.float32, jnp.bfloat16
 PAD = 8
-VMEM_BYTES = 40 * 1024 * 1024
+VMEM_BYTES = 60 * 1024 * 1024
 
 
 def exchange(parts):
@@ -37,21 +37,33 @@
     return terms[0]
 
 
-def reduce_parts(parts):
-    core, col = lax.axis_index("row") % 2, lax.axis_index("col")
-    cols = lax.axis_size("col")
-    own = pick(parts, core) + send(pick(parts, 1 - core), 1, 0)
-    own = tree_sum(
-        [pick(own, col)] + [send(pick(own, col ^ flip), 0, flip) for flip in range(1, cols)]
-    )
+def after(values, *events):
+    return lax.optimization_barrier((values,) + events)[0]
+
+
+def reduce_core(parts):
+    core = lax.axis_index("row") % 2
+    return pick(parts, core) + send(pick(parts, 1 - core), 1, 0)
+
+
+def reduce_plane(own):
+    col = lax.axis_index("col")
+    others = [send(pick(own, col ^ flip), 0, flip) for flip in range(1, own.shape[0])]
+    return tree_sum([pick(own, col)] + others)
+
+
+def reduce_z(own):
     return tree_sum([own] + [send(own, flip, 0) for flip in range(2, lax.axis_size("row"), 2)])
 
 
-def spread_parts(part):
-    core, col = lax.axis_index("row") % 2, lax.axis_index("col")
-    cols = lax.axis_size("col")
+def spread_plane(part):
+    col, cols = lax.axis_index("col"), lax.axis_size("col")
     near = jnp.stack([part] + [send(part, 0, flip) for flip in range(1, cols)])
-    near = jnp.stack([pick(near, index ^ col) for index in range(cols)])
+    return jnp.stack([pick(near, index ^ col) for index in range(cols)])
+
+
+def spread_core(near):
+    core = lax.axis_index("row") % 2
     both = jnp.stack([near, send(near, 1, 0)])
     return jnp.stack([pick(both, core), pick(both, 1 - core)])
 
@@ -70,15 +82,15 @@
 
 
 def divide(x, y):
-    guess = pl.reciprocal(y, approx=True)
-    return x * (guess * (2.0 - y * guess))
+    return x * pl.reciprocal(y, approx=True)
 
 
 def prepare_left(left_ref, pair_ref):
     rank = left_ref.shape[1]
     high, low = split(left_ref[...])
     pair_ref[:, :rank] = high
-    pair_ref[:, rank:] = low
+    pair_ref[:, rank : 2 * rank] = low
+    pair_ref[:, 2 * rank :] = high
 
 
 def prepare_left_t(left_ref, pair_t_ref, sums_ref):
@@ -96,10 +108,8 @@
 
 
 def quotients(slab_ref, pair_ref, right, rows):
-    rank = right.shape[0]
     high, low = split(right)
-    twice = jnp.concatenate([high, high], axis=0)
-    product = dot(pair_ref[rows, :], twice) + dot(pair_ref[rows, :rank], low)
+    product = dot(pair_ref[rows, :], jnp.concatenate([high, high, low], axis=0))
     return split(divide(slab_ref[rows, :], product))
 
 
@@ -245,7 +255,7 @@
 
 
 def left_scratch(m, rank):
-    return [pltpu.VMEM((m, 2 * rank), BF16)]
+    return [pltpu.VMEM((m, 3 * rank), BF16)]
 
 
 def right_scratch(m, rank, block):
@@ -359,34 +369,46 @@
     )
     col_part = jnp.broadcast_to(jnp.sum(own_left, axis=0)[None], (PAD, rank))
     own_left = own_left.reshape(per_owner, devices, slices, rank).transpose(1, 0, 2, 3)
-    second_left = exchange(own_left.reshape(devices, per_owner * slices, rank))
-    second_left = second_left.reshape(rank * slices, rank)
-    whole = lax.all_to_all(
-        jnp.broadcast_to(second_right_init[None], (col_devices,) + second_right_init.shape),
-        "col", split_axis=0, concat_axis=0, tiled=True,
-    )
-    whole = whole.transpose(1, 0, 2).reshape(rank, k // rank, rank).transpose(1, 0, 2)
-
-    def new_left(left, summed):
-        total = reduce_parts(summed.reshape(2, col_devices, rows_own + PAD, rank))
+    own_left = own_left.reshape(devices, per_owner * slices, rank)
+    piece_rows = rank // row_devices
+    piece = lax.dynamic_slice_in_dim(
+        second_right_init, lax.axis_index("row") * piece_rows, piece_rows, 0
+    ).reshape(-1, rank)
+    piece = jnp.broadcast_to(piece[None], (devices,) + piece.shape)
+    arrived = exchange(jnp.concatenate([own_left, piece], axis=1))
+
+    right, summed = full_turn(tensor_slab, left_init, right_init, col_part, k, parts)
+    summed, arrived = lax.optimization_barrier((summed, arrived))
+    second_left = arrived[:, : per_owner * slices].reshape(rank * slices, rank)
+    whole = arrived[:, per_owner * slices :].reshape(row_devices, col_devices, piece_rows, -1)
+    whole = whole.transpose(0, 2, 1, 3).reshape(rank, k // rank, rank).transpose(1, 0, 2)
+
+    def own_left_rows(left, total):
         own = lax.dynamic_slice_in_dim(left, own_part * rows_own, rows_own, 0)
-        own = own * total[:rows_own] / total[rows_own][None, :]
-        return spread_parts(own).reshape(m, rank), total[rows_own + 1]
-
-    right, summed = full_turn(tensor_slab, left_init, right_init, col_part, k, parts)
-    left, col_totals = new_left(left_init, summed)
+        return own * total[:rows_own] / total[rows_own][None, :]
+
+    summed = summed.reshape(2, col_devices, rows_own + PAD, rank)
+    total = reduce_z(reduce_plane(reduce_core(summed)))
+    left = spread_core(spread_plane(own_left_rows(left_init, total))).reshape(m, rank)
     right, numerator = right_half(tensor_slab, left, right, second_left, whole, k)
     summed = left_half(tensor_slab, left, right, k, parts)
+    summed = summed.reshape(2, col_devices, rows_own + PAD, rank)
 
     rows_part = k // parts
-    part = reduce_parts(numerator.reshape(2, col_devices, rows_part, rank))
-    init_over = (whole / col_totals[None, :, None]).reshape(k, rank)
-    part = part * lax.dynamic_slice_in_dim(init_over, own_part * rows_part, rows_part, 0)
-    second_right = spread_parts(part).reshape(k // rank, rank, rank)
+    init_over = (whole / total[rows_own + 1][None, :, None]).reshape(k, rank)
+    init_over = lax.dynamic_slice_in_dim(init_over, own_part * rows_part, rows_part, 0)
+    plane = reduce_plane(reduce_core(numerator.reshape(2, col_devices, rows_part, rank)))
+    left_core = reduce_core(after(summed, plane))
+    part = init_over * reduce_z(plane)
+    left_plane = reduce_plane(after(left_core, part))
+    near = spread_plane(part)
+    left_total = reduce_z(after(left_plane, near))
+    second_right = spread_core(near).reshape(k // rank, rank, rank)
     rows_out = second_rows_out(right, second_left, second_right, slices)
     returned = exchange(rows_out.reshape(devices, per_owner * slices, rank))
     returned = returned.reshape(devices, per_owner, slices, rank).transpose(1, 0, 2, 3)
-    left_out, _ = new_left(left, summed)
+    left_part = after(own_left_rows(left, left_total), rows_out)
+    left_out = spread_core(spread_plane(left_part)).reshape(m, rank)
     return (left_out, returned.reshape(second_rows, rank))
 
 

time: 149 us -> 136 us (0.913)
  waiting for transfers between devices: 56.4 us -> 36.8 us
  Pallas kernels: 29.9 us -> 36.3 us
  other arithmetic: 3.5 us -> 8.7 us
  local copies, waits for them, and re-layouts: 11.6 us -> 6.99 us
    unnamed x10 -> x4, local copies, waits for them, and re-layouts: 9.03 us -> 0.01 us
    all_to_all x2, waiting for transfers between devices: 20.6 us -> 12.1 us  [exchange(): return lax.all_to_all(parts, AXES, split_axis=0, concat_axis=0, tiled=True)]
    ppermute x33, waiting for transfers between devices: 31.6 us -> 24.7 us  [send(): return lax.ppermute(values, AXES, pairs)]
    all_to_all x1 -> x0, waiting for transfers between devices: 4.23 us -> none  [body(): lax.all_to_all(jnp.broadcast_to(second_right_init[None], (col_devices,) +...]
    all_to_all x2, starting transfers between devices: 5.92 us -> 9.88 us  [exchange(): return lax.all_to_all(parts, AXES, split_axis=0, concat_axis=0, tiled=True)]
    all_to_all x1 -> x0, starting transfers between devices: 3.41 us -> none  [body(): lax.all_to_all(jnp.broadcast_to(second_right_init[None], (col_devices,) +...]
    add x3, other arithmetic: 0.08 us -> 2.91 us  [reduce_core(): return pick(parts, core) + send(pick(parts, 1 - core), 1, 0)]
    squeeze x6, local copies, waits for them, and re-layouts: 0.13 us -> 2.93 us  [pick(): return lax.dynamic_index_in_dim(values, index, 0, keepdims=False)]
  transfers between devices with their start and end apart: 36 -> 35, of which waited for: 24 -> 20; matrix products, arithmetic and copies ran while one was open for 2% -> 4% of each run, Pallas kernels for 7% -> 20%
where the time goes in v1:
time: 136 us; the launch traced here: 135 us
  starting transfers between devices  45.4 us (33%)
  waiting for transfers between devices  36.8 us (27%)
  Pallas kernels  36.3 us (27%)
  other arithmetic  8.7 us (6%)
  local copies, waits for them, and re-layouts  6.99 us (5%)
    ppermute x33, starting transfers between devices, send(): return lax.ppermute(values, AXES, pairs)  35.5 us
    ppermute x33, waiting for transfers between devices, send(): return lax.ppermute(values, AXES, pairs)  24.7 us
    pallas_call x1, Pallas kernels, full_turn(): pl.pallas_call(turn_kernel, grid=(columns // block,), in_specs=[columns_s...  14.1 us
    all_to_all x2, waiting for transfers between devices, exchange(): return lax.all_to_all(parts, AXES, split_axis=0, concat_axis=0, tiled=True)  12.1 us
    all_to_all x2, starting transfers between devices, exchange(): return lax.all_to_all(parts, AXES, split_axis=0, concat_axis=0, tiled=True)  9.88 us
    pallas_call x1, Pallas kernels, right_half(): pl.pallas_call(functools.partial(right_kernel, slices), grid=(slices,), i...  9.42 us
    pallas_call x1, Pallas kernels, left_half(): pl.pallas_call(left_kernel, grid=(columns // block,), in_specs=[columns_s...  9.27 us
    pallas_call x1, Pallas kernels, second_rows_out(): pl.pallas_call(functools.partial(second_kernel, slices), out_shape=jax.Sh...  3.54 us
  transfers between devices with their start and end apart: 35, of which 20 were waited for; matrix products, arithmetic and copies ran while one was open for 4% of the time, Pallas kernels for 20%

profile of v1, /device:TPU:0, one launch (start us, length us, event | category | flops | bytes accessed | tf_op | source)
XLA Modules:
  0.0 135.3 jit_solution(11864645160369891819)
XLA Ops:
  0.7 1.1 fusion.14
  1.8 1.1 copy.16
  2.9 7.3 %all-to-all-start = ((f32[32,32,128]{2,1,0:T(8,128)}), f32[32,32,128]{2,1,0:T(8,128)S(1)}, u32[]{:S(2)}, u32[]{:S(2)}) async-start(f32[32,32,128]{2,1,0:T(8,128)} %copy.16), calls=%async_computation | async-start | bytes 1048576 | tf_op jit(solution)/shard_map/all_to_all | solution.py:17
  10.3 0.6 broadcast_in_dim.4.extra_ref
  10.9 14.1 %turn.1 = (f32[128,2048]{1,0:T(8,128)}, f32[8,136,128]{2,1,0:T(8,128)}) custom-call(f32[1024,2048]{1,0:T(8,128)} %slab_ref.5, f32[1024,128]{1,0:T(8,128)} %left_ref.1, f32[128,2048]{1,0:T(8,128)} %right_ref.1, f32[8,128]{1,0:T(8,128)} %broadcast_in_dim.4.extra_ref), custom_call_target="tpu_custom_call" | custom-call | flops 6442450944 | bytes 8388608 | tf_op jit(solution)/shard_map/turn/pallas_call | solution.py:284
  24.9 1.6 %all-to-all-done = f32[32,32,128]{2,1,0:T(8,128)S(1)} async-done(((f32[32,32,128]{2,1,0:T(8,128)}), f32[32,32,128]{2,1,0:T(8,128)S(1)}, u32[]{:S(2)}, u32[]{:S(2)}) %all-to-all-start) | async-done | bytes 524320 | tf_op jit(solution)/shard_map/all_to_all | solution.py:17
  26.5 1.0 dynamic-slice_bitcast_fusion.1
  27.6 1.5 %collective-permute-done = f32[4,136,128]{2,1,0:T(8,128)S(1)} collective-permute-done((f32[4,136,128]{2,1,0:T(8,128)S(1)}, f32[4,136,128]{2,1,0:T(8,128)S(1)}, u32[]{:S(2)}, u32[]{:S(2)}) %collective-permute-start) | collective-permute-done | bytes 278560 | tf_op jit(solution)/shard_map/ppermute | solution.py:27
  29.1 1.0 bitcast_add_fusion.1
  30.4 1.5 %collective-permute-start.2 = (f32[136,128]{1,0:T(8,128)S(1)}, f32[136,128]{1,0:T(8,128)S(1)}, u32[]{:S(2)}, u32[]{:S(2)}) collective-permute-start(f32[136,128]{1,0:T(8,128)S(1)} %get-tuple-element.34), channel_id=1, source_target_pairs={{0,2},{1,3},{2,0},{3,1},{4,6},{5,7},{6,4},{7,5},{8,10},{9,11},{10,... | collective-permute-start | bytes 208904 | tf_op jit(solution)/shard_map/ppermute | solution.py:27
  31.9 1.8 %collective-permute-start.3 = (f32[136,128]{1,0:T(8,128)S(1)}, f32[136,128]{1,0:T(8,128)S(1)}, u32[]{:S(2)}, u32[]{:S(2)}) collective-permute-start(f32[136,128]{1,0:T(8,128)S(1)} %get-tuple-element.33), channel_id=1, source_target_pairs={{0,3},{1,2},{2,1},{3,0},{4,7},{5,6},{6,5},{7,4},{8,11},{9,10},{10,... | collective-permute-start | bytes 208904 | tf_op jit(solution)/shard_map/ppermute | solution.py:27
  33.7 1.2 collective-permute-done.1
  34.9 2.2 %collective-permute-done.3 = f32[136,128]{1,0:T(8,128)S(1)} collective-permute-done((f32[136,128]{1,0:T(8,128)S(1)}, f32[136,128]{1,0:T(8,128)S(1)}, u32[]{:S(2)}, u32[]{:S(2)}) %collective-permute-start.3) | collective-permute-done | bytes 69664 | tf_op jit(solution)/shard_map/ppermute | solution.py:27
  37.1 1.5 %collective-permute-start.4 = (f32[136,128]{1,0:T(8,128)S(1)}, f32[136,128]{1,0:T(8,128)S(1)}, u32[]{:S(2)}, u32[]{:S(2)}) collective-permute-start(f32[136,128]{1,0:T(8,128)S(1)} %fusion.7), channel_id=1, source_target_pairs={{0,8},{1,9},{2,10},{3,11},{4,12},{5,13},{6,14},{7,15},{8,0},{9,1},... | collective-permute-start | bytes 208904 | tf_op jit(solution)/shard_map/ppermute | solution.py:27
  38.6 2.5 %collective-permute-start.5 = (f32[136,128]{1,0:T(8,128)S(1)}, f32[136,128]{1,0:T(8,128)S(1)}, u32[]{:S(2)}, u32[]{:S(2)}) collective-permute-start(f32[136,128]{1,0:T(8,128)S(1)} %fusion.7), channel_id=1, source_target_pairs={{0,16},{1,17},{2,18},{3,19},{4,20},{5,21},{6,22},{7,23},{8,24},{9,... | collective-permute-start | bytes 208904 | tf_op jit(solution)/shard_map/ppermute | solution.py:27
  41.6 3.7 %collective-permute-done.5 = f32[136,128]{1,0:T(8,128)S(1)} collective-permute-done((f32[136,128]{1,0:T(8,128)S(1)}, f32[136,128]{1,0:T(8,128)S(1)}, u32[]{:S(2)}, u32[]{:S(2)}) %collective-permute-start.5) | collective-permute-done | bytes 69664 | tf_op jit(solution)/shard_map/ppermute | solution.py:27
  45.3 1.9 %collective-permute-done.6 = f32[136,128]{1,0:T(8,128)S(1)} collective-permute-done((f32[136,128]{1,0:T(8,128)S(1)}, f32[136,128]{1,0:T(8,128)S(1)}, u32[]{:S(2)}, u32[]{:S(2)}) %collective-permute-start.6) | collective-permute-done | bytes 69664 | tf_op jit(solution)/shard_map/ppermute | solution.py:27
  47.2 0.9 fusion.9
  48.1 0.6 collective-permute-start.7
  48.7 0.6 collective-permute-start.8
  49.3 2.3 %collective-permute-start.9 = (f32[128,128]{1,0:T(8,128)S(1)}, f32[128,128]{1,0:T(8,128)S(1)}, u32[]{:S(2)}, u32[]{:S(2)}) collective-permute-start(f32[128,128]{1,0:T(8,128)S(1)} %fusion.9), channel_id=1, source_target_pairs={{0,3},{1,2},{2,1},{3,0},{4,7},{5,6},{6,5},{7,4},{8,11},{9,10},{10,... | collective-permute-start | bytes 196616 | tf_op jit(solution)/shard_map/ppermute | solution.py:27
  51.6 0.8 collective-permute-done.7
  52.4 0.6 collective-permute-done.8
  53.0 1.5 %collective-permute-done.9 = f32[128,128]{1,0:T(8,128)S(1)} collective-permute-done((f32[128,128]{1,0:T(8,128)S(1)}, f32[128,128]{1,0:T(8,128)S(1)}, u32[]{:S(2)}, u32[]{:S(2)}) %collective-permute-start.9) | collective-permute-done | bytes 65568 | tf_op jit(solution)/shard_map/ppermute | solution.py:27
  54.6 0.7 fusion.15
  55.4 0.7 copy.17
  56.3 0.8 pad_maximum_fusion.1
  57.1 9.4 %right_half.1 = (f32[128,2048]{1,0:T(8,128)}, f32[4,128,128]{2,1,0:T(8,128)}) custom-call(f32[1024,2048]{1,0:T(8,128)} %slab_ref.5, f32[1024,128]{1,0:T(8,128)} %bitcast.102, f32[128,2048]{1,0:T(8,128)} %get-tuple-element.14.right_ref, f32[512,128]{1,0:T(8,128)} %bitcast.96, f32[4,128,128]{2,1,0:T(8,128)} %bitcast.95), custom_call_target="tpu_custom_call" | custom-call | flops 3221225472 | bytes 8388608 | tf_op jit(solution)/shard_map/right_half/pallas_call | solution.py:306
  66.5 0.9 dynamic-slice_bitcast_fusion.2
  67.4 0.5 collective-permute-start.11
  68.0 1.0 collective-permute-done.11
  68.9 0.9 bitcast_add_fusion.2
  69.9 1.5 %collective-permute-start.12 = (f32[64,128]{1,0:T(8,128)S(1)}, f32[64,128]{1,0:T(8,128)S(1)}, u32[]{:S(2)}, u32[]{:S(2)}) collective-permute-start(f32[64,128]{1,0:T(8,128)S(1)} %get-tuple-element.58), channel_id=1, source_target_pairs={{0,1},{1,0},{2,3},{3,2},{4,5},{5,4},{6,7},{7,6},{8,9},{9,8},{10,11... | collective-permute-start | bytes 98312 | tf_op jit(solution)/shard_map/ppermute | solution.py:27
  71.4 1.4 %collective-permute-start.13 = (f32[64,128]{1,0:T(8,128)S(1)}, f32[64,128]{1,0:T(8,128)S(1)}, u32[]{:S(2)}, u32[]{:S(2)}) collective-permute-start(f32[64,128]{1,0:T(8,128)S(1)} %get-tuple-element.57), channel_id=1, source_target_pairs={{0,2},{1,3},{2,0},{3,1},{4,6},{5,7},{6,4},{7,5},{8,10},{9,11},{10,... | collective-permute-start | bytes 98312 | tf_op jit(solution)/shard_map/ppermute | solution.py:27
  72.9 0.6 collective-permute-start.14
  73.9 1.5 %collective-permute-done.13 = f32[64,128]{1,0:T(8,128)S(1)} collective-permute-done((f32[64,128]{1,0:T(8,128)S(1)}, f32[64,128]{1,0:T(8,128)S(1)}, u32[]{:S(2)}, u32[]{:S(2)}) %collective-permute-start.13) | collective-permute-done | bytes 32800 | tf_op jit(solution)/shard_map/ppermute | solution.py:27
  75.3 2.3 %collective-permute-done.14 = f32[64,128]{1,0:T(8,128)S(1)} collective-permute-done((f32[64,128]{1,0:T(8,128)S(1)}, f32[64,128]{1,0:T(8,128)S(1)}, u32[]{:S(2)}, u32[]{:S(2)}) %collective-permute-start.14) | collective-permute-done | bytes 32800 | tf_op jit(solution)/shard_map/ppermute | solution.py:27
  77.8 1.5 %collective-permute-start.17 = (f32[64,128]{1,0:T(8,128)S(1)}, f32[64,128]{1,0:T(8,128)S(1)}, u32[]{:S(2)}, u32[]{:S(2)}) collective-permute-start(f32[64,128]{1,0:T(8,128)S(1)} %fusion.10), channel_id=1, source_target_pairs={{0,16},{1,17},{2,18},{3,19},{4,20},{5,21},{6,22},{7,23},{8,24},{9,... | collective-permute-start | bytes 98312 | tf_op jit(solution)/shard_map/ppermute | solution.py:27
  79.3 2.9 %collective-permute-start.18 = (f32[64,128]{1,0:T(8,128)S(1)}, f32[64,128]{1,0:T(8,128)S(1)}, u32[]{:S(2)}, u32[]{:S(2)}) collective-permute-start(f32[64,128]{1,0:T(8,128)S(1)} %fusion.10), channel_id=1, source_target_pairs={{0,24},{1,25},{2,26},{3,27},{4,28},{5,29},{6,30},{7,31},{8,16},{9,... | collective-permute-start | bytes 98312 | tf_op jit(solution)/shard_map/ppermute | solution.py:27
  82.2 9.3 %left_half.1 = f32[8,136,128]{2,1,0:T(8,128)} custom-call(f32[1024,2048]{1,0:T(8,128)} %slab_ref.5, f32[1024,128]{1,0:T(8,128)} %bitcast.103, f32[128,2048]{1,0:T(8,128)} %get-tuple-element.16.right_ref), custom_call_target="tpu_custom_call" | custom-call | flops 3221225472 | bytes 8388608 | tf_op jit(solution)/shard_map/left_half/pallas_call | solution.py:331
  91.5 0.6 collective-permute-start.22
  92.1 0.6 collective-permute-start.23
  92.7 2.3 %collective-permute-start.24 = (f32[64,128]{1,0:T(8,128)S(1)}, f32[64,128]{1,0:T(8,128)S(1)}, u32[]{:S(2)}, u32[]{:S(2)}) collective-permute-start(f32[64,128]{1,0:T(8,128)S(1)} %add_multiply_fusion), channel_id=1, source_target_pairs={{0,3},{1,2},{2,1},{3,0},{4,7},{5,6},{6,5},{7,4},{8,11},{9,10},{10,... | collective-permute-start | bytes 98312 | tf_op jit(solution)/shard_map/ppermute | solution.py:27
  95.0 1.0 dynamic-slice_bitcast_fusion
  96.1 1.4 %collective-permute-done.24 = f32[64,128]{1,0:T(8,128)S(1)} collective-permute-done((f32[64,128]{1,0:T(8,128)S(1)}, f32[64,128]{1,0:T(8,128)S(1)}, u32[]{:S(2)}, u32[]{:S(2)}) %collective-permute-start.24) | collective-permute-done | bytes 32800 | tf_op jit(solution)/shard_map/ppermute | solution.py:27
  97.7 1.0 bitcast_add_fusion
  98.7 1.5 %collective-permute-start.19 = (f32[136,128]{1,0:T(8,128)S(1)}, f32[136,128]{1,0:T(8,128)S(1)}, u32[]{:S(2)}, u32[]{:S(2)}) collective-permute-start(f32[136,128]{1,0:T(8,128)S(1)} %get-tuple-element.32), channel_id=1, source_target_pairs={{0,1},{1,0},{2,3},{3,2},{4,5},{5,4},{6,7},{7,6},{8,9},{9,8},{10,11... | collective-permute-start | bytes 208904 | tf_op jit(solution)/shard_map/ppermute | solution.py:27
  100.2 1.4 %collective-permute-start.20 = (f32[136,128]{1,0:T(8,128)S(1)}, f32[136,128]{1,0:T(8,128)S(1)}, u32[]{:S(2)}, u32[]{:S(2)}) collective-permute-start(f32[136,128]{1,0:T(8,128)S(1)} %get-tuple-element.31), channel_id=1, source_target_pairs={{0,2},{1,3},{2,0},{3,1},{4,6},{5,7},{6,4},{7,5},{8,10},{9,11},{10,... | collective-permute-start | bytes 208904 | tf_op jit(solution)/shard_map/ppermute | solution.py:27
  101.7 0.6 collective-permute-start.21
  102.3 1.0 collective-permute-done.19
  103.3 1.2 collective-permute-done.20
  104.5 2.3 %collective-permute-done.21 = f32[136,128]{1,0:T(8,128)S(1)} collective-permute-done((f32[136,128]{1,0:T(8,128)S(1)}, f32[136,128]{1,0:T(8,128)S(1)}, u32[]{:S(2)}, u32[]{:S(2)}) %collective-permute-start.21) | collective-permute-done | bytes 69664 | tf_op jit(solution)/shard_map/ppermute | solution.py:27
  107.0 1.5 %collective-permute-start.26 = (f32[136,128]{1,0:T(8,128)S(1)}, f32[136,128]{1,0:T(8,128)S(1)}, u32[]{:S(2)}, u32[]{:S(2)}) collective-permute-start(f32[136,128]{1,0:T(8,128)S(1)} %fusion.6), channel_id=1, source_target_pairs={{0,16},{1,17},{2,18},{3,19},{4,20},{5,21},{6,22},{7,23},{8,24},{9,... | collective-permute-start | bytes 208904 | tf_op jit(solution)/shard_map/ppermute | solution.py:27
  108.4 2.9 %collective-permute-start.27 = (f32[136,128]{1,0:T(8,128)S(1)}, f32[136,128]{1,0:T(8,128)S(1)}, u32[]{:S(2)}, u32[]{:S(2)}) collective-permute-start(f32[136,128]{1,0:T(8,128)S(1)} %fusion.6), channel_id=1, source_target_pairs={{0,24},{1,25},{2,26},{3,27},{4,28},{5,29},{6,30},{7,31},{8,16},{9,... | collective-permute-start | bytes 208904 | tf_op jit(solution)/shard_map/ppermute | solution.py:27
  111.3 0.7 pad_maximum_fusion.5
  112.0 3.5 %second_rows.1 = f32[512,128]{1,0:T(8,128)} custom-call(f32[128,2048]{1,0:T(8,128)} %get-tuple-element.16.right_ref, f32[512,128]{1,0:T(8,128)} %bitcast.97, f32[4,128,128]{2,1,0:T(8,128)} %bitcast.94), custom_call_target="tpu_custom_call" | custom-call | flops 402653184 | bytes 1048576 | tf_op jit(solution)/shard_map/second_rows/pallas_call | solution.py:345
  115.6 0.9 fusion.8
  116.5 0.6 collective-permute-start.29
  117.1 0.6 collective-permute-start.30
  117.7 2.3 %collective-permute-start.31 = (f32[128,128]{1,0:T(8,128)S(1)}, f32[128,128]{1,0:T(8,128)S(1)}, u32[]{:S(2)}, u32[]{:S(2)}) collective-permute-start(f32[128,128]{1,0:T(8,128)S(1)} %fusion.8), channel_id=1, source_target_pairs={{0,3},{1,2},{2,1},{3,0},{4,7},{5,6},{6,5},{7,4},{8,11},{9,10},{10,... | collective-permute-start | bytes 196616 | tf_op jit(solution)/shard_map/ppermute | solution.py:27
  120.1 2.6 %all-to-all-start.1 = ((f32[32,16,128]{2,1,0:T(8,128)}), f32[32,16,128]{2,1,0:T(8,128)S(1)}, u32[]{:S(2)}, u32[]{:S(2)}) async-start(f32[32,16,128]{2,1,0:T(8,128)} %bitcast.93), calls=%async_computation.1 | async-start | bytes 524288 | tf_op jit(solution)/shard_map/all_to_all | solution.py:17
  123.1 10.5 %all-to-all-done.1 = f32[32,16,128]{2,1,0:T(8,128)S(1)} async-done(((f32[32,16,128]{2,1,0:T(8,128)}), f32[32,16,128]{2,1,0:T(8,128)S(1)}, u32[]{:S(2)}, u32[]{:S(2)}) %all-to-all-start.1) | async-done | bytes 262176 | tf_op jit(solution)/shard_map/all_to_all | solution.py:17
  133.6 0.7 copy.18
  134.4 0.8 pad_maximum_fusion.2
  (59 shorter events, 2.8 us)
Async XLA Ops:
  0.6 1.1 copy-start
  2.9 23.6 %all-to-all-start = ((f32[32,32,128]{2,1,0:T(8,128)}), f32[32,32,128]{2,1,0:T(8,128)S(1)}, u32[]{:S(2)}, u32[]{:S(2)}) async-start(f32[32,32,128]{2,1,0:T(8,128)} %copy.16), calls=%async_computation | async-start | bytes 1048576 | tf_op jit(solution)/shard_map/all_to_all | solution.py:17
  27.5 1.6 %collective-permute-start = (f32[4,136,128]{2,1,0:T(8,128)S(1)}, f32[4,136,128]{2,1,0:T(8,128)S(1)}, u32[]{:S(2)}, u32[]{:S(2)}) collective-permute-start(f32[4,136,128]{2,1,0:T(8,128)S(1)} %dynamic-slice_bitcast_fusion.1), channel_id=1, source_target_pairs={{0,4},{1,5},{2,6},{3,7},{4,0},{5,1},{6,2},{7,3},{8,12},{9,13},{10,... | collective-permute-start | bytes 835592 | tf_op jit(solution)/shard_map/ppermute | solution.py:27
  30.1 4.8 %collective-permute-start.1 = (f32[136,128]{1,0:T(8,128)S(1)}, f32[136,128]{1,0:T(8,128)S(1)}, u32[]{:S(2)}, u32[]{:S(2)}) collective-permute-start(f32[136,128]{1,0:T(8,128)S(1)} %get-tuple-element.35), channel_id=1, source_target_pairs={{0,1},{1,0},{2,3},{3,2},{4,5},{5,4},{6,7},{7,6},{8,9},{9,8},{10,11... | collective-permute-start | bytes 208904 | tf_op jit(solution)/shard_map/ppermute | solution.py:27
  30.4 4.5 %collective-permute-start.2 = (f32[136,128]{1,0:T(8,128)S(1)}, f32[136,128]{1,0:T(8,128)S(1)}, u32[]{:S(2)}, u32[]{:S(2)}) collective-permute-start(f32[136,128]{1,0:T(8,128)S(1)} %get-tuple-element.34), channel_id=1, source_target_pairs={{0,2},{1,3},{2,0},{3,1},{4,6},{5,7},{6,4},{7,5},{8,10},{9,11},{10,... | collective-permute-start | bytes 208904 | tf_op jit(solution)/shard_map/ppermute | solution.py:27
  31.9 5.2 %collective-permute-start.3 = (f32[136,128]{1,0:T(8,128)S(1)}, f32[136,128]{1,0:T(8,128)S(1)}, u32[]{:S(2)}, u32[]{:S(2)}) collective-permute-start(f32[136,128]{1,0:T(8,128)S(1)} %get-tuple-element.33), channel_id=1, source_target_pairs={{0,3},{1,2},{2,1},{3,0},{4,7},{5,6},{6,5},{7,4},{8,11},{9,10},{10,... | collective-permute-start | bytes 208904 | tf_op jit(solution)/shard_map/ppermute | solution.py:27
  37.1 4.5 %collective-permute-start.4 = (f32[136,128]{1,0:T(8,128)S(1)}, f32[136,128]{1,0:T(8,128)S(1)}, u32[]{:S(2)}, u32[]{:S(2)}) collective-permute-start(f32[136,128]{1,0:T(8,128)S(1)} %fusion.7), channel_id=1, source_target_pairs={{0,8},{1,9},{2,10},{3,11},{4,12},{5,13},{6,14},{7,15},{8,0},{9,1},... | collective-permute-start | bytes 208904 | tf_op jit(solution)/shard_map/ppermute | solution.py:27
  38.6 6.7 %collective-permute-start.5 = (f32[136,128]{1,0:T(8,128)S(1)}, f32[136,128]{1,0:T(8,128)S(1)}, u32[]{:S(2)}, u32[]{:S(2)}) collective-permute-start(f32[136,128]{1,0:T(8,128)S(1)} %fusion.7), channel_id=1, source_target_pairs={{0,16},{1,17},{2,18},{3,19},{4,20},{5,21},{6,22},{7,23},{8,24},{9,... | collective-permute-start | bytes 208904 | tf_op jit(solution)/shard_map/ppermute | solution.py:27
  41.1 6.1 %collective-permute-start.6 = (f32[136,128]{1,0:T(8,128)S(1)}, f32[136,128]{1,0:T(8,128)S(1)}, u32[]{:S(2)}, u32[]{:S(2)}) collective-permute-start(f32[136,128]{1,0:T(8,128)S(1)} %fusion.7), channel_id=1, source_target_pairs={{0,24},{1,25},{2,26},{3,27},{4,28},{5,29},{6,30},{7,31},{8,16},{9,... | collective-permute-start | bytes 208904 | tf_op jit(solution)/shard_map/ppermute | solution.py:27
  48.1 4.3 %collective-permute-start.7 = (f32[128,128]{1,0:T(8,128)S(1)}, f32[128,128]{1,0:T(8,128)S(1)}, u32[]{:S(2)}, u32[]{:S(2)}) collective-permute-start(f32[128,128]{1,0:T(8,128)S(1)} %fusion.9), channel_id=1, source_target_pairs={{0,1},{1,0},{2,3},{3,2},{4,5},{5,4},{6,7},{7,6},{8,9},{9,8},{10,11... | collective-permute-start | bytes 196616 | tf_op jit(solution)/shard_map/ppermute | solution.py:27
  48.7 4.3 %collective-permute-start.8 = (f32[128,128]{1,0:T(8,128)S(1)}, f32[128,128]{1,0:T(8,128)S(1)}, u32[]{:S(2)}, u32[]{:S(2)}) collective-permute-start(f32[128,128]{1,0:T(8,128)S(1)} %fusion.9), channel_id=1, source_target_pairs={{0,2},{1,3},{2,0},{3,1},{4,6},{5,7},{6,4},{7,5},{8,10},{9,11},{10,... | collective-permute-start | bytes 196616 | tf_op jit(solution)/shard_map/ppermute | solution.py:27
  49.3 5.2 %collective-permute-start.9 = (f32[128,128]{1,0:T(8,128)S(1)}, f32[128,128]{1,0:T(8,128)S(1)}, u32[]{:S(2)}, u32[]{:S(2)}) collective-permute-start(f32[128,128]{1,0:T(8,128)S(1)} %fusion.9), channel_id=1, source_target_pairs={{0,3},{1,2},{2,1},{3,0},{4,7},{5,6},{6,5},{7,4},{8,11},{9,10},{10,... | collective-permute-start | bytes 196616 | tf_op jit(solution)/shard_map/ppermute | solution.py:27
  54.6 1.6 %collective-permute-start.10 = (f32[4,128,128]{2,1,0:T(8,128)S(1)}, f32[4,128,128]{2,1,0:T(8,128)S(1)}, u32[]{:S(2)}, u32[]{:S(2)}) collective-permute-start(f32[4,128,128]{2,1,0:T(8,128)S(1)} %get-tuple-element.44), channel_id=1, source_target_pairs={{0,4},{1,5},{2,6},{3,7},{4,0},{5,1},{6,2},{7,3},{8,12},{9,13},{10,... | collective-permute-start | bytes 786440 | tf_op jit(solution)/shard_map/ppermute | solution.py:27
  56.1 17.4 %copy-start.1 = (f32[8,4,16,128]{3,2,0,1:T(8,128)S(1)}, f32[8,4,16,128]{3,2,0,1:T(8,128)}, u32[]{:S(2)}) copy-start(f32[8,4,16,128]{3,2,0,1:T(8,128)} %copy.17) | copy-start | bytes 786436
  67.4 1.5 %collective-permute-start.11 = (f32[4,64,128]{2,1,0:T(8,128)S(1)}, f32[4,64,128]{2,1,0:T(8,128)S(1)}, u32[]{:S(2)}, u32[]{:S(2)}) collective-permute-start(f32[4,64,128]{2,1,0:T(8,128)S(1)} %dynamic-slice_bitcast_fusion.2), channel_id=1, source_target_pairs={{0,4},{1,5},{2,6},{3,7},{4,0},{5,1},{6,2},{7,3},{8,12},{9,13},{10,... | collective-permute-start | bytes 393224 | tf_op jit(solution)/shard_map/ppermute | solution.py:27
  69.9 4.0 %collective-permute-start.12 = (f32[64,128]{1,0:T(8,128)S(1)}, f32[64,128]{1,0:T(8,128)S(1)}, u32[]{:S(2)}, u32[]{:S(2)}) collective-permute-start(f32[64,128]{1,0:T(8,128)S(1)} %get-tuple-element.58), channel_id=1, source_target_pairs={{0,1},{1,0},{2,3},{3,2},{4,5},{5,4},{6,7},{7,6},{8,9},{9,8},{10,11... | collective-permute-start | bytes 98312 | tf_op jit(solution)/shard_map/ppermute | solution.py:27
  71.4 3.9 %collective-permute-start.13 = (f32[64,128]{1,0:T(8,128)S(1)}, f32[64,128]{1,0:T(8,128)S(1)}, u32[]{:S(2)}, u32[]{:S(2)}) collective-permute-start(f32[64,128]{1,0:T(8,128)S(1)} %get-tuple-element.57), channel_id=1, source_target_pairs={{0,2},{1,3},{2,0},{3,1},{4,6},{5,7},{6,4},{7,5},{8,10},{9,11},{10,... | collective-permute-start | bytes 98312 | tf_op jit(solution)/shard_map/ppermute | solution.py:27
  72.9 4.8 %collective-permute-start.14 = (f32[64,128]{1,0:T(8,128)S(1)}, f32[64,128]{1,0:T(8,128)S(1)}, u32[]{:S(2)}, u32[]{:S(2)}) collective-permute-start(f32[64,128]{1,0:T(8,128)S(1)} %get-tuple-element.56), channel_id=1, source_target_pairs={{0,3},{1,2},{2,1},{3,0},{4,7},{5,6},{6,5},{7,4},{8,11},{9,10},{10,... | collective-permute-start | bytes 98312 | tf_op jit(solution)/shard_map/ppermute | solution.py:27
  77.7 13.7 %collective-permute-start.16 = (f32[64,128]{1,0:T(8,128)S(1)}, f32[64,128]{1,0:T(8,128)S(1)}, u32[]{:S(2)}, u32[]{:S(2)}) collective-permute-start(f32[64,128]{1,0:T(8,128)S(1)} %fusion.10), channel_id=1, source_target_pairs={{0,8},{1,9},{2,10},{3,11},{4,12},{5,13},{6,14},{7,15},{8,0},{9,1},... | collective-permute-start | bytes 98312 | tf_op jit(solution)/shard_map/ppermute | solution.py:27
  77.8 13.6 %collective-permute-start.17 = (f32[64,128]{1,0:T(8,128)S(1)}, f32[64,128]{1,0:T(8,128)S(1)}, u32[]{:S(2)}, u32[]{:S(2)}) collective-permute-start(f32[64,128]{1,0:T(8,128)S(1)} %fusion.10), channel_id=1, source_target_pairs={{0,16},{1,17},{2,18},{3,19},{4,20},{5,21},{6,22},{7,23},{8,24},{9,... | collective-permute-start | bytes 98312 | tf_op jit(solution)/shard_map/ppermute | solution.py:27
  79.3 12.2 %collective-permute-start.18 = (f32[64,128]{1,0:T(8,128)S(1)}, f32[64,128]{1,0:T(8,128)S(1)}, u32[]{:S(2)}, u32[]{:S(2)}) collective-permute-start(f32[64,128]{1,0:T(8,128)S(1)} %fusion.10), channel_id=1, source_target_pairs={{0,24},{1,25},{2,26},{3,27},{4,28},{5,29},{6,30},{7,31},{8,16},{9,... | collective-permute-start | bytes 98312 | tf_op jit(solution)/shard_map/ppermute | solution.py:27
  91.5 4.6 %collective-permute-start.22 = (f32[64,128]{1,0:T(8,128)S(1)}, f32[64,128]{1,0:T(8,128)S(1)}, u32[]{:S(2)}, u32[]{:S(2)}) collective-permute-start(f32[64,128]{1,0:T(8,128)S(1)} %add_multiply_fusion), channel_id=1, source_target_pairs={{0,1},{1,0},{2,3},{3,2},{4,5},{5,4},{6,7},{7,6},{8,9},{9,8},{10,11... | collective-permute-start | bytes 98312 | tf_op jit(solution)/shard_map/ppermute | solution.py:27
  92.1 4.0 %collective-permute-start.23 = (f32[64,128]{1,0:T(8,128)S(1)}, f32[64,128]{1,0:T(8,128)S(1)}, u32[]{:S(2)}, u32[]{:S(2)}) collective-permute-start(f32[64,128]{1,0:T(8,128)S(1)} %add_multiply_fusion), channel_id=1, source_target_pairs={{0,2},{1,3},{2,0},{3,1},{4,6},{5,7},{6,4},{7,5},{8,10},{9,11},{10,... | collective-permute-start | bytes 98312 | tf_op jit(solution)/shard_map/ppermute | solution.py:27
  92.7 4.8 %collective-permute-start.24 = (f32[64,128]{1,0:T(8,128)S(1)}, f32[64,128]{1,0:T(8,128)S(1)}, u32[]{:S(2)}, u32[]{:S(2)}) collective-permute-start(f32[64,128]{1,0:T(8,128)S(1)} %add_multiply_fusion), channel_id=1, source_target_pairs={{0,3},{1,2},{2,1},{3,0},{4,7},{5,6},{6,5},{7,4},{8,11},{9,10},{10,... | collective-permute-start | bytes 98312 | tf_op jit(solution)/shard_map/ppermute | solution.py:27
  96.0 1.7 %collective-permute-start.15 = (f32[4,136,128]{2,1,0:T(8,128)S(1)}, f32[4,136,128]{2,1,0:T(8,128)S(1)}, u32[]{:S(2)}, u32[]{:S(2)}) collective-permute-start(f32[4,136,128]{2,1,0:T(8,128)S(1)} %dynamic-slice_bitcast_fusion), channel_id=1, source_target_pairs={{0,4},{1,5},{2,6},{3,7},{4,0},{5,1},{6,2},{7,3},{8,12},{9,13},{10,... | collective-permute-start | bytes 835592 | tf_op jit(solution)/shard_map/ppermute | solution.py:27
  97.6 4.7 %collective-permute-start.28 = (f32[4,64,128]{2,1,0:T(8,128)S(1)}, f32[4,64,128]{2,1,0:T(8,128)S(1)}, u32[]{:S(2)}, u32[]{:S(2)}) collective-permute-start(f32[4,64,128]{2,1,0:T(8,128)S(1)} %get-tuple-element.51), channel_id=1, source_target_pairs={{0,4},{1,5},{2,6},{3,7},{4,0},{5,1},{6,2},{7,3},{8,12},{9,13},{10,... | collective-permute-start | bytes 393224 | tf_op jit(solution)/shard_map/ppermute | solution.py:27
  98.7 4.6 %collective-permute-start.19 = (f32[136,128]{1,0:T(8,128)S(1)}, f32[136,128]{1,0:T(8,128)S(1)}, u32[]{:S(2)}, u32[]{:S(2)}) collective-permute-start(f32[136,128]{1,0:T(8,128)S(1)} %get-tuple-element.32), channel_id=1, source_target_pairs={{0,1},{1,0},{2,3},{3,2},{4,5},{5,4},{6,7},{7,6},{8,9},{9,8},{10,11... | collective-permute-start | bytes 208904 | tf_op jit(solution)/shard_map/ppermute | solution.py:27
  100.2 4.3 %collective-permute-start.20 = (f32[136,128]{1,0:T(8,128)S(1)}, f32[136,128]{1,0:T(8,128)S(1)}, u32[]{:S(2)}, u32[]{:S(2)}) collective-permute-start(f32[136,128]{1,0:T(8,128)S(1)} %get-tuple-element.31), channel_id=1, source_target_pairs={{0,2},{1,3},{2,0},{3,1},{4,6},{5,7},{6,4},{7,5},{8,10},{9,11},{10,... | collective-permute-start | bytes 208904 | tf_op jit(solution)/shard_map/ppermute | solution.py:27
  101.7 5.2 %collective-permute-start.21 = (f32[136,128]{1,0:T(8,128)S(1)}, f32[136,128]{1,0:T(8,128)S(1)}, u32[]{:S(2)}, u32[]{:S(2)}) collective-permute-start(f32[136,128]{1,0:T(8,128)S(1)} %get-tuple-element.30), channel_id=1, source_target_pairs={{0,3},{1,2},{2,1},{3,0},{4,7},{5,6},{6,5},{7,4},{8,11},{9,10},{10,... | collective-permute-start | bytes 208904 | tf_op jit(solution)/shard_map/ppermute | solution.py:27
  106.9 8.7 %collective-permute-start.25 = (f32[136,128]{1,0:T(8,128)S(1)}, f32[136,128]{1,0:T(8,128)S(1)}, u32[]{:S(2)}, u32[]{:S(2)}) collective-permute-start(f32[136,128]{1,0:T(8,128)S(1)} %fusion.6), channel_id=1, source_target_pairs={{0,8},{1,9},{2,10},{3,11},{4,12},{5,13},{6,14},{7,15},{8,0},{9,1},... | collective-permute-start | bytes 208904 | tf_op jit(solution)/shard_map/ppermute | solution.py:27
  107.0 8.6 %collective-permute-start.26 = (f32[136,128]{1,0:T(8,128)S(1)}, f32[136,128]{1,0:T(8,128)S(1)}, u32[]{:S(2)}, u32[]{:S(2)}) collective-permute-start(f32[136,128]{1,0:T(8,128)S(1)} %fusion.6), channel_id=1, source_target_pairs={{0,16},{1,17},{2,18},{3,19},{4,20},{5,21},{6,22},{7,23},{8,24},{9,... | collective-permute-start | bytes 208904 | tf_op jit(solution)/shard_map/ppermute | solution.py:27
  108.4 7.2 %collective-permute-start.27 = (f32[136,128]{1,0:T(8,128)S(1)}, f32[136,128]{1,0:T(8,128)S(1)}, u32[]{:S(2)}, u32[]{:S(2)}) collective-permute-start(f32[136,128]{1,0:T(8,128)S(1)} %fusion.6), channel_id=1, source_target_pairs={{0,24},{1,25},{2,26},{3,27},{4,28},{5,29},{6,30},{7,31},{8,16},{9,... | collective-permute-start | bytes 208904 | tf_op jit(solution)/shard_map/ppermute | solution.py:27
  116.5 6.1 %collective-permute-start.29 = (f32[128,128]{1,0:T(8,128)S(1)}, f32[128,128]{1,0:T(8,128)S(1)}, u32[]{:S(2)}, u32[]{:S(2)}) collective-permute-start(f32[128,128]{1,0:T(8,128)S(1)} %fusion.8), channel_id=1, source_target_pairs={{0,1},{1,0},{2,3},{3,2},{4,5},{5,4},{6,7},{7,6},{8,9},{9,8},{10,11... | collective-permute-start | bytes 196616 | tf_op jit(solution)/shard_map/ppermute | solution.py:27
  117.1 5.5 %collective-permute-start.30 = (f32[128,128]{1,0:T(8,128)S(1)}, f32[128,128]{1,0:T(8,128)S(1)}, u32[]{:S(2)}, u32[]{:S(2)}) collective-permute-start(f32[128,128]{1,0:T(8,128)S(1)} %fusion.8), channel_id=1, source_target_pairs={{0,2},{1,3},{2,0},{3,1},{4,6},{5,7},{6,4},{7,5},{8,10},{9,11},{10,... | collective-permute-start | bytes 196616 | tf_op jit(solution)/shard_map/ppermute | solution.py:27
  117.7 5.2 %collective-permute-start.31 = (f32[128,128]{1,0:T(8,128)S(1)}, f32[128,128]{1,0:T(8,128)S(1)}, u32[]{:S(2)}, u32[]{:S(2)}) collective-permute-start(f32[128,128]{1,0:T(8,128)S(1)} %fusion.8), channel_id=1, source_target_pairs={{0,3},{1,2},{2,1},{3,0},{4,7},{5,6},{6,5},{7,4},{8,11},{9,10},{10,... | collective-permute-start | bytes 196616 | tf_op jit(solution)/shard_map/ppermute | solution.py:27
  120.1 13.5 %all-to-all-start.1 = ((f32[32,16,128]{2,1,0:T(8,128)}), f32[32,16,128]{2,1,0:T(8,128)S(1)}, u32[]{:S(2)}, u32[]{:S(2)}) async-start(f32[32,16,128]{2,1,0:T(8,128)} %bitcast.93), calls=%async_computation.1 | async-start | bytes 524288 | tf_op jit(solution)/shard_map/all_to_all | solution.py:17
  123.0 11.4 %collective-permute-start.32 = (f32[4,128,128]{2,1,0:T(8,128)S(1)}, f32[4,128,128]{2,1,0:T(8,128)S(1)}, u32[]{:S(2)}, u32[]{:S(2)}) collective-permute-start(f32[4,128,128]{2,1,0:T(8,128)S(1)} %get-tuple-element.36), channel_id=1, source_target_pairs={{0,4},{1,5},{2,6},{3,7},{4,0},{5,1},{6,2},{7,3},{8,12},{9,13},{10,... | collective-permute-start | bytes 786440 | tf_op jit(solution)/shard_map/ppermute | solution.py:27

commit v2 on v1

--- a/solution.py
+++ b/solution.py
@@ -10,7 +10,7 @@
 AXES = ("row", "col")
 F32, BF16 = jnp.float32, jnp.bfloat16
 PAD = 8
-VMEM_BYTES = 60 * 1024 * 1024
+VMEM_BYTES = 54 * 1024 * 1024
 
 
 def exchange(parts):
@@ -175,52 +175,23 @@
     high, low = split(second_left)
     right_high, right_low = pairs
     product = dot(high, right_high) + (dot(low, right_high) + dot(high, right_low))
-    return split(divide(block, product)), (high, low)
-
-
-def right_kernel(
-    slices, slab_ref, left_ref, right_ref, second_left_ref, second_right_ref, right_out, numer_out,
-    pair_ref, pair_t_ref, sums_ref, high_ref, low_ref, numer_ref,
-):
-    step = pl.program_id(0)
-
-    @pl.when(step == 0)
-    def _():
-        prepare_left(left_ref, pair_ref)
-        prepare_left_t(left_ref, pair_t_ref, sums_ref)
-
-    right = right_update(
-        slab_ref, pair_ref, pair_t_ref, sums_ref, right_ref[...], high_ref, low_ref
-    )
-    right_out[...] = right
-    rank, k = right.shape
-    second_left = second_left_ref[pl.ds(step, rank, stride=slices), :]
-    second_right = jnp.concatenate(
-        [second_right_ref[block] for block in range(k // rank)], axis=1
-    )
-    (high, low), _ = second_quotient(right, second_left, split(second_right))
-    left_high, left_low = split(second_left.T)
-    term = dot(left_high, high) + (dot(left_low, high) + dot(left_high, low))
-    numer_ref[...] = jnp.where(step == 0, term, numer_ref[...] + term)
-
-    @pl.when(step == pl.num_programs(0) - 1)
-    def _():
-        for block in range(k // rank):
-            numer_out[block] = numer_ref[:, pl.ds(block * rank, rank)]
-
-
-def left_kernel(slab_ref, left_ref, right_ref, left_out, pair_ref, total_ref, row_sums_ref):
-    step = pl.program_id(0)
-
-    @pl.when(step == 0)
-    def _():
-        prepare_left(left_ref, pair_ref)
-
-    left_numerator(slab_ref, pair_ref, right_ref[...], total_ref, row_sums_ref, step == 0)
-
-    @pl.when(step == pl.num_programs(0) - 1)
-    def _():
-        write_left(total_ref, row_sums_ref, row_sums_ref, left_out)
+    return split(divide(block, product))
+
+
+def numerator_kernel(slices, right_ref, second_left_ref, second_right_ref, numer_out):
+    rank = right_ref.shape[0]
+    k = right_ref.shape[1] // slices
+    pairs = split(
+        jnp.concatenate([second_right_ref[block] for block in range(k // rank)], axis=1)
+    )
+    total = 0.0
+    for index in range(slices):
+        second_left = second_left_ref[pl.ds(index, rank, stride=slices), :]
+        high, low = second_quotient(right_ref[:, pl.ds(index * k, k)], second_left, pairs)
+        left_high, left_low = split(second_left.T)
+        total = total + (dot(left_high, high) + (dot(left_low, high) + dot(left_high, low)))
+    for block in range(k // rank):
+        numer_out[block] = total[:, block * rank : (block + 1) * rank]
 
 
 def second_kernel(slices, right_ref, second_left_ref, second_right_ref, out_ref):
@@ -236,7 +207,7 @@
     for index in range(slices):
         rows = pl.ds(index, rank, stride=slices)
         second_left = second_left_ref[rows, :]
-        (high, low), _ = second_quotient(
+        high, low = second_quotient(
             right_ref[:, pl.ds(index * k, k)], second_left, (right_high, right_low)
         )
         both = dot_nt(high, right_both)
@@ -299,46 +270,14 @@
     )(slab, left, right, extra)
 
 
-def right_half(slab, left, right, second_left, second_right, block):
-    (m, columns), rank = slab.shape, left.shape[1]
-    slices = columns // block
-    columns_spec = lambda height: pl.BlockSpec((height, block), lambda step: (0, step))
+def second_numerator(right, second_left, second_right, slices):
     return pl.pallas_call(
-        functools.partial(right_kernel, slices),
-        grid=(slices,),
-        in_specs=[
-            columns_spec(m), full((m, rank)), columns_spec(rank),
-            full(second_left.shape), full(second_right.shape),
-        ],
-        out_specs=[columns_spec(rank), full(second_right.shape)],
-        out_shape=[
-            jax.ShapeDtypeStruct((rank, columns), F32),
-            jax.ShapeDtypeStruct(second_right.shape, F32),
-        ],
-        scratch_shapes=left_scratch(m, rank)
-        + right_scratch(m, rank, block)
-        + [pltpu.VMEM((rank, block), F32)],
-        compiler_params=params(),
-        cost_estimate=cost(m, rank, columns, 2),
-        name="right_half",
-    )(slab, left, right, second_left, second_right)
-
-
-def left_half(slab, left, right, block, parts):
-    (m, columns), rank = slab.shape, left.shape[1]
-    columns_spec = lambda height: pl.BlockSpec((height, block), lambda step: (0, step))
-    tall = m // parts + PAD
-    return pl.pallas_call(
-        left_kernel,
-        grid=(columns // block,),
-        in_specs=[columns_spec(m), full((m, rank)), columns_spec(rank)],
-        out_specs=full((parts, tall, rank)),
-        out_shape=jax.ShapeDtypeStruct((parts, tall, rank), F32),
-        scratch_shapes=left_scratch(m, rank) + total_scratch(m, rank),
-        compiler_params=params(),
-        cost_estimate=cost(m, rank, columns, 2),
-        name="left_half",
-    )(slab, left, right)
+        functools.partial(numerator_kernel, slices),
+        out_shape=jax.ShapeDtypeStruct(second_right.shape, F32),
+        compiler_params=pltpu.CompilerParams(vmem_limit_bytes=VMEM_BYTES),
+        cost_estimate=cost(right.shape[0], right.shape[0], right.shape[1], 2),
+        name="second_numerator",
+    )(right, second_left, second_right)
 
 
 def second_rows_out(right, second_left, second_right, slices):
@@ -375,40 +314,40 @@
         second_right_init, lax.axis_index("row") * piece_rows, piece_rows, 0
     ).reshape(-1, rank)
     piece = jnp.broadcast_to(piece[None], (devices,) + piece.shape)
-    arrived = exchange(jnp.concatenate([own_left, piece], axis=1))
-
-    right, summed = full_turn(tensor_slab, left_init, right_init, col_part, k, parts)
-    summed, arrived = lax.optimization_barrier((summed, arrived))
+    second_factors = jnp.concatenate([own_left, piece], axis=1)
+
+    def own_left_rows(left, total):
+        own = lax.dynamic_slice_in_dim(left, own_part * rows_own, rows_own, 0)
+        return own * total[:rows_own] / total[rows_own][None, :]
+
+    right, summed = full_turn(tensor_slab, left_init, right_init, left_init, k, parts)
+    summed = summed.reshape(2, col_devices, rows_own + PAD, rank)
+    total = reduce_z(reduce_plane(reduce_core(summed)))
+    left = spread_core(spread_plane(own_left_rows(left_init, total))).reshape(m, rank)
+
+    arrived = exchange(after(second_factors, left))
+    right, summed = full_turn(tensor_slab, left, right, col_part, k, parts)
+    arrived = after(arrived, summed)
     second_left = arrived[:, : per_owner * slices].reshape(rank * slices, rank)
     whole = arrived[:, per_owner * slices :].reshape(row_devices, col_devices, piece_rows, -1)
     whole = whole.transpose(0, 2, 1, 3).reshape(rank, k // rank, rank).transpose(1, 0, 2)
-
-    def own_left_rows(left, total):
-        own = lax.dynamic_slice_in_dim(left, own_part * rows_own, rows_own, 0)
-        return own * total[:rows_own] / total[rows_own][None, :]
-
+    numerator = second_numerator(right, second_left, whole, slices)
+
+    rows_part = k // parts
     summed = summed.reshape(2, col_devices, rows_own + PAD, rank)
-    total = reduce_z(reduce_plane(reduce_core(summed)))
-    left = spread_core(spread_plane(own_left_rows(left_init, total))).reshape(m, rank)
-    right, numerator = right_half(tensor_slab, left, right, second_left, whole, k)
-    summed = left_half(tensor_slab, left, right, k, parts)
-    summed = summed.reshape(2, col_devices, rows_own + PAD, rank)
-
-    rows_part = k // parts
+    numerator = numerator.reshape(2, col_devices, rows_part, rank)
+    total = reduce_z(reduce_plane(reduce_core(jnp.concatenate([summed, numerator], axis=2))))
     init_over = (whole / total[rows_own + 1][None, :, None]).reshape(k, rank)
     init_over = lax.dynamic_slice_in_dim(init_over, own_part * rows_part, rows_part, 0)
-    plane = reduce_plane(reduce_core(numerator.reshape(2, col_devices, rows_part, rank)))
-    left_core = reduce_core(after(summed, plane))
-    part = init_over * reduce_z(plane)
-    left_plane = reduce_plane(after(left_core, part))
-    near = spread_plane(part)
-    left_total = reduce_z(after(left_plane, near))
-    second_right = spread_core(near).reshape(k // rank, rank, rank)
+    second_part = init_over * total[rows_own + PAD :]
+    both = spread_core(
+        spread_plane(jnp.concatenate([own_left_rows(left, total), second_part], axis=0))
+    )
+    left_out = both[:, :, :rows_own].reshape(m, rank)
+    second_right = both[:, :, rows_own:].reshape(k // rank, rank, rank)
     rows_out = second_rows_out(right, second_left, second_right, slices)
     returned = exchange(rows_out.reshape(devices, per_owner * slices, rank))
     returned = returned.reshape(devices, per_owner, slices, rank).transpose(1, 0, 2, 3)
-    left_part = after(own_left_rows(left, left_total), rows_out)
-    left_out = spread_core(spread_plane(left_part)).reshape(m, rank)
     return (left_out, returned.reshape(second_rows, rank))
 
 

time: 136 us -> 129 us (0.949)
  starting transfers between devices: 45.4 us -> 32 us
  waiting for transfers between devices: 36.8 us -> 45.3 us
  local copies, waits for them, and re-layouts: 6.99 us -> 5.06 us
    pallas_call x2 -> x1, Pallas kernels: 18.7 us -> 3.63 us  [second_numerator(): pl.pallas_call(functools.partial(numerator_kernel, slices), out_shape=jax...]
    pallas_call x1 -> x2, Pallas kernels: 14.1 us -> 28.7 us  [full_turn(): pl.pallas_call(turn_kernel, grid=(columns // block,), in_specs=[columns_s...]
    ppermute x33 -> x22, starting transfers between devices: 35.5 us -> 24.8 us  [send(): return lax.ppermute(values, AXES, pairs)]
    ppermute x33 -> x22, waiting for transfers between devices: 24.7 us -> 33.6 us  [send(): return lax.ppermute(values, AXES, pairs)]
    all_to_all x2, starting transfers between devices: 9.88 us -> 7.18 us  [exchange(): return lax.all_to_all(parts, AXES, split_axis=0, concat_axis=0, tiled=True)]
    squeeze x6 -> x3, local copies, waits for them, and re-layouts: 2.93 us -> 1.03 us  [pick(): return lax.dynamic_index_in_dim(values, index, 0, keepdims=False)]
    add x3 -> x2, other arithmetic: 2.91 us -> 2.03 us  [reduce_core(): return pick(parts, core) + send(pick(parts, 1 - core), 1, 0)]
  transfers between devices with their start and end apart: 35 -> 24, of which waited for: 20 -> 20; matrix products, arithmetic and copies ran while one was open for 4% -> 2% of each run, Pallas kernels for 20% -> 11%
where the time goes in v2:
time: 129 us
  waiting for transfers between devices  45.3 us (35%)
  Pallas kernels  35.8 us (28%)
  starting transfers between devices  32 us (25%)
  other arithmetic  9.77 us (8%)
  local copies, waits for them, and re-layouts  5.06 us (4%)
    ppermute x22, waiting for transfers between devices, send(): return lax.ppermute(values, AXES, pairs)  33.6 us
    pallas_call x2, Pallas kernels, full_turn(): pl.pallas_call(turn_kernel, grid=(columns // block,), in_specs=[columns_s...  28.7 us
    ppermute x22, starting transfers between devices, send(): return lax.ppermute(values, AXES, pairs)  24.8 us
    all_to_all x2, waiting for transfers between devices, exchange(): return lax.all_to_all(parts, AXES, split_axis=0, concat_axis=0, tiled=True)  11.7 us
    all_to_all x2, starting transfers between devices, exchange(): return lax.all_to_all(parts, AXES, split_axis=0, concat_axis=0, tiled=True)  7.18 us
    pallas_call x1, Pallas kernels, second_numerator(): pl.pallas_call(functools.partial(numerator_kernel, slices), out_shape=jax...  3.63 us
    pallas_call x1, Pallas kernels, second_rows_out(): pl.pallas_call(functools.partial(second_kernel, slices), out_shape=jax.Sh...  3.52 us
  transfers between devices with their start and end apart: 24, of which 20 were waited for; matrix products, arithmetic and copies ran while one was open for 2% of the time, Pallas kernels for 11%

profile of v2, /device:TPU:0, one launch (start us, length us, event | category | flops | bytes accessed | tf_op | source)
XLA Modules:
  0.0 128.9 jit_solution(6868246842288638702)
XLA Ops:
  0.7 14.6 %turn.2 = (f32[128,2048]{1,0:T(8,128)}, f32[8,136,128]{2,1,0:T(8,128)}) custom-call(f32[1024,2048]{1,0:T(8,128)} %slab_ref.3, f32[1024,128]{1,0:T(8,128)} %extra_ref.1, f32[128,2048]{1,0:T(8,128)} %right_ref.1, f32[1024,128]{1,0:T(8,128)} %extra_ref.1), custom_call_target="tpu_custom_call" | custom-call | flops 6442450944 | bytes 8388608 | tf_op jit(solution)/shard_map/turn/pallas_call | solution.py:255
  15.3 1.0 dynamic-slice_bitcast_fusion
  16.3 0.5 collective-permute-start
  16.8 1.2 collective-permute-done
  18.0 1.0 bitcast_add_fusion
  19.0 3.9 %collective-permute-start.3 = (f32[136,128]{1,0:T(8,128)S(1)}, f32[136,128]{1,0:T(8,128)S(1)}, u32[]{:S(2)}, u32[]{:S(2)}) collective-permute-start(f32[136,128]{1,0:T(8,128)S(1)} %get-tuple-element.31), channel_id=1, source_target_pairs={{0,3},{1,2},{2,1},{3,0},{4,7},{5,6},{6,5},{7,4},{8,11},{9,10},{10,... | collective-permute-start | bytes 208904 | tf_op jit(solution)/shard_map/ppermute | solution.py:27
  22.9 0.5 collective-permute-start.2
  23.4 0.1 collective-permute-start.1
  23.5 1.9 %collective-permute-done.3 = f32[136,128]{1,0:T(8,128)S(1)} collective-permute-done((f32[136,128]{1,0:T(8,128)S(1)}, f32[136,128]{1,0:T(8,128)S(1)}, u32[]{:S(2)}, u32[]{:S(2)}) %collective-permute-start.3) | collective-permute-done | bytes 69664 | tf_op jit(solution)/shard_map/ppermute | solution.py:27
  25.4 1.8 %collective-permute-done.2 = f32[136,128]{1,0:T(8,128)S(1)} collective-permute-done((f32[136,128]{1,0:T(8,128)S(1)}, f32[136,128]{1,0:T(8,128)S(1)}, u32[]{:S(2)}, u32[]{:S(2)}) %collective-permute-start.2) | collective-permute-done | bytes 69664 | tf_op jit(solution)/shard_map/ppermute | solution.py:27
  27.2 0.5 collective-permute-done.1
  27.7 3.7 %collective-permute-start.6 = (f32[136,128]{1,0:T(8,128)S(1)}, f32[136,128]{1,0:T(8,128)S(1)}, u32[]{:S(2)}, u32[]{:S(2)}) collective-permute-start(f32[136,128]{1,0:T(8,128)S(1)} %fusion.11), channel_id=1, source_target_pairs={{0,24},{1,25},{2,26},{3,27},{4,28},{5,29},{6,30},{7,31},{8,16},{9,... | collective-permute-start | bytes 208904 | tf_op jit(solution)/shard_map/ppermute | solution.py:27
  31.4 0.8 collective-permute-start.4
  32.2 1.9 %collective-permute-done.6 = f32[136,128]{1,0:T(8,128)S(1)} collective-permute-done((f32[136,128]{1,0:T(8,128)S(1)}, f32[136,128]{1,0:T(8,128)S(1)}, u32[]{:S(2)}, u32[]{:S(2)}) %collective-permute-start.6) | collective-permute-done | bytes 69664 | tf_op jit(solution)/shard_map/ppermute | solution.py:27
  34.0 2.8 %collective-permute-done.5 = f32[136,128]{1,0:T(8,128)S(1)} collective-permute-done((f32[136,128]{1,0:T(8,128)S(1)}, f32[136,128]{1,0:T(8,128)S(1)}, u32[]{:S(2)}, u32[]{:S(2)}) %collective-permute-start.5) | collective-permute-done | bytes 69664 | tf_op jit(solution)/shard_map/ppermute | solution.py:27
  36.9 0.9 fusion.13
  37.7 1.6 %collective-permute-start.9 = (f32[128,128]{1,0:T(8,128)S(1)}, f32[128,128]{1,0:T(8,128)S(1)}, u32[]{:S(2)}, u32[]{:S(2)}) collective-permute-start(f32[128,128]{1,0:T(8,128)S(1)} %fusion.13), channel_id=1, source_target_pairs={{0,3},{1,2},{2,1},{3,0},{4,7},{5,6},{6,5},{7,4},{8,11},{9,10},{10,... | collective-permute-start | bytes 196616 | tf_op jit(solution)/shard_map/ppermute | solution.py:27
  39.3 1.4 %collective-permute-start.8 = (f32[128,128]{1,0:T(8,128)S(1)}, f32[128,128]{1,0:T(8,128)S(1)}, u32[]{:S(2)}, u32[]{:S(2)}) collective-permute-start(f32[128,128]{1,0:T(8,128)S(1)} %fusion.13), channel_id=1, source_target_pairs={{0,2},{1,3},{2,0},{3,1},{4,6},{5,7},{6,4},{7,5},{8,10},{9,11},{10,... | collective-permute-start | bytes 196616 | tf_op jit(solution)/shard_map/ppermute | solution.py:27
  40.7 0.6 collective-permute-start.7
  41.3 2.3 %collective-permute-done.9 = f32[128,128]{1,0:T(8,128)S(1)} collective-permute-done((f32[128,128]{1,0:T(8,128)S(1)}, f32[128,128]{1,0:T(8,128)S(1)}, u32[]{:S(2)}, u32[]{:S(2)}) %collective-permute-start.9) | collective-permute-done | bytes 65568 | tf_op jit(solution)/shard_map/ppermute | solution.py:27
  43.6 0.3 collective-permute-done.8
  44.0 1.0 collective-permute-done.7
  45.1 0.1 collective-permute-start.10
  45.2 1.0 fusion.17
  46.3 0.4 collective-permute-done.10
  46.7 0.1 fusion.9
  46.8 0.8 pad_maximum_fusion
  47.6 1.1 copy.16
  48.7 4.0 %all-to-all-start = ((f32[32,32,128]{2,1,0:T(8,128)}), f32[32,32,128]{2,1,0:T(8,128)S(1)}, u32[]{:S(2)}, u32[]{:S(2)}) async-start(f32[32,32,128]{2,1,0:T(8,128)} %copy.16), calls=%async_computation | async-start | bytes 1048576 | tf_op jit(solution)/shard_map/all_to_all | solution.py:17
  52.7 0.6 broadcast_in_dim.4.extra_ref
  53.3 14.0 %turn.3 = (f32[128,2048]{1,0:T(8,128)}, f32[8,136,128]{2,1,0:T(8,128)}) custom-call(f32[1024,2048]{1,0:T(8,128)} %slab_ref.3, f32[1024,128]{1,0:T(8,128)} %bitcast.88, f32[128,2048]{1,0:T(8,128)} %get-tuple-element.9.right_ref, f32[8,128]{1,0:T(8,128)} %broadcast_in_dim.4.extra_ref), custom_call_target="tpu_custom_call" | custom-call | flops 6442450944 | bytes 8388608 | tf_op jit(solution)/shard_map/turn/pallas_call | solution.py:255
  67.4 1.6 %all-to-all-done = f32[32,32,128]{2,1,0:T(8,128)S(1)} async-done(((f32[32,32,128]{2,1,0:T(8,128)}), f32[32,32,128]{2,1,0:T(8,128)S(1)}, u32[]{:S(2)}, u32[]{:S(2)}) %all-to-all-start) | async-done | bytes 524320 | tf_op jit(solution)/shard_map/all_to_all | solution.py:17
  69.0 0.7 fusion.18
  69.7 0.7 copy.17
  70.4 3.6 %second_numerator.1 = f32[4,128,128]{2,1,0:T(8,128)} custom-call(f32[128,2048]{1,0:T(8,128)} %get-tuple-element.11.right_ref, f32[512,128]{1,0:T(8,128)} %bitcast.75, f32[4,128,128]{2,1,0:T(8,128)} %bitcast.77), custom_call_target="tpu_custom_call" | custom-call | flops 402653184 | bytes 1048576 | tf_op jit(solution)/shard_map/second_numerator/pallas_call | solution.py:274
  74.1 1.0 fusion.2
  75.1 0.1 collective-permute-start.11
  75.2 1.7 %collective-permute-done.11 = f32[4,200,128]{2,1,0:T(8,128)S(1)} collective-permute-done((f32[4,200,128]{2,1,0:T(8,128)S(1)}, f32[4,200,128]{2,1,0:T(8,128)S(1)}, u32[]{:S(2)}, u32[]{:S(2)}) %collective-permute-start.11) | collective-permute-done | bytes 409632 | tf_op jit(solution)/shard_map/ppermute | solution.py:27
  76.9 1.0 fusion.5
  78.0 1.2 collective-permute-start.14
  79.2 0.5 collective-permute-start.13
  79.7 1.8 %collective-permute-start.12 = (f32[200,128]{1,0:T(8,128)S(1)}, f32[200,128]{1,0:T(8,128)S(1)}, u32[]{:S(2)}, u32[]{:S(2)}) collective-permute-start(f32[200,128]{1,0:T(8,128)S(1)} %get-tuple-element.24), channel_id=1, source_target_pairs={{0,1},{1,0},{2,3},{3,2},{4,5},{5,4},{6,7},{7,6},{8,9},{9,8},{10,11... | collective-permute-start | bytes 307208 | tf_op jit(solution)/shard_map/ppermute | solution.py:27
  81.5 3.2 %collective-permute-done.14 = f32[200,128]{1,0:T(8,128)S(1)} collective-permute-done((f32[200,128]{1,0:T(8,128)S(1)}, f32[200,128]{1,0:T(8,128)S(1)}, u32[]{:S(2)}, u32[]{:S(2)}) %collective-permute-start.14) | collective-permute-done | bytes 102432 | tf_op jit(solution)/shard_map/ppermute | solution.py:27
  84.7 1.3 %collective-permute-done.13 = f32[200,128]{1,0:T(8,128)S(1)} collective-permute-done((f32[200,128]{1,0:T(8,128)S(1)}, f32[200,128]{1,0:T(8,128)S(1)}, u32[]{:S(2)}, u32[]{:S(2)}) %collective-permute-start.13) | collective-permute-done | bytes 102432 | tf_op jit(solution)/shard_map/ppermute | solution.py:27
  86.1 2.2 %collective-permute-start.17 = (f32[200,128]{1,0:T(8,128)S(1)}, f32[200,128]{1,0:T(8,128)S(1)}, u32[]{:S(2)}, u32[]{:S(2)}) collective-permute-start(f32[200,128]{1,0:T(8,128)S(1)} %fusion.10), channel_id=1, source_target_pairs={{0,24},{1,25},{2,26},{3,27},{4,28},{5,29},{6,30},{7,31},{8,16},{9,... | collective-permute-start | bytes 307208 | tf_op jit(solution)/shard_map/ppermute | solution.py:27
  88.2 0.4 collective-permute-start.16
  88.6 1.9 %collective-permute-start.15 = (f32[200,128]{1,0:T(8,128)S(1)}, f32[200,128]{1,0:T(8,128)S(1)}, u32[]{:S(2)}, u32[]{:S(2)}) collective-permute-start(f32[200,128]{1,0:T(8,128)S(1)} %fusion.10), channel_id=1, source_target_pairs={{0,8},{1,9},{2,10},{3,11},{4,12},{5,13},{6,14},{7,15},{8,0},{9,1},... | collective-permute-start | bytes 307208 | tf_op jit(solution)/shard_map/ppermute | solution.py:27
  90.5 3.2 %collective-permute-done.17 = f32[200,128]{1,0:T(8,128)S(1)} collective-permute-done((f32[200,128]{1,0:T(8,128)S(1)}, f32[200,128]{1,0:T(8,128)S(1)}, u32[]{:S(2)}, u32[]{:S(2)}) %collective-permute-start.17) | collective-permute-done | bytes 102432 | tf_op jit(solution)/shard_map/ppermute | solution.py:27
  93.8 4.2 %collective-permute-done.16 = f32[200,128]{1,0:T(8,128)S(1)} collective-permute-done((f32[200,128]{1,0:T(8,128)S(1)}, f32[200,128]{1,0:T(8,128)S(1)}, u32[]{:S(2)}, u32[]{:S(2)}) %collective-permute-start.16) | collective-permute-done | bytes 102432 | tf_op jit(solution)/shard_map/ppermute | solution.py:27
  98.0 0.9 fusion.12
  98.9 1.0 broadcast_divide_fusion
  100.0 0.7 collective-permute-start.19
  100.7 1.5 %collective-permute-start.18 = (f32[192,128]{1,0:T(8,128)S(1)}, f32[192,128]{1,0:T(8,128)S(1)}, u32[]{:S(2)}, u32[]{:S(2)}) collective-permute-start(f32[192,128]{1,0:T(8,128)S(1)} %get-tuple-element.43), channel_id=1, source_target_pairs={{0,1},{1,0},{2,3},{3,2},{4,5},{5,4},{6,7},{7,6},{8,9},{9,8},{10,11... | collective-permute-start | bytes 294920 | tf_op jit(solution)/shard_map/ppermute | solution.py:27
  102.2 1.3 %collective-permute-start.20 = (f32[192,128]{1,0:T(8,128)S(1)}, f32[192,128]{1,0:T(8,128)S(1)}, u32[]{:S(2)}, u32[]{:S(2)}) collective-permute-start(f32[192,128]{1,0:T(8,128)S(1)} %get-tuple-element.43), channel_id=1, source_target_pairs={{0,3},{1,2},{2,1},{3,0},{4,7},{5,6},{6,5},{7,4},{8,11},{9,10},{10,... | collective-permute-start | bytes 294920 | tf_op jit(solution)/shard_map/ppermute | solution.py:27
  103.5 2.2 %collective-permute-done.19 = f32[192,128]{1,0:T(8,128)S(1)} collective-permute-done((f32[192,128]{1,0:T(8,128)S(1)}, f32[192,128]{1,0:T(8,128)S(1)}, u32[]{:S(2)}, u32[]{:S(2)}) %collective-permute-start.19) | collective-permute-done | bytes 98336 | tf_op jit(solution)/shard_map/ppermute | solution.py:27
  105.7 2.0 %collective-permute-done.20 = f32[192,128]{1,0:T(8,128)S(1)} collective-permute-done((f32[192,128]{1,0:T(8,128)S(1)}, f32[192,128]{1,0:T(8,128)S(1)}, u32[]{:S(2)}, u32[]{:S(2)}) %collective-permute-start.20) | collective-permute-done | bytes 98336 | tf_op jit(solution)/shard_map/ppermute | solution.py:27
  107.9 1.7 %collective-permute-done.21 = f32[4,192,128]{2,1,0:T(8,128)S(1)} collective-permute-done((f32[4,192,128]{2,1,0:T(8,128)S(1)}, f32[4,192,128]{2,1,0:T(8,128)S(1)}, u32[]{:S(2)}, u32[]{:S(2)}) %collective-permute-start.21) | collective-permute-done | bytes 393248 | tf_op jit(solution)/shard_map/ppermute | solution.py:27
  109.6 0.2 fusion.6
  109.8 0.7 pad_maximum_fusion.4
  110.5 3.5 %second_rows.1 = f32[512,128]{1,0:T(8,128)} custom-call(f32[128,2048]{1,0:T(8,128)} %get-tuple-element.11.right_ref, f32[512,128]{1,0:T(8,128)} %bitcast.76, f32[4,128,128]{2,1,0:T(8,128)} %bitcast.85), custom_call_target="tpu_custom_call" | custom-call | flops 402653184 | bytes 1048576 | tf_op jit(solution)/shard_map/second_rows/pallas_call | solution.py:284
  114.0 3.2 %all-to-all-start.1 = ((f32[32,16,128]{2,1,0:T(8,128)}), f32[32,16,128]{2,1,0:T(8,128)S(1)}, u32[]{:S(2)}, u32[]{:S(2)}) async-start(f32[32,16,128]{2,1,0:T(8,128)} %bitcast.82), calls=%async_computation.1 | async-start | bytes 524288 | tf_op jit(solution)/shard_map/all_to_all | solution.py:17
  117.2 0.8 fusion
  118.0 10.1 %all-to-all-done.1 = f32[32,16,128]{2,1,0:T(8,128)S(1)} async-done(((f32[32,16,128]{2,1,0:T(8,128)}), f32[32,16,128]{2,1,0:T(8,128)S(1)}, u32[]{:S(2)}, u32[]{:S(2)}) %all-to-all-start.1) | async-done | bytes 262176 | tf_op jit(solution)/shard_map/all_to_all | solution.py:17
  128.2 0.7 copy.18
  (28 shorter events, 0.6 us)
Async XLA Ops:
  0.6 45.6 %copy-start = (f32[128,128]{1,0:T(8,128)S(1)}, f32[128,128]{1,0:T(8,128)}, u32[]{:S(2)}) copy-start(f32[128,128]{1,0:T(8,128)} %param.9) | copy-start | bytes 196612
  16.3 1.7 %collective-permute-start = (f32[4,136,128]{2,1,0:T(8,128)S(1)}, f32[4,136,128]{2,1,0:T(8,128)S(1)}, u32[]{:S(2)}, u32[]{:S(2)}) collective-permute-start(f32[4,136,128]{2,1,0:T(8,128)S(1)} %dynamic-slice_bitcast_fusion), channel_id=1, source_target_pairs={{0,4},{1,5},{2,6},{3,7},{4,0},{5,1},{6,2},{7,3},{8,12},{9,13},{10,... | collective-permute-start | bytes 835592 | tf_op jit(solution)/shard_map/ppermute | solution.py:27
  19.0 6.4 %collective-permute-start.3 = (f32[136,128]{1,0:T(8,128)S(1)}, f32[136,128]{1,0:T(8,128)S(1)}, u32[]{:S(2)}, u32[]{:S(2)}) collective-permute-start(f32[136,128]{1,0:T(8,128)S(1)} %get-tuple-element.31), channel_id=1, source_target_pairs={{0,3},{1,2},{2,1},{3,0},{4,7},{5,6},{6,5},{7,4},{8,11},{9,10},{10,... | collective-permute-start | bytes 208904 | tf_op jit(solution)/shard_map/ppermute | solution.py:27
  22.9 4.3 %collective-permute-start.2 = (f32[136,128]{1,0:T(8,128)S(1)}, f32[136,128]{1,0:T(8,128)S(1)}, u32[]{:S(2)}, u32[]{:S(2)}) collective-permute-start(f32[136,128]{1,0:T(8,128)S(1)} %get-tuple-element.32), channel_id=1, source_target_pairs={{0,2},{1,3},{2,0},{3,1},{4,6},{5,7},{6,4},{7,5},{8,10},{9,11},{10,... | collective-permute-start | bytes 208904 | tf_op jit(solution)/shard_map/ppermute | solution.py:27
  23.4 4.3 %collective-permute-start.1 = (f32[136,128]{1,0:T(8,128)S(1)}, f32[136,128]{1,0:T(8,128)S(1)}, u32[]{:S(2)}, u32[]{:S(2)}) collective-permute-start(f32[136,128]{1,0:T(8,128)S(1)} %get-tuple-element.33), channel_id=1, source_target_pairs={{0,1},{1,0},{2,3},{3,2},{4,5},{5,4},{6,7},{7,6},{8,9},{9,8},{10,11... | collective-permute-start | bytes 208904 | tf_op jit(solution)/shard_map/ppermute | solution.py:27
  27.7 6.3 %collective-permute-start.6 = (f32[136,128]{1,0:T(8,128)S(1)}, f32[136,128]{1,0:T(8,128)S(1)}, u32[]{:S(2)}, u32[]{:S(2)}) collective-permute-start(f32[136,128]{1,0:T(8,128)S(1)} %fusion.11), channel_id=1, source_target_pairs={{0,24},{1,25},{2,26},{3,27},{4,28},{5,29},{6,30},{7,31},{8,16},{9,... | collective-permute-start | bytes 208904 | tf_op jit(solution)/shard_map/ppermute | solution.py:27
  31.4 5.5 %collective-permute-start.5 = (f32[136,128]{1,0:T(8,128)S(1)}, f32[136,128]{1,0:T(8,128)S(1)}, u32[]{:S(2)}, u32[]{:S(2)}) collective-permute-start(f32[136,128]{1,0:T(8,128)S(1)} %fusion.11), channel_id=1, source_target_pairs={{0,16},{1,17},{2,18},{3,19},{4,20},{5,21},{6,22},{7,23},{8,24},{9,... | collective-permute-start | bytes 208904 | tf_op jit(solution)/shard_map/ppermute | solution.py:27
  31.4 5.5 %collective-permute-start.4 = (f32[136,128]{1,0:T(8,128)S(1)}, f32[136,128]{1,0:T(8,128)S(1)}, u32[]{:S(2)}, u32[]{:S(2)}) collective-permute-start(f32[136,128]{1,0:T(8,128)S(1)} %fusion.11), channel_id=1, source_target_pairs={{0,8},{1,9},{2,10},{3,11},{4,12},{5,13},{6,14},{7,15},{8,0},{9,1},... | collective-permute-start | bytes 208904 | tf_op jit(solution)/shard_map/ppermute | solution.py:27
  37.7 5.9 %collective-permute-start.9 = (f32[128,128]{1,0:T(8,128)S(1)}, f32[128,128]{1,0:T(8,128)S(1)}, u32[]{:S(2)}, u32[]{:S(2)}) collective-permute-start(f32[128,128]{1,0:T(8,128)S(1)} %fusion.13), channel_id=1, source_target_pairs={{0,3},{1,2},{2,1},{3,0},{4,7},{5,6},{6,5},{7,4},{8,11},{9,10},{10,... | collective-permute-start | bytes 196616 | tf_op jit(solution)/shard_map/ppermute | solution.py:27
  39.3 4.7 %collective-permute-start.8 = (f32[128,128]{1,0:T(8,128)S(1)}, f32[128,128]{1,0:T(8,128)S(1)}, u32[]{:S(2)}, u32[]{:S(2)}) collective-permute-start(f32[128,128]{1,0:T(8,128)S(1)} %fusion.13), channel_id=1, source_target_pairs={{0,2},{1,3},{2,0},{3,1},{4,6},{5,7},{6,4},{7,5},{8,10},{9,11},{10,... | collective-permute-start | bytes 196616 | tf_op jit(solution)/shard_map/ppermute | solution.py:27
  40.7 4.3 %collective-permute-start.7 = (f32[128,128]{1,0:T(8,128)S(1)}, f32[128,128]{1,0:T(8,128)S(1)}, u32[]{:S(2)}, u32[]{:S(2)}) collective-permute-start(f32[128,128]{1,0:T(8,128)S(1)} %fusion.13), channel_id=1, source_target_pairs={{0,1},{1,0},{2,3},{3,2},{4,5},{5,4},{6,7},{7,6},{8,9},{9,8},{10,11... | collective-permute-start | bytes 196616 | tf_op jit(solution)/shard_map/ppermute | solution.py:27
  45.1 1.6 %collective-permute-start.10 = (f32[4,128,128]{2,1,0:T(8,128)S(1)}, f32[4,128,128]{2,1,0:T(8,128)S(1)}, u32[]{:S(2)}, u32[]{:S(2)}) collective-permute-start(f32[4,128,128]{2,1,0:T(8,128)S(1)} %get-tuple-element.34), channel_id=1, source_target_pairs={{0,4},{1,5},{2,6},{3,7},{4,0},{5,1},{6,2},{7,3},{8,12},{9,13},{10,... | collective-permute-start | bytes 786440 | tf_op jit(solution)/shard_map/ppermute | solution.py:27
  48.7 20.3 %all-to-all-start = ((f32[32,32,128]{2,1,0:T(8,128)}), f32[32,32,128]{2,1,0:T(8,128)S(1)}, u32[]{:S(2)}, u32[]{:S(2)}) async-start(f32[32,32,128]{2,1,0:T(8,128)} %copy.16), calls=%async_computation | async-start | bytes 1048576 | tf_op jit(solution)/shard_map/all_to_all | solution.py:17
  75.1 1.8 %collective-permute-start.11 = (f32[4,200,128]{2,1,0:T(8,128)S(1)}, f32[4,200,128]{2,1,0:T(8,128)S(1)}, u32[]{:S(2)}, u32[]{:S(2)}) collective-permute-start(f32[4,200,128]{2,1,0:T(8,128)S(1)} %fusion.2), channel_id=1, source_target_pairs={{0,4},{1,5},{2,6},{3,7},{4,0},{5,1},{6,2},{7,3},{8,12},{9,13},{10,... | collective-permute-start | bytes 1228808 | tf_op jit(solution)/shard_map/ppermute | solution.py:27
  78.0 6.7 %collective-permute-start.14 = (f32[200,128]{1,0:T(8,128)S(1)}, f32[200,128]{1,0:T(8,128)S(1)}, u32[]{:S(2)}, u32[]{:S(2)}) collective-permute-start(f32[200,128]{1,0:T(8,128)S(1)} %get-tuple-element.22), channel_id=1, source_target_pairs={{0,3},{1,2},{2,1},{3,0},{4,7},{5,6},{6,5},{7,4},{8,11},{9,10},{10,... | collective-permute-start | bytes 307208 | tf_op jit(solution)/shard_map/ppermute | solution.py:27
  79.2 6.8 %collective-permute-start.13 = (f32[200,128]{1,0:T(8,128)S(1)}, f32[200,128]{1,0:T(8,128)S(1)}, u32[]{:S(2)}, u32[]{:S(2)}) collective-permute-start(f32[200,128]{1,0:T(8,128)S(1)} %get-tuple-element.23), channel_id=1, source_target_pairs={{0,2},{1,3},{2,0},{3,1},{4,6},{5,7},{6,4},{7,5},{8,10},{9,11},{10,... | collective-permute-start | bytes 307208 | tf_op jit(solution)/shard_map/ppermute | solution.py:27
  79.7 6.3 %collective-permute-start.12 = (f32[200,128]{1,0:T(8,128)S(1)}, f32[200,128]{1,0:T(8,128)S(1)}, u32[]{:S(2)}, u32[]{:S(2)}) collective-permute-start(f32[200,128]{1,0:T(8,128)S(1)} %get-tuple-element.24), channel_id=1, source_target_pairs={{0,1},{1,0},{2,3},{3,2},{4,5},{5,4},{6,7},{7,6},{8,9},{9,8},{10,11... | collective-permute-start | bytes 307208 | tf_op jit(solution)/shard_map/ppermute | solution.py:27
  86.1 7.7 %collective-permute-start.17 = (f32[200,128]{1,0:T(8,128)S(1)}, f32[200,128]{1,0:T(8,128)S(1)}, u32[]{:S(2)}, u32[]{:S(2)}) collective-permute-start(f32[200,128]{1,0:T(8,128)S(1)} %fusion.10), channel_id=1, source_target_pairs={{0,24},{1,25},{2,26},{3,27},{4,28},{5,29},{6,30},{7,31},{8,16},{9,... | collective-permute-start | bytes 307208 | tf_op jit(solution)/shard_map/ppermute | solution.py:27
  88.2 9.7 %collective-permute-start.16 = (f32[200,128]{1,0:T(8,128)S(1)}, f32[200,128]{1,0:T(8,128)S(1)}, u32[]{:S(2)}, u32[]{:S(2)}) collective-permute-start(f32[200,128]{1,0:T(8,128)S(1)} %fusion.10), channel_id=1, source_target_pairs={{0,16},{1,17},{2,18},{3,19},{4,20},{5,21},{6,22},{7,23},{8,24},{9,... | collective-permute-start | bytes 307208 | tf_op jit(solution)/shard_map/ppermute | solution.py:27
  88.6 9.4 %collective-permute-start.15 = (f32[200,128]{1,0:T(8,128)S(1)}, f32[200,128]{1,0:T(8,128)S(1)}, u32[]{:S(2)}, u32[]{:S(2)}) collective-permute-start(f32[200,128]{1,0:T(8,128)S(1)} %fusion.10), channel_id=1, source_target_pairs={{0,8},{1,9},{2,10},{3,11},{4,12},{5,13},{6,14},{7,15},{8,0},{9,1},... | collective-permute-start | bytes 307208 | tf_op jit(solution)/shard_map/ppermute | solution.py:27
  100.0 5.7 %collective-permute-start.19 = (f32[192,128]{1,0:T(8,128)S(1)}, f32[192,128]{1,0:T(8,128)S(1)}, u32[]{:S(2)}, u32[]{:S(2)}) collective-permute-start(f32[192,128]{1,0:T(8,128)S(1)} %get-tuple-element.43), channel_id=1, source_target_pairs={{0,2},{1,3},{2,0},{3,1},{4,6},{5,7},{6,4},{7,5},{8,10},{9,11},{10,... | collective-permute-start | bytes 294920 | tf_op jit(solution)/shard_map/ppermute | solution.py:27
  100.7 5.0 %collective-permute-start.18 = (f32[192,128]{1,0:T(8,128)S(1)}, f32[192,128]{1,0:T(8,128)S(1)}, u32[]{:S(2)}, u32[]{:S(2)}) collective-permute-start(f32[192,128]{1,0:T(8,128)S(1)} %get-tuple-element.43), channel_id=1, source_target_pairs={{0,1},{1,0},{2,3},{3,2},{4,5},{5,4},{6,7},{7,6},{8,9},{9,8},{10,11... | collective-permute-start | bytes 294920 | tf_op jit(solution)/shard_map/ppermute | solution.py:27
  102.2 5.5 %collective-permute-start.20 = (f32[192,128]{1,0:T(8,128)S(1)}, f32[192,128]{1,0:T(8,128)S(1)}, u32[]{:S(2)}, u32[]{:S(2)}) collective-permute-start(f32[192,128]{1,0:T(8,128)S(1)} %get-tuple-element.43), channel_id=1, source_target_pairs={{0,3},{1,2},{2,1},{3,0},{4,7},{5,6},{6,5},{7,4},{8,11},{9,10},{10,... | collective-permute-start | bytes 294920 | tf_op jit(solution)/shard_map/ppermute | solution.py:27
  107.8 1.8 %collective-permute-start.21 = (f32[4,192,128]{2,1,0:T(8,128)S(1)}, f32[4,192,128]{2,1,0:T(8,128)S(1)}, u32[]{:S(2)}, u32[]{:S(2)}) collective-permute-start(f32[4,192,128]{2,1,0:T(8,128)S(1)} %get-tuple-element.25), channel_id=1, source_target_pairs={{0,4},{1,5},{2,6},{3,7},{4,0},{5,1},{6,2},{7,3},{8,12},{9,13},{10,... | collective-permute-start | bytes 1179656 | tf_op jit(solution)/shard_map/ppermute | solution.py:27
  114.0 14.1 %all-to-all-start.1 = ((f32[32,16,128]{2,1,0:T(8,128)}), f32[32,16,128]{2,1,0:T(8,128)S(1)}, u32[]{:S(2)}, u32[]{:S(2)}) async-start(f32[32,16,128]{2,1,0:T(8,128)} %bitcast.82), calls=%async_computation.1 | async-start | bytes 524288 | tf_op jit(solution)/shard_map/all_to_all | solution.py:17

commit v3 on v2

--- a/solution.py
+++ b/solution.py
@@ -10,7 +10,7 @@
 AXES = ("row", "col")
 F32, BF16 = jnp.float32, jnp.bfloat16
 PAD = 8
-VMEM_BYTES = 54 * 1024 * 1024
+VMEM_BYTES = 48 * 1024 * 1024
 
 
 def exchange(parts):
@@ -102,26 +102,37 @@
     sums_ref[...] = jnp.broadcast_to(jnp.sum(turned, axis=1, keepdims=True), sums_ref.shape)
 
 
-def row_chunks(m):
-    size = min(256, m)
-    return [pl.ds(start, size) for start in range(0, m, size)]
-
-
-def quotients(slab_ref, pair_ref, right, rows):
+def chunks(extent, size):
+    size = min(size, extent)
+    return [pl.ds(start, size) for start in range(0, extent, size)]
+
+
+def stacked(right):
     high, low = split(right)
-    product = dot(pair_ref[rows, :], jnp.concatenate([high, high, low], axis=0))
-    return split(divide(slab_ref[rows, :], product))
-
-
-def right_update(slab_ref, pair_ref, pair_t_ref, sums_ref, right, high_ref, low_ref):
-    rank = right.shape[0]
-    for rows in row_chunks(slab_ref.shape[0]):
-        high, low = quotients(slab_ref, pair_ref, right, rows)
-        high_ref[rows, :] = high
-        low_ref[rows, :] = low
-    both = dot(pair_t_ref[...], high_ref[...])
-    numerator = both[:rank] + both[rank:] + dot(pair_t_ref[:rank, :], low_ref[...])
-    return right * numerator / sums_ref[:, :1]
+    return jnp.concatenate([high, high, low], axis=0)
+
+
+def quotients(slab_ref, pair_ref, right_stack, rows, columns):
+    product = dot(pair_ref[rows, :], right_stack)
+    return split(divide(slab_ref[rows, columns], product))
+
+
+def right_update(
+    slab_ref, pair_ref, pair_t_ref, sums_ref, right_ref, right_out, high_ref, low_ref
+):
+    m, block = slab_ref.shape
+    rank = right_ref.shape[0]
+    for columns in chunks(block, 256):
+        right = right_ref[:, columns]
+        stack = stacked(right)
+        for rows in chunks(m, 512):
+            high, low = quotients(slab_ref, pair_ref, stack, rows, columns)
+            high_ref[rows, columns] = high
+            low_ref[rows, columns] = low
+        both = dot(pair_t_ref[...], high_ref[:, columns])
+        numerator = both[:rank] + both[rank:]
+        numerator = numerator + dot(pair_t_ref[:rank, :], low_ref[:, columns])
+        right_out[:, columns] = right * numerator / sums_ref[:, :1]
 
 
 def left_numerator(slab_ref, pair_ref, right, total_ref, sums_ref, first):
@@ -132,8 +143,9 @@
     row_sums = dot_nt(ones, right_both)[:PAD]
     row_sums = row_sums[:, :rank] + row_sums[:, rank:]
     sums_ref[...] = jnp.where(first, row_sums, sums_ref[...] + row_sums)
-    for rows in row_chunks(slab_ref.shape[0]):
-        high, low = quotients(slab_ref, pair_ref, right, rows)
+    stack = stacked(right)
+    for rows in chunks(slab_ref.shape[0], 256):
+        high, low = quotients(slab_ref, pair_ref, stack, rows, slice(None))
         both = dot_nt(high, right_both)
         term = both[:, :rank] + both[:, rank:] + dot_nt(low, right_high)
         total_ref[rows, :] = jnp.where(first, term, total_ref[rows, :] + term)
@@ -143,7 +155,7 @@
     parts, tall, rank = out_ref.shape
     height = tall - PAD
     first = lax.broadcasted_iota(jnp.int32, (PAD, rank), 0) == 0
-    stats = jnp.where(first, row_sums_ref[...], extra_ref[...])
+    stats = jnp.where(first, row_sums_ref[...], extra_ref[:1, :])
     for part in range(parts):
         out_ref[part, :height, :] = total_ref[pl.ds(part * height, height), :]
         out_ref[part, height:, :] = stats
@@ -160,11 +172,10 @@
         prepare_left(left_ref, pair_ref)
         prepare_left_t(left_ref, pair_t_ref, sums_ref)
 
-    right = right_update(
-        slab_ref, pair_ref, pair_t_ref, sums_ref, right_ref[...], high_ref, low_ref
-    )
-    right_out[...] = right
-    left_numerator(slab_ref, pair_ref, right, total_ref, row_sums_ref, step == 0)
+    right_update(
+        slab_ref, pair_ref, pair_t_ref, sums_ref, right_ref, right_out, high_ref, low_ref
+    )
+    left_numerator(slab_ref, pair_ref, right_out[...], total_ref, row_sums_ref, step == 0)
 
     @pl.when(step == pl.num_programs(0) - 1)
     def _():
@@ -255,7 +266,7 @@
     return pl.pallas_call(
         turn_kernel,
         grid=(columns // block,),
-        in_specs=[columns_spec(m), full((m, rank)), columns_spec(rank), full((PAD, rank))],
+        in_specs=[columns_spec(m), full((m, rank)), columns_spec(rank), full((min(PAD, extra.shape[0]), rank))],
         out_specs=[columns_spec(rank), full((parts, tall, rank))],
         out_shape=[
             jax.ShapeDtypeStruct((rank, columns), F32),
@@ -306,7 +317,7 @@
     own_left = lax.dynamic_slice_in_dim(
         second_left_init, lax.axis_index("col") * second_rows, second_rows, 0
     )
-    col_part = jnp.broadcast_to(jnp.sum(own_left, axis=0)[None], (PAD, rank))
+    col_part = jnp.sum(own_left, axis=0)[None]
     own_left = own_left.reshape(per_owner, devices, slices, rank).transpose(1, 0, 2, 3)
     own_left = own_left.reshape(devices, per_owner * slices, rank)
     piece_rows = rank // row_devices

time: 129 us -> 121 us (0.938)
  other arithmetic: 9.77 us -> 3.57 us
  Pallas kernels: 35.8 us -> 32.2 us
  local copies, waits for them, and re-layouts: 5.06 us -> 6.58 us
    unnamed x2 -> x10, local copies, waits for them, and re-layouts: 0.01 us -> 4.48 us
    pallas_call x1, Pallas kernels: 3.63 us -> 1.59 us  [second_numerator(): pl.pallas_call(functools.partial(numerator_kernel, slices), out_shape=jax...]
    add x2, other arithmetic: 2.03 us -> 0.07 us  [reduce_core(): return pick(parts, core) + send(pick(parts, 1 - core), 1, 0)]
    another operation x3, other arithmetic: 2.38 us -> 0.9 us  [spread_core(): return jnp.stack([pick(both, core), pick(both, 1 - core)])]
    pallas_call x1, Pallas kernels: 3.52 us -> 2.19 us  [second_rows_out(): pl.pallas_call(functools.partial(second_kernel, slices), out_shape=jax.Sh...]
  transfers between devices with their start and end apart: 24 -> 24, of which waited for: 20 -> 21; matrix products, arithmetic and copies ran while one was open for 2% -> 2% of each run, Pallas kernels for 11% -> 12%
where the time goes in v3:
time: 121 us; the launch traced here: 120 us
  waiting for transfers between devices  44.6 us (37%)
  starting transfers between devices  32.4 us (27%)
  Pallas kernels  32.2 us (27%)
  local copies, waits for them, and re-layouts  6.58 us (5%)
  other arithmetic  3.57 us (3%)
    ppermute x22, waiting for transfers between devices, send(): return lax.ppermute(values, AXES, pairs)  33.7 us
    pallas_call x2, Pallas kernels, full_turn(): pl.pallas_call(turn_kernel, grid=(columns // block,), in_specs=[columns_s...  28.4 us
    ppermute x22, starting transfers between devices, send(): return lax.ppermute(values, AXES, pairs)  24.8 us
    all_to_all x2, waiting for transfers between devices, exchange(): return lax.all_to_all(parts, AXES, split_axis=0, concat_axis=0, tiled=True)  10.9 us
    all_to_all x2, starting transfers between devices, exchange(): return lax.all_to_all(parts, AXES, split_axis=0, concat_axis=0, tiled=True)  7.58 us
    unnamed x10, local copies, waits for them, and re-layouts  4.48 us
  transfers between devices with their start and end apart: 24, of which 21 were waited for; matrix products, arithmetic and copies ran while one was open for 2% of the time, Pallas kernels for 12%

profile of v3, /device:TPU:0, one launch (start us, length us, event | category | flops | bytes accessed | tf_op | source)
XLA Modules:
  0.0 120.3 jit_solution(4073314740593155399)
XLA Ops:
  0.6 0.0 copy-start
  0.7 0.0 copy-start.1
  0.7 1.0 copy-done.1
  1.7 1.2 %copy-done.2 = f32[128,2048]{1,0:T(8,128)S(1)} copy-done((f32[128,2048]{1,0:T(8,128)S(1)}, f32[128,2048]{1,0:T(8,128)}, u32[]{:S(2)}) %copy-start.2) | copy-done | bytes 1048600
  2.9 14.2 %turn.2 = (f32[128,2048]{1,0:T(8,128)S(1)}, f32[8,136,128]{2,1,0:T(8,128)S(1)}) custom-call(f32[1024,2048]{1,0:T(8,128)} %slab_ref.3, f32[1024,128]{1,0:T(8,128)S(1)} %copy-done.1, f32[128,2048]{1,0:T(8,128)S(1)} %copy-done.2, f32[1024,128]{1,0:T(8,128)S(1)} %copy-done.1), custom_call_target="tpu_custom_call" | custom-call | flops 6442450944 | bytes 8388608 | tf_op jit(solution)/shard_map/turn/pallas_call | solution.py:266
  17.1 1.0 copy-done.3
  18.2 0.5 collective-permute-start
  18.7 1.2 collective-permute-done
  19.9 3.9 %collective-permute-start.3 = (f32[136,128]{1,0:T(8,128)S(1)}, f32[136,128]{1,0:T(8,128)S(1)}, u32[]{:S(2)}, u32[]{:S(2)}) collective-permute-start(f32[136,128]{1,0:T(8,128)S(1)} %get-tuple-element.31), channel_id=1, source_target_pairs={{0,3},{1,2},{2,1},{3,0},{4,7},{5,6},{6,5},{7,4},{8,11},{9,10},{10,... | collective-permute-start | bytes 208904 | tf_op jit(solution)/shard_map/ppermute | solution.py:27
  23.8 0.5 collective-permute-start.2
  24.3 0.1 collective-permute-start.1
  24.5 1.9 %collective-permute-done.3 = f32[136,128]{1,0:T(8,128)S(1)} collective-permute-done((f32[136,128]{1,0:T(8,128)S(1)}, f32[136,128]{1,0:T(8,128)S(1)}, u32[]{:S(2)}, u32[]{:S(2)}) %collective-permute-start.3) | collective-permute-done | bytes 69664 | tf_op jit(solution)/shard_map/ppermute | solution.py:27
  26.3 1.8 %collective-permute-done.2 = f32[136,128]{1,0:T(8,128)S(1)} collective-permute-done((f32[136,128]{1,0:T(8,128)S(1)}, f32[136,128]{1,0:T(8,128)S(1)}, u32[]{:S(2)}, u32[]{:S(2)}) %collective-permute-start.2) | collective-permute-done | bytes 69664 | tf_op jit(solution)/shard_map/ppermute | solution.py:27
  28.1 0.5 collective-permute-done.1
  28.6 3.7 %collective-permute-start.6 = (f32[136,128]{1,0:T(8,128)S(1)}, f32[136,128]{1,0:T(8,128)S(1)}, u32[]{:S(2)}, u32[]{:S(2)}) collective-permute-start(f32[136,128]{1,0:T(8,128)S(1)} %fusion.11), channel_id=1, source_target_pairs={{0,24},{1,25},{2,26},{3,27},{4,28},{5,29},{6,30},{7,31},{8,16},{9,... | collective-permute-start | bytes 208904 | tf_op jit(solution)/shard_map/ppermute | solution.py:27
  32.3 0.8 collective-permute-start.4
  33.1 1.9 %collective-permute-done.6 = f32[136,128]{1,0:T(8,128)S(1)} collective-permute-done((f32[136,128]{1,0:T(8,128)S(1)}, f32[136,128]{1,0:T(8,128)S(1)}, u32[]{:S(2)}, u32[]{:S(2)}) %collective-permute-start.6) | collective-permute-done | bytes 69664 | tf_op jit(solution)/shard_map/ppermute | solution.py:27
  35.0 2.8 %collective-permute-done.5 = f32[136,128]{1,0:T(8,128)S(1)} collective-permute-done((f32[136,128]{1,0:T(8,128)S(1)}, f32[136,128]{1,0:T(8,128)S(1)}, u32[]{:S(2)}, u32[]{:S(2)}) %collective-permute-start.5) | collective-permute-done | bytes 69664 | tf_op jit(solution)/shard_map/ppermute | solution.py:27
  37.8 0.0 collective-permute-done.4
  37.8 0.9 fusion.13
  38.7 1.6 %collective-permute-start.9 = (f32[128,128]{1,0:T(8,128)S(1)}, f32[128,128]{1,0:T(8,128)S(1)}, u32[]{:S(2)}, u32[]{:S(2)}) collective-permute-start(f32[128,128]{1,0:T(8,128)S(1)} %fusion.13), channel_id=1, source_target_pairs={{0,3},{1,2},{2,1},{3,0},{4,7},{5,6},{6,5},{7,4},{8,11},{9,10},{10,... | collective-permute-start | bytes 196616 | tf_op jit(solution)/shard_map/ppermute | solution.py:27
  40.2 1.4 %collective-permute-start.8 = (f32[128,128]{1,0:T(8,128)S(1)}, f32[128,128]{1,0:T(8,128)S(1)}, u32[]{:S(2)}, u32[]{:S(2)}) collective-permute-start(f32[128,128]{1,0:T(8,128)S(1)} %fusion.13), channel_id=1, source_target_pairs={{0,2},{1,3},{2,0},{3,1},{4,6},{5,7},{6,4},{7,5},{8,10},{9,11},{10,... | collective-permute-start | bytes 196616 | tf_op jit(solution)/shard_map/ppermute | solution.py:27
  41.6 0.6 collective-permute-start.7
  42.2 2.3 %collective-permute-done.9 = f32[128,128]{1,0:T(8,128)S(1)} collective-permute-done((f32[128,128]{1,0:T(8,128)S(1)}, f32[128,128]{1,0:T(8,128)S(1)}, u32[]{:S(2)}, u32[]{:S(2)}) %collective-permute-start.9) | collective-permute-done | bytes 65568 | tf_op jit(solution)/shard_map/ppermute | solution.py:27
  44.6 0.3 collective-permute-done.8
  44.9 1.0 collective-permute-done.7
  46.0 0.1 collective-permute-start.10
  46.1 1.0 fusion.17
  47.3 0.4 collective-permute-done.10
  47.6 0.1 fusion.9
  47.7 0.1 pad_maximum_fusion
  47.8 1.1 copy.16
  48.9 4.0 %all-to-all-start = ((f32[32,32,128]{2,1,0:T(8,128)}), f32[32,32,128]{2,1,0:T(8,128)S(1)}, u32[]{:S(2)}, u32[]{:S(2)}) async-start(f32[32,32,128]{2,1,0:T(8,128)} %copy.16), calls=%async_computation | async-start | bytes 1048576 | tf_op jit(solution)/shard_map/all_to_all | solution.py:17
  52.9 1.2 %copy-done.4 = f32[128,2048]{1,0:T(8,128)S(1)} copy-done((f32[128,2048]{1,0:T(8,128)S(1)}, f32[128,2048]{1,0:T(8,128)}, u32[]{:S(2)}) %copy-start.4) | copy-done | bytes 1048600
  54.1 14.2 %turn.3 = (f32[128,2048]{1,0:T(8,128)S(1)}, f32[8,136,128]{2,1,0:T(8,128)S(1)}) custom-call(f32[1024,2048]{1,0:T(8,128)} %slab_ref.3, f32[1024,128]{1,0:T(8,128)S(1)} %bitcast.84, f32[128,2048]{1,0:T(8,128)S(1)} %copy-done.4, f32[1,128]{1,0:T(1,128)S(1)} %bitcast.88), custom_call_target="tpu_custom_call" | custom-call | flops 6442450944 | bytes 8388608 | tf_op jit(solution)/shard_map/turn/pallas_call | solution.py:266
  68.3 0.8 all-to-all-done
  69.2 1.6 %second_numerator.1 = f32[4,128,128]{2,1,0:T(8,128)S(1)} custom-call(f32[128,2048]{1,0:T(8,128)S(1)} %get-tuple-element.11.right_ref, f32[512,128]{1,0:T(8,128)S(1)} %bitcast.76, f32[4,128,128]{2,1,0:T(8,128)S(1)} %bitcast.78), custom_call_target="tpu_custom_call" | custom-call | flops 402653184 | bytes 1048576 | tf_op jit(solution)/shard_map/second_numerator/pallas_call | solution.py:285
  70.8 0.1 collective-permute-start.11
  70.9 1.7 %collective-permute-done.11 = f32[4,200,128]{2,1,0:T(8,128)S(1)} collective-permute-done((f32[4,200,128]{2,1,0:T(8,128)S(1)}, f32[4,200,128]{2,1,0:T(8,128)S(1)}, u32[]{:S(2)}, u32[]{:S(2)}) %collective-permute-start.11) | collective-permute-done | bytes 409632 | tf_op jit(solution)/shard_map/ppermute | solution.py:27
  72.7 1.9 %collective-permute-start.14 = (f32[200,128]{1,0:T(8,128)S(1)}, f32[200,128]{1,0:T(8,128)S(1)}, u32[]{:S(2)}, u32[]{:S(2)}) collective-permute-start(f32[200,128]{1,0:T(8,128)S(1)} %get-tuple-element.22), channel_id=1, source_target_pairs={{0,3},{1,2},{2,1},{3,0},{4,7},{5,6},{6,5},{7,4},{8,11},{9,10},{10,... | collective-permute-start | bytes 307208 | tf_op jit(solution)/shard_map/ppermute | solution.py:27
  74.7 0.6 collective-permute-start.13
  75.2 1.1 collective-permute-start.12
  76.3 2.6 %collective-permute-done.14 = f32[200,128]{1,0:T(8,128)S(1)} collective-permute-done((f32[200,128]{1,0:T(8,128)S(1)}, f32[200,128]{1,0:T(8,128)S(1)}, u32[]{:S(2)}, u32[]{:S(2)}) %collective-permute-start.14) | collective-permute-done | bytes 102432 | tf_op jit(solution)/shard_map/ppermute | solution.py:27
  78.9 1.9 %collective-permute-done.13 = f32[200,128]{1,0:T(8,128)S(1)} collective-permute-done((f32[200,128]{1,0:T(8,128)S(1)}, f32[200,128]{1,0:T(8,128)S(1)}, u32[]{:S(2)}, u32[]{:S(2)}) %collective-permute-start.13) | collective-permute-done | bytes 102432 | tf_op jit(solution)/shard_map/ppermute | solution.py:27
  80.9 2.9 %collective-permute-start.17 = (f32[200,128]{1,0:T(8,128)S(1)}, f32[200,128]{1,0:T(8,128)S(1)}, u32[]{:S(2)}, u32[]{:S(2)}) collective-permute-start(f32[200,128]{1,0:T(8,128)S(1)} %fusion.10), channel_id=1, source_target_pairs={{0,24},{1,25},{2,26},{3,27},{4,28},{5,29},{6,30},{7,31},{8,16},{9,... | collective-permute-start | bytes 307208 | tf_op jit(solution)/shard_map/ppermute | solution.py:27
  83.8 1.5 %collective-permute-start.15 = (f32[200,128]{1,0:T(8,128)S(1)}, f32[200,128]{1,0:T(8,128)S(1)}, u32[]{:S(2)}, u32[]{:S(2)}) collective-permute-start(f32[200,128]{1,0:T(8,128)S(1)} %fusion.10), channel_id=1, source_target_pairs={{0,8},{1,9},{2,10},{3,11},{4,12},{5,13},{6,14},{7,15},{8,0},{9,1},... | collective-permute-start | bytes 307208 | tf_op jit(solution)/shard_map/ppermute | solution.py:27
  85.3 3.3 %collective-permute-done.17 = f32[200,128]{1,0:T(8,128)S(1)} collective-permute-done((f32[200,128]{1,0:T(8,128)S(1)}, f32[200,128]{1,0:T(8,128)S(1)}, u32[]{:S(2)}, u32[]{:S(2)}) %collective-permute-start.17) | collective-permute-done | bytes 102432 | tf_op jit(solution)/shard_map/ppermute | solution.py:27
  88.6 4.2 %collective-permute-done.16 = f32[200,128]{1,0:T(8,128)S(1)} collective-permute-done((f32[200,128]{1,0:T(8,128)S(1)}, f32[200,128]{1,0:T(8,128)S(1)}, u32[]{:S(2)}, u32[]{:S(2)}) %collective-permute-start.16) | collective-permute-done | bytes 102432 | tf_op jit(solution)/shard_map/ppermute | solution.py:27
  92.8 0.1 broadcast_divide_fusion
  92.9 1.5 %collective-permute-start.19 = (f32[192,128]{1,0:T(8,128)S(1)}, f32[192,128]{1,0:T(8,128)S(1)}, u32[]{:S(2)}, u32[]{:S(2)}) collective-permute-start(f32[192,128]{1,0:T(8,128)S(1)} %get-tuple-element.43), channel_id=1, source_target_pairs={{0,2},{1,3},{2,0},{3,1},{4,6},{5,7},{6,4},{7,5},{8,10},{9,11},{10,... | collective-permute-start | bytes 294920 | tf_op jit(solution)/shard_map/ppermute | solution.py:27
  94.5 0.7 collective-permute-start.18
  95.2 1.3 %collective-permute-start.20 = (f32[192,128]{1,0:T(8,128)S(1)}, f32[192,128]{1,0:T(8,128)S(1)}, u32[]{:S(2)}, u32[]{:S(2)}) collective-permute-start(f32[192,128]{1,0:T(8,128)S(1)} %get-tuple-element.43), channel_id=1, source_target_pairs={{0,3},{1,2},{2,1},{3,0},{4,7},{5,6},{6,5},{7,4},{8,11},{9,10},{10,... | collective-permute-start | bytes 294920 | tf_op jit(solution)/shard_map/ppermute | solution.py:27
  96.5 1.2 collective-permute-done.19
  97.7 1.5 %collective-permute-done.18 = f32[192,128]{1,0:T(8,128)S(1)} collective-permute-done((f32[192,128]{1,0:T(8,128)S(1)}, f32[192,128]{1,0:T(8,128)S(1)}, u32[]{:S(2)}, u32[]{:S(2)}) %collective-permute-start.18) | collective-permute-done | bytes 98336 | tf_op jit(solution)/shard_map/ppermute | solution.py:27
  99.2 1.5 %collective-permute-done.20 = f32[192,128]{1,0:T(8,128)S(1)} collective-permute-done((f32[192,128]{1,0:T(8,128)S(1)}, f32[192,128]{1,0:T(8,128)S(1)}, u32[]{:S(2)}, u32[]{:S(2)}) %collective-permute-start.20) | collective-permute-done | bytes 98336 | tf_op jit(solution)/shard_map/ppermute | solution.py:27
  100.8 0.1 pad_maximum_fusion.3
  100.9 0.1 collective-permute-start.21
  100.9 1.7 %collective-permute-done.21 = f32[4,192,128]{2,1,0:T(8,128)S(1)} collective-permute-done((f32[4,192,128]{2,1,0:T(8,128)S(1)}, f32[4,192,128]{2,1,0:T(8,128)S(1)}, u32[]{:S(2)}, u32[]{:S(2)}) %collective-permute-start.21) | collective-permute-done | bytes 393248 | tf_op jit(solution)/shard_map/ppermute | solution.py:27
  102.7 0.2 fusion.6
  102.8 2.2 %second_rows.1 = f32[512,128]{1,0:T(8,128)} custom-call(f32[128,2048]{1,0:T(8,128)S(1)} %get-tuple-element.11.right_ref, f32[512,128]{1,0:T(8,128)S(1)} %bitcast.77, f32[4,128,128]{2,1,0:T(8,128)S(1)} %bitcast.83), custom_call_target="tpu_custom_call" | custom-call | flops 402653184 | bytes 1048576 | tf_op jit(solution)/shard_map/second_rows/pallas_call | solution.py:295
  105.0 3.6 %all-to-all-start.1 = ((f32[32,16,128]{2,1,0:T(8,128)}), f32[32,16,128]{2,1,0:T(8,128)S(1)}, u32[]{:S(2)}, u32[]{:S(2)}) async-start(f32[32,16,128]{2,1,0:T(8,128)} %bitcast.45), calls=%async_computation.1 | async-start | bytes 524288 | tf_op jit(solution)/shard_map/all_to_all | solution.py:17
  108.6 0.8 fusion
  109.4 10.1 %all-to-all-done.1 = f32[32,16,128]{2,1,0:T(8,128)S(1)} async-done(((f32[32,16,128]{2,1,0:T(8,128)}), f32[32,16,128]{2,1,0:T(8,128)S(1)}, u32[]{:S(2)}, u32[]{:S(2)}) %all-to-all-start.1) | async-done | bytes 262176 | tf_op jit(solution)/shard_map/all_to_all | solution.py:17
  119.6 0.7 copy.18
  (35 shorter events, 0.7 us)
Async XLA Ops:
  0.6 46.5 %copy-start = (f32[128,128]{1,0:T(8,128)S(1)}, f32[128,128]{1,0:T(8,128)}, u32[]{:S(2)}) copy-start(f32[128,128]{1,0:T(8,128)} %param.9) | copy-start | bytes 196612
  0.7 1.0 copy-start.1
  1.7 1.2 %copy-start.2 = (f32[128,2048]{1,0:T(8,128)S(1)}, f32[128,2048]{1,0:T(8,128)}, u32[]{:S(2)}) copy-start(f32[128,2048]{1,0:T(8,128)} %right_ref.1) | copy-start | bytes 3145732
  17.1 1.0 copy-start.3
  18.2 1.7 %collective-permute-start = (f32[4,136,128]{2,1,0:T(8,128)S(1)}, f32[4,136,128]{2,1,0:T(8,128)S(1)}, u32[]{:S(2)}, u32[]{:S(2)}) collective-permute-start(f32[4,136,128]{2,1,0:T(8,128)S(1)} %dynamic-slice_bitcast_fusion), channel_id=1, source_target_pairs={{0,4},{1,5},{2,6},{3,7},{4,0},{5,1},{6,2},{7,3},{8,12},{9,13},{10,... | collective-permute-start | bytes 835592 | tf_op jit(solution)/shard_map/ppermute | solution.py:27
  19.9 6.4 %collective-permute-start.3 = (f32[136,128]{1,0:T(8,128)S(1)}, f32[136,128]{1,0:T(8,128)S(1)}, u32[]{:S(2)}, u32[]{:S(2)}) collective-permute-start(f32[136,128]{1,0:T(8,128)S(1)} %get-tuple-element.31), channel_id=1, source_target_pairs={{0,3},{1,2},{2,1},{3,0},{4,7},{5,6},{6,5},{7,4},{8,11},{9,10},{10,... | collective-permute-start | bytes 208904 | tf_op jit(solution)/shard_map/ppermute | solution.py:27
  23.8 4.3 %collective-permute-start.2 = (f32[136,128]{1,0:T(8,128)S(1)}, f32[136,128]{1,0:T(8,128)S(1)}, u32[]{:S(2)}, u32[]{:S(2)}) collective-permute-start(f32[136,128]{1,0:T(8,128)S(1)} %get-tuple-element.32), channel_id=1, source_target_pairs={{0,2},{1,3},{2,0},{3,1},{4,6},{5,7},{6,4},{7,5},{8,10},{9,11},{10,... | collective-permute-start | bytes 208904 | tf_op jit(solution)/shard_map/ppermute | solution.py:27
  24.3 4.3 %collective-permute-start.1 = (f32[136,128]{1,0:T(8,128)S(1)}, f32[136,128]{1,0:T(8,128)S(1)}, u32[]{:S(2)}, u32[]{:S(2)}) collective-permute-start(f32[136,128]{1,0:T(8,128)S(1)} %get-tuple-element.33), channel_id=1, source_target_pairs={{0,1},{1,0},{2,3},{3,2},{4,5},{5,4},{6,7},{7,6},{8,9},{9,8},{10,11... | collective-permute-start | bytes 208904 | tf_op jit(solution)/shard_map/ppermute | solution.py:27
  28.6 6.3 %collective-permute-start.6 = (f32[136,128]{1,0:T(8,128)S(1)}, f32[136,128]{1,0:T(8,128)S(1)}, u32[]{:S(2)}, u32[]{:S(2)}) collective-permute-start(f32[136,128]{1,0:T(8,128)S(1)} %fusion.11), channel_id=1, source_target_pairs={{0,24},{1,25},{2,26},{3,27},{4,28},{5,29},{6,30},{7,31},{8,16},{9,... | collective-permute-start | bytes 208904 | tf_op jit(solution)/shard_map/ppermute | solution.py:27
  32.3 5.4 %collective-permute-start.5 = (f32[136,128]{1,0:T(8,128)S(1)}, f32[136,128]{1,0:T(8,128)S(1)}, u32[]{:S(2)}, u32[]{:S(2)}) collective-permute-start(f32[136,128]{1,0:T(8,128)S(1)} %fusion.11), channel_id=1, source_target_pairs={{0,16},{1,17},{2,18},{3,19},{4,20},{5,21},{6,22},{7,23},{8,24},{9,... | collective-permute-start | bytes 208904 | tf_op jit(solution)/shard_map/ppermute | solution.py:27
  32.3 5.4 %collective-permute-start.4 = (f32[136,128]{1,0:T(8,128)S(1)}, f32[136,128]{1,0:T(8,128)S(1)}, u32[]{:S(2)}, u32[]{:S(2)}) collective-permute-start(f32[136,128]{1,0:T(8,128)S(1)} %fusion.11), channel_id=1, source_target_pairs={{0,8},{1,9},{2,10},{3,11},{4,12},{5,13},{6,14},{7,15},{8,0},{9,1},... | collective-permute-start | bytes 208904 | tf_op jit(solution)/shard_map/ppermute | solution.py:27
  38.7 5.9 %collective-permute-start.9 = (f32[128,128]{1,0:T(8,128)S(1)}, f32[128,128]{1,0:T(8,128)S(1)}, u32[]{:S(2)}, u32[]{:S(2)}) collective-permute-start(f32[128,128]{1,0:T(8,128)S(1)} %fusion.13), channel_id=1, source_target_pairs={{0,3},{1,2},{2,1},{3,0},{4,7},{5,6},{6,5},{7,4},{8,11},{9,10},{10,... | collective-permute-start | bytes 196616 | tf_op jit(solution)/shard_map/ppermute | solution.py:27
  40.2 4.7 %collective-permute-start.8 = (f32[128,128]{1,0:T(8,128)S(1)}, f32[128,128]{1,0:T(8,128)S(1)}, u32[]{:S(2)}, u32[]{:S(2)}) collective-permute-start(f32[128,128]{1,0:T(8,128)S(1)} %fusion.13), channel_id=1, source_target_pairs={{0,2},{1,3},{2,0},{3,1},{4,6},{5,7},{6,4},{7,5},{8,10},{9,11},{10,... | collective-permute-start | bytes 196616 | tf_op jit(solution)/shard_map/ppermute | solution.py:27
  41.6 4.3 %collective-permute-start.7 = (f32[128,128]{1,0:T(8,128)S(1)}, f32[128,128]{1,0:T(8,128)S(1)}, u32[]{:S(2)}, u32[]{:S(2)}) collective-permute-start(f32[128,128]{1,0:T(8,128)S(1)} %fusion.13), channel_id=1, source_target_pairs={{0,1},{1,0},{2,3},{3,2},{4,5},{5,4},{6,7},{7,6},{8,9},{9,8},{10,11... | collective-permute-start | bytes 196616 | tf_op jit(solution)/shard_map/ppermute | solution.py:27
  46.0 1.6 %collective-permute-start.10 = (f32[4,128,128]{2,1,0:T(8,128)S(1)}, f32[4,128,128]{2,1,0:T(8,128)S(1)}, u32[]{:S(2)}, u32[]{:S(2)}) collective-permute-start(f32[4,128,128]{2,1,0:T(8,128)S(1)} %get-tuple-element.34), channel_id=1, source_target_pairs={{0,4},{1,5},{2,6},{3,7},{4,0},{5,1},{6,2},{7,3},{8,12},{9,13},{10,... | collective-permute-start | bytes 786440 | tf_op jit(solution)/shard_map/ppermute | solution.py:27
  48.9 20.3 %all-to-all-start = ((f32[32,32,128]{2,1,0:T(8,128)}), f32[32,32,128]{2,1,0:T(8,128)S(1)}, u32[]{:S(2)}, u32[]{:S(2)}) async-start(f32[32,32,128]{2,1,0:T(8,128)} %copy.16), calls=%async_computation | async-start | bytes 1048576 | tf_op jit(solution)/shard_map/all_to_all | solution.py:17
  52.9 1.2 %copy-start.4 = (f32[128,2048]{1,0:T(8,128)S(1)}, f32[128,2048]{1,0:T(8,128)}, u32[]{:S(2)}) copy-start(f32[128,2048]{1,0:T(8,128)} %copy-done.3) | copy-start | bytes 3145732
  70.8 1.8 %collective-permute-start.11 = (f32[4,200,128]{2,1,0:T(8,128)S(1)}, f32[4,200,128]{2,1,0:T(8,128)S(1)}, u32[]{:S(2)}, u32[]{:S(2)}) collective-permute-start(f32[4,200,128]{2,1,0:T(8,128)S(1)} %fusion.2), channel_id=1, source_target_pairs={{0,4},{1,5},{2,6},{3,7},{4,0},{5,1},{6,2},{7,3},{8,12},{9,13},{10,... | collective-permute-start | bytes 1228808 | tf_op jit(solution)/shard_map/ppermute | solution.py:27
  72.7 6.2 %collective-permute-start.14 = (f32[200,128]{1,0:T(8,128)S(1)}, f32[200,128]{1,0:T(8,128)S(1)}, u32[]{:S(2)}, u32[]{:S(2)}) collective-permute-start(f32[200,128]{1,0:T(8,128)S(1)} %get-tuple-element.22), channel_id=1, source_target_pairs={{0,3},{1,2},{2,1},{3,0},{4,7},{5,6},{6,5},{7,4},{8,11},{9,10},{10,... | collective-permute-start | bytes 307208 | tf_op jit(solution)/shard_map/ppermute | solution.py:27
  74.7 6.2 %collective-permute-start.13 = (f32[200,128]{1,0:T(8,128)S(1)}, f32[200,128]{1,0:T(8,128)S(1)}, u32[]{:S(2)}, u32[]{:S(2)}) collective-permute-start(f32[200,128]{1,0:T(8,128)S(1)} %get-tuple-element.23), channel_id=1, source_target_pairs={{0,2},{1,3},{2,0},{3,1},{4,6},{5,7},{6,4},{7,5},{8,10},{9,11},{10,... | collective-permute-start | bytes 307208 | tf_op jit(solution)/shard_map/ppermute | solution.py:27
  75.2 5.6 %collective-permute-start.12 = (f32[200,128]{1,0:T(8,128)S(1)}, f32[200,128]{1,0:T(8,128)S(1)}, u32[]{:S(2)}, u32[]{:S(2)}) collective-permute-start(f32[200,128]{1,0:T(8,128)S(1)} %get-tuple-element.24), channel_id=1, source_target_pairs={{0,1},{1,0},{2,3},{3,2},{4,5},{5,4},{6,7},{7,6},{8,9},{9,8},{10,11... | collective-permute-start | bytes 307208 | tf_op jit(solution)/shard_map/ppermute | solution.py:27
  80.9 7.7 %collective-permute-start.17 = (f32[200,128]{1,0:T(8,128)S(1)}, f32[200,128]{1,0:T(8,128)S(1)}, u32[]{:S(2)}, u32[]{:S(2)}) collective-permute-start(f32[200,128]{1,0:T(8,128)S(1)} %fusion.10), channel_id=1, source_target_pairs={{0,24},{1,25},{2,26},{3,27},{4,28},{5,29},{6,30},{7,31},{8,16},{9,... | collective-permute-start | bytes 307208 | tf_op jit(solution)/shard_map/ppermute | solution.py:27
  83.8 8.9 %collective-permute-start.16 = (f32[200,128]{1,0:T(8,128)S(1)}, f32[200,128]{1,0:T(8,128)S(1)}, u32[]{:S(2)}, u32[]{:S(2)}) collective-permute-start(f32[200,128]{1,0:T(8,128)S(1)} %fusion.10), channel_id=1, source_target_pairs={{0,16},{1,17},{2,18},{3,19},{4,20},{5,21},{6,22},{7,23},{8,24},{9,... | collective-permute-start | bytes 307208 | tf_op jit(solution)/shard_map/ppermute | solution.py:27
  83.8 8.9 %collective-permute-start.15 = (f32[200,128]{1,0:T(8,128)S(1)}, f32[200,128]{1,0:T(8,128)S(1)}, u32[]{:S(2)}, u32[]{:S(2)}) collective-permute-start(f32[200,128]{1,0:T(8,128)S(1)} %fusion.10), channel_id=1, source_target_pairs={{0,8},{1,9},{2,10},{3,11},{4,12},{5,13},{6,14},{7,15},{8,0},{9,1},... | collective-permute-start | bytes 307208 | tf_op jit(solution)/shard_map/ppermute | solution.py:27
  92.9 4.7 %collective-permute-start.19 = (f32[192,128]{1,0:T(8,128)S(1)}, f32[192,128]{1,0:T(8,128)S(1)}, u32[]{:S(2)}, u32[]{:S(2)}) collective-permute-start(f32[192,128]{1,0:T(8,128)S(1)} %get-tuple-element.43), channel_id=1, source_target_pairs={{0,2},{1,3},{2,0},{3,1},{4,6},{5,7},{6,4},{7,5},{8,10},{9,11},{10,... | collective-permute-start | bytes 294920 | tf_op jit(solution)/shard_map/ppermute | solution.py:27
  94.5 4.7 %collective-permute-start.18 = (f32[192,128]{1,0:T(8,128)S(1)}, f32[192,128]{1,0:T(8,128)S(1)}, u32[]{:S(2)}, u32[]{:S(2)}) collective-permute-start(f32[192,128]{1,0:T(8,128)S(1)} %get-tuple-element.43), channel_id=1, source_target_pairs={{0,1},{1,0},{2,3},{3,2},{4,5},{5,4},{6,7},{7,6},{8,9},{9,8},{10,11... | collective-permute-start | bytes 294920 | tf_op jit(solution)/shard_map/ppermute | solution.py:27
  95.2 5.5 %collective-permute-start.20 = (f32[192,128]{1,0:T(8,128)S(1)}, f32[192,128]{1,0:T(8,128)S(1)}, u32[]{:S(2)}, u32[]{:S(2)}) collective-permute-start(f32[192,128]{1,0:T(8,128)S(1)} %get-tuple-element.43), channel_id=1, source_target_pairs={{0,3},{1,2},{2,1},{3,0},{4,7},{5,6},{6,5},{7,4},{8,11},{9,10},{10,... | collective-permute-start | bytes 294920 | tf_op jit(solution)/shard_map/ppermute | solution.py:27
  100.9 1.8 %collective-permute-start.21 = (f32[4,192,128]{2,1,0:T(8,128)S(1)}, f32[4,192,128]{2,1,0:T(8,128)S(1)}, u32[]{:S(2)}, u32[]{:S(2)}) collective-permute-start(f32[4,192,128]{2,1,0:T(8,128)S(1)} %get-tuple-element.25), channel_id=1, source_target_pairs={{0,4},{1,5},{2,6},{3,7},{4,0},{5,1},{6,2},{7,3},{8,12},{9,13},{10,... | collective-permute-start | bytes 1179656 | tf_op jit(solution)/shard_map/ppermute | solution.py:27
  105.0 14.5 %all-to-all-start.1 = ((f32[32,16,128]{2,1,0:T(8,128)}), f32[32,16,128]{2,1,0:T(8,128)S(1)}, u32[]{:S(2)}, u32[]{:S(2)}) async-start(f32[32,16,128]{2,1,0:T(8,128)} %bitcast.45), calls=%async_computation.1 | async-start | bytes 524288 | tf_op jit(solution)/shard_map/all_to_all | solution.py:17

commit v4 on v3

--- a/solution.py
+++ b/solution.py
@@ -10,7 +10,9 @@
 AXES = ("row", "col")
 F32, BF16 = jnp.float32, jnp.bfloat16
 PAD = 8
-VMEM_BYTES = 48 * 1024 * 1024
+ROWS = 1024
+MIB = 1024 * 1024
+VMEM_BYTES = 48 * MIB
 
 
 def exchange(parts):
@@ -118,37 +120,36 @@
 
 
 def right_update(
-    slab_ref, pair_ref, pair_t_ref, sums_ref, right_ref, right_out, high_ref, low_ref
+    slab_ref, pair_ref, pair_t_ref, sums_ref, right_ref, high_ref, low_ref, columns
 ):
-    m, block = slab_ref.shape
     rank = right_ref.shape[0]
-    for columns in chunks(block, 256):
-        right = right_ref[:, columns]
-        stack = stacked(right)
-        for rows in chunks(m, 512):
-            high, low = quotients(slab_ref, pair_ref, stack, rows, columns)
-            high_ref[rows, columns] = high
-            low_ref[rows, columns] = low
-        both = dot(pair_t_ref[...], high_ref[:, columns])
-        numerator = both[:rank] + both[rank:]
-        numerator = numerator + dot(pair_t_ref[:rank, :], low_ref[:, columns])
-        right_out[:, columns] = right * numerator / sums_ref[:, :1]
-
-
-def left_numerator(slab_ref, pair_ref, right, total_ref, sums_ref, first):
+    right = right_ref[:, columns]
+    stack = stacked(right)
+    for rows in chunks(slab_ref.shape[0], ROWS):
+        high, low = quotients(slab_ref, pair_ref, stack, rows, columns)
+        high_ref[rows, columns] = high
+        low_ref[rows, columns] = low
+    both = dot(pair_t_ref[...], high_ref[:, columns])
+    numerator = both[:rank] + both[rank:]
+    numerator = numerator + dot(pair_t_ref[:rank, :], low_ref[:, columns])
+    return right * numerator / sums_ref[:, :1]
+
+
+def left_numerator(slab_ref, pair_ref, right, total_ref, sums_ref, high_ref, low_ref, columns, first):
     rank = right.shape[0]
-    right_high, right_low = split(right)
-    right_both = jnp.concatenate([right_high, right_low], axis=0)
-    ones = jnp.ones((16, right.shape[1]), BF16)
-    row_sums = dot_nt(ones, right_both)[:PAD]
+    turned_high, turned_low = split(right.T)
+    turned = jnp.concatenate([turned_high, turned_low], axis=1)
+    row_sums = dot(jnp.ones((16, right.shape[1]), BF16), turned)[:PAD]
     row_sums = row_sums[:, :rank] + row_sums[:, rank:]
     sums_ref[...] = jnp.where(first, row_sums, sums_ref[...] + row_sums)
     stack = stacked(right)
-    for rows in chunks(slab_ref.shape[0], 256):
-        high, low = quotients(slab_ref, pair_ref, stack, rows, slice(None))
-        both = dot_nt(high, right_both)
-        term = both[:, :rank] + both[:, rank:] + dot_nt(low, right_high)
-        total_ref[rows, :] = jnp.where(first, term, total_ref[rows, :] + term)
+    for rows in chunks(slab_ref.shape[0], ROWS):
+        high, low = quotients(slab_ref, pair_ref, stack, rows, columns)
+        high_ref[rows, columns] = high
+        low_ref[rows, columns] = low
+    both = dot(high_ref[:, columns], turned)
+    term = both[:, :rank] + both[:, rank:] + dot(low_ref[:, columns], turned_high)
+    total_ref[...] = jnp.where(first, term, total_ref[...] + term)
 
 
 def write_left(total_ref, row_sums_ref, extra_ref, out_ref):
@@ -163,7 +164,7 @@
 
 def turn_kernel(
     slab_ref, left_ref, right_ref, extra_ref, right_out, left_out,
-    pair_ref, pair_t_ref, sums_ref, high_ref, low_ref, total_ref, row_sums_ref,
+    pair_ref, pair_t_ref, sums_ref, high_ref, low_ref, high2_ref, low2_ref, total_ref, row_sums_ref,
 ):
     step = pl.program_id(0)
 
@@ -172,10 +173,15 @@
         prepare_left(left_ref, pair_ref)
         prepare_left_t(left_ref, pair_t_ref, sums_ref)
 
-    right_update(
-        slab_ref, pair_ref, pair_t_ref, sums_ref, right_ref, right_out, high_ref, low_ref
-    )
-    left_numerator(slab_ref, pair_ref, right_out[...], total_ref, row_sums_ref, step == 0)
+    for index, columns in enumerate(chunks(slab_ref.shape[1], 256)):
+        right = right_update(
+            slab_ref, pair_ref, pair_t_ref, sums_ref, right_ref, high_ref, low_ref, columns
+        )
+        right_out[:, columns] = right
+        left_numerator(
+            slab_ref, pair_ref, right, total_ref, row_sums_ref, high2_ref, low2_ref, columns,
+            (step == 0) if index == 0 else False,
+        )
 
     @pl.when(step == pl.num_programs(0) - 1)
     def _():
@@ -230,9 +236,9 @@
     return pl.BlockSpec(shape, lambda step: (0,) * len(shape))
 
 
-def params():
+def params(vmem_bytes):
     return pltpu.CompilerParams(
-        dimension_semantics=("arbitrary",), vmem_limit_bytes=VMEM_BYTES
+        dimension_semantics=("arbitrary",), vmem_limit_bytes=vmem_bytes
     )
 
 
@@ -244,9 +250,7 @@
     return [
         pltpu.VMEM((2 * rank, m), BF16),
         pltpu.VMEM((rank, rank), F32),
-        pltpu.VMEM((m, block), BF16),
-        pltpu.VMEM((m, block), BF16),
-    ]
+    ] + [pltpu.VMEM((m, block), BF16)] * 4
 
 
 def total_scratch(m, rank):
@@ -259,7 +263,7 @@
     )
 
 
-def full_turn(slab, left, right, extra, block, parts):
+def full_turn(slab, left, right, extra, block, parts, vmem_bytes):
     (m, columns), rank = slab.shape, left.shape[1]
     columns_spec = lambda height: pl.BlockSpec((height, block), lambda step: (0, step))
     tall = m // parts + PAD
@@ -275,7 +279,7 @@
         scratch_shapes=left_scratch(m, rank)
         + right_scratch(m, rank, block)
         + total_scratch(m, rank),
-        compiler_params=params(),
+        compiler_params=params(vmem_bytes),
         cost_estimate=cost(m, rank, columns, 4),
         name="turn",
     )(slab, left, right, extra)
@@ -299,6 +303,30 @@
         cost_estimate=cost(right.shape[0], right.shape[0], right.shape[1], 2),
         name="second_rows",
     )(right, second_left, second_right)
+
+
+def left_rows_kernel(part_ref, left_ref, total_ref, out_ref):
+    height = out_ref.shape[0]
+    out_ref[...] = left_ref[...] * total_ref[:height, :] / total_ref[height : height + 1, :]
+
+
+def left_rows(part, left, total, height):
+    rank = left.shape[1]
+    return pl.pallas_call(
+        left_rows_kernel,
+        grid_spec=pltpu.PrefetchScalarGridSpec(
+            num_scalar_prefetch=1,
+            grid=(1,),
+            in_specs=[
+                pl.BlockSpec((height, rank), lambda step, part: (part[0], 0)),
+                pl.BlockSpec(total.shape, lambda step, part: (0, 0)),
+            ],
+            out_specs=pl.BlockSpec((height, rank), lambda step, part: (0, 0)),
+        ),
+        out_shape=jax.ShapeDtypeStruct((height, rank), F32),
+        cost_estimate=cost(left.shape[0], rank, 16 * rank, 1),
+        name="left_rows",
+    )(part.astype(jnp.int32)[None], left, total)
 
 
 def body(tensor_slab, left_init, right_init, second_left_init, second_right_init):
@@ -331,13 +359,15 @@
         own = lax.dynamic_slice_in_dim(left, own_part * rows_own, rows_own, 0)
         return own * total[:rows_own] / total[rows_own][None, :]
 
-    right, summed = full_turn(tensor_slab, left_init, right_init, left_init, k, parts)
+    right, summed = full_turn(
+        tensor_slab, after(left_init, second_factors), right_init, left_init, k, parts, 52 * MIB
+    )
     summed = summed.reshape(2, col_devices, rows_own + PAD, rank)
     total = reduce_z(reduce_plane(reduce_core(summed)))
     left = spread_core(spread_plane(own_left_rows(left_init, total))).reshape(m, rank)
 
     arrived = exchange(after(second_factors, left))
-    right, summed = full_turn(tensor_slab, left, right, col_part, k, parts)
+    right, summed = full_turn(tensor_slab, left, right, col_part, k, parts, VMEM_BYTES)
     arrived = after(arrived, summed)
     second_left = arrived[:, : per_owner * slices].reshape(rank * slices, rank)
     whole = arrived[:, per_owner * slices :].reshape(row_devices, col_devices, piece_rows, -1)
@@ -351,12 +381,10 @@
     init_over = (whole / total[rows_own + 1][None, :, None]).reshape(k, rank)
     init_over = lax.dynamic_slice_in_dim(init_over, own_part * rows_part, rows_part, 0)
     second_part = init_over * total[rows_own + PAD :]
-    both = spread_core(
-        spread_plane(jnp.concatenate([own_left_rows(left, total), second_part], axis=0))
-    )
-    left_out = both[:, :, :rows_own].reshape(m, rank)
-    second_right = both[:, :, rows_own:].reshape(k // rank, rank, rank)
+    second_right = spread_core(spread_plane(second_part)).reshape(k // rank, rank, rank)
     rows_out = second_rows_out(right, second_left, second_right, slices)
+    left_part = left_rows(own_part, left, after(total, rows_out), rows_own)
+    left_out = spread_core(spread_plane(left_part)).reshape(m, rank)
     returned = exchange(rows_out.reshape(devices, per_owner * slices, rank))
     returned = returned.reshape(devices, per_owner, slices, rank).transpose(1, 0, 2, 3)
     return (left_out, returned.reshape(second_rows, rank))

time: 121 us -> 136 us (1.12)
  Pallas kernels: 32.2 us -> 41.3 us
  waiting for transfers between devices: 44.6 us -> 48.5 us
  starting transfers between devices: 32.4 us -> 35.9 us
  local copies, waits for them, and re-layouts: 6.58 us -> 4.41 us
    pallas_call x2, Pallas kernels: 28.4 us -> 36 us  [full_turn(): pl.pallas_call(turn_kernel, grid=(columns // block,), in_specs=[columns_s...]
    ppermute x22 -> x26, waiting for transfers between devices: 33.7 us -> 38.5 us  [send(): return lax.ppermute(values, AXES, pairs)]
    ppermute x22 -> x26, starting transfers between devices: 24.8 us -> 28.4 us  [send(): return lax.ppermute(values, AXES, pairs)]
    unnamed x10, local copies, waits for them, and re-layouts: 4.48 us -> 2.27 us
    pallas_call x0 -> x1, Pallas kernels: none -> 1.56 us  [left_rows(): pl.pallas_call(left_rows_kernel, grid_spec=pltpu.PrefetchScalarGridSpec(n...]
  transfers between devices with their start and end apart: 24 -> 28, of which waited for: 21 -> 25; matrix products, arithmetic and copies ran while one was open for 2% -> 1% of each run, Pallas kernels for 12% -> 13%
where the time goes in v4:
time: 136 us
  waiting for transfers between devices  48.5 us (36%)
  Pallas kernels  41.3 us (30%)
  starting transfers between devices  35.9 us (26%)
  local copies, waits for them, and re-layouts  4.41 us (3%)
  other arithmetic  4.39 us (3%)
    ppermute x26, waiting for transfers between devices, send(): return lax.ppermute(values, AXES, pairs)  38.5 us
    pallas_call x2, Pallas kernels, full_turn(): pl.pallas_call(turn_kernel, grid=(columns // block,), in_specs=[columns_s...  36 us
    ppermute x26, starting transfers between devices, send(): return lax.ppermute(values, AXES, pairs)  28.4 us
    all_to_all x2, waiting for transfers between devices, exchange(): return lax.all_to_all(parts, AXES, split_axis=0, concat_axis=0, tiled=True)  9.99 us
    all_to_all x2, starting transfers between devices, exchange(): return lax.all_to_all(parts, AXES, split_axis=0, concat_axis=0, tiled=True)  7.52 us
  transfers between devices with their start and end apart: 28, of which 25 were waited for; matrix products, arithmetic and copies ran while one was open for 1% of the time, Pallas kernels for 13%

profile of v4, /device:TPU:0, one launch (start us, length us, event | category | flops | bytes accessed | tf_op | source)
XLA Modules:
  0.0 135.5 jit_solution(7793470389753564366)
XLA Ops:
  0.7 1.0 fusion.17
  1.8 1.0 copy-done.2
  2.9 18.3 %turn.2 = (f32[128,2048]{1,0:T(8,128)}, f32[8,136,128]{2,1,0:T(8,128)S(1)}) custom-call(f32[1024,2048]{1,0:T(8,128)} %slab_ref.3, f32[1024,128]{1,0:T(8,128)S(1)} %copy-done.2, f32[128,2048]{1,0:T(8,128)} %right_ref.1, f32[1024,128]{1,0:T(8,128)S(1)} %copy-done.2), custom_call_target="tpu_custom_call" | custom-call | flops 6442450944 | bytes 8388608 | tf_op jit(solution)/shard_map/turn/pallas_call | solution.py:270
  21.2 0.5 collective-permute-start
  21.7 1.2 collective-permute-done
  23.0 2.9 %collective-permute-start.1 = (f32[136,128]{1,0:T(8,128)S(1)}, f32[136,128]{1,0:T(8,128)S(1)}, u32[]{:S(2)}, u32[]{:S(2)}) collective-permute-start(f32[136,128]{1,0:T(8,128)S(1)} %get-tuple-element.31), channel_id=1, source_target_pairs={{0,1},{1,0},{2,3},{3,2},{4,5},{5,4},{6,7},{7,6},{8,9},{9,8},{10,11... | collective-permute-start | bytes 208904 | tf_op jit(solution)/shard_map/ppermute | solution.py:29
  25.9 1.5 %collective-permute-start.2 = (f32[136,128]{1,0:T(8,128)S(1)}, f32[136,128]{1,0:T(8,128)S(1)}, u32[]{:S(2)}, u32[]{:S(2)}) collective-permute-start(f32[136,128]{1,0:T(8,128)S(1)} %get-tuple-element.30), channel_id=1, source_target_pairs={{0,2},{1,3},{2,0},{3,1},{4,6},{5,7},{6,4},{7,5},{8,10},{9,11},{10,... | collective-permute-start | bytes 208904 | tf_op jit(solution)/shard_map/ppermute | solution.py:29
  27.4 0.9 collective-permute-done.1
  28.4 1.8 %collective-permute-done.2 = f32[136,128]{1,0:T(8,128)S(1)} collective-permute-done((f32[136,128]{1,0:T(8,128)S(1)}, f32[136,128]{1,0:T(8,128)S(1)}, u32[]{:S(2)}, u32[]{:S(2)}) %collective-permute-start.2) | collective-permute-done | bytes 69664 | tf_op jit(solution)/shard_map/ppermute | solution.py:29
  30.2 2.4 %collective-permute-done.3 = f32[136,128]{1,0:T(8,128)S(1)} collective-permute-done((f32[136,128]{1,0:T(8,128)S(1)}, f32[136,128]{1,0:T(8,128)S(1)}, u32[]{:S(2)}, u32[]{:S(2)}) %collective-permute-start.3) | collective-permute-done | bytes 69664 | tf_op jit(solution)/shard_map/ppermute | solution.py:29
  32.6 1.6 %collective-permute-start.4 = (f32[136,128]{1,0:T(8,128)S(1)}, f32[136,128]{1,0:T(8,128)S(1)}, u32[]{:S(2)}, u32[]{:S(2)}) collective-permute-start(f32[136,128]{1,0:T(8,128)S(1)} %fusion.12), channel_id=1, source_target_pairs={{0,8},{1,9},{2,10},{3,11},{4,12},{5,13},{6,14},{7,15},{8,0},{9,1},... | collective-permute-start | bytes 208904 | tf_op jit(solution)/shard_map/ppermute | solution.py:29
  34.3 2.6 %collective-permute-start.5 = (f32[136,128]{1,0:T(8,128)S(1)}, f32[136,128]{1,0:T(8,128)S(1)}, u32[]{:S(2)}, u32[]{:S(2)}) collective-permute-start(f32[136,128]{1,0:T(8,128)S(1)} %fusion.12), channel_id=1, source_target_pairs={{0,16},{1,17},{2,18},{3,19},{4,20},{5,21},{6,22},{7,23},{8,24},{9,... | collective-permute-start | bytes 208904 | tf_op jit(solution)/shard_map/ppermute | solution.py:29
  36.9 0.2 collective-permute-start.6
  37.1 0.3 collective-permute-done.4
  37.3 3.6 %collective-permute-done.5 = f32[136,128]{1,0:T(8,128)S(1)} collective-permute-done((f32[136,128]{1,0:T(8,128)S(1)}, f32[136,128]{1,0:T(8,128)S(1)}, u32[]{:S(2)}, u32[]{:S(2)}) %collective-permute-start.5) | collective-permute-done | bytes 69664 | tf_op jit(solution)/shard_map/ppermute | solution.py:29
  41.0 2.0 %collective-permute-done.6 = f32[136,128]{1,0:T(8,128)S(1)} collective-permute-done((f32[136,128]{1,0:T(8,128)S(1)}, f32[136,128]{1,0:T(8,128)S(1)}, u32[]{:S(2)}, u32[]{:S(2)}) %collective-permute-start.6) | collective-permute-done | bytes 69664 | tf_op jit(solution)/shard_map/ppermute | solution.py:29
  43.0 0.9 fusion.13
  43.9 0.6 collective-permute-start.7
  44.5 0.6 collective-permute-start.8
  45.1 2.4 %collective-permute-start.9 = (f32[128,128]{1,0:T(8,128)S(1)}, f32[128,128]{1,0:T(8,128)S(1)}, u32[]{:S(2)}, u32[]{:S(2)}) collective-permute-start(f32[128,128]{1,0:T(8,128)S(1)} %fusion.13), channel_id=1, source_target_pairs={{0,3},{1,2},{2,1},{3,0},{4,7},{5,6},{6,5},{7,4},{8,11},{9,10},{10,... | collective-permute-start | bytes 196616 | tf_op jit(solution)/shard_map/ppermute | solution.py:29
  47.4 0.8 collective-permute-done.7
  48.2 0.5 collective-permute-done.8
  48.7 1.5 %collective-permute-done.9 = f32[128,128]{1,0:T(8,128)S(1)} collective-permute-done((f32[128,128]{1,0:T(8,128)S(1)}, f32[128,128]{1,0:T(8,128)S(1)}, u32[]{:S(2)}, u32[]{:S(2)}) %collective-permute-start.9) | collective-permute-done | bytes 65568 | tf_op jit(solution)/shard_map/ppermute | solution.py:29
  50.4 1.5 %collective-permute-done.10 = f32[4,128,128]{2,1,0:T(8,128)S(1)} collective-permute-done((f32[4,128,128]{2,1,0:T(8,128)S(1)}, f32[4,128,128]{2,1,0:T(8,128)S(1)}, u32[]{:S(2)}, u32[]{:S(2)}) %collective-permute-start.10) | collective-permute-done | bytes 262176 | tf_op jit(solution)/shard_map/ppermute | solution.py:29
  51.9 0.1 fusion.8
  52.1 1.1 copy.16
  53.2 3.3 %all-to-all-start = ((f32[32,32,128]{2,1,0:T(8,128)}), f32[32,32,128]{2,1,0:T(8,128)S(1)}, u32[]{:S(2)}, u32[]{:S(2)}) async-start(f32[32,32,128]{2,1,0:T(8,128)} %copy.16), calls=%async_computation | async-start | bytes 1048576 | tf_op jit(solution)/shard_map/all_to_all | solution.py:19
  56.5 1.2 copy-done.3
  57.7 17.7 %turn.3 = (f32[128,2048]{1,0:T(8,128)S(1)}, f32[8,136,128]{2,1,0:T(8,128)S(1)}) custom-call(f32[1024,2048]{1,0:T(8,128)} %slab_ref.3, f32[1024,128]{1,0:T(8,128)S(1)} %bitcast.91, f32[128,2048]{1,0:T(8,128)S(1)} %copy-done.3, f32[1,128]{1,0:T(1,128)S(1)} %bitcast.93), custom_call_target="tpu_custom_call" | custom-call | flops 6442450944 | bytes 8388608 | tf_op jit(solution)/shard_map/turn/pallas_call | solution.py:270
  75.5 1.6 %second_numerator.1 = f32[4,128,128]{2,1,0:T(8,128)S(1)} custom-call(f32[128,2048]{1,0:T(8,128)S(1)} %get-tuple-element.14.right_ref, f32[512,128]{1,0:T(8,128)S(1)} %bitcast.81, f32[4,128,128]{2,1,0:T(8,128)S(1)} %bitcast.83), custom_call_target="tpu_custom_call" | custom-call | flops 402653184 | bytes 1048576 | tf_op jit(solution)/shard_map/second_numerator/pallas_call | solution.py:289
  77.1 0.1 collective-permute-start.11
  77.3 1.7 %collective-permute-done.11 = f32[4,200,128]{2,1,0:T(8,128)S(1)} collective-permute-done((f32[4,200,128]{2,1,0:T(8,128)S(1)}, f32[4,200,128]{2,1,0:T(8,128)S(1)}, u32[]{:S(2)}, u32[]{:S(2)}) %collective-permute-start.11) | collective-permute-done | bytes 409632 | tf_op jit(solution)/shard_map/ppermute | solution.py:29
  79.0 1.7 %collective-permute-start.12 = (f32[200,128]{1,0:T(8,128)S(1)}, f32[200,128]{1,0:T(8,128)S(1)}, u32[]{:S(2)}, u32[]{:S(2)}) collective-permute-start(f32[200,128]{1,0:T(8,128)S(1)} %get-tuple-element.28), channel_id=1, source_target_pairs={{0,1},{1,0},{2,3},{3,2},{4,5},{5,4},{6,7},{7,6},{8,9},{9,8},{10,11... | collective-permute-start | bytes 307208 | tf_op jit(solution)/shard_map/ppermute | solution.py:29
  80.7 1.5 %collective-permute-start.13 = (f32[200,128]{1,0:T(8,128)S(1)}, f32[200,128]{1,0:T(8,128)S(1)}, u32[]{:S(2)}, u32[]{:S(2)}) collective-permute-start(f32[200,128]{1,0:T(8,128)S(1)} %get-tuple-element.27), channel_id=1, source_target_pairs={{0,2},{1,3},{2,0},{3,1},{4,6},{5,7},{6,4},{7,5},{8,10},{9,11},{10,... | collective-permute-start | bytes 307208 | tf_op jit(solution)/shard_map/ppermute | solution.py:29
  82.1 0.4 collective-permute-start.14
  82.6 1.4 %collective-permute-done.12 = f32[200,128]{1,0:T(8,128)S(1)} collective-permute-done((f32[200,128]{1,0:T(8,128)S(1)}, f32[200,128]{1,0:T(8,128)S(1)}, u32[]{:S(2)}, u32[]{:S(2)}) %collective-permute-start.12) | collective-permute-done | bytes 102432 | tf_op jit(solution)/shard_map/ppermute | solution.py:29
  84.0 2.5 %collective-permute-done.13 = f32[200,128]{1,0:T(8,128)S(1)} collective-permute-done((f32[200,128]{1,0:T(8,128)S(1)}, f32[200,128]{1,0:T(8,128)S(1)}, u32[]{:S(2)}, u32[]{:S(2)}) %collective-permute-start.13) | collective-permute-done | bytes 102432 | tf_op jit(solution)/shard_map/ppermute | solution.py:29
  86.5 1.2 collective-permute-done.14
  87.7 1.5 %collective-permute-start.15 = (f32[200,128]{1,0:T(8,128)S(1)}, f32[200,128]{1,0:T(8,128)S(1)}, u32[]{:S(2)}, u32[]{:S(2)}) collective-permute-start(f32[200,128]{1,0:T(8,128)S(1)} %fusion.11), channel_id=1, source_target_pairs={{0,8},{1,9},{2,10},{3,11},{4,12},{5,13},{6,14},{7,15},{8,0},{9,1},... | collective-permute-start | bytes 307208 | tf_op jit(solution)/shard_map/ppermute | solution.py:29
  89.3 2.5 %collective-permute-start.16 = (f32[200,128]{1,0:T(8,128)S(1)}, f32[200,128]{1,0:T(8,128)S(1)}, u32[]{:S(2)}, u32[]{:S(2)}) collective-permute-start(f32[200,128]{1,0:T(8,128)S(1)} %fusion.11), channel_id=1, source_target_pairs={{0,16},{1,17},{2,18},{3,19},{4,20},{5,21},{6,22},{7,23},{8,24},{9,... | collective-permute-start | bytes 307208 | tf_op jit(solution)/shard_map/ppermute | solution.py:29
  91.7 0.5 collective-permute-start.17
  92.2 0.9 collective-permute-done.15
  93.0 5.7 %collective-permute-done.16 = f32[200,128]{1,0:T(8,128)S(1)} collective-permute-done((f32[200,128]{1,0:T(8,128)S(1)}, f32[200,128]{1,0:T(8,128)S(1)}, u32[]{:S(2)}, u32[]{:S(2)}) %collective-permute-start.16) | collective-permute-done | bytes 102432 | tf_op jit(solution)/shard_map/ppermute | solution.py:29
  98.9 1.9 %collective-permute-start.18 = (f32[64,128]{1,0:T(8,128)S(1)}, f32[64,128]{1,0:T(8,128)S(1)}, u32[]{:S(2)}, u32[]{:S(2)}) collective-permute-start(f32[64,128]{1,0:T(8,128)S(1)} %slice_multiply_fusion.1), channel_id=1, source_target_pairs={{0,1},{1,0},{2,3},{3,2},{4,5},{5,4},{6,7},{7,6},{8,9},{9,8},{10,11... | collective-permute-start | bytes 98312 | tf_op jit(solution)/shard_map/ppermute | solution.py:29
  100.7 0.6 collective-permute-start.19
  101.3 1.1 collective-permute-start.20
  102.4 0.4 collective-permute-done.18
  102.9 1.8 %collective-permute-done.19 = f32[64,128]{1,0:T(8,128)S(1)} collective-permute-done((f32[64,128]{1,0:T(8,128)S(1)}, f32[64,128]{1,0:T(8,128)S(1)}, u32[]{:S(2)}, u32[]{:S(2)}) %collective-permute-start.19) | collective-permute-done | bytes 32800 | tf_op jit(solution)/shard_map/ppermute | solution.py:29
  104.7 1.5 %collective-permute-done.20 = f32[64,128]{1,0:T(8,128)S(1)} collective-permute-done((f32[64,128]{1,0:T(8,128)S(1)}, f32[64,128]{1,0:T(8,128)S(1)}, u32[]{:S(2)}, u32[]{:S(2)}) %collective-permute-start.20) | collective-permute-done | bytes 32800 | tf_op jit(solution)/shard_map/ppermute | solution.py:29
  106.3 1.3 collective-permute-done.21
  107.7 2.2 %second_rows.1 = f32[512,128]{1,0:T(8,128)} custom-call(f32[128,2048]{1,0:T(8,128)S(1)} %get-tuple-element.14.right_ref, f32[512,128]{1,0:T(8,128)S(1)} %bitcast.82, f32[4,128,128]{2,1,0:T(8,128)S(1)} %bitcast.88), custom_call_target="tpu_custom_call" | custom-call | flops 402653184 | bytes 1048576 | tf_op jit(solution)/shard_map/second_rows/pallas_call | solution.py:299
  109.9 1.6 %left_rows.1 = f32[128,128]{1,0:T(8,128)} custom-call(s32[1]{0:T(128)} %bitcast.part_ref, f32[1024,128]{1,0:T(8,128)} %bitcast.92, f32[200,128]{1,0:T(8,128)} %copy-done.4), custom_call_target="tpu_custom_call" | custom-call | flops 1610612736 | bytes 8388608 | tf_op jit(solution)/shard_map/left_rows/pallas_call | solution.py:315
  111.4 0.6 collective-permute-start.22
  112.0 1.1 collective-permute-start.23
  113.1 1.8 %collective-permute-start.24 = (f32[128,128]{1,0:T(8,128)}, f32[128,128]{1,0:T(8,128)S(1)}, u32[]{:S(2)}, u32[]{:S(2)}) collective-permute-start(f32[128,128]{1,0:T(8,128)} %left_rows.1), channel_id=1, source_target_pairs={{0,3},{1,2},{2,1},{3,0},{4,7},{5,6},{6,5},{7,4},{8,11},{9,10},{10,... | collective-permute-start | bytes 196616 | tf_op jit(solution)/shard_map/ppermute | solution.py:29
  114.9 1.1 collective-permute-done.22
  116.0 0.4 collective-permute-done.23
  116.5 2.0 %collective-permute-done.24 = f32[128,128]{1,0:T(8,128)S(1)} collective-permute-done((f32[128,128]{1,0:T(8,128)}, f32[128,128]{1,0:T(8,128)S(1)}, u32[]{:S(2)}, u32[]{:S(2)}) %collective-permute-start.24) | collective-permute-done | bytes 65568 | tf_op jit(solution)/shard_map/ppermute | solution.py:29
  118.5 0.9 pad_maximum_fusion.6
  119.5 4.3 %all-to-all-start.1 = ((f32[32,16,128]{2,1,0:T(8,128)}), f32[32,16,128]{2,1,0:T(8,128)S(1)}, u32[]{:S(2)}, u32[]{:S(2)}) async-start(f32[32,16,128]{2,1,0:T(8,128)} %bitcast.51), calls=%async_computation.1 | async-start | bytes 524288 | tf_op jit(solution)/shard_map/all_to_all | solution.py:19
  123.8 0.1 fusion.6
  124.0 0.8 pad_maximum_fusion.2
  124.8 10.0 %all-to-all-done.1 = f32[32,16,128]{2,1,0:T(8,128)S(1)} async-done(((f32[32,16,128]{2,1,0:T(8,128)}), f32[32,16,128]{2,1,0:T(8,128)S(1)}, u32[]{:S(2)}, u32[]{:S(2)}) %all-to-all-start.1) | async-done | bytes 262176 | tf_op jit(solution)/shard_map/all_to_all | solution.py:19
  134.8 0.7 copy.18
  (46 shorter events, 1.1 us)
Async XLA Ops:
  0.6 1.1 copy-start
  1.8 1.0 copy-start.2
  21.2 1.7 %collective-permute-start = (f32[4,136,128]{2,1,0:T(8,128)S(1)}, f32[4,136,128]{2,1,0:T(8,128)S(1)}, u32[]{:S(2)}, u32[]{:S(2)}) collective-permute-start(f32[4,136,128]{2,1,0:T(8,128)S(1)} %dynamic-slice_bitcast_fusion), channel_id=1, source_target_pairs={{0,4},{1,5},{2,6},{3,7},{4,0},{5,1},{6,2},{7,3},{8,12},{9,13},{10,... | collective-permute-start | bytes 835592 | tf_op jit(solution)/shard_map/ppermute | solution.py:29
  23.0 5.4 %collective-permute-start.1 = (f32[136,128]{1,0:T(8,128)S(1)}, f32[136,128]{1,0:T(8,128)S(1)}, u32[]{:S(2)}, u32[]{:S(2)}) collective-permute-start(f32[136,128]{1,0:T(8,128)S(1)} %get-tuple-element.31), channel_id=1, source_target_pairs={{0,1},{1,0},{2,3},{3,2},{4,5},{5,4},{6,7},{7,6},{8,9},{9,8},{10,11... | collective-permute-start | bytes 208904 | tf_op jit(solution)/shard_map/ppermute | solution.py:29
  25.9 4.3 %collective-permute-start.2 = (f32[136,128]{1,0:T(8,128)S(1)}, f32[136,128]{1,0:T(8,128)S(1)}, u32[]{:S(2)}, u32[]{:S(2)}) collective-permute-start(f32[136,128]{1,0:T(8,128)S(1)} %get-tuple-element.30), channel_id=1, source_target_pairs={{0,2},{1,3},{2,0},{3,1},{4,6},{5,7},{6,4},{7,5},{8,10},{9,11},{10,... | collective-permute-start | bytes 208904 | tf_op jit(solution)/shard_map/ppermute | solution.py:29
  27.4 5.2 %collective-permute-start.3 = (f32[136,128]{1,0:T(8,128)S(1)}, f32[136,128]{1,0:T(8,128)S(1)}, u32[]{:S(2)}, u32[]{:S(2)}) collective-permute-start(f32[136,128]{1,0:T(8,128)S(1)} %get-tuple-element.29), channel_id=1, source_target_pairs={{0,3},{1,2},{2,1},{3,0},{4,7},{5,6},{6,5},{7,4},{8,11},{9,10},{10,... | collective-permute-start | bytes 208904 | tf_op jit(solution)/shard_map/ppermute | solution.py:29
  32.6 4.7 %collective-permute-start.4 = (f32[136,128]{1,0:T(8,128)S(1)}, f32[136,128]{1,0:T(8,128)S(1)}, u32[]{:S(2)}, u32[]{:S(2)}) collective-permute-start(f32[136,128]{1,0:T(8,128)S(1)} %fusion.12), channel_id=1, source_target_pairs={{0,8},{1,9},{2,10},{3,11},{4,12},{5,13},{6,14},{7,15},{8,0},{9,1},... | collective-permute-start | bytes 208904 | tf_op jit(solution)/shard_map/ppermute | solution.py:29
  34.3 6.7 %collective-permute-start.5 = (f32[136,128]{1,0:T(8,128)S(1)}, f32[136,128]{1,0:T(8,128)S(1)}, u32[]{:S(2)}, u32[]{:S(2)}) collective-permute-start(f32[136,128]{1,0:T(8,128)S(1)} %fusion.12), channel_id=1, source_target_pairs={{0,16},{1,17},{2,18},{3,19},{4,20},{5,21},{6,22},{7,23},{8,24},{9,... | collective-permute-start | bytes 208904 | tf_op jit(solution)/shard_map/ppermute | solution.py:29
  36.9 6.1 %collective-permute-start.6 = (f32[136,128]{1,0:T(8,128)S(1)}, f32[136,128]{1,0:T(8,128)S(1)}, u32[]{:S(2)}, u32[]{:S(2)}) collective-permute-start(f32[136,128]{1,0:T(8,128)S(1)} %fusion.12), channel_id=1, source_target_pairs={{0,24},{1,25},{2,26},{3,27},{4,28},{5,29},{6,30},{7,31},{8,16},{9,... | collective-permute-start | bytes 208904 | tf_op jit(solution)/shard_map/ppermute | solution.py:29
  43.9 4.3 %collective-permute-start.7 = (f32[128,128]{1,0:T(8,128)S(1)}, f32[128,128]{1,0:T(8,128)S(1)}, u32[]{:S(2)}, u32[]{:S(2)}) collective-permute-start(f32[128,128]{1,0:T(8,128)S(1)} %fusion.13), channel_id=1, source_target_pairs={{0,1},{1,0},{2,3},{3,2},{4,5},{5,4},{6,7},{7,6},{8,9},{9,8},{10,11... | collective-permute-start | bytes 196616 | tf_op jit(solution)/shard_map/ppermute | solution.py:29
  44.5 4.3 %collective-permute-start.8 = (f32[128,128]{1,0:T(8,128)S(1)}, f32[128,128]{1,0:T(8,128)S(1)}, u32[]{:S(2)}, u32[]{:S(2)}) collective-permute-start(f32[128,128]{1,0:T(8,128)S(1)} %fusion.13), channel_id=1, source_target_pairs={{0,2},{1,3},{2,0},{3,1},{4,6},{5,7},{6,4},{7,5},{8,10},{9,11},{10,... | collective-permute-start | bytes 196616 | tf_op jit(solution)/shard_map/ppermute | solution.py:29
  45.1 5.2 %collective-permute-start.9 = (f32[128,128]{1,0:T(8,128)S(1)}, f32[128,128]{1,0:T(8,128)S(1)}, u32[]{:S(2)}, u32[]{:S(2)}) collective-permute-start(f32[128,128]{1,0:T(8,128)S(1)} %fusion.13), channel_id=1, source_target_pairs={{0,3},{1,2},{2,1},{3,0},{4,7},{5,6},{6,5},{7,4},{8,11},{9,10},{10,... | collective-permute-start | bytes 196616 | tf_op jit(solution)/shard_map/ppermute | solution.py:29
  50.3 1.6 %collective-permute-start.10 = (f32[4,128,128]{2,1,0:T(8,128)S(1)}, f32[4,128,128]{2,1,0:T(8,128)S(1)}, u32[]{:S(2)}, u32[]{:S(2)}) collective-permute-start(f32[4,128,128]{2,1,0:T(8,128)S(1)} %get-tuple-element.40), channel_id=1, source_target_pairs={{0,4},{1,5},{2,6},{3,7},{4,0},{5,1},{6,2},{7,3},{8,12},{9,13},{10,... | collective-permute-start | bytes 786440 | tf_op jit(solution)/shard_map/ppermute | solution.py:29
  52.1 23.3 %copy-start.1 = (f32[2,4,128,128]{3,2,1,0:T(8,128)}, f32[2,4,128,128]{3,2,1,0:T(8,128)S(1)}, u32[]{:S(2)}) copy-start(f32[2,4,128,128]{3,2,1,0:T(8,128)S(1)} %pad_maximum_fusion.1) | copy-start | bytes 1572868
  53.2 22.2 %all-to-all-start = ((f32[32,32,128]{2,1,0:T(8,128)}), f32[32,32,128]{2,1,0:T(8,128)S(1)}, u32[]{:S(2)}, u32[]{:S(2)}) async-start(f32[32,32,128]{2,1,0:T(8,128)} %copy.16), calls=%async_computation | async-start | bytes 1048576 | tf_op jit(solution)/shard_map/all_to_all | solution.py:19
  56.5 1.2 copy-start.3
  77.1 1.8 %collective-permute-start.11 = (f32[4,200,128]{2,1,0:T(8,128)S(1)}, f32[4,200,128]{2,1,0:T(8,128)S(1)}, u32[]{:S(2)}, u32[]{:S(2)}) collective-permute-start(f32[4,200,128]{2,1,0:T(8,128)S(1)} %fusion.1), channel_id=1, source_target_pairs={{0,4},{1,5},{2,6},{3,7},{4,0},{5,1},{6,2},{7,3},{8,12},{9,13},{10,... | collective-permute-start | bytes 1228808 | tf_op jit(solution)/shard_map/ppermute | solution.py:29
  79.0 5.0 %collective-permute-start.12 = (f32[200,128]{1,0:T(8,128)S(1)}, f32[200,128]{1,0:T(8,128)S(1)}, u32[]{:S(2)}, u32[]{:S(2)}) collective-permute-start(f32[200,128]{1,0:T(8,128)S(1)} %get-tuple-element.28), channel_id=1, source_target_pairs={{0,1},{1,0},{2,3},{3,2},{4,5},{5,4},{6,7},{7,6},{8,9},{9,8},{10,11... | collective-permute-start | bytes 307208 | tf_op jit(solution)/shard_map/ppermute | solution.py:29
  80.7 5.8 %collective-permute-start.13 = (f32[200,128]{1,0:T(8,128)S(1)}, f32[200,128]{1,0:T(8,128)S(1)}, u32[]{:S(2)}, u32[]{:S(2)}) collective-permute-start(f32[200,128]{1,0:T(8,128)S(1)} %get-tuple-element.27), channel_id=1, source_target_pairs={{0,2},{1,3},{2,0},{3,1},{4,6},{5,7},{6,4},{7,5},{8,10},{9,11},{10,... | collective-permute-start | bytes 307208 | tf_op jit(solution)/shard_map/ppermute | solution.py:29
  82.1 5.6 %collective-permute-start.14 = (f32[200,128]{1,0:T(8,128)S(1)}, f32[200,128]{1,0:T(8,128)S(1)}, u32[]{:S(2)}, u32[]{:S(2)}) collective-permute-start(f32[200,128]{1,0:T(8,128)S(1)} %get-tuple-element.26), channel_id=1, source_target_pairs={{0,3},{1,2},{2,1},{3,0},{4,7},{5,6},{6,5},{7,4},{8,11},{9,10},{10,... | collective-permute-start | bytes 307208 | tf_op jit(solution)/shard_map/ppermute | solution.py:29
  87.7 5.3 %collective-permute-start.15 = (f32[200,128]{1,0:T(8,128)S(1)}, f32[200,128]{1,0:T(8,128)S(1)}, u32[]{:S(2)}, u32[]{:S(2)}) collective-permute-start(f32[200,128]{1,0:T(8,128)S(1)} %fusion.11), channel_id=1, source_target_pairs={{0,8},{1,9},{2,10},{3,11},{4,12},{5,13},{6,14},{7,15},{8,0},{9,1},... | collective-permute-start | bytes 307208 | tf_op jit(solution)/shard_map/ppermute | solution.py:29
  89.3 9.4 %collective-permute-start.16 = (f32[200,128]{1,0:T(8,128)S(1)}, f32[200,128]{1,0:T(8,128)S(1)}, u32[]{:S(2)}, u32[]{:S(2)}) collective-permute-start(f32[200,128]{1,0:T(8,128)S(1)} %fusion.11), channel_id=1, source_target_pairs={{0,16},{1,17},{2,18},{3,19},{4,20},{5,21},{6,22},{7,23},{8,24},{9,... | collective-permute-start | bytes 307208 | tf_op jit(solution)/shard_map/ppermute | solution.py:29
  91.7 7.0 %collective-permute-start.17 = (f32[200,128]{1,0:T(8,128)S(1)}, f32[200,128]{1,0:T(8,128)S(1)}, u32[]{:S(2)}, u32[]{:S(2)}) collective-permute-start(f32[200,128]{1,0:T(8,128)S(1)} %fusion.11), channel_id=1, source_target_pairs={{0,24},{1,25},{2,26},{3,27},{4,28},{5,29},{6,30},{7,31},{8,16},{9,... | collective-permute-start | bytes 307208 | tf_op jit(solution)/shard_map/ppermute | solution.py:29
  98.7 11.1 %copy-start.4 = (f32[200,128]{1,0:T(8,128)}, f32[200,128]{1,0:T(8,128)S(1)}, u32[]{:S(2)}) copy-start(f32[200,128]{1,0:T(8,128)S(1)} %add_add_fusion.total_ref) | copy-start | bytes 307204
  98.9 4.0 %collective-permute-start.18 = (f32[64,128]{1,0:T(8,128)S(1)}, f32[64,128]{1,0:T(8,128)S(1)}, u32[]{:S(2)}, u32[]{:S(2)}) collective-permute-start(f32[64,128]{1,0:T(8,128)S(1)} %slice_multiply_fusion.1), channel_id=1, source_target_pairs={{0,1},{1,0},{2,3},{3,2},{4,5},{5,4},{6,7},{7,6},{8,9},{9,8},{10,11... | collective-permute-start | bytes 98312 | tf_op jit(solution)/shard_map/ppermute | solution.py:29
  100.7 3.9 %collective-permute-start.19 = (f32[64,128]{1,0:T(8,128)S(1)}, f32[64,128]{1,0:T(8,128)S(1)}, u32[]{:S(2)}, u32[]{:S(2)}) collective-permute-start(f32[64,128]{1,0:T(8,128)S(1)} %slice_multiply_fusion.1), channel_id=1, source_target_pairs={{0,2},{1,3},{2,0},{3,1},{4,6},{5,7},{6,4},{7,5},{8,10},{9,11},{10,... | collective-permute-start | bytes 98312 | tf_op jit(solution)/shard_map/ppermute | solution.py:29
  101.3 4.8 %collective-permute-start.20 = (f32[64,128]{1,0:T(8,128)S(1)}, f32[64,128]{1,0:T(8,128)S(1)}, u32[]{:S(2)}, u32[]{:S(2)}) collective-permute-start(f32[64,128]{1,0:T(8,128)S(1)} %slice_multiply_fusion.1), channel_id=1, source_target_pairs={{0,3},{1,2},{2,1},{3,0},{4,7},{5,6},{6,5},{7,4},{8,11},{9,10},{10,... | collective-permute-start | bytes 98312 | tf_op jit(solution)/shard_map/ppermute | solution.py:29
  106.2 1.4 %collective-permute-start.21 = (f32[4,64,128]{2,1,0:T(8,128)S(1)}, f32[4,64,128]{2,1,0:T(8,128)S(1)}, u32[]{:S(2)}, u32[]{:S(2)}) collective-permute-start(f32[4,64,128]{2,1,0:T(8,128)S(1)} %get-tuple-element.46), channel_id=1, source_target_pairs={{0,4},{1,5},{2,6},{3,7},{4,0},{5,1},{6,2},{7,3},{8,12},{9,13},{10,... | collective-permute-start | bytes 393224 | tf_op jit(solution)/shard_map/ppermute | solution.py:29
  111.4 4.6 %collective-permute-start.22 = (f32[128,128]{1,0:T(8,128)}, f32[128,128]{1,0:T(8,128)S(1)}, u32[]{:S(2)}, u32[]{:S(2)}) collective-permute-start(f32[128,128]{1,0:T(8,128)} %left_rows.1), channel_id=1, source_target_pairs={{0,1},{1,0},{2,3},{3,2},{4,5},{5,4},{6,7},{7,6},{8,9},{9,8},{10,11... | collective-permute-start | bytes 196616 | tf_op jit(solution)/shard_map/ppermute | solution.py:29
  112.0 4.5 %collective-permute-start.23 = (f32[128,128]{1,0:T(8,128)}, f32[128,128]{1,0:T(8,128)S(1)}, u32[]{:S(2)}, u32[]{:S(2)}) collective-permute-start(f32[128,128]{1,0:T(8,128)} %left_rows.1), channel_id=1, source_target_pairs={{0,2},{1,3},{2,0},{3,1},{4,6},{5,7},{6,4},{7,5},{8,10},{9,11},{10,... | collective-permute-start | bytes 196616 | tf_op jit(solution)/shard_map/ppermute | solution.py:29
  113.1 5.4 %collective-permute-start.24 = (f32[128,128]{1,0:T(8,128)}, f32[128,128]{1,0:T(8,128)S(1)}, u32[]{:S(2)}, u32[]{:S(2)}) collective-permute-start(f32[128,128]{1,0:T(8,128)} %left_rows.1), channel_id=1, source_target_pairs={{0,3},{1,2},{2,1},{3,0},{4,7},{5,6},{6,5},{7,4},{8,11},{9,10},{10,... | collective-permute-start | bytes 196616 | tf_op jit(solution)/shard_map/ppermute | solution.py:29
  119.5 4.4 %collective-permute-start.25 = (f32[4,128,128]{2,1,0:T(8,128)S(1)}, f32[4,128,128]{2,1,0:T(8,128)S(1)}, u32[]{:S(2)}, u32[]{:S(2)}) collective-permute-start(f32[4,128,128]{2,1,0:T(8,128)S(1)} %get-tuple-element.32), channel_id=1, source_target_pairs={{0,4},{1,5},{2,6},{3,7},{4,0},{5,1},{6,2},{7,3},{8,12},{9,13},{10,... | collective-permute-start | bytes 786440 | tf_op jit(solution)/shard_map/ppermute | solution.py:29
  119.5 15.2 %all-to-all-start.1 = ((f32[32,16,128]{2,1,0:T(8,128)}), f32[32,16,128]{2,1,0:T(8,128)S(1)}, u32[]{:S(2)}, u32[]{:S(2)}) async-start(f32[32,16,128]{2,1,0:T(8,128)} %bitcast.51), calls=%async_computation.1 | async-start | bytes 524288 | tf_op jit(solution)/shard_map/all_to_all | solution.py:19

commit v5 on v3

--- a/solution.py
+++ b/solution.py
@@ -10,7 +10,9 @@
 AXES = ("row", "col")
 F32, BF16 = jnp.float32, jnp.bfloat16
 PAD = 8
-VMEM_BYTES = 48 * 1024 * 1024
+ROWS, WIDTH = 256, 256
+MIB = 1024 * 1024
+VMEM_BYTES = 51 * MIB
 
 
 def exchange(parts):
@@ -118,36 +120,45 @@
 
 
 def right_update(
-    slab_ref, pair_ref, pair_t_ref, sums_ref, right_ref, right_out, high_ref, low_ref
+    slab_ref, pair_ref, pair_t_ref, sums_ref, right_ref, right_out, high_ref, low_ref, start, arrive
 ):
-    m, block = slab_ref.shape
+    block = high_ref.shape[1]
     rank = right_ref.shape[0]
-    for columns in chunks(block, 256):
+    for index, half in enumerate(chunks(block, WIDTH)):
+        columns = pl.ds(start + half.start, half.size)
         right = right_ref[:, columns]
         stack = stacked(right)
-        for rows in chunks(m, 512):
+        for piece, rows in enumerate(chunks(slab_ref.shape[0], ROWS)):
+            if index == 0:
+                arrive(piece)
             high, low = quotients(slab_ref, pair_ref, stack, rows, columns)
-            high_ref[rows, columns] = high
-            low_ref[rows, columns] = low
-        both = dot(pair_t_ref[...], high_ref[:, columns])
+            high_ref[rows, half] = high
+            low_ref[rows, half] = low
+        both = dot(pair_t_ref[...], high_ref[:, half])
         numerator = both[:rank] + both[rank:]
-        numerator = numerator + dot(pair_t_ref[:rank, :], low_ref[:, columns])
+        numerator = numerator + dot(pair_t_ref[:rank, :], low_ref[:, half])
         right_out[:, columns] = right * numerator / sums_ref[:, :1]
 
 
-def left_numerator(slab_ref, pair_ref, right, total_ref, sums_ref, first):
-    rank = right.shape[0]
-    right_high, right_low = split(right)
+def left_numerator(slab_ref, pair_ref, right_ref, total_ref, sums_ref, high_ref, low_ref, start, first):
+    block = high_ref.shape[1]
+    rank = right_ref.shape[0]
+    right = right_ref[:, pl.ds(start, block)]
+    stack = stacked(right)
+    right_high, right_low = stack[:rank], stack[2 * rank :]
     right_both = jnp.concatenate([right_high, right_low], axis=0)
-    ones = jnp.ones((16, right.shape[1]), BF16)
-    row_sums = dot_nt(ones, right_both)[:PAD]
+    row_sums = dot_nt(jnp.ones((16, block), BF16), right_both)[:PAD]
     row_sums = row_sums[:, :rank] + row_sums[:, rank:]
     sums_ref[...] = jnp.where(first, row_sums, sums_ref[...] + row_sums)
-    stack = stacked(right)
-    for rows in chunks(slab_ref.shape[0], 256):
-        high, low = quotients(slab_ref, pair_ref, stack, rows, slice(None))
-        both = dot_nt(high, right_both)
-        term = both[:, :rank] + both[:, rank:] + dot_nt(low, right_high)
+    for rows in chunks(slab_ref.shape[0], ROWS):
+        for half in chunks(block, WIDTH):
+            columns = pl.ds(start + half.start, half.size)
+            part = stack[:, half.start : half.start + half.size]
+            high, low = quotients(slab_ref, pair_ref, part, rows, columns)
+            high_ref[rows, half] = high
+            low_ref[rows, half] = low
+        both = dot_nt(high_ref[rows, :], right_both)
+        term = both[:, :rank] + both[:, rank:] + dot_nt(low_ref[rows, :], right_high)
         total_ref[rows, :] = jnp.where(first, term, total_ref[rows, :] + term)
 
 
@@ -162,24 +173,39 @@
 
 
 def turn_kernel(
-    slab_ref, left_ref, right_ref, extra_ref, right_out, left_out,
-    pair_ref, pair_t_ref, sums_ref, high_ref, low_ref, total_ref, row_sums_ref,
+    block, slab_hbm, left_ref, right_ref, extra_ref, right_out, left_out, slab_ref,
+    pair_ref, pair_t_ref, sums_ref, high_ref, low_ref, total_ref, row_sums_ref, arrivals,
 ):
-    step = pl.program_id(0)
-
-    @pl.when(step == 0)
-    def _():
-        prepare_left(left_ref, pair_ref)
-        prepare_left_t(left_ref, pair_t_ref, sums_ref)
-
-    right_update(
-        slab_ref, pair_ref, pair_t_ref, sums_ref, right_ref, right_out, high_ref, low_ref
-    )
-    left_numerator(slab_ref, pair_ref, right_out[...], total_ref, row_sums_ref, step == 0)
-
-    @pl.when(step == pl.num_programs(0) - 1)
-    def _():
-        write_left(total_ref, row_sums_ref, extra_ref, left_out)
+    m, width = slab_ref.shape
+    steps = width // block
+    pieces = chunks(m, ROWS)
+
+    def copy(step, piece):
+        where = (pieces[piece], pl.ds(pl.multiple_of(step * block, block), block))
+        return pltpu.make_async_copy(
+            slab_hbm.at[where], slab_ref.at[where], arrivals.at[step, piece]
+        )
+
+    for step in range(steps):
+        for piece in range(len(pieces)):
+            copy(step, piece).start()
+    prepare_left(left_ref, pair_ref)
+    prepare_left_t(left_ref, pair_t_ref, sums_ref)
+
+    def one(step, carry):
+        start = pl.multiple_of(step * block, block)
+        right_update(
+            slab_ref, pair_ref, pair_t_ref, sums_ref, right_ref, right_out, high_ref, low_ref,
+            start, lambda piece: copy(step, piece).wait(),
+        )
+        left_numerator(
+            slab_ref, pair_ref, right_out, total_ref, row_sums_ref, high_ref, low_ref,
+            start, step == 0,
+        )
+        return carry
+
+    lax.fori_loop(0, steps, one, 0)
+    write_left(total_ref, row_sums_ref, extra_ref, left_out)
 
 
 def second_quotient(block, second_left, pairs):
@@ -230,9 +256,9 @@
     return pl.BlockSpec(shape, lambda step: (0,) * len(shape))
 
 
-def params():
+def params(vmem_bytes):
     return pltpu.CompilerParams(
-        dimension_semantics=("arbitrary",), vmem_limit_bytes=VMEM_BYTES
+        dimension_semantics=("arbitrary",), vmem_limit_bytes=vmem_bytes
     )
 
 
@@ -259,23 +285,29 @@
     )
 
 
-def full_turn(slab, left, right, extra, block, parts):
+def full_turn(slab, left, right, extra, block, parts, vmem_bytes):
     (m, columns), rank = slab.shape, left.shape[1]
-    columns_spec = lambda height: pl.BlockSpec((height, block), lambda step: (0, step))
     tall = m // parts + PAD
     return pl.pallas_call(
-        turn_kernel,
-        grid=(columns // block,),
-        in_specs=[columns_spec(m), full((m, rank)), columns_spec(rank), full((min(PAD, extra.shape[0]), rank))],
-        out_specs=[columns_spec(rank), full((parts, tall, rank))],
+        functools.partial(turn_kernel, block),
+        grid=(1,),
+        in_specs=[
+            pl.BlockSpec(memory_space=pl.ANY),
+            full((m, rank)),
+            full((rank, columns)),
+            full((min(PAD, extra.shape[0]), rank)),
+        ],
+        out_specs=[full((rank, columns)), full((parts, tall, rank))],
         out_shape=[
             jax.ShapeDtypeStruct((rank, columns), F32),
             jax.ShapeDtypeStruct((parts, tall, rank), F32),
         ],
-        scratch_shapes=left_scratch(m, rank)
+        scratch_shapes=[pltpu.VMEM((m, columns), F32)]
+        + left_scratch(m, rank)
         + right_scratch(m, rank, block)
-        + total_scratch(m, rank),
-        compiler_params=params(),
+        + total_scratch(m, rank)
+        + [pltpu.SemaphoreType.DMA((columns // block, max(1, m // ROWS)))],
+        compiler_params=params(vmem_bytes),
         cost_estimate=cost(m, rank, columns, 4),
         name="turn",
     )(slab, left, right, extra)
@@ -331,13 +363,15 @@
         own = lax.dynamic_slice_in_dim(left, own_part * rows_own, rows_own, 0)
         return own * total[:rows_own] / total[rows_own][None, :]
 
-    right, summed = full_turn(tensor_slab, left_init, right_init, left_init, k, parts)
+    right, summed = full_turn(
+        tensor_slab, after(left_init, second_factors), right_init, left_init, k, parts, 52 * MIB
+    )
     summed = summed.reshape(2, col_devices, rows_own + PAD, rank)
     total = reduce_z(reduce_plane(reduce_core(summed)))
     left = spread_core(spread_plane(own_left_rows(left_init, total))).reshape(m, rank)
 
     arrived = exchange(after(second_factors, left))
-    right, summed = full_turn(tensor_slab, left, right, col_part, k, parts)
+    right, summed = full_turn(tensor_slab, left, right, col_part, k, parts, VMEM_BYTES)
     arrived = after(arrived, summed)
     second_left = arrived[:, : per_owner * slices].reshape(rank * slices, rank)
     whole = arrived[:, per_owner * slices :].reshape(row_devices, col_devices, piece_rows, -1)

time: 121 us -> 126 us (1.041)
  Pallas kernels: 32.2 us -> 39.5 us
  local copies, waits for them, and re-layouts: 6.58 us -> 3.16 us
    pallas_call x2, Pallas kernels: 28.4 us -> 35.7 us  [full_turn(): pl.pallas_call(functools.partial(turn_kernel, block), grid=(1,), in_specs...]
    unnamed x10 -> x4, local copies, waits for them, and re-layouts: 4.48 us -> 1.05 us
    ppermute x22, waiting for transfers between devices: 33.7 us -> 35.1 us  [send(): return lax.ppermute(values, AXES, pairs)]
  transfers between devices with their start and end apart: 24 -> 24, of which waited for: 21 -> 21; matrix products, arithmetic and copies ran while one was open for 2% -> 1% of each run, Pallas kernels for 12% -> 14%
where the time goes in v5:
time: 126 us; the launch traced here: 125 us
  waiting for transfers between devices  45.2 us (36%)
  Pallas kernels  39.5 us (31%)
  starting transfers between devices  32.9 us (26%)
  other arithmetic  3.55 us (3%)
  local copies, waits for them, and re-layouts  3.16 us (3%)
    pallas_call x2, Pallas kernels, full_turn(): pl.pallas_call(functools.partial(turn_kernel, block), grid=(1,), in_specs...  35.7 us
    ppermute x22, waiting for transfers between devices, send(): return lax.ppermute(values, AXES, pairs)  35.1 us
    ppermute x22, starting transfers between devices, send(): return lax.ppermute(values, AXES, pairs)  25.1 us
    all_to_all x2, waiting for transfers between devices, exchange(): return lax.all_to_all(parts, AXES, split_axis=0, concat_axis=0, tiled=True)  10.1 us
    all_to_all x2, starting transfers between devices, exchange(): return lax.all_to_all(parts, AXES, split_axis=0, concat_axis=0, tiled=True)  7.79 us
  transfers between devices with their start and end apart: 24, of which 21 were waited for; matrix products, arithmetic and copies ran while one was open for 1% of the time, Pallas kernels for 14%

profile of v5, /device:TPU:0, one launch (start us, length us, event | category | flops | bytes accessed | tf_op | source)
XLA Modules:
  0.0 125.3 jit_solution(9123986113180406576)
XLA Ops:
  0.6 0.0 copy-start
  0.7 1.0 fusion.17
  1.8 0.0 copy-start.1
  1.8 1.0 copy-done.1
  2.9 17.9 %turn.2 = (f32[128,2048]{1,0:T(8,128)}, f32[8,136,128]{2,1,0:T(8,128)S(1)}) custom-call(f32[1024,2048]{1,0:T(8,128)} %slab_hbm.3, f32[1024,128]{1,0:T(8,128)S(1)} %copy-done.1, f32[128,2048]{1,0:T(8,128)} %right_ref.1, f32[1024,128]{1,0:T(8,128)S(1)} %copy-done.1), custom_call_target="tpu_custom_call" | custom-call | flops 6442450944 | bytes 8388608 | tf_op jit(solution)/shard_map/turn/pallas_call | solution.py:291
  20.8 0.5 collective-permute-start
  21.3 1.2 collective-permute-done
  22.6 3.9 %collective-permute-start.3 = (f32[136,128]{1,0:T(8,128)S(1)}, f32[136,128]{1,0:T(8,128)S(1)}, u32[]{:S(2)}, u32[]{:S(2)}) collective-permute-start(f32[136,128]{1,0:T(8,128)S(1)} %get-tuple-element.33), channel_id=1, source_target_pairs={{0,3},{1,2},{2,1},{3,0},{4,7},{5,6},{6,5},{7,4},{8,11},{9,10},{10,... | collective-permute-start | bytes 208904 | tf_op jit(solution)/shard_map/ppermute | solution.py:29
  26.4 0.5 collective-permute-start.2
  27.0 0.1 collective-permute-start.1
  27.1 1.9 %collective-permute-done.3 = f32[136,128]{1,0:T(8,128)S(1)} collective-permute-done((f32[136,128]{1,0:T(8,128)S(1)}, f32[136,128]{1,0:T(8,128)S(1)}, u32[]{:S(2)}, u32[]{:S(2)}) %collective-permute-start.3) | collective-permute-done | bytes 69664 | tf_op jit(solution)/shard_map/ppermute | solution.py:29
  29.0 1.8 %collective-permute-done.2 = f32[136,128]{1,0:T(8,128)S(1)} collective-permute-done((f32[136,128]{1,0:T(8,128)S(1)}, f32[136,128]{1,0:T(8,128)S(1)}, u32[]{:S(2)}, u32[]{:S(2)}) %collective-permute-start.2) | collective-permute-done | bytes 69664 | tf_op jit(solution)/shard_map/ppermute | solution.py:29
  30.8 0.5 collective-permute-done.1
  31.3 3.7 %collective-permute-start.6 = (f32[136,128]{1,0:T(8,128)S(1)}, f32[136,128]{1,0:T(8,128)S(1)}, u32[]{:S(2)}, u32[]{:S(2)}) collective-permute-start(f32[136,128]{1,0:T(8,128)S(1)} %fusion.11), channel_id=1, source_target_pairs={{0,24},{1,25},{2,26},{3,27},{4,28},{5,29},{6,30},{7,31},{8,16},{9,... | collective-permute-start | bytes 208904 | tf_op jit(solution)/shard_map/ppermute | solution.py:29
  34.9 0.0 collective-permute-start.5
  34.9 0.8 collective-permute-start.4
  35.7 1.9 %collective-permute-done.6 = f32[136,128]{1,0:T(8,128)S(1)} collective-permute-done((f32[136,128]{1,0:T(8,128)S(1)}, f32[136,128]{1,0:T(8,128)S(1)}, u32[]{:S(2)}, u32[]{:S(2)}) %collective-permute-start.6) | collective-permute-done | bytes 69664 | tf_op jit(solution)/shard_map/ppermute | solution.py:29
  37.6 2.8 %collective-permute-done.5 = f32[136,128]{1,0:T(8,128)S(1)} collective-permute-done((f32[136,128]{1,0:T(8,128)S(1)}, f32[136,128]{1,0:T(8,128)S(1)}, u32[]{:S(2)}, u32[]{:S(2)}) %collective-permute-start.5) | collective-permute-done | bytes 69664 | tf_op jit(solution)/shard_map/ppermute | solution.py:29
  40.4 0.0 collective-permute-done.4
  40.4 0.9 fusion.13
  41.3 1.6 %collective-permute-start.9 = (f32[128,128]{1,0:T(8,128)S(1)}, f32[128,128]{1,0:T(8,128)S(1)}, u32[]{:S(2)}, u32[]{:S(2)}) collective-permute-start(f32[128,128]{1,0:T(8,128)S(1)} %fusion.13), channel_id=1, source_target_pairs={{0,3},{1,2},{2,1},{3,0},{4,7},{5,6},{6,5},{7,4},{8,11},{9,10},{10,... | collective-permute-start | bytes 196616 | tf_op jit(solution)/shard_map/ppermute | solution.py:29
  42.9 1.4 %collective-permute-start.8 = (f32[128,128]{1,0:T(8,128)S(1)}, f32[128,128]{1,0:T(8,128)S(1)}, u32[]{:S(2)}, u32[]{:S(2)}) collective-permute-start(f32[128,128]{1,0:T(8,128)S(1)} %fusion.13), channel_id=1, source_target_pairs={{0,2},{1,3},{2,0},{3,1},{4,6},{5,7},{6,4},{7,5},{8,10},{9,11},{10,... | collective-permute-start | bytes 196616 | tf_op jit(solution)/shard_map/ppermute | solution.py:29
  44.3 0.6 collective-permute-start.7
  44.8 2.3 %collective-permute-done.9 = f32[128,128]{1,0:T(8,128)S(1)} collective-permute-done((f32[128,128]{1,0:T(8,128)S(1)}, f32[128,128]{1,0:T(8,128)S(1)}, u32[]{:S(2)}, u32[]{:S(2)}) %collective-permute-start.9) | collective-permute-done | bytes 65568 | tf_op jit(solution)/shard_map/ppermute | solution.py:29
  47.2 0.3 collective-permute-done.8
  47.5 1.0 collective-permute-done.7
  48.6 0.1 collective-permute-start.10
  48.7 1.5 %collective-permute-done.10 = f32[4,128,128]{2,1,0:T(8,128)S(1)} collective-permute-done((f32[4,128,128]{2,1,0:T(8,128)S(1)}, f32[4,128,128]{2,1,0:T(8,128)S(1)}, u32[]{:S(2)}, u32[]{:S(2)}) %collective-permute-start.10) | collective-permute-done | bytes 262176 | tf_op jit(solution)/shard_map/ppermute | solution.py:29
  50.2 0.1 fusion.9
  50.4 1.1 copy.16
  51.5 4.0 %all-to-all-start = ((f32[32,32,128]{2,1,0:T(8,128)}), f32[32,32,128]{2,1,0:T(8,128)S(1)}, u32[]{:S(2)}, u32[]{:S(2)}) async-start(f32[32,32,128]{2,1,0:T(8,128)} %copy.16), calls=%async_computation | async-start | bytes 1048576 | tf_op jit(solution)/shard_map/all_to_all | solution.py:19
  55.5 17.9 %turn.3 = (f32[128,2048]{1,0:T(8,128)S(1)}, f32[8,136,128]{2,1,0:T(8,128)S(1)}) custom-call(f32[1024,2048]{1,0:T(8,128)} %slab_hbm.3, f32[1024,128]{1,0:T(8,128)S(1)} %bitcast.84, f32[128,2048]{1,0:T(8,128)} %get-tuple-element.11.right_ref, f32[1,128]{1,0:T(1,128)S(1)} %bitcast.88), custom_call_target="tpu_custom_call" | custom-call | flops 6442450944 | bytes 8388608 | tf_op jit(solution)/shard_map/turn/pallas_call | solution.py:291
  73.4 0.0 all-to-all-done
  73.5 1.6 %second_numerator.1 = f32[4,128,128]{2,1,0:T(8,128)S(1)} custom-call(f32[128,2048]{1,0:T(8,128)S(1)} %get-tuple-element.13.right_ref, f32[512,128]{1,0:T(8,128)S(1)} %bitcast.76, f32[4,128,128]{2,1,0:T(8,128)S(1)} %bitcast.78), custom_call_target="tpu_custom_call" | custom-call | flops 402653184 | bytes 1048576 | tf_op jit(solution)/shard_map/second_numerator/pallas_call | solution.py:317
  75.1 0.3 collective-permute-start.11
  75.4 1.5 %collective-permute-done.11 = f32[4,200,128]{2,1,0:T(8,128)S(1)} collective-permute-done((f32[4,200,128]{2,1,0:T(8,128)S(1)}, f32[4,200,128]{2,1,0:T(8,128)S(1)}, u32[]{:S(2)}, u32[]{:S(2)}) %collective-permute-start.11) | collective-permute-done | bytes 409632 | tf_op jit(solution)/shard_map/ppermute | solution.py:29
  77.0 2.7 %collective-permute-start.14 = (f32[200,128]{1,0:T(8,128)S(1)}, f32[200,128]{1,0:T(8,128)S(1)}, u32[]{:S(2)}, u32[]{:S(2)}) collective-permute-start(f32[200,128]{1,0:T(8,128)S(1)} %get-tuple-element.24), channel_id=1, source_target_pairs={{0,3},{1,2},{2,1},{3,0},{4,7},{5,6},{6,5},{7,4},{8,11},{9,10},{10,... | collective-permute-start | bytes 307208 | tf_op jit(solution)/shard_map/ppermute | solution.py:29
  79.7 0.6 collective-permute-start.13
  80.3 0.3 collective-permute-start.12
  80.6 2.5 %collective-permute-done.14 = f32[200,128]{1,0:T(8,128)S(1)} collective-permute-done((f32[200,128]{1,0:T(8,128)S(1)}, f32[200,128]{1,0:T(8,128)S(1)}, u32[]{:S(2)}, u32[]{:S(2)}) %collective-permute-start.14) | collective-permute-done | bytes 102432 | tf_op jit(solution)/shard_map/ppermute | solution.py:29
  83.1 2.1 %collective-permute-done.13 = f32[200,128]{1,0:T(8,128)S(1)} collective-permute-done((f32[200,128]{1,0:T(8,128)S(1)}, f32[200,128]{1,0:T(8,128)S(1)}, u32[]{:S(2)}, u32[]{:S(2)}) %collective-permute-start.13) | collective-permute-done | bytes 102432 | tf_op jit(solution)/shard_map/ppermute | solution.py:29
  85.2 0.2 collective-permute-done.12
  85.4 3.4 %collective-permute-start.17 = (f32[200,128]{1,0:T(8,128)S(1)}, f32[200,128]{1,0:T(8,128)S(1)}, u32[]{:S(2)}, u32[]{:S(2)}) collective-permute-start(f32[200,128]{1,0:T(8,128)S(1)} %fusion.10), channel_id=1, source_target_pairs={{0,24},{1,25},{2,26},{3,27},{4,28},{5,29},{6,30},{7,31},{8,16},{9,... | collective-permute-start | bytes 307208 | tf_op jit(solution)/shard_map/ppermute | solution.py:29
  88.8 0.0 collective-permute-start.16
  88.8 1.0 collective-permute-start.15
  89.9 3.0 %collective-permute-done.17 = f32[200,128]{1,0:T(8,128)S(1)} collective-permute-done((f32[200,128]{1,0:T(8,128)S(1)}, f32[200,128]{1,0:T(8,128)S(1)}, u32[]{:S(2)}, u32[]{:S(2)}) %collective-permute-start.17) | collective-permute-done | bytes 102432 | tf_op jit(solution)/shard_map/ppermute | solution.py:29
  92.9 4.9 %collective-permute-done.16 = f32[200,128]{1,0:T(8,128)S(1)} collective-permute-done((f32[200,128]{1,0:T(8,128)S(1)}, f32[200,128]{1,0:T(8,128)S(1)}, u32[]{:S(2)}, u32[]{:S(2)}) %collective-permute-start.16) | collective-permute-done | bytes 102432 | tf_op jit(solution)/shard_map/ppermute | solution.py:29
  97.8 0.0 collective-permute-done.15
  97.9 0.1 broadcast_divide_fusion
  98.0 1.5 %collective-permute-start.19 = (f32[192,128]{1,0:T(8,128)S(1)}, f32[192,128]{1,0:T(8,128)S(1)}, u32[]{:S(2)}, u32[]{:S(2)}) collective-permute-start(f32[192,128]{1,0:T(8,128)S(1)} %get-tuple-element.45), channel_id=1, source_target_pairs={{0,2},{1,3},{2,0},{3,1},{4,6},{5,7},{6,4},{7,5},{8,10},{9,11},{10,... | collective-permute-start | bytes 294920 | tf_op jit(solution)/shard_map/ppermute | solution.py:29
  99.5 0.2 collective-permute-start.18
  99.8 1.8 %collective-permute-start.20 = (f32[192,128]{1,0:T(8,128)S(1)}, f32[192,128]{1,0:T(8,128)S(1)}, u32[]{:S(2)}, u32[]{:S(2)}) collective-permute-start(f32[192,128]{1,0:T(8,128)S(1)} %get-tuple-element.45), channel_id=1, source_target_pairs={{0,3},{1,2},{2,1},{3,0},{4,7},{5,6},{6,5},{7,4},{8,11},{9,10},{10,... | collective-permute-start | bytes 294920 | tf_op jit(solution)/shard_map/ppermute | solution.py:29
  101.6 2.2 %collective-permute-done.19 = f32[192,128]{1,0:T(8,128)S(1)} collective-permute-done((f32[192,128]{1,0:T(8,128)S(1)}, f32[192,128]{1,0:T(8,128)S(1)}, u32[]{:S(2)}, u32[]{:S(2)}) %collective-permute-start.19) | collective-permute-done | bytes 98336 | tf_op jit(solution)/shard_map/ppermute | solution.py:29
  103.7 0.5 collective-permute-done.18
  104.3 1.2 collective-permute-done.20
  105.6 0.1 pad_maximum_fusion.3
  105.6 0.1 collective-permute-start.21
  105.7 1.7 %collective-permute-done.21 = f32[4,192,128]{2,1,0:T(8,128)S(1)} collective-permute-done((f32[4,192,128]{2,1,0:T(8,128)S(1)}, f32[4,192,128]{2,1,0:T(8,128)S(1)}, u32[]{:S(2)}, u32[]{:S(2)}) %collective-permute-start.21) | collective-permute-done | bytes 393248 | tf_op jit(solution)/shard_map/ppermute | solution.py:29
  107.4 0.2 fusion.6
  107.6 2.2 %second_rows.1 = f32[512,128]{1,0:T(8,128)} custom-call(f32[128,2048]{1,0:T(8,128)S(1)} %get-tuple-element.13.right_ref, f32[512,128]{1,0:T(8,128)S(1)} %bitcast.77, f32[4,128,128]{2,1,0:T(8,128)S(1)} %bitcast.83), custom_call_target="tpu_custom_call" | custom-call | flops 402653184 | bytes 1048576 | tf_op jit(solution)/shard_map/second_rows/pallas_call | solution.py:327
  109.8 3.8 %all-to-all-start.1 = ((f32[32,16,128]{2,1,0:T(8,128)}), f32[32,16,128]{2,1,0:T(8,128)S(1)}, u32[]{:S(2)}, u32[]{:S(2)}) async-start(f32[32,16,128]{2,1,0:T(8,128)} %bitcast.45), calls=%async_computation.1 | async-start | bytes 524288 | tf_op jit(solution)/shard_map/all_to_all | solution.py:19
  113.6 0.8 fusion
  114.4 10.1 %all-to-all-done.1 = f32[32,16,128]{2,1,0:T(8,128)S(1)} async-done(((f32[32,16,128]{2,1,0:T(8,128)}), f32[32,16,128]{2,1,0:T(8,128)S(1)}, u32[]{:S(2)}, u32[]{:S(2)}) %all-to-all-start.1) | async-done | bytes 262176 | tf_op jit(solution)/shard_map/all_to_all | solution.py:19
  124.5 0.7 copy.18
  (29 shorter events, 0.7 us)
Async XLA Ops:
  0.6 1.1 copy-start
  1.8 1.0 copy-start.1
  20.8 1.7 %collective-permute-start = (f32[4,136,128]{2,1,0:T(8,128)S(1)}, f32[4,136,128]{2,1,0:T(8,128)S(1)}, u32[]{:S(2)}, u32[]{:S(2)}) collective-permute-start(f32[4,136,128]{2,1,0:T(8,128)S(1)} %dynamic-slice_bitcast_fusion), channel_id=1, source_target_pairs={{0,4},{1,5},{2,6},{3,7},{4,0},{5,1},{6,2},{7,3},{8,12},{9,13},{10,... | collective-permute-start | bytes 835592 | tf_op jit(solution)/shard_map/ppermute | solution.py:29
  22.6 6.4 %collective-permute-start.3 = (f32[136,128]{1,0:T(8,128)S(1)}, f32[136,128]{1,0:T(8,128)S(1)}, u32[]{:S(2)}, u32[]{:S(2)}) collective-permute-start(f32[136,128]{1,0:T(8,128)S(1)} %get-tuple-element.33), channel_id=1, source_target_pairs={{0,3},{1,2},{2,1},{3,0},{4,7},{5,6},{6,5},{7,4},{8,11},{9,10},{10,... | collective-permute-start | bytes 208904 | tf_op jit(solution)/shard_map/ppermute | solution.py:29
  26.4 4.3 %collective-permute-start.2 = (f32[136,128]{1,0:T(8,128)S(1)}, f32[136,128]{1,0:T(8,128)S(1)}, u32[]{:S(2)}, u32[]{:S(2)}) collective-permute-start(f32[136,128]{1,0:T(8,128)S(1)} %get-tuple-element.34), channel_id=1, source_target_pairs={{0,2},{1,3},{2,0},{3,1},{4,6},{5,7},{6,4},{7,5},{8,10},{9,11},{10,... | collective-permute-start | bytes 208904 | tf_op jit(solution)/shard_map/ppermute | solution.py:29
  27.0 4.3 %collective-permute-start.1 = (f32[136,128]{1,0:T(8,128)S(1)}, f32[136,128]{1,0:T(8,128)S(1)}, u32[]{:S(2)}, u32[]{:S(2)}) collective-permute-start(f32[136,128]{1,0:T(8,128)S(1)} %get-tuple-element.35), channel_id=1, source_target_pairs={{0,1},{1,0},{2,3},{3,2},{4,5},{5,4},{6,7},{7,6},{8,9},{9,8},{10,11... | collective-permute-start | bytes 208904 | tf_op jit(solution)/shard_map/ppermute | solution.py:29
  31.3 6.3 %collective-permute-start.6 = (f32[136,128]{1,0:T(8,128)S(1)}, f32[136,128]{1,0:T(8,128)S(1)}, u32[]{:S(2)}, u32[]{:S(2)}) collective-permute-start(f32[136,128]{1,0:T(8,128)S(1)} %fusion.11), channel_id=1, source_target_pairs={{0,24},{1,25},{2,26},{3,27},{4,28},{5,29},{6,30},{7,31},{8,16},{9,... | collective-permute-start | bytes 208904 | tf_op jit(solution)/shard_map/ppermute | solution.py:29
  34.9 5.4 %collective-permute-start.5 = (f32[136,128]{1,0:T(8,128)S(1)}, f32[136,128]{1,0:T(8,128)S(1)}, u32[]{:S(2)}, u32[]{:S(2)}) collective-permute-start(f32[136,128]{1,0:T(8,128)S(1)} %fusion.11), channel_id=1, source_target_pairs={{0,16},{1,17},{2,18},{3,19},{4,20},{5,21},{6,22},{7,23},{8,24},{9,... | collective-permute-start | bytes 208904 | tf_op jit(solution)/shard_map/ppermute | solution.py:29
  34.9 5.4 %collective-permute-start.4 = (f32[136,128]{1,0:T(8,128)S(1)}, f32[136,128]{1,0:T(8,128)S(1)}, u32[]{:S(2)}, u32[]{:S(2)}) collective-permute-start(f32[136,128]{1,0:T(8,128)S(1)} %fusion.11), channel_id=1, source_target_pairs={{0,8},{1,9},{2,10},{3,11},{4,12},{5,13},{6,14},{7,15},{8,0},{9,1},... | collective-permute-start | bytes 208904 | tf_op jit(solution)/shard_map/ppermute | solution.py:29
  41.3 5.9 %collective-permute-start.9 = (f32[128,128]{1,0:T(8,128)S(1)}, f32[128,128]{1,0:T(8,128)S(1)}, u32[]{:S(2)}, u32[]{:S(2)}) collective-permute-start(f32[128,128]{1,0:T(8,128)S(1)} %fusion.13), channel_id=1, source_target_pairs={{0,3},{1,2},{2,1},{3,0},{4,7},{5,6},{6,5},{7,4},{8,11},{9,10},{10,... | collective-permute-start | bytes 196616 | tf_op jit(solution)/shard_map/ppermute | solution.py:29
  42.9 4.7 %collective-permute-start.8 = (f32[128,128]{1,0:T(8,128)S(1)}, f32[128,128]{1,0:T(8,128)S(1)}, u32[]{:S(2)}, u32[]{:S(2)}) collective-permute-start(f32[128,128]{1,0:T(8,128)S(1)} %fusion.13), channel_id=1, source_target_pairs={{0,2},{1,3},{2,0},{3,1},{4,6},{5,7},{6,4},{7,5},{8,10},{9,11},{10,... | collective-permute-start | bytes 196616 | tf_op jit(solution)/shard_map/ppermute | solution.py:29
  44.3 4.3 %collective-permute-start.7 = (f32[128,128]{1,0:T(8,128)S(1)}, f32[128,128]{1,0:T(8,128)S(1)}, u32[]{:S(2)}, u32[]{:S(2)}) collective-permute-start(f32[128,128]{1,0:T(8,128)S(1)} %fusion.13), channel_id=1, source_target_pairs={{0,1},{1,0},{2,3},{3,2},{4,5},{5,4},{6,7},{7,6},{8,9},{9,8},{10,11... | collective-permute-start | bytes 196616 | tf_op jit(solution)/shard_map/ppermute | solution.py:29
  48.6 1.6 %collective-permute-start.10 = (f32[4,128,128]{2,1,0:T(8,128)S(1)}, f32[4,128,128]{2,1,0:T(8,128)S(1)}, u32[]{:S(2)}, u32[]{:S(2)}) collective-permute-start(f32[4,128,128]{2,1,0:T(8,128)S(1)} %get-tuple-element.36), channel_id=1, source_target_pairs={{0,4},{1,5},{2,6},{3,7},{4,0},{5,1},{6,2},{7,3},{8,12},{9,13},{10,... | collective-permute-start | bytes 786440 | tf_op jit(solution)/shard_map/ppermute | solution.py:29
  51.5 21.9 %all-to-all-start = ((f32[32,32,128]{2,1,0:T(8,128)}), f32[32,32,128]{2,1,0:T(8,128)S(1)}, u32[]{:S(2)}, u32[]{:S(2)}) async-start(f32[32,32,128]{2,1,0:T(8,128)} %copy.16), calls=%async_computation | async-start | bytes 1048576 | tf_op jit(solution)/shard_map/all_to_all | solution.py:19
  75.1 1.8 %collective-permute-start.11 = (f32[4,200,128]{2,1,0:T(8,128)S(1)}, f32[4,200,128]{2,1,0:T(8,128)S(1)}, u32[]{:S(2)}, u32[]{:S(2)}) collective-permute-start(f32[4,200,128]{2,1,0:T(8,128)S(1)} %fusion.2), channel_id=1, source_target_pairs={{0,4},{1,5},{2,6},{3,7},{4,0},{5,1},{6,2},{7,3},{8,12},{9,13},{10,... | collective-permute-start | bytes 1228808 | tf_op jit(solution)/shard_map/ppermute | solution.py:29
  77.0 6.1 %collective-permute-start.14 = (f32[200,128]{1,0:T(8,128)S(1)}, f32[200,128]{1,0:T(8,128)S(1)}, u32[]{:S(2)}, u32[]{:S(2)}) collective-permute-start(f32[200,128]{1,0:T(8,128)S(1)} %get-tuple-element.24), channel_id=1, source_target_pairs={{0,3},{1,2},{2,1},{3,0},{4,7},{5,6},{6,5},{7,4},{8,11},{9,10},{10,... | collective-permute-start | bytes 307208 | tf_op jit(solution)/shard_map/ppermute | solution.py:29
  79.7 5.5 %collective-permute-start.13 = (f32[200,128]{1,0:T(8,128)S(1)}, f32[200,128]{1,0:T(8,128)S(1)}, u32[]{:S(2)}, u32[]{:S(2)}) collective-permute-start(f32[200,128]{1,0:T(8,128)S(1)} %get-tuple-element.25), channel_id=1, source_target_pairs={{0,2},{1,3},{2,0},{3,1},{4,6},{5,7},{6,4},{7,5},{8,10},{9,11},{10,... | collective-permute-start | bytes 307208 | tf_op jit(solution)/shard_map/ppermute | solution.py:29
  80.3 5.1 %collective-permute-start.12 = (f32[200,128]{1,0:T(8,128)S(1)}, f32[200,128]{1,0:T(8,128)S(1)}, u32[]{:S(2)}, u32[]{:S(2)}) collective-permute-start(f32[200,128]{1,0:T(8,128)S(1)} %get-tuple-element.26), channel_id=1, source_target_pairs={{0,1},{1,0},{2,3},{3,2},{4,5},{5,4},{6,7},{7,6},{8,9},{9,8},{10,11... | collective-permute-start | bytes 307208 | tf_op jit(solution)/shard_map/ppermute | solution.py:29
  85.4 7.4 %collective-permute-start.17 = (f32[200,128]{1,0:T(8,128)S(1)}, f32[200,128]{1,0:T(8,128)S(1)}, u32[]{:S(2)}, u32[]{:S(2)}) collective-permute-start(f32[200,128]{1,0:T(8,128)S(1)} %fusion.10), channel_id=1, source_target_pairs={{0,24},{1,25},{2,26},{3,27},{4,28},{5,29},{6,30},{7,31},{8,16},{9,... | collective-permute-start | bytes 307208 | tf_op jit(solution)/shard_map/ppermute | solution.py:29
  88.8 9.0 %collective-permute-start.16 = (f32[200,128]{1,0:T(8,128)S(1)}, f32[200,128]{1,0:T(8,128)S(1)}, u32[]{:S(2)}, u32[]{:S(2)}) collective-permute-start(f32[200,128]{1,0:T(8,128)S(1)} %fusion.10), channel_id=1, source_target_pairs={{0,16},{1,17},{2,18},{3,19},{4,20},{5,21},{6,22},{7,23},{8,24},{9,... | collective-permute-start | bytes 307208 | tf_op jit(solution)/shard_map/ppermute | solution.py:29
  88.8 9.0 %collective-permute-start.15 = (f32[200,128]{1,0:T(8,128)S(1)}, f32[200,128]{1,0:T(8,128)S(1)}, u32[]{:S(2)}, u32[]{:S(2)}) collective-permute-start(f32[200,128]{1,0:T(8,128)S(1)} %fusion.10), channel_id=1, source_target_pairs={{0,8},{1,9},{2,10},{3,11},{4,12},{5,13},{6,14},{7,15},{8,0},{9,1},... | collective-permute-start | bytes 307208 | tf_op jit(solution)/shard_map/ppermute | solution.py:29
  98.0 5.7 %collective-permute-start.19 = (f32[192,128]{1,0:T(8,128)S(1)}, f32[192,128]{1,0:T(8,128)S(1)}, u32[]{:S(2)}, u32[]{:S(2)}) collective-permute-start(f32[192,128]{1,0:T(8,128)S(1)} %get-tuple-element.45), channel_id=1, source_target_pairs={{0,2},{1,3},{2,0},{3,1},{4,6},{5,7},{6,4},{7,5},{8,10},{9,11},{10,... | collective-permute-start | bytes 294920 | tf_op jit(solution)/shard_map/ppermute | solution.py:29
  99.5 4.8 %collective-permute-start.18 = (f32[192,128]{1,0:T(8,128)S(1)}, f32[192,128]{1,0:T(8,128)S(1)}, u32[]{:S(2)}, u32[]{:S(2)}) collective-permute-start(f32[192,128]{1,0:T(8,128)S(1)} %get-tuple-element.45), channel_id=1, source_target_pairs={{0,1},{1,0},{2,3},{3,2},{4,5},{5,4},{6,7},{7,6},{8,9},{9,8},{10,11... | collective-permute-start | bytes 294920 | tf_op jit(solution)/shard_map/ppermute | solution.py:29
  99.8 5.7 %collective-permute-start.20 = (f32[192,128]{1,0:T(8,128)S(1)}, f32[192,128]{1,0:T(8,128)S(1)}, u32[]{:S(2)}, u32[]{:S(2)}) collective-permute-start(f32[192,128]{1,0:T(8,128)S(1)} %get-tuple-element.45), channel_id=1, source_target_pairs={{0,3},{1,2},{2,1},{3,0},{4,7},{5,6},{6,5},{7,4},{8,11},{9,10},{10,... | collective-permute-start | bytes 294920 | tf_op jit(solution)/shard_map/ppermute | solution.py:29
  105.6 1.8 %collective-permute-start.21 = (f32[4,192,128]{2,1,0:T(8,128)S(1)}, f32[4,192,128]{2,1,0:T(8,128)S(1)}, u32[]{:S(2)}, u32[]{:S(2)}) collective-permute-start(f32[4,192,128]{2,1,0:T(8,128)S(1)} %get-tuple-element.27), channel_id=1, source_target_pairs={{0,4},{1,5},{2,6},{3,7},{4,0},{5,1},{6,2},{7,3},{8,12},{9,13},{10,... | collective-permute-start | bytes 1179656 | tf_op jit(solution)/shard_map/ppermute | solution.py:29
  109.8 14.7 %all-to-all-start.1 = ((f32[32,16,128]{2,1,0:T(8,128)}), f32[32,16,128]{2,1,0:T(8,128)S(1)}, u32[]{:S(2)}, u32[]{:S(2)}) async-start(f32[32,16,128]{2,1,0:T(8,128)} %bitcast.45), calls=%async_computation.1 | async-start | bytes 524288 | tf_op jit(solution)/shard_map/all_to_all | solution.py:19

commit v6 on v2

--- a/solution.py
+++ b/solution.py
@@ -10,7 +10,9 @@
 AXES = ("row", "col")
 F32, BF16 = jnp.float32, jnp.bfloat16
 PAD = 8
-VMEM_BYTES = 54 * 1024 * 1024
+ROWS = 256
+MIB = 1024 * 1024
+VMEM_BYTES = 51 * MIB
 
 
 def exchange(parts):
@@ -102,38 +104,43 @@
     sums_ref[...] = jnp.broadcast_to(jnp.sum(turned, axis=1, keepdims=True), sums_ref.shape)
 
 
-def row_chunks(m):
-    size = min(256, m)
-    return [pl.ds(start, size) for start in range(0, m, size)]
-
-
-def quotients(slab_ref, pair_ref, right, rows):
+def chunks(extent, size):
+    size = min(size, extent)
+    return [pl.ds(start, size) for start in range(0, extent, size)]
+
+
+def stacked(right):
     high, low = split(right)
-    product = dot(pair_ref[rows, :], jnp.concatenate([high, high, low], axis=0))
+    return jnp.concatenate([high, high, low], axis=0)
+
+
+def quotients(slab_ref, pair_ref, right_stack, rows):
+    product = dot(pair_ref[rows, :], right_stack)
     return split(divide(slab_ref[rows, :], product))
 
 
-def right_update(slab_ref, pair_ref, pair_t_ref, sums_ref, right, high_ref, low_ref):
+def right_update(slab_ref, pair_ref, pair_t_ref, sums_ref, right):
     rank = right.shape[0]
-    for rows in row_chunks(slab_ref.shape[0]):
-        high, low = quotients(slab_ref, pair_ref, right, rows)
-        high_ref[rows, :] = high
-        low_ref[rows, :] = low
-    both = dot(pair_t_ref[...], high_ref[...])
-    numerator = both[:rank] + both[rank:] + dot(pair_t_ref[:rank, :], low_ref[...])
+    stack = stacked(right)
+    parts = [quotients(slab_ref, pair_ref, stack, rows) for rows in chunks(slab_ref.shape[0], ROWS)]
+    both = dot(pair_t_ref[...], jnp.concatenate([high for high, _ in parts], axis=0))
+    numerator = both[:rank] + both[rank:]
+    numerator = numerator + dot(
+        pair_t_ref[:rank, :], jnp.concatenate([low for _, low in parts], axis=0)
+    )
     return right * numerator / sums_ref[:, :1]
 
 
 def left_numerator(slab_ref, pair_ref, right, total_ref, sums_ref, first):
     rank = right.shape[0]
-    right_high, right_low = split(right)
+    stack = stacked(right)
+    right_high, right_low = stack[:rank], stack[2 * rank :]
     right_both = jnp.concatenate([right_high, right_low], axis=0)
-    ones = jnp.ones((16, right.shape[1]), BF16)
-    row_sums = dot_nt(ones, right_both)[:PAD]
+    row_sums = dot_nt(jnp.ones((16, right.shape[1]), BF16), right_both)[:PAD]
     row_sums = row_sums[:, :rank] + row_sums[:, rank:]
     sums_ref[...] = jnp.where(first, row_sums, sums_ref[...] + row_sums)
-    for rows in row_chunks(slab_ref.shape[0]):
-        high, low = quotients(slab_ref, pair_ref, right, rows)
+    for rows in chunks(slab_ref.shape[0], ROWS):
+        high, low = quotients(slab_ref, pair_ref, stack, rows)
         both = dot_nt(high, right_both)
         term = both[:, :rank] + both[:, rank:] + dot_nt(low, right_high)
         total_ref[rows, :] = jnp.where(first, term, total_ref[rows, :] + term)
@@ -143,7 +150,7 @@
     parts, tall, rank = out_ref.shape
     height = tall - PAD
     first = lax.broadcasted_iota(jnp.int32, (PAD, rank), 0) == 0
-    stats = jnp.where(first, row_sums_ref[...], extra_ref[...])
+    stats = jnp.where(first, row_sums_ref[...], extra_ref[:1, :])
     for part in range(parts):
         out_ref[part, :height, :] = total_ref[pl.ds(part * height, height), :]
         out_ref[part, height:, :] = stats
@@ -151,7 +158,7 @@
 
 def turn_kernel(
     slab_ref, left_ref, right_ref, extra_ref, right_out, left_out,
-    pair_ref, pair_t_ref, sums_ref, high_ref, low_ref, total_ref, row_sums_ref,
+    pair_ref, pair_t_ref, sums_ref, total_ref, row_sums_ref,
 ):
     step = pl.program_id(0)
 
@@ -160,9 +167,7 @@
         prepare_left(left_ref, pair_ref)
         prepare_left_t(left_ref, pair_t_ref, sums_ref)
 
-    right = right_update(
-        slab_ref, pair_ref, pair_t_ref, sums_ref, right_ref[...], high_ref, low_ref
-    )
+    right = right_update(slab_ref, pair_ref, pair_t_ref, sums_ref, right_ref[...])
     right_out[...] = right
     left_numerator(slab_ref, pair_ref, right, total_ref, row_sums_ref, step == 0)
 
@@ -219,9 +224,9 @@
     return pl.BlockSpec(shape, lambda step: (0,) * len(shape))
 
 
-def params():
+def params(vmem_bytes):
     return pltpu.CompilerParams(
-        dimension_semantics=("arbitrary",), vmem_limit_bytes=VMEM_BYTES
+        dimension_semantics=("arbitrary",), vmem_limit_bytes=vmem_bytes
     )
 
 
@@ -229,13 +234,8 @@
     return [pltpu.VMEM((m, 3 * rank), BF16)]
 
 
-def right_scratch(m, rank, block):
-    return [
-        pltpu.VMEM((2 * rank, m), BF16),
-        pltpu.VMEM((rank, rank), F32),
-        pltpu.VMEM((m, block), BF16),
-        pltpu.VMEM((m, block), BF16),
-    ]
+def right_scratch(m, rank):
+    return [pltpu.VMEM((2 * rank, m), BF16), pltpu.VMEM((rank, rank), F32)]
 
 
 def total_scratch(m, rank):
@@ -248,23 +248,23 @@
     )
 
 
-def full_turn(slab, left, right, extra, block, parts):
+def full_turn(slab, left, right, extra, block, parts, vmem_bytes):
     (m, columns), rank = slab.shape, left.shape[1]
     columns_spec = lambda height: pl.BlockSpec((height, block), lambda step: (0, step))
     tall = m // parts + PAD
     return pl.pallas_call(
         turn_kernel,
         grid=(columns // block,),
-        in_specs=[columns_spec(m), full((m, rank)), columns_spec(rank), full((PAD, rank))],
+        in_specs=[columns_spec(m), full((m, rank)), columns_spec(rank), full((min(PAD, extra.shape[0]), rank))],
         out_specs=[columns_spec(rank), full((parts, tall, rank))],
         out_shape=[
             jax.ShapeDtypeStruct((rank, columns), F32),
             jax.ShapeDtypeStruct((parts, tall, rank), F32),
         ],
         scratch_shapes=left_scratch(m, rank)
-        + right_scratch(m, rank, block)
+        + right_scratch(m, rank)
         + total_scratch(m, rank),
-        compiler_params=params(),
+        compiler_params=params(vmem_bytes),
         cost_estimate=cost(m, rank, columns, 4),
         name="turn",
     )(slab, left, right, extra)
@@ -306,7 +306,7 @@
     own_left = lax.dynamic_slice_in_dim(
         second_left_init, lax.axis_index("col") * second_rows, second_rows, 0
     )
-    col_part = jnp.broadcast_to(jnp.sum(own_left, axis=0)[None], (PAD, rank))
+    col_part = jnp.sum(own_left, axis=0)[None]
     own_left = own_left.reshape(per_owner, devices, slices, rank).transpose(1, 0, 2, 3)
     own_left = own_left.reshape(devices, per_owner * slices, rank)
     piece_rows = rank // row_devices
@@ -320,13 +320,15 @@
         own = lax.dynamic_slice_in_dim(left, own_part * rows_own, rows_own, 0)
         return own * total[:rows_own] / total[rows_own][None, :]
 
-    right, summed = full_turn(tensor_slab, left_init, right_init, left_init, k, parts)
+    right, summed = full_turn(
+        tensor_slab, after(left_init, second_factors), right_init, left_init, k, parts, 52 * MIB
+    )
     summed = summed.reshape(2, col_devices, rows_own + PAD, rank)
     total = reduce_z(reduce_plane(reduce_core(summed)))
     left = spread_core(spread_plane(own_left_rows(left_init, total))).reshape(m, rank)
 
     arrived = exchange(after(second_factors, left))
-    right, summed = full_turn(tensor_slab, left, right, col_part, k, parts)
+    right, summed = full_turn(tensor_slab, left, right, col_part, k, parts, VMEM_BYTES)
     arrived = after(arrived, summed)
     second_left = arrived[:, : per_owner * slices].reshape(rank * slices, rank)
     whole = arrived[:, per_owner * slices :].reshape(row_devices, col_devices, piece_rows, -1)

time: 129 us -> 118 us (0.915)
  other arithmetic: 9.77 us -> 3.55 us
  Pallas kernels: 35.8 us -> 30.4 us
  waiting for transfers between devices: 45.3 us -> 47.6 us
  local copies, waits for them, and re-layouts: 5.06 us -> 3.15 us
    pallas_call x1, Pallas kernels: 3.63 us -> 1.59 us  [second_numerator(): pl.pallas_call(functools.partial(numerator_kernel, slices), out_shape=jax...]
    pallas_call x2, Pallas kernels: 28.7 us -> 26.7 us  [full_turn(): pl.pallas_call(turn_kernel, grid=(columns // block,), in_specs=[columns_s...]
    add x2, other arithmetic: 2.03 us -> 0.08 us  [reduce_core(): return pick(parts, core) + send(pick(parts, 1 - core), 1, 0)]
    all_to_all x2, waiting for transfers between devices: 11.7 us -> 13.3 us  [exchange(): return lax.all_to_all(parts, AXES, split_axis=0, concat_axis=0, tiled=True)]
    another operation x3, other arithmetic: 2.38 us -> 0.89 us  [spread_core(): return jnp.stack([pick(both, core), pick(both, 1 - core)])]
    pallas_call x1, Pallas kernels: 3.52 us -> 2.19 us  [second_rows_out(): pl.pallas_call(functools.partial(second_kernel, slices), out_shape=jax.Sh...]
  transfers between devices with their start and end apart: 24 -> 24, of which waited for: 20 -> 21; matrix products, arithmetic and copies ran while one was open for 2% -> 1% of each run, Pallas kernels for 11% -> 11%
where the time goes in v6:
time: 118 us; the launch traced here: 117 us
  waiting for transfers between devices  47.6 us (40%)
  starting transfers between devices  31.8 us (27%)
  Pallas kernels  30.4 us (26%)
  other arithmetic  3.55 us (3%)
  local copies, waits for them, and re-layouts  3.15 us (3%)
    ppermute x22, waiting for transfers between devices, send(): return lax.ppermute(values, AXES, pairs)  34.3 us
    pallas_call x2, Pallas kernels, full_turn(): pl.pallas_call(turn_kernel, grid=(columns // block,), in_specs=[columns_s...  26.7 us
    ppermute x22, starting transfers between devices, send(): return lax.ppermute(values, AXES, pairs)  24.8 us
    all_to_all x2, waiting for transfers between devices, exchange(): return lax.all_to_all(parts, AXES, split_axis=0, concat_axis=0, tiled=True)  13.3 us
    all_to_all x2, starting transfers between devices, exchange(): return lax.all_to_all(parts, AXES, split_axis=0, concat_axis=0, tiled=True)  6.93 us
  transfers between devices with their start and end apart: 24, of which 21 were waited for; matrix products, arithmetic and copies ran while one was open for 1% of the time, Pallas kernels for 11%

profile of v6, /device:TPU:0, one launch (start us, length us, event | category | flops | bytes accessed | tf_op | source)
XLA Modules:
  0.0 117.4 jit_solution(6578395167279541635)
XLA Ops:
  0.6 0.0 copy-start
  0.7 1.0 fusion.17
  1.8 0.0 copy-start.1
  1.8 1.0 copy-done.1
  2.9 13.7 %turn.2 = (f32[128,2048]{1,0:T(8,128)}, f32[8,136,128]{2,1,0:T(8,128)S(1)}) custom-call(f32[1024,2048]{1,0:T(8,128)} %slab_ref.3, f32[1024,128]{1,0:T(8,128)S(1)} %copy-done.1, f32[128,2048]{1,0:T(8,128)} %right_ref.1, f32[1024,128]{1,0:T(8,128)S(1)} %copy-done.1), custom_call_target="tpu_custom_call" | custom-call | flops 6442450944 | bytes 8388608 | tf_op jit(solution)/shard_map/turn/pallas_call | solution.py:255
  16.5 0.5 collective-permute-start
  17.1 1.2 %collective-permute-done = f32[4,136,128]{2,1,0:T(8,128)S(1)} collective-permute-done((f32[4,136,128]{2,1,0:T(8,128)S(1)}, f32[4,136,128]{2,1,0:T(8,128)S(1)}, u32[]{:S(2)}, u32[]{:S(2)}) %collective-permute-start) | collective-permute-done | bytes 278560 | tf_op jit(solution)/shard_map/ppermute | solution.py:29
  18.3 3.9 %collective-permute-start.3 = (f32[136,128]{1,0:T(8,128)S(1)}, f32[136,128]{1,0:T(8,128)S(1)}, u32[]{:S(2)}, u32[]{:S(2)}) collective-permute-start(f32[136,128]{1,0:T(8,128)S(1)} %get-tuple-element.33), channel_id=1, source_target_pairs={{0,3},{1,2},{2,1},{3,0},{4,7},{5,6},{6,5},{7,4},{8,11},{9,10},{10,... | collective-permute-start | bytes 208904 | tf_op jit(solution)/shard_map/ppermute | solution.py:29
  22.2 0.5 collective-permute-start.2
  22.7 0.1 collective-permute-start.1
  22.9 1.9 %collective-permute-done.3 = f32[136,128]{1,0:T(8,128)S(1)} collective-permute-done((f32[136,128]{1,0:T(8,128)S(1)}, f32[136,128]{1,0:T(8,128)S(1)}, u32[]{:S(2)}, u32[]{:S(2)}) %collective-permute-start.3) | collective-permute-done | bytes 69664 | tf_op jit(solution)/shard_map/ppermute | solution.py:29
  24.7 1.8 %collective-permute-done.2 = f32[136,128]{1,0:T(8,128)S(1)} collective-permute-done((f32[136,128]{1,0:T(8,128)S(1)}, f32[136,128]{1,0:T(8,128)S(1)}, u32[]{:S(2)}, u32[]{:S(2)}) %collective-permute-start.2) | collective-permute-done | bytes 69664 | tf_op jit(solution)/shard_map/ppermute | solution.py:29
  26.5 0.5 collective-permute-done.1
  27.0 3.7 %collective-permute-start.6 = (f32[136,128]{1,0:T(8,128)S(1)}, f32[136,128]{1,0:T(8,128)S(1)}, u32[]{:S(2)}, u32[]{:S(2)}) collective-permute-start(f32[136,128]{1,0:T(8,128)S(1)} %fusion.11), channel_id=1, source_target_pairs={{0,24},{1,25},{2,26},{3,27},{4,28},{5,29},{6,30},{7,31},{8,16},{9,... | collective-permute-start | bytes 208904 | tf_op jit(solution)/shard_map/ppermute | solution.py:29
  30.7 0.0 collective-permute-start.5
  30.7 0.8 collective-permute-start.4
  31.5 1.9 %collective-permute-done.6 = f32[136,128]{1,0:T(8,128)S(1)} collective-permute-done((f32[136,128]{1,0:T(8,128)S(1)}, f32[136,128]{1,0:T(8,128)S(1)}, u32[]{:S(2)}, u32[]{:S(2)}) %collective-permute-start.6) | collective-permute-done | bytes 69664 | tf_op jit(solution)/shard_map/ppermute | solution.py:29
  33.4 2.7 %collective-permute-done.5 = f32[136,128]{1,0:T(8,128)S(1)} collective-permute-done((f32[136,128]{1,0:T(8,128)S(1)}, f32[136,128]{1,0:T(8,128)S(1)}, u32[]{:S(2)}, u32[]{:S(2)}) %collective-permute-start.5) | collective-permute-done | bytes 69664 | tf_op jit(solution)/shard_map/ppermute | solution.py:29
  36.2 0.0 collective-permute-done.4
  36.2 0.9 fusion.13
  37.1 1.6 %collective-permute-start.9 = (f32[128,128]{1,0:T(8,128)S(1)}, f32[128,128]{1,0:T(8,128)S(1)}, u32[]{:S(2)}, u32[]{:S(2)}) collective-permute-start(f32[128,128]{1,0:T(8,128)S(1)} %fusion.13), channel_id=1, source_target_pairs={{0,3},{1,2},{2,1},{3,0},{4,7},{5,6},{6,5},{7,4},{8,11},{9,10},{10,... | collective-permute-start | bytes 196616 | tf_op jit(solution)/shard_map/ppermute | solution.py:29
  38.6 1.4 %collective-permute-start.8 = (f32[128,128]{1,0:T(8,128)S(1)}, f32[128,128]{1,0:T(8,128)S(1)}, u32[]{:S(2)}, u32[]{:S(2)}) collective-permute-start(f32[128,128]{1,0:T(8,128)S(1)} %fusion.13), channel_id=1, source_target_pairs={{0,2},{1,3},{2,0},{3,1},{4,6},{5,7},{6,4},{7,5},{8,10},{9,11},{10,... | collective-permute-start | bytes 196616 | tf_op jit(solution)/shard_map/ppermute | solution.py:29
  40.0 0.6 collective-permute-start.7
  40.6 2.3 %collective-permute-done.9 = f32[128,128]{1,0:T(8,128)S(1)} collective-permute-done((f32[128,128]{1,0:T(8,128)S(1)}, f32[128,128]{1,0:T(8,128)S(1)}, u32[]{:S(2)}, u32[]{:S(2)}) %collective-permute-start.9) | collective-permute-done | bytes 65568 | tf_op jit(solution)/shard_map/ppermute | solution.py:29
  43.0 0.3 collective-permute-done.8
  43.3 1.0 collective-permute-done.7
  44.4 0.1 collective-permute-start.10
  44.5 1.5 %collective-permute-done.10 = f32[4,128,128]{2,1,0:T(8,128)S(1)} collective-permute-done((f32[4,128,128]{2,1,0:T(8,128)S(1)}, f32[4,128,128]{2,1,0:T(8,128)S(1)}, u32[]{:S(2)}, u32[]{:S(2)}) %collective-permute-start.10) | collective-permute-done | bytes 262176 | tf_op jit(solution)/shard_map/ppermute | solution.py:29
  46.0 0.1 fusion.9
  46.2 1.1 copy.16
  47.3 4.0 %all-to-all-start = ((f32[32,32,128]{2,1,0:T(8,128)}), f32[32,32,128]{2,1,0:T(8,128)S(1)}, u32[]{:S(2)}, u32[]{:S(2)}) async-start(f32[32,32,128]{2,1,0:T(8,128)} %copy.16), calls=%async_computation | async-start | bytes 1048576 | tf_op jit(solution)/shard_map/all_to_all | solution.py:19
  51.3 13.0 %turn.3 = (f32[128,2048]{1,0:T(8,128)S(1)}, f32[8,136,128]{2,1,0:T(8,128)S(1)}) custom-call(f32[1024,2048]{1,0:T(8,128)} %slab_ref.3, f32[1024,128]{1,0:T(8,128)S(1)} %bitcast.84, f32[128,2048]{1,0:T(8,128)} %get-tuple-element.11.right_ref, f32[1,128]{1,0:T(1,128)S(1)} %bitcast.88), custom_call_target="tpu_custom_call" | custom-call | flops 6442450944 | bytes 8388608 | tf_op jit(solution)/shard_map/turn/pallas_call | solution.py:255
  64.3 3.2 %all-to-all-done = f32[32,32,128]{2,1,0:T(8,128)S(1)} async-done(((f32[32,32,128]{2,1,0:T(8,128)}), f32[32,32,128]{2,1,0:T(8,128)S(1)}, u32[]{:S(2)}, u32[]{:S(2)}) %all-to-all-start) | async-done | bytes 524320 | tf_op jit(solution)/shard_map/all_to_all | solution.py:19
  67.6 1.6 %second_numerator.1 = f32[4,128,128]{2,1,0:T(8,128)S(1)} custom-call(f32[128,2048]{1,0:T(8,128)S(1)} %get-tuple-element.13.right_ref, f32[512,128]{1,0:T(8,128)S(1)} %bitcast.76, f32[4,128,128]{2,1,0:T(8,128)S(1)} %bitcast.78), custom_call_target="tpu_custom_call" | custom-call | flops 402653184 | bytes 1048576 | tf_op jit(solution)/shard_map/second_numerator/pallas_call | solution.py:274
  69.3 0.1 collective-permute-start.11
  69.3 1.7 %collective-permute-done.11 = f32[4,200,128]{2,1,0:T(8,128)S(1)} collective-permute-done((f32[4,200,128]{2,1,0:T(8,128)S(1)}, f32[4,200,128]{2,1,0:T(8,128)S(1)}, u32[]{:S(2)}, u32[]{:S(2)}) %collective-permute-start.11) | collective-permute-done | bytes 409632 | tf_op jit(solution)/shard_map/ppermute | solution.py:29
  71.2 1.2 %collective-permute-start.14 = (f32[200,128]{1,0:T(8,128)S(1)}, f32[200,128]{1,0:T(8,128)S(1)}, u32[]{:S(2)}, u32[]{:S(2)}) collective-permute-start(f32[200,128]{1,0:T(8,128)S(1)} %get-tuple-element.24), channel_id=1, source_target_pairs={{0,3},{1,2},{2,1},{3,0},{4,7},{5,6},{6,5},{7,4},{8,11},{9,10},{10,... | collective-permute-start | bytes 307208 | tf_op jit(solution)/shard_map/ppermute | solution.py:29
  72.4 0.5 collective-permute-start.13
  72.9 1.8 %collective-permute-start.12 = (f32[200,128]{1,0:T(8,128)S(1)}, f32[200,128]{1,0:T(8,128)S(1)}, u32[]{:S(2)}, u32[]{:S(2)}) collective-permute-start(f32[200,128]{1,0:T(8,128)S(1)} %get-tuple-element.26), channel_id=1, source_target_pairs={{0,1},{1,0},{2,3},{3,2},{4,5},{5,4},{6,7},{7,6},{8,9},{9,8},{10,11... | collective-permute-start | bytes 307208 | tf_op jit(solution)/shard_map/ppermute | solution.py:29
  74.7 3.2 %collective-permute-done.14 = f32[200,128]{1,0:T(8,128)S(1)} collective-permute-done((f32[200,128]{1,0:T(8,128)S(1)}, f32[200,128]{1,0:T(8,128)S(1)}, u32[]{:S(2)}, u32[]{:S(2)}) %collective-permute-start.14) | collective-permute-done | bytes 102432 | tf_op jit(solution)/shard_map/ppermute | solution.py:29
  77.9 1.3 %collective-permute-done.13 = f32[200,128]{1,0:T(8,128)S(1)} collective-permute-done((f32[200,128]{1,0:T(8,128)S(1)}, f32[200,128]{1,0:T(8,128)S(1)}, u32[]{:S(2)}, u32[]{:S(2)}) %collective-permute-start.13) | collective-permute-done | bytes 102432 | tf_op jit(solution)/shard_map/ppermute | solution.py:29
  79.2 0.0 collective-permute-done.12
  79.2 1.6 %collective-permute-start.17 = (f32[200,128]{1,0:T(8,128)S(1)}, f32[200,128]{1,0:T(8,128)S(1)}, u32[]{:S(2)}, u32[]{:S(2)}) collective-permute-start(f32[200,128]{1,0:T(8,128)S(1)} %fusion.10), channel_id=1, source_target_pairs={{0,24},{1,25},{2,26},{3,27},{4,28},{5,29},{6,30},{7,31},{8,16},{9,... | collective-permute-start | bytes 307208 | tf_op jit(solution)/shard_map/ppermute | solution.py:29
  80.8 0.1 collective-permute-start.16
  81.0 2.7 %collective-permute-start.15 = (f32[200,128]{1,0:T(8,128)S(1)}, f32[200,128]{1,0:T(8,128)S(1)}, u32[]{:S(2)}, u32[]{:S(2)}) collective-permute-start(f32[200,128]{1,0:T(8,128)S(1)} %fusion.10), channel_id=1, source_target_pairs={{0,8},{1,9},{2,10},{3,11},{4,12},{5,13},{6,14},{7,15},{8,0},{9,1},... | collective-permute-start | bytes 307208 | tf_op jit(solution)/shard_map/ppermute | solution.py:29
  83.7 3.3 %collective-permute-done.17 = f32[200,128]{1,0:T(8,128)S(1)} collective-permute-done((f32[200,128]{1,0:T(8,128)S(1)}, f32[200,128]{1,0:T(8,128)S(1)}, u32[]{:S(2)}, u32[]{:S(2)}) %collective-permute-start.17) | collective-permute-done | bytes 102432 | tf_op jit(solution)/shard_map/ppermute | solution.py:29
  87.0 3.3 %collective-permute-done.16 = f32[200,128]{1,0:T(8,128)S(1)} collective-permute-done((f32[200,128]{1,0:T(8,128)S(1)}, f32[200,128]{1,0:T(8,128)S(1)}, u32[]{:S(2)}, u32[]{:S(2)}) %collective-permute-start.16) | collective-permute-done | bytes 102432 | tf_op jit(solution)/shard_map/ppermute | solution.py:29
  90.3 0.0 collective-permute-done.15
  90.3 0.1 broadcast_divide_fusion
  90.5 1.4 %collective-permute-start.19 = (f32[192,128]{1,0:T(8,128)S(1)}, f32[192,128]{1,0:T(8,128)S(1)}, u32[]{:S(2)}, u32[]{:S(2)}) collective-permute-start(f32[192,128]{1,0:T(8,128)S(1)} %get-tuple-element.45), channel_id=1, source_target_pairs={{0,2},{1,3},{2,0},{3,1},{4,6},{5,7},{6,4},{7,5},{8,10},{9,11},{10,... | collective-permute-start | bytes 294920 | tf_op jit(solution)/shard_map/ppermute | solution.py:29
  91.9 0.4 collective-permute-start.18
  92.3 1.7 %collective-permute-start.20 = (f32[192,128]{1,0:T(8,128)S(1)}, f32[192,128]{1,0:T(8,128)S(1)}, u32[]{:S(2)}, u32[]{:S(2)}) collective-permute-start(f32[192,128]{1,0:T(8,128)S(1)} %get-tuple-element.45), channel_id=1, source_target_pairs={{0,3},{1,2},{2,1},{3,0},{4,7},{5,6},{6,5},{7,4},{8,11},{9,10},{10,... | collective-permute-start | bytes 294920 | tf_op jit(solution)/shard_map/ppermute | solution.py:29
  94.0 1.2 %collective-permute-done.19 = f32[192,128]{1,0:T(8,128)S(1)} collective-permute-done((f32[192,128]{1,0:T(8,128)S(1)}, f32[192,128]{1,0:T(8,128)S(1)}, u32[]{:S(2)}, u32[]{:S(2)}) %collective-permute-start.19) | collective-permute-done | bytes 98336 | tf_op jit(solution)/shard_map/ppermute | solution.py:29
  95.3 1.4 %collective-permute-done.18 = f32[192,128]{1,0:T(8,128)S(1)} collective-permute-done((f32[192,128]{1,0:T(8,128)S(1)}, f32[192,128]{1,0:T(8,128)S(1)}, u32[]{:S(2)}, u32[]{:S(2)}) %collective-permute-start.18) | collective-permute-done | bytes 98336 | tf_op jit(solution)/shard_map/ppermute | solution.py:29
  96.7 1.9 %collective-permute-done.20 = f32[192,128]{1,0:T(8,128)S(1)} collective-permute-done((f32[192,128]{1,0:T(8,128)S(1)}, f32[192,128]{1,0:T(8,128)S(1)}, u32[]{:S(2)}, u32[]{:S(2)}) %collective-permute-start.20) | collective-permute-done | bytes 98336 | tf_op jit(solution)/shard_map/ppermute | solution.py:29
  98.6 0.1 pad_maximum_fusion.3
  98.7 0.1 collective-permute-start.21
  98.8 1.7 %collective-permute-done.21 = f32[4,192,128]{2,1,0:T(8,128)S(1)} collective-permute-done((f32[4,192,128]{2,1,0:T(8,128)S(1)}, f32[4,192,128]{2,1,0:T(8,128)S(1)}, u32[]{:S(2)}, u32[]{:S(2)}) %collective-permute-start.21) | collective-permute-done | bytes 393248 | tf_op jit(solution)/shard_map/ppermute | solution.py:29
  100.5 0.2 fusion.6
  100.7 2.2 %second_rows.1 = f32[512,128]{1,0:T(8,128)} custom-call(f32[128,2048]{1,0:T(8,128)S(1)} %get-tuple-element.13.right_ref, f32[512,128]{1,0:T(8,128)S(1)} %bitcast.77, f32[4,128,128]{2,1,0:T(8,128)S(1)} %bitcast.83), custom_call_target="tpu_custom_call" | custom-call | flops 402653184 | bytes 1048576 | tf_op jit(solution)/shard_map/second_rows/pallas_call | solution.py:284
  102.9 2.9 %all-to-all-start.1 = ((f32[32,16,128]{2,1,0:T(8,128)}), f32[32,16,128]{2,1,0:T(8,128)S(1)}, u32[]{:S(2)}, u32[]{:S(2)}) async-start(f32[32,16,128]{2,1,0:T(8,128)} %bitcast.45), calls=%async_computation.1 | async-start | bytes 524288 | tf_op jit(solution)/shard_map/all_to_all | solution.py:19
  105.7 0.8 fusion
  106.6 10.1 %all-to-all-done.1 = f32[32,16,128]{2,1,0:T(8,128)S(1)} async-done(((f32[32,16,128]{2,1,0:T(8,128)}), f32[32,16,128]{2,1,0:T(8,128)S(1)}, u32[]{:S(2)}, u32[]{:S(2)}) %all-to-all-start.1) | async-done | bytes 262176 | tf_op jit(solution)/shard_map/all_to_all | solution.py:19
  116.7 0.7 copy.18
  (29 shorter events, 0.7 us)
Async XLA Ops:
  0.6 1.1 copy-start
  1.8 1.0 copy-start.1
  16.5 1.7 %collective-permute-start = (f32[4,136,128]{2,1,0:T(8,128)S(1)}, f32[4,136,128]{2,1,0:T(8,128)S(1)}, u32[]{:S(2)}, u32[]{:S(2)}) collective-permute-start(f32[4,136,128]{2,1,0:T(8,128)S(1)} %dynamic-slice_bitcast_fusion), channel_id=1, source_target_pairs={{0,4},{1,5},{2,6},{3,7},{4,0},{5,1},{6,2},{7,3},{8,12},{9,13},{10,... | collective-permute-start | bytes 835592 | tf_op jit(solution)/shard_map/ppermute | solution.py:29
  18.3 6.4 %collective-permute-start.3 = (f32[136,128]{1,0:T(8,128)S(1)}, f32[136,128]{1,0:T(8,128)S(1)}, u32[]{:S(2)}, u32[]{:S(2)}) collective-permute-start(f32[136,128]{1,0:T(8,128)S(1)} %get-tuple-element.33), channel_id=1, source_target_pairs={{0,3},{1,2},{2,1},{3,0},{4,7},{5,6},{6,5},{7,4},{8,11},{9,10},{10,... | collective-permute-start | bytes 208904 | tf_op jit(solution)/shard_map/ppermute | solution.py:29
  22.2 4.3 %collective-permute-start.2 = (f32[136,128]{1,0:T(8,128)S(1)}, f32[136,128]{1,0:T(8,128)S(1)}, u32[]{:S(2)}, u32[]{:S(2)}) collective-permute-start(f32[136,128]{1,0:T(8,128)S(1)} %get-tuple-element.34), channel_id=1, source_target_pairs={{0,2},{1,3},{2,0},{3,1},{4,6},{5,7},{6,4},{7,5},{8,10},{9,11},{10,... | collective-permute-start | bytes 208904 | tf_op jit(solution)/shard_map/ppermute | solution.py:29
  22.7 4.3 %collective-permute-start.1 = (f32[136,128]{1,0:T(8,128)S(1)}, f32[136,128]{1,0:T(8,128)S(1)}, u32[]{:S(2)}, u32[]{:S(2)}) collective-permute-start(f32[136,128]{1,0:T(8,128)S(1)} %get-tuple-element.35), channel_id=1, source_target_pairs={{0,1},{1,0},{2,3},{3,2},{4,5},{5,4},{6,7},{7,6},{8,9},{9,8},{10,11... | collective-permute-start | bytes 208904 | tf_op jit(solution)/shard_map/ppermute | solution.py:29
  27.0 6.4 %collective-permute-start.6 = (f32[136,128]{1,0:T(8,128)S(1)}, f32[136,128]{1,0:T(8,128)S(1)}, u32[]{:S(2)}, u32[]{:S(2)}) collective-permute-start(f32[136,128]{1,0:T(8,128)S(1)} %fusion.11), channel_id=1, source_target_pairs={{0,24},{1,25},{2,26},{3,27},{4,28},{5,29},{6,30},{7,31},{8,16},{9,... | collective-permute-start | bytes 208904 | tf_op jit(solution)/shard_map/ppermute | solution.py:29
  30.7 5.5 %collective-permute-start.5 = (f32[136,128]{1,0:T(8,128)S(1)}, f32[136,128]{1,0:T(8,128)S(1)}, u32[]{:S(2)}, u32[]{:S(2)}) collective-permute-start(f32[136,128]{1,0:T(8,128)S(1)} %fusion.11), channel_id=1, source_target_pairs={{0,16},{1,17},{2,18},{3,19},{4,20},{5,21},{6,22},{7,23},{8,24},{9,... | collective-permute-start | bytes 208904 | tf_op jit(solution)/shard_map/ppermute | solution.py:29
  30.7 5.5 %collective-permute-start.4 = (f32[136,128]{1,0:T(8,128)S(1)}, f32[136,128]{1,0:T(8,128)S(1)}, u32[]{:S(2)}, u32[]{:S(2)}) collective-permute-start(f32[136,128]{1,0:T(8,128)S(1)} %fusion.11), channel_id=1, source_target_pairs={{0,8},{1,9},{2,10},{3,11},{4,12},{5,13},{6,14},{7,15},{8,0},{9,1},... | collective-permute-start | bytes 208904 | tf_op jit(solution)/shard_map/ppermute | solution.py:29
  37.1 5.9 %collective-permute-start.9 = (f32[128,128]{1,0:T(8,128)S(1)}, f32[128,128]{1,0:T(8,128)S(1)}, u32[]{:S(2)}, u32[]{:S(2)}) collective-permute-start(f32[128,128]{1,0:T(8,128)S(1)} %fusion.13), channel_id=1, source_target_pairs={{0,3},{1,2},{2,1},{3,0},{4,7},{5,6},{6,5},{7,4},{8,11},{9,10},{10,... | collective-permute-start | bytes 196616 | tf_op jit(solution)/shard_map/ppermute | solution.py:29
  38.6 4.7 %collective-permute-start.8 = (f32[128,128]{1,0:T(8,128)S(1)}, f32[128,128]{1,0:T(8,128)S(1)}, u32[]{:S(2)}, u32[]{:S(2)}) collective-permute-start(f32[128,128]{1,0:T(8,128)S(1)} %fusion.13), channel_id=1, source_target_pairs={{0,2},{1,3},{2,0},{3,1},{4,6},{5,7},{6,4},{7,5},{8,10},{9,11},{10,... | collective-permute-start | bytes 196616 | tf_op jit(solution)/shard_map/ppermute | solution.py:29
  40.0 4.3 %collective-permute-start.7 = (f32[128,128]{1,0:T(8,128)S(1)}, f32[128,128]{1,0:T(8,128)S(1)}, u32[]{:S(2)}, u32[]{:S(2)}) collective-permute-start(f32[128,128]{1,0:T(8,128)S(1)} %fusion.13), channel_id=1, source_target_pairs={{0,1},{1,0},{2,3},{3,2},{4,5},{5,4},{6,7},{7,6},{8,9},{9,8},{10,11... | collective-permute-start | bytes 196616 | tf_op jit(solution)/shard_map/ppermute | solution.py:29
  44.4 1.6 %collective-permute-start.10 = (f32[4,128,128]{2,1,0:T(8,128)S(1)}, f32[4,128,128]{2,1,0:T(8,128)S(1)}, u32[]{:S(2)}, u32[]{:S(2)}) collective-permute-start(f32[4,128,128]{2,1,0:T(8,128)S(1)} %get-tuple-element.36), channel_id=1, source_target_pairs={{0,4},{1,5},{2,6},{3,7},{4,0},{5,1},{6,2},{7,3},{8,12},{9,13},{10,... | collective-permute-start | bytes 786440 | tf_op jit(solution)/shard_map/ppermute | solution.py:29
  47.3 20.3 %all-to-all-start = ((f32[32,32,128]{2,1,0:T(8,128)}), f32[32,32,128]{2,1,0:T(8,128)S(1)}, u32[]{:S(2)}, u32[]{:S(2)}) async-start(f32[32,32,128]{2,1,0:T(8,128)} %copy.16), calls=%async_computation | async-start | bytes 1048576 | tf_op jit(solution)/shard_map/all_to_all | solution.py:19
  69.3 1.8 %collective-permute-start.11 = (f32[4,200,128]{2,1,0:T(8,128)S(1)}, f32[4,200,128]{2,1,0:T(8,128)S(1)}, u32[]{:S(2)}, u32[]{:S(2)}) collective-permute-start(f32[4,200,128]{2,1,0:T(8,128)S(1)} %fusion.2), channel_id=1, source_target_pairs={{0,4},{1,5},{2,6},{3,7},{4,0},{5,1},{6,2},{7,3},{8,12},{9,13},{10,... | collective-permute-start | bytes 1228808 | tf_op jit(solution)/shard_map/ppermute | solution.py:29
  71.2 6.7 %collective-permute-start.14 = (f32[200,128]{1,0:T(8,128)S(1)}, f32[200,128]{1,0:T(8,128)S(1)}, u32[]{:S(2)}, u32[]{:S(2)}) collective-permute-start(f32[200,128]{1,0:T(8,128)S(1)} %get-tuple-element.24), channel_id=1, source_target_pairs={{0,3},{1,2},{2,1},{3,0},{4,7},{5,6},{6,5},{7,4},{8,11},{9,10},{10,... | collective-permute-start | bytes 307208 | tf_op jit(solution)/shard_map/ppermute | solution.py:29
  72.4 6.8 %collective-permute-start.13 = (f32[200,128]{1,0:T(8,128)S(1)}, f32[200,128]{1,0:T(8,128)S(1)}, u32[]{:S(2)}, u32[]{:S(2)}) collective-permute-start(f32[200,128]{1,0:T(8,128)S(1)} %get-tuple-element.25), channel_id=1, source_target_pairs={{0,2},{1,3},{2,0},{3,1},{4,6},{5,7},{6,4},{7,5},{8,10},{9,11},{10,... | collective-permute-start | bytes 307208 | tf_op jit(solution)/shard_map/ppermute | solution.py:29
  72.9 6.3 %collective-permute-start.12 = (f32[200,128]{1,0:T(8,128)S(1)}, f32[200,128]{1,0:T(8,128)S(1)}, u32[]{:S(2)}, u32[]{:S(2)}) collective-permute-start(f32[200,128]{1,0:T(8,128)S(1)} %get-tuple-element.26), channel_id=1, source_target_pairs={{0,1},{1,0},{2,3},{3,2},{4,5},{5,4},{6,7},{7,6},{8,9},{9,8},{10,11... | collective-permute-start | bytes 307208 | tf_op jit(solution)/shard_map/ppermute | solution.py:29
  79.2 7.7 %collective-permute-start.17 = (f32[200,128]{1,0:T(8,128)S(1)}, f32[200,128]{1,0:T(8,128)S(1)}, u32[]{:S(2)}, u32[]{:S(2)}) collective-permute-start(f32[200,128]{1,0:T(8,128)S(1)} %fusion.10), channel_id=1, source_target_pairs={{0,24},{1,25},{2,26},{3,27},{4,28},{5,29},{6,30},{7,31},{8,16},{9,... | collective-permute-start | bytes 307208 | tf_op jit(solution)/shard_map/ppermute | solution.py:29
  80.8 9.4 %collective-permute-start.16 = (f32[200,128]{1,0:T(8,128)S(1)}, f32[200,128]{1,0:T(8,128)S(1)}, u32[]{:S(2)}, u32[]{:S(2)}) collective-permute-start(f32[200,128]{1,0:T(8,128)S(1)} %fusion.10), channel_id=1, source_target_pairs={{0,16},{1,17},{2,18},{3,19},{4,20},{5,21},{6,22},{7,23},{8,24},{9,... | collective-permute-start | bytes 307208 | tf_op jit(solution)/shard_map/ppermute | solution.py:29
  81.0 9.3 %collective-permute-start.15 = (f32[200,128]{1,0:T(8,128)S(1)}, f32[200,128]{1,0:T(8,128)S(1)}, u32[]{:S(2)}, u32[]{:S(2)}) collective-permute-start(f32[200,128]{1,0:T(8,128)S(1)} %fusion.10), channel_id=1, source_target_pairs={{0,8},{1,9},{2,10},{3,11},{4,12},{5,13},{6,14},{7,15},{8,0},{9,1},... | collective-permute-start | bytes 307208 | tf_op jit(solution)/shard_map/ppermute | solution.py:29
  90.5 4.8 %collective-permute-start.19 = (f32[192,128]{1,0:T(8,128)S(1)}, f32[192,128]{1,0:T(8,128)S(1)}, u32[]{:S(2)}, u32[]{:S(2)}) collective-permute-start(f32[192,128]{1,0:T(8,128)S(1)} %get-tuple-element.45), channel_id=1, source_target_pairs={{0,2},{1,3},{2,0},{3,1},{4,6},{5,7},{6,4},{7,5},{8,10},{9,11},{10,... | collective-permute-start | bytes 294920 | tf_op jit(solution)/shard_map/ppermute | solution.py:29
  91.9 4.8 %collective-permute-start.18 = (f32[192,128]{1,0:T(8,128)S(1)}, f32[192,128]{1,0:T(8,128)S(1)}, u32[]{:S(2)}, u32[]{:S(2)}) collective-permute-start(f32[192,128]{1,0:T(8,128)S(1)} %get-tuple-element.45), channel_id=1, source_target_pairs={{0,1},{1,0},{2,3},{3,2},{4,5},{5,4},{6,7},{7,6},{8,9},{9,8},{10,11... | collective-permute-start | bytes 294920 | tf_op jit(solution)/shard_map/ppermute | solution.py:29
  92.3 6.2 %collective-permute-start.20 = (f32[192,128]{1,0:T(8,128)S(1)}, f32[192,128]{1,0:T(8,128)S(1)}, u32[]{:S(2)}, u32[]{:S(2)}) collective-permute-start(f32[192,128]{1,0:T(8,128)S(1)} %get-tuple-element.45), channel_id=1, source_target_pairs={{0,3},{1,2},{2,1},{3,0},{4,7},{5,6},{6,5},{7,4},{8,11},{9,10},{10,... | collective-permute-start | bytes 294920 | tf_op jit(solution)/shard_map/ppermute | solution.py:29
  98.7 1.8 %collective-permute-start.21 = (f32[4,192,128]{2,1,0:T(8,128)S(1)}, f32[4,192,128]{2,1,0:T(8,128)S(1)}, u32[]{:S(2)}, u32[]{:S(2)}) collective-permute-start(f32[4,192,128]{2,1,0:T(8,128)S(1)} %get-tuple-element.27), channel_id=1, source_target_pairs={{0,4},{1,5},{2,6},{3,7},{4,0},{5,1},{6,2},{7,3},{8,12},{9,13},{10,... | collective-permute-start | bytes 1179656 | tf_op jit(solution)/shard_map/ppermute | solution.py:29
  102.9 13.8 %all-to-all-start.1 = ((f32[32,16,128]{2,1,0:T(8,128)}), f32[32,16,128]{2,1,0:T(8,128)S(1)}, u32[]{:S(2)}, u32[]{:S(2)}) async-start(f32[32,16,128]{2,1,0:T(8,128)} %bitcast.45), calls=%async_computation.1 | async-start | bytes 524288 | tf_op jit(solution)/shard_map/all_to_all | solution.py:19

commit v7 on v6

--- a/solution.py
+++ b/solution.py
@@ -10,8 +10,9 @@
 AXES = ("row", "col")
 F32, BF16 = jnp.float32, jnp.bfloat16
 PAD = 8
-ROWS = 256
+ROWS = 128
 MIB = 1024 * 1024
+T1_MIB = 52
 VMEM_BYTES = 51 * MIB
 
 
@@ -307,29 +308,30 @@
         second_left_init, lax.axis_index("col") * second_rows, second_rows, 0
     )
     col_part = jnp.sum(own_left, axis=0)[None]
-    own_left = own_left.reshape(per_owner, devices, slices, rank).transpose(1, 0, 2, 3)
-    own_left = own_left.reshape(devices, per_owner * slices, rank)
+    own_left = own_left.reshape(per_owner, devices, slices, rank)
     piece_rows = rank // row_devices
     piece = lax.dynamic_slice_in_dim(
         second_right_init, lax.axis_index("row") * piece_rows, piece_rows, 0
     ).reshape(-1, rank)
     piece = jnp.broadcast_to(piece[None], (devices,) + piece.shape)
-    second_factors = jnp.concatenate([own_left, piece], axis=1)
-
-    def own_left_rows(left, total):
-        own = lax.dynamic_slice_in_dim(left, own_part * rows_own, rows_own, 0)
+    second_factors = [own_left[index] for index in range(per_owner)] + [piece]
+    arrived = exchange(jnp.concatenate(second_factors, axis=1))
+
+    def own_rows(left):
+        return lax.dynamic_slice_in_dim(left, own_part * rows_own, rows_own, 0)
+
+    def own_left_rows(own, total):
         return own * total[:rows_own] / total[rows_own][None, :]
 
+    own_init = own_rows(left_init)
     right, summed = full_turn(
-        tensor_slab, after(left_init, second_factors), right_init, left_init, k, parts, 52 * MIB
-    )
+        tensor_slab, after(left_init, own_init), right_init, left_init, k, parts, T1_MIB * MIB
+    )
+    summed, arrived = lax.optimization_barrier((summed, arrived))
     summed = summed.reshape(2, col_devices, rows_own + PAD, rank)
     total = reduce_z(reduce_plane(reduce_core(summed)))
-    left = spread_core(spread_plane(own_left_rows(left_init, total))).reshape(m, rank)
-
-    arrived = exchange(after(second_factors, left))
+    left = spread_core(spread_plane(own_left_rows(own_init, total))).reshape(m, rank)
     right, summed = full_turn(tensor_slab, left, right, col_part, k, parts, VMEM_BYTES)
-    arrived = after(arrived, summed)
     second_left = arrived[:, : per_owner * slices].reshape(rank * slices, rank)
     whole = arrived[:, per_owner * slices :].reshape(row_devices, col_devices, piece_rows, -1)
     whole = whole.transpose(0, 2, 1, 3).reshape(rank, k // rank, rank).transpose(1, 0, 2)
@@ -343,7 +345,7 @@
     init_over = lax.dynamic_slice_in_dim(init_over, own_part * rows_part, rows_part, 0)
     second_part = init_over * total[rows_own + PAD :]
     both = spread_core(
-        spread_plane(jnp.concatenate([own_left_rows(left, total), second_part], axis=0))
+        spread_plane(jnp.concatenate([own_left_rows(own_rows(left), total), second_part], axis=0))
     )
     left_out = both[:, :, :rows_own].reshape(m, rank)
     second_right = both[:, :, rows_own:].reshape(k // rank, rank, rank)

time: 118 us -> 125 us (1.059)
  Pallas kernels: 30.4 us -> 35.7 us
  waiting for transfers between devices: 47.6 us -> 43.6 us
  local copies, waits for them, and re-layouts: 3.15 us -> 5.92 us
  starting transfers between devices: 31.8 us -> 34.5 us
    pallas_call x2, Pallas kernels: 26.7 us -> 32 us  [full_turn(): pl.pallas_call(turn_kernel, grid=(columns // block,), in_specs=[columns_s...]
    all_to_all x2, starting transfers between devices: 6.93 us -> 10.8 us  [exchange(): return lax.all_to_all(parts, AXES, split_axis=0, concat_axis=0, tiled=True)]
    all_to_all x2, waiting for transfers between devices: 13.3 us -> 10.1 us  [exchange(): return lax.all_to_all(parts, AXES, split_axis=0, concat_axis=0, tiled=True)]
    concatenate x0 -> x1, local copies, waits for them, and re-layouts: none -> 2.13 us  [body(): arrived = exchange(jnp.concatenate(second_factors, axis=1))]
  transfers between devices with their start and end apart: 24 -> 24, of which waited for: 21 -> 20; matrix products, arithmetic and copies ran while one was open for 1% -> 2% of each run, Pallas kernels for 11% -> 13%
where the time goes in v7:
time: 125 us; the launch traced here: 124 us
  waiting for transfers between devices  43.6 us (35%)
  Pallas kernels  35.7 us (29%)
  starting transfers between devices  34.5 us (28%)
  local copies, waits for them, and re-layouts  5.92 us (5%)
  other arithmetic  3.52 us (3%)
    ppermute x22, waiting for transfers between devices, send(): return lax.ppermute(values, AXES, pairs)  33.5 us
    pallas_call x2, Pallas kernels, full_turn(): pl.pallas_call(turn_kernel, grid=(columns // block,), in_specs=[columns_s...  32 us
    ppermute x22, starting transfers between devices, send(): return lax.ppermute(values, AXES, pairs)  23.8 us
    all_to_all x2, starting transfers between devices, exchange(): return lax.all_to_all(parts, AXES, split_axis=0, concat_axis=0, tiled=True)  10.8 us
    all_to_all x2, waiting for transfers between devices, exchange(): return lax.all_to_all(parts, AXES, split_axis=0, concat_axis=0, tiled=True)  10.1 us
  transfers between devices with their start and end apart: 24, of which 20 were waited for; matrix products, arithmetic and copies ran while one was open for 2% of the time, Pallas kernels for 13%

profile of v7, /device:TPU:0, one launch (start us, length us, event | category | flops | bytes accessed | tf_op | source)
XLA Modules:
  0.0 124.3 jit_solution(14692519820350360040)
XLA Ops:
  0.6 0.0 copy-start
  0.7 0.8 copy-done
  1.5 1.0 constant_dynamic-slice_fusion
  2.5 2.1 %concatenate.9 = f32[32,32,128]{2,1,0:T(8,128)} concatenate(f32[32,4,128]{2,1,0:T(4,128)S(1)} %bitcast.100, f32[32,4,128]{2,1,0:T(4,128)S(1)} %bitcast.99, f32[32,4,128]{2,1,0:T(4,128)S(1)} %bitcast.98, f32[32,4,128]{2,1,0:T(4,128)S(1)} %bitcast.97, f32[32,16,128]{2,1,0:T(8,128)S(1)} %broadcast_in_dim.4), dimensions={1} | concatenate | bytes 1048576 | tf_op jit(solution)/shard_map/concatenate | solution.py:318
  4.6 7.3 %all-to-all-start = ((f32[32,32,128]{2,1,0:T(8,128)}), f32[32,32,128]{2,1,0:T(8,128)S(1)}, u32[]{:S(2)}, u32[]{:S(2)}) async-start(f32[32,32,128]{2,1,0:T(8,128)} %concatenate.9), calls=%async_computation | async-start | bytes 1048576 | tf_op jit(solution)/shard_map/all_to_all | solution.py:20
  11.9 0.0 copy-start.1
  11.9 1.0 copy-done.1
  13.0 16.3 %turn.2 = (f32[128,2048]{1,0:T(8,128)}, f32[8,136,128]{2,1,0:T(8,128)S(1)}) custom-call(f32[1024,2048]{1,0:T(8,128)} %slab_ref.3, f32[1024,128]{1,0:T(8,128)S(1)} %copy-done.1, f32[128,2048]{1,0:T(8,128)} %right_ref.1, f32[1024,128]{1,0:T(8,128)S(1)} %copy-done.1), custom_call_target="tpu_custom_call" | custom-call | flops 6442450944 | bytes 8388608 | tf_op jit(solution)/shard_map/turn/pallas_call | solution.py:256
  29.3 0.0 all-to-all-done
  29.3 0.3 collective-permute-start
  29.6 1.3 %collective-permute-done = f32[4,136,128]{2,1,0:T(8,128)S(1)} collective-permute-done((f32[4,136,128]{2,1,0:T(8,128)S(1)}, f32[4,136,128]{2,1,0:T(8,128)S(1)}, u32[]{:S(2)}, u32[]{:S(2)}) %collective-permute-start) | collective-permute-done | bytes 278560 | tf_op jit(solution)/shard_map/ppermute | solution.py:30
  31.0 2.7 %collective-permute-start.3 = (f32[136,128]{1,0:T(8,128)S(1)}, f32[136,128]{1,0:T(8,128)S(1)}, u32[]{:S(2)}, u32[]{:S(2)}) collective-permute-start(f32[136,128]{1,0:T(8,128)S(1)} %get-tuple-element.35), channel_id=1, source_target_pairs={{0,3},{1,2},{2,1},{3,0},{4,7},{5,6},{6,5},{7,4},{8,11},{9,10},{10,... | collective-permute-start | bytes 208904 | tf_op jit(solution)/shard_map/ppermute | solution.py:30
  33.7 0.6 collective-permute-start.2
  34.3 0.3 collective-permute-start.1
  34.6 1.7 %collective-permute-done.3 = f32[136,128]{1,0:T(8,128)S(1)} collective-permute-done((f32[136,128]{1,0:T(8,128)S(1)}, f32[136,128]{1,0:T(8,128)S(1)}, u32[]{:S(2)}, u32[]{:S(2)}) %collective-permute-start.3) | collective-permute-done | bytes 69664 | tf_op jit(solution)/shard_map/ppermute | solution.py:30
  36.3 1.7 %collective-permute-done.2 = f32[136,128]{1,0:T(8,128)S(1)} collective-permute-done((f32[136,128]{1,0:T(8,128)S(1)}, f32[136,128]{1,0:T(8,128)S(1)}, u32[]{:S(2)}, u32[]{:S(2)}) %collective-permute-start.2) | collective-permute-done | bytes 69664 | tf_op jit(solution)/shard_map/ppermute | solution.py:30
  38.0 0.6 collective-permute-done.1
  38.6 3.4 %collective-permute-start.6 = (f32[136,128]{1,0:T(8,128)S(1)}, f32[136,128]{1,0:T(8,128)S(1)}, u32[]{:S(2)}, u32[]{:S(2)}) collective-permute-start(f32[136,128]{1,0:T(8,128)S(1)} %fusion.11), channel_id=1, source_target_pairs={{0,24},{1,25},{2,26},{3,27},{4,28},{5,29},{6,30},{7,31},{8,16},{9,... | collective-permute-start | bytes 208904 | tf_op jit(solution)/shard_map/ppermute | solution.py:30
  42.0 1.1 collective-permute-start.4
  43.1 1.7 %collective-permute-done.6 = f32[136,128]{1,0:T(8,128)S(1)} collective-permute-done((f32[136,128]{1,0:T(8,128)S(1)}, f32[136,128]{1,0:T(8,128)S(1)}, u32[]{:S(2)}, u32[]{:S(2)}) %collective-permute-start.6) | collective-permute-done | bytes 69664 | tf_op jit(solution)/shard_map/ppermute | solution.py:30
  44.8 2.8 %collective-permute-done.5 = f32[136,128]{1,0:T(8,128)S(1)} collective-permute-done((f32[136,128]{1,0:T(8,128)S(1)}, f32[136,128]{1,0:T(8,128)S(1)}, u32[]{:S(2)}, u32[]{:S(2)}) %collective-permute-start.5) | collective-permute-done | bytes 69664 | tf_op jit(solution)/shard_map/ppermute | solution.py:30
  47.6 0.0 collective-permute-done.4
  47.6 0.9 fusion.13
  48.5 1.5 %collective-permute-start.9 = (f32[128,128]{1,0:T(8,128)S(1)}, f32[128,128]{1,0:T(8,128)S(1)}, u32[]{:S(2)}, u32[]{:S(2)}) collective-permute-start(f32[128,128]{1,0:T(8,128)S(1)} %fusion.13), channel_id=1, source_target_pairs={{0,3},{1,2},{2,1},{3,0},{4,7},{5,6},{6,5},{7,4},{8,11},{9,10},{10,... | collective-permute-start | bytes 196616 | tf_op jit(solution)/shard_map/ppermute | solution.py:30
  50.0 1.6 %collective-permute-start.8 = (f32[128,128]{1,0:T(8,128)S(1)}, f32[128,128]{1,0:T(8,128)S(1)}, u32[]{:S(2)}, u32[]{:S(2)}) collective-permute-start(f32[128,128]{1,0:T(8,128)S(1)} %fusion.13), channel_id=1, source_target_pairs={{0,2},{1,3},{2,0},{3,1},{4,6},{5,7},{6,4},{7,5},{8,10},{9,11},{10,... | collective-permute-start | bytes 196616 | tf_op jit(solution)/shard_map/ppermute | solution.py:30
  51.6 0.5 collective-permute-start.7
  52.0 2.4 %collective-permute-done.9 = f32[128,128]{1,0:T(8,128)S(1)} collective-permute-done((f32[128,128]{1,0:T(8,128)S(1)}, f32[128,128]{1,0:T(8,128)S(1)}, u32[]{:S(2)}, u32[]{:S(2)}) %collective-permute-start.9) | collective-permute-done | bytes 65568 | tf_op jit(solution)/shard_map/ppermute | solution.py:30
  54.5 0.2 collective-permute-done.8
  54.7 1.1 collective-permute-done.7
  56.0 0.1 collective-permute-start.10
  56.0 1.0 dynamic-slice_reduce_fusion
  57.1 0.4 collective-permute-done.10
  57.6 0.1 fusion.9
  57.7 15.6 %turn.3 = (f32[128,2048]{1,0:T(8,128)S(1)}, f32[8,136,128]{2,1,0:T(8,128)S(1)}) custom-call(f32[1024,2048]{1,0:T(8,128)} %slab_ref.3, f32[1024,128]{1,0:T(8,128)S(1)} %bitcast.84, f32[128,2048]{1,0:T(8,128)} %get-tuple-element.12.right_ref, f32[1,128]{1,0:T(1,128)S(1)} %bitcast.88), custom_call_target="tpu_custom_call" | custom-call | flops 6442450944 | bytes 8388608 | tf_op jit(solution)/shard_map/turn/pallas_call | solution.py:256
  73.4 1.6 %second_numerator.1 = f32[4,128,128]{2,1,0:T(8,128)S(1)} custom-call(f32[128,2048]{1,0:T(8,128)S(1)} %get-tuple-element.14.right_ref, f32[512,128]{1,0:T(8,128)S(1)} %bitcast.76, f32[4,128,128]{2,1,0:T(8,128)S(1)} %bitcast.78), custom_call_target="tpu_custom_call" | custom-call | flops 402653184 | bytes 1048576 | tf_op jit(solution)/shard_map/second_numerator/pallas_call | solution.py:275
  75.0 0.2 collective-permute-start.11
  75.2 1.6 %collective-permute-done.11 = f32[4,200,128]{2,1,0:T(8,128)S(1)} collective-permute-done((f32[4,200,128]{2,1,0:T(8,128)S(1)}, f32[4,200,128]{2,1,0:T(8,128)S(1)}, u32[]{:S(2)}, u32[]{:S(2)}) %collective-permute-start.11) | collective-permute-done | bytes 409632 | tf_op jit(solution)/shard_map/ppermute | solution.py:30
  76.8 0.1 fusion.5
  76.9 1.6 %collective-permute-start.14 = (f32[200,128]{1,0:T(8,128)S(1)}, f32[200,128]{1,0:T(8,128)S(1)}, u32[]{:S(2)}, u32[]{:S(2)}) collective-permute-start(f32[200,128]{1,0:T(8,128)S(1)} %get-tuple-element.26), channel_id=1, source_target_pairs={{0,3},{1,2},{2,1},{3,0},{4,7},{5,6},{6,5},{7,4},{8,11},{9,10},{10,... | collective-permute-start | bytes 307208 | tf_op jit(solution)/shard_map/ppermute | solution.py:30
  78.5 0.4 collective-permute-start.13
  78.9 1.6 %collective-permute-start.12 = (f32[200,128]{1,0:T(8,128)S(1)}, f32[200,128]{1,0:T(8,128)S(1)}, u32[]{:S(2)}, u32[]{:S(2)}) collective-permute-start(f32[200,128]{1,0:T(8,128)S(1)} %get-tuple-element.28), channel_id=1, source_target_pairs={{0,1},{1,0},{2,3},{3,2},{4,5},{5,4},{6,7},{7,6},{8,9},{9,8},{10,11... | collective-permute-start | bytes 307208 | tf_op jit(solution)/shard_map/ppermute | solution.py:30
  80.5 3.0 %collective-permute-done.14 = f32[200,128]{1,0:T(8,128)S(1)} collective-permute-done((f32[200,128]{1,0:T(8,128)S(1)}, f32[200,128]{1,0:T(8,128)S(1)}, u32[]{:S(2)}, u32[]{:S(2)}) %collective-permute-start.14) | collective-permute-done | bytes 102432 | tf_op jit(solution)/shard_map/ppermute | solution.py:30
  83.5 1.5 %collective-permute-done.13 = f32[200,128]{1,0:T(8,128)S(1)} collective-permute-done((f32[200,128]{1,0:T(8,128)S(1)}, f32[200,128]{1,0:T(8,128)S(1)}, u32[]{:S(2)}, u32[]{:S(2)}) %collective-permute-start.13) | collective-permute-done | bytes 102432 | tf_op jit(solution)/shard_map/ppermute | solution.py:30
  85.0 0.0 collective-permute-done.12
  85.0 2.5 %collective-permute-start.17 = (f32[200,128]{1,0:T(8,128)S(1)}, f32[200,128]{1,0:T(8,128)S(1)}, u32[]{:S(2)}, u32[]{:S(2)}) collective-permute-start(f32[200,128]{1,0:T(8,128)S(1)} %fusion.10), channel_id=1, source_target_pairs={{0,24},{1,25},{2,26},{3,27},{4,28},{5,29},{6,30},{7,31},{8,16},{9,... | collective-permute-start | bytes 307208 | tf_op jit(solution)/shard_map/ppermute | solution.py:30
  87.6 1.9 %collective-permute-start.15 = (f32[200,128]{1,0:T(8,128)S(1)}, f32[200,128]{1,0:T(8,128)S(1)}, u32[]{:S(2)}, u32[]{:S(2)}) collective-permute-start(f32[200,128]{1,0:T(8,128)S(1)} %fusion.10), channel_id=1, source_target_pairs={{0,8},{1,9},{2,10},{3,11},{4,12},{5,13},{6,14},{7,15},{8,0},{9,1},... | collective-permute-start | bytes 307208 | tf_op jit(solution)/shard_map/ppermute | solution.py:30
  89.5 3.3 %collective-permute-done.17 = f32[200,128]{1,0:T(8,128)S(1)} collective-permute-done((f32[200,128]{1,0:T(8,128)S(1)}, f32[200,128]{1,0:T(8,128)S(1)}, u32[]{:S(2)}, u32[]{:S(2)}) %collective-permute-start.17) | collective-permute-done | bytes 102432 | tf_op jit(solution)/shard_map/ppermute | solution.py:30
  92.7 4.0 %collective-permute-done.16 = f32[200,128]{1,0:T(8,128)S(1)} collective-permute-done((f32[200,128]{1,0:T(8,128)S(1)}, f32[200,128]{1,0:T(8,128)S(1)}, u32[]{:S(2)}, u32[]{:S(2)}) %collective-permute-start.16) | collective-permute-done | bytes 102432 | tf_op jit(solution)/shard_map/ppermute | solution.py:30
  96.8 0.1 broadcast_divide_fusion
  96.9 0.5 collective-permute-start.19
  97.4 1.6 %collective-permute-start.18 = (f32[192,128]{1,0:T(8,128)S(1)}, f32[192,128]{1,0:T(8,128)S(1)}, u32[]{:S(2)}, u32[]{:S(2)}) collective-permute-start(f32[192,128]{1,0:T(8,128)S(1)} %get-tuple-element.47), channel_id=1, source_target_pairs={{0,1},{1,0},{2,3},{3,2},{4,5},{5,4},{6,7},{7,6},{8,9},{9,8},{10,11... | collective-permute-start | bytes 294920 | tf_op jit(solution)/shard_map/ppermute | solution.py:30
  99.1 1.4 %collective-permute-start.20 = (f32[192,128]{1,0:T(8,128)S(1)}, f32[192,128]{1,0:T(8,128)S(1)}, u32[]{:S(2)}, u32[]{:S(2)}) collective-permute-start(f32[192,128]{1,0:T(8,128)S(1)} %get-tuple-element.47), channel_id=1, source_target_pairs={{0,3},{1,2},{2,1},{3,0},{4,7},{5,6},{6,5},{7,4},{8,11},{9,10},{10,... | collective-permute-start | bytes 294920 | tf_op jit(solution)/shard_map/ppermute | solution.py:30
  100.5 1.1 collective-permute-done.19
  101.6 1.1 collective-permute-done.18
  102.7 2.1 %collective-permute-done.20 = f32[192,128]{1,0:T(8,128)S(1)} collective-permute-done((f32[192,128]{1,0:T(8,128)S(1)}, f32[192,128]{1,0:T(8,128)S(1)}, u32[]{:S(2)}, u32[]{:S(2)}) %collective-permute-start.20) | collective-permute-done | bytes 98336 | tf_op jit(solution)/shard_map/ppermute | solution.py:30
  104.9 0.1 pad_maximum_fusion.2
  104.9 0.1 collective-permute-start.21
  105.0 1.7 %collective-permute-done.21 = f32[4,192,128]{2,1,0:T(8,128)S(1)} collective-permute-done((f32[4,192,128]{2,1,0:T(8,128)S(1)}, f32[4,192,128]{2,1,0:T(8,128)S(1)}, u32[]{:S(2)}, u32[]{:S(2)}) %collective-permute-start.21) | collective-permute-done | bytes 393248 | tf_op jit(solution)/shard_map/ppermute | solution.py:30
  106.7 0.2 fusion.6
  106.9 2.2 %second_rows.1 = f32[512,128]{1,0:T(8,128)} custom-call(f32[128,2048]{1,0:T(8,128)S(1)} %get-tuple-element.14.right_ref, f32[512,128]{1,0:T(8,128)S(1)} %bitcast.77, f32[4,128,128]{2,1,0:T(8,128)S(1)} %bitcast.83), custom_call_target="tpu_custom_call" | custom-call | flops 402653184 | bytes 1048576 | tf_op jit(solution)/shard_map/second_rows/pallas_call | solution.py:285
  109.1 3.5 %all-to-all-start.1 = ((f32[32,16,128]{2,1,0:T(8,128)}), f32[32,16,128]{2,1,0:T(8,128)S(1)}, u32[]{:S(2)}, u32[]{:S(2)}) async-start(f32[32,16,128]{2,1,0:T(8,128)} %bitcast.46), calls=%async_computation.1 | async-start | bytes 524288 | tf_op jit(solution)/shard_map/all_to_all | solution.py:20
  112.6 0.8 fusion
  113.4 10.1 %all-to-all-done.1 = f32[32,16,128]{2,1,0:T(8,128)S(1)} async-done(((f32[32,16,128]{2,1,0:T(8,128)}), f32[32,16,128]{2,1,0:T(8,128)S(1)}, u32[]{:S(2)}, u32[]{:S(2)}) %all-to-all-start.1) | async-done | bytes 262176 | tf_op jit(solution)/shard_map/all_to_all | solution.py:20
  123.5 0.7 copy.8
  (28 shorter events, 0.6 us)
Async XLA Ops:
  0.6 0.8 copy-start
  4.6 24.7 %all-to-all-start = ((f32[32,32,128]{2,1,0:T(8,128)}), f32[32,32,128]{2,1,0:T(8,128)S(1)}, u32[]{:S(2)}, u32[]{:S(2)}) async-start(f32[32,32,128]{2,1,0:T(8,128)} %concatenate.9), calls=%async_computation | async-start | bytes 1048576 | tf_op jit(solution)/shard_map/all_to_all | solution.py:20
  11.9 1.0 copy-start.1
  29.3 1.6 %collective-permute-start = (f32[4,136,128]{2,1,0:T(8,128)S(1)}, f32[4,136,128]{2,1,0:T(8,128)S(1)}, u32[]{:S(2)}, u32[]{:S(2)}) collective-permute-start(f32[4,136,128]{2,1,0:T(8,128)S(1)} %dynamic-slice_bitcast_fusion), channel_id=1, source_target_pairs={{0,4},{1,5},{2,6},{3,7},{4,0},{5,1},{6,2},{7,3},{8,12},{9,13},{10,... | collective-permute-start | bytes 835592 | tf_op jit(solution)/shard_map/ppermute | solution.py:30
  31.0 5.3 %collective-permute-start.3 = (f32[136,128]{1,0:T(8,128)S(1)}, f32[136,128]{1,0:T(8,128)S(1)}, u32[]{:S(2)}, u32[]{:S(2)}) collective-permute-start(f32[136,128]{1,0:T(8,128)S(1)} %get-tuple-element.35), channel_id=1, source_target_pairs={{0,3},{1,2},{2,1},{3,0},{4,7},{5,6},{6,5},{7,4},{8,11},{9,10},{10,... | collective-permute-start | bytes 208904 | tf_op jit(solution)/shard_map/ppermute | solution.py:30
  33.7 4.3 %collective-permute-start.2 = (f32[136,128]{1,0:T(8,128)S(1)}, f32[136,128]{1,0:T(8,128)S(1)}, u32[]{:S(2)}, u32[]{:S(2)}) collective-permute-start(f32[136,128]{1,0:T(8,128)S(1)} %get-tuple-element.36), channel_id=1, source_target_pairs={{0,2},{1,3},{2,0},{3,1},{4,6},{5,7},{6,4},{7,5},{8,10},{9,11},{10,... | collective-permute-start | bytes 208904 | tf_op jit(solution)/shard_map/ppermute | solution.py:30
  34.3 4.3 %collective-permute-start.1 = (f32[136,128]{1,0:T(8,128)S(1)}, f32[136,128]{1,0:T(8,128)S(1)}, u32[]{:S(2)}, u32[]{:S(2)}) collective-permute-start(f32[136,128]{1,0:T(8,128)S(1)} %get-tuple-element.37), channel_id=1, source_target_pairs={{0,1},{1,0},{2,3},{3,2},{4,5},{5,4},{6,7},{7,6},{8,9},{9,8},{10,11... | collective-permute-start | bytes 208904 | tf_op jit(solution)/shard_map/ppermute | solution.py:30
  38.6 6.2 %collective-permute-start.6 = (f32[136,128]{1,0:T(8,128)S(1)}, f32[136,128]{1,0:T(8,128)S(1)}, u32[]{:S(2)}, u32[]{:S(2)}) collective-permute-start(f32[136,128]{1,0:T(8,128)S(1)} %fusion.11), channel_id=1, source_target_pairs={{0,24},{1,25},{2,26},{3,27},{4,28},{5,29},{6,30},{7,31},{8,16},{9,... | collective-permute-start | bytes 208904 | tf_op jit(solution)/shard_map/ppermute | solution.py:30
  42.0 5.6 %collective-permute-start.5 = (f32[136,128]{1,0:T(8,128)S(1)}, f32[136,128]{1,0:T(8,128)S(1)}, u32[]{:S(2)}, u32[]{:S(2)}) collective-permute-start(f32[136,128]{1,0:T(8,128)S(1)} %fusion.11), channel_id=1, source_target_pairs={{0,16},{1,17},{2,18},{3,19},{4,20},{5,21},{6,22},{7,23},{8,24},{9,... | collective-permute-start | bytes 208904 | tf_op jit(solution)/shard_map/ppermute | solution.py:30
  42.0 5.6 %collective-permute-start.4 = (f32[136,128]{1,0:T(8,128)S(1)}, f32[136,128]{1,0:T(8,128)S(1)}, u32[]{:S(2)}, u32[]{:S(2)}) collective-permute-start(f32[136,128]{1,0:T(8,128)S(1)} %fusion.11), channel_id=1, source_target_pairs={{0,8},{1,9},{2,10},{3,11},{4,12},{5,13},{6,14},{7,15},{8,0},{9,1},... | collective-permute-start | bytes 208904 | tf_op jit(solution)/shard_map/ppermute | solution.py:30
  48.5 6.0 %collective-permute-start.9 = (f32[128,128]{1,0:T(8,128)S(1)}, f32[128,128]{1,0:T(8,128)S(1)}, u32[]{:S(2)}, u32[]{:S(2)}) collective-permute-start(f32[128,128]{1,0:T(8,128)S(1)} %fusion.13), channel_id=1, source_target_pairs={{0,3},{1,2},{2,1},{3,0},{4,7},{5,6},{6,5},{7,4},{8,11},{9,10},{10,... | collective-permute-start | bytes 196616 | tf_op jit(solution)/shard_map/ppermute | solution.py:30
  50.0 4.7 %collective-permute-start.8 = (f32[128,128]{1,0:T(8,128)S(1)}, f32[128,128]{1,0:T(8,128)S(1)}, u32[]{:S(2)}, u32[]{:S(2)}) collective-permute-start(f32[128,128]{1,0:T(8,128)S(1)} %fusion.13), channel_id=1, source_target_pairs={{0,2},{1,3},{2,0},{3,1},{4,6},{5,7},{6,4},{7,5},{8,10},{9,11},{10,... | collective-permute-start | bytes 196616 | tf_op jit(solution)/shard_map/ppermute | solution.py:30
  51.6 4.3 %collective-permute-start.7 = (f32[128,128]{1,0:T(8,128)S(1)}, f32[128,128]{1,0:T(8,128)S(1)}, u32[]{:S(2)}, u32[]{:S(2)}) collective-permute-start(f32[128,128]{1,0:T(8,128)S(1)} %fusion.13), channel_id=1, source_target_pairs={{0,1},{1,0},{2,3},{3,2},{4,5},{5,4},{6,7},{7,6},{8,9},{9,8},{10,11... | collective-permute-start | bytes 196616 | tf_op jit(solution)/shard_map/ppermute | solution.py:30
  56.0 1.6 %collective-permute-start.10 = (f32[4,128,128]{2,1,0:T(8,128)S(1)}, f32[4,128,128]{2,1,0:T(8,128)S(1)}, u32[]{:S(2)}, u32[]{:S(2)}) collective-permute-start(f32[4,128,128]{2,1,0:T(8,128)S(1)} %get-tuple-element.38), channel_id=1, source_target_pairs={{0,4},{1,5},{2,6},{3,7},{4,0},{5,1},{6,2},{7,3},{8,12},{9,13},{10,... | collective-permute-start | bytes 786440 | tf_op jit(solution)/shard_map/ppermute | solution.py:30
  75.0 1.8 %collective-permute-start.11 = (f32[4,200,128]{2,1,0:T(8,128)S(1)}, f32[4,200,128]{2,1,0:T(8,128)S(1)}, u32[]{:S(2)}, u32[]{:S(2)}) collective-permute-start(f32[4,200,128]{2,1,0:T(8,128)S(1)} %fusion.2), channel_id=1, source_target_pairs={{0,4},{1,5},{2,6},{3,7},{4,0},{5,1},{6,2},{7,3},{8,12},{9,13},{10,... | collective-permute-start | bytes 1228808 | tf_op jit(solution)/shard_map/ppermute | solution.py:30
  76.9 6.6 %collective-permute-start.14 = (f32[200,128]{1,0:T(8,128)S(1)}, f32[200,128]{1,0:T(8,128)S(1)}, u32[]{:S(2)}, u32[]{:S(2)}) collective-permute-start(f32[200,128]{1,0:T(8,128)S(1)} %get-tuple-element.26), channel_id=1, source_target_pairs={{0,3},{1,2},{2,1},{3,0},{4,7},{5,6},{6,5},{7,4},{8,11},{9,10},{10,... | collective-permute-start | bytes 307208 | tf_op jit(solution)/shard_map/ppermute | solution.py:30
  78.5 6.5 %collective-permute-start.13 = (f32[200,128]{1,0:T(8,128)S(1)}, f32[200,128]{1,0:T(8,128)S(1)}, u32[]{:S(2)}, u32[]{:S(2)}) collective-permute-start(f32[200,128]{1,0:T(8,128)S(1)} %get-tuple-element.27), channel_id=1, source_target_pairs={{0,2},{1,3},{2,0},{3,1},{4,6},{5,7},{6,4},{7,5},{8,10},{9,11},{10,... | collective-permute-start | bytes 307208 | tf_op jit(solution)/shard_map/ppermute | solution.py:30
  78.9 6.1 %collective-permute-start.12 = (f32[200,128]{1,0:T(8,128)S(1)}, f32[200,128]{1,0:T(8,128)S(1)}, u32[]{:S(2)}, u32[]{:S(2)}) collective-permute-start(f32[200,128]{1,0:T(8,128)S(1)} %get-tuple-element.28), channel_id=1, source_target_pairs={{0,1},{1,0},{2,3},{3,2},{4,5},{5,4},{6,7},{7,6},{8,9},{9,8},{10,11... | collective-permute-start | bytes 307208 | tf_op jit(solution)/shard_map/ppermute | solution.py:30
  85.0 7.7 %collective-permute-start.17 = (f32[200,128]{1,0:T(8,128)S(1)}, f32[200,128]{1,0:T(8,128)S(1)}, u32[]{:S(2)}, u32[]{:S(2)}) collective-permute-start(f32[200,128]{1,0:T(8,128)S(1)} %fusion.10), channel_id=1, source_target_pairs={{0,24},{1,25},{2,26},{3,27},{4,28},{5,29},{6,30},{7,31},{8,16},{9,... | collective-permute-start | bytes 307208 | tf_op jit(solution)/shard_map/ppermute | solution.py:30
  87.6 9.2 %collective-permute-start.16 = (f32[200,128]{1,0:T(8,128)S(1)}, f32[200,128]{1,0:T(8,128)S(1)}, u32[]{:S(2)}, u32[]{:S(2)}) collective-permute-start(f32[200,128]{1,0:T(8,128)S(1)} %fusion.10), channel_id=1, source_target_pairs={{0,16},{1,17},{2,18},{3,19},{4,20},{5,21},{6,22},{7,23},{8,24},{9,... | collective-permute-start | bytes 307208 | tf_op jit(solution)/shard_map/ppermute | solution.py:30
  87.6 9.2 %collective-permute-start.15 = (f32[200,128]{1,0:T(8,128)S(1)}, f32[200,128]{1,0:T(8,128)S(1)}, u32[]{:S(2)}, u32[]{:S(2)}) collective-permute-start(f32[200,128]{1,0:T(8,128)S(1)} %fusion.10), channel_id=1, source_target_pairs={{0,8},{1,9},{2,10},{3,11},{4,12},{5,13},{6,14},{7,15},{8,0},{9,1},... | collective-permute-start | bytes 307208 | tf_op jit(solution)/shard_map/ppermute | solution.py:30
  96.9 4.7 %collective-permute-start.19 = (f32[192,128]{1,0:T(8,128)S(1)}, f32[192,128]{1,0:T(8,128)S(1)}, u32[]{:S(2)}, u32[]{:S(2)}) collective-permute-start(f32[192,128]{1,0:T(8,128)S(1)} %get-tuple-element.47), channel_id=1, source_target_pairs={{0,2},{1,3},{2,0},{3,1},{4,6},{5,7},{6,4},{7,5},{8,10},{9,11},{10,... | collective-permute-start | bytes 294920 | tf_op jit(solution)/shard_map/ppermute | solution.py:30
  97.4 5.3 %collective-permute-start.18 = (f32[192,128]{1,0:T(8,128)S(1)}, f32[192,128]{1,0:T(8,128)S(1)}, u32[]{:S(2)}, u32[]{:S(2)}) collective-permute-start(f32[192,128]{1,0:T(8,128)S(1)} %get-tuple-element.47), channel_id=1, source_target_pairs={{0,1},{1,0},{2,3},{3,2},{4,5},{5,4},{6,7},{7,6},{8,9},{9,8},{10,11... | collective-permute-start | bytes 294920 | tf_op jit(solution)/shard_map/ppermute | solution.py:30
  99.1 5.7 %collective-permute-start.20 = (f32[192,128]{1,0:T(8,128)S(1)}, f32[192,128]{1,0:T(8,128)S(1)}, u32[]{:S(2)}, u32[]{:S(2)}) collective-permute-start(f32[192,128]{1,0:T(8,128)S(1)} %get-tuple-element.47), channel_id=1, source_target_pairs={{0,3},{1,2},{2,1},{3,0},{4,7},{5,6},{6,5},{7,4},{8,11},{9,10},{10,... | collective-permute-start | bytes 294920 | tf_op jit(solution)/shard_map/ppermute | solution.py:30
  104.9 1.8 %collective-permute-start.21 = (f32[4,192,128]{2,1,0:T(8,128)S(1)}, f32[4,192,128]{2,1,0:T(8,128)S(1)}, u32[]{:S(2)}, u32[]{:S(2)}) collective-permute-start(f32[4,192,128]{2,1,0:T(8,128)S(1)} %get-tuple-element.29), channel_id=1, source_target_pairs={{0,4},{1,5},{2,6},{3,7},{4,0},{5,1},{6,2},{7,3},{8,12},{9,13},{10,... | collective-permute-start | bytes 1179656 | tf_op jit(solution)/shard_map/ppermute | solution.py:30
  109.1 14.4 %all-to-all-start.1 = ((f32[32,16,128]{2,1,0:T(8,128)}), f32[32,16,128]{2,1,0:T(8,128)S(1)}, u32[]{:S(2)}, u32[]{:S(2)}) async-start(f32[32,16,128]{2,1,0:T(8,128)} %bitcast.46), calls=%async_computation.1 | async-start | bytes 524288 | tf_op jit(solution)/shard_map/all_to_all | solution.py:20

commit v8 on v7

--- a/solution.py
+++ b/solution.py
@@ -10,9 +10,10 @@
 AXES = ("row", "col")
 F32, BF16 = jnp.float32, jnp.bfloat16
 PAD = 8
-ROWS = 128
+ROWS = 512
 MIB = 1024 * 1024
 T1_MIB = 52
+PREP_KIB = 54528
 VMEM_BYTES = 51 * MIB
 
 
@@ -291,6 +292,58 @@
     )(right, second_left, second_right)
 
 
+def prepare_kernel(slices, place_ref, second_left_ref, second_right_ref, left_ref, out_ref, sums_out, left_out):
+    devices, tall, rank = out_ref.shape
+    second_left = second_left_ref[...]
+    sums_out[...] = jnp.sum(second_left, axis=0, keepdims=True)
+    left_out[...] = left_ref[...]
+    per_owner = second_left.shape[0] // (devices * slices)
+    for index in range(per_owner):
+        for device in range(devices):
+            start = (index * devices + device) * slices
+            out_ref[device, index * slices : (index + 1) * slices, :] = second_left[
+                start : start + slices
+            ]
+    rows = tall - per_owner * slices
+    piece = second_right_ref[...]
+    piece = jnp.concatenate(
+        [piece[start : start + rows] for start in range(0, piece.shape[0], rows)], axis=1
+    )
+    for device in range(devices):
+        out_ref[device, per_owner * slices :, :] = piece
+
+
+def prepare(place, second_left, second_right, left, sizes):
+    devices, slices, second_rows, piece_rows, rows_own = sizes
+    rank, width = left.shape[1], second_right.shape[1]
+    tall = second_rows // devices + piece_rows * width // rank
+    block = lambda shape, which: pl.BlockSpec(shape, lambda step, place: (place[which], 0))
+    fixed = lambda shape: pl.BlockSpec(shape, lambda step, place: (0,) * len(shape))
+    return pl.pallas_call(
+        functools.partial(prepare_kernel, slices),
+        grid_spec=pltpu.PrefetchScalarGridSpec(
+            num_scalar_prefetch=1,
+            grid=(1,),
+            in_specs=[
+                block((second_rows, rank), 0),
+                block((piece_rows, width), 1),
+                block((rows_own, rank), 2),
+            ],
+            out_specs=[fixed((devices, tall, rank)), fixed((1, rank)), fixed((rows_own, rank))],
+        ),
+        out_shape=[
+            jax.ShapeDtypeStruct((devices, tall, rank), F32),
+            jax.ShapeDtypeStruct((1, rank), F32),
+            jax.ShapeDtypeStruct((rows_own, rank), F32),
+        ],
+        compiler_params=params(PREP_KIB * 1024),
+        cost_estimate=pl.CostEstimate(
+            flops=second_rows * rank, bytes_accessed=12 * second_rows * rank, transcendentals=0
+        ),
+        name="prepare",
+    )(place, second_left, second_right, left)
+
+
 def body(tensor_slab, left_init, right_init, second_left_init, second_right_init):
     row_devices = lax.axis_size("row")
     col_devices = lax.axis_size("col")
@@ -304,18 +357,14 @@
     rows_own = m // parts
 
     second_rows = second_left_init.shape[0] // col_devices
-    own_left = lax.dynamic_slice_in_dim(
-        second_left_init, lax.axis_index("col") * second_rows, second_rows, 0
-    )
-    col_part = jnp.sum(own_left, axis=0)[None]
-    own_left = own_left.reshape(per_owner, devices, slices, rank)
     piece_rows = rank // row_devices
-    piece = lax.dynamic_slice_in_dim(
-        second_right_init, lax.axis_index("row") * piece_rows, piece_rows, 0
-    ).reshape(-1, rank)
-    piece = jnp.broadcast_to(piece[None], (devices,) + piece.shape)
-    second_factors = [own_left[index] for index in range(per_owner)] + [piece]
-    arrived = exchange(jnp.concatenate(second_factors, axis=1))
+    groups = rank // second_right_init.shape[1]
+    place = jnp.stack([lax.axis_index("col"), lax.axis_index("row"), own_part]).astype(jnp.int32)
+    second_factors, col_part, own_init = prepare(
+        place, second_left_init, second_right_init, left_init,
+        (devices, slices, second_rows, piece_rows, rows_own),
+    )
+    arrived = exchange(second_factors)
 
     def own_rows(left):
         return lax.dynamic_slice_in_dim(left, own_part * rows_own, rows_own, 0)
@@ -323,9 +372,8 @@
     def own_left_rows(own, total):
         return own * total[:rows_own] / total[rows_own][None, :]
 
-    own_init = own_rows(left_init)
     right, summed = full_turn(
-        tensor_slab, after(left_init, own_init), right_init, left_init, k, parts, T1_MIB * MIB
+        tensor_slab, left_init, right_init, left_init, k, parts, T1_MIB * MIB
     )
     summed, arrived = lax.optimization_barrier((summed, arrived))
     summed = summed.reshape(2, col_devices, rows_own + PAD, rank)
@@ -333,8 +381,10 @@
     left = spread_core(spread_plane(own_left_rows(own_init, total))).reshape(m, rank)
     right, summed = full_turn(tensor_slab, left, right, col_part, k, parts, VMEM_BYTES)
     second_left = arrived[:, : per_owner * slices].reshape(rank * slices, rank)
-    whole = arrived[:, per_owner * slices :].reshape(row_devices, col_devices, piece_rows, -1)
-    whole = whole.transpose(0, 2, 1, 3).reshape(rank, k // rank, rank).transpose(1, 0, 2)
+    whole = arrived[:, per_owner * slices :].reshape(
+        row_devices, col_devices, piece_rows // groups, groups, -1
+    )
+    whole = whole.transpose(0, 3, 2, 1, 4).reshape(rank, k // rank, rank).transpose(1, 0, 2)
     numerator = second_numerator(right, second_left, whole, slices)
 
     rows_part = k // parts

time: 125 us -> 115 us (0.920)
  Pallas kernels: 35.7 us -> 30.8 us
  local copies, waits for them, and re-layouts: 5.92 us -> 2.83 us
  other arithmetic: 3.52 us -> 1.72 us
    pallas_call x2, Pallas kernels: 32 us -> 24.7 us  [full_turn(): pl.pallas_call(turn_kernel, grid=(columns // block,), in_specs=[columns_s...]
    all_to_all x2, waiting for transfers between devices: 10.1 us -> 12.7 us  [exchange(): return lax.all_to_all(parts, AXES, split_axis=0, concat_axis=0, tiled=True)]
    pallas_call x0 -> x1, Pallas kernels: none -> 2.38 us  [prepare(): pl.pallas_call(functools.partial(prepare_kernel, slices), grid_spec=pltpu...]
    concatenate x1 -> x0, local copies, waits for them, and re-layouts: 2.13 us -> none  [body(): arrived = exchange(jnp.concatenate(second_factors, axis=1))]
    ppermute x22, waiting for transfers between devices: 33.5 us -> 31.7 us  [send(): return lax.ppermute(values, AXES, pairs)]
  transfers between devices with their start and end apart: 24 -> 24, of which waited for: 20 -> 21; matrix products, arithmetic and copies ran while one was open for 2% -> 1% of each run, Pallas kernels for 13% -> 11%
where the time goes in v8:
time: 115 us
  waiting for transfers between devices  44.3 us (39%)
  starting transfers between devices  34.4 us (30%)
  Pallas kernels  30.8 us (27%)
  local copies, waits for them, and re-layouts  2.83 us (2%)
  other arithmetic  1.72 us (1%)
    ppermute x22, waiting for transfers between devices, send(): return lax.ppermute(values, AXES, pairs)  31.7 us
    pallas_call x2, Pallas kernels, full_turn(): pl.pallas_call(turn_kernel, grid=(columns // block,), in_specs=[columns_s...  24.7 us
    ppermute x22, starting transfers between devices, send(): return lax.ppermute(values, AXES, pairs)  23.5 us
    all_to_all x2, waiting for transfers between devices, exchange(): return lax.all_to_all(parts, AXES, split_axis=0, concat_axis=0, tiled=True)  12.7 us
    all_to_all x2, starting transfers between devices, exchange(): return lax.all_to_all(parts, AXES, split_axis=0, concat_axis=0, tiled=True)  10.9 us
    pallas_call x1, Pallas kernels, prepare(): pl.pallas_call(functools.partial(prepare_kernel, slices), grid_spec=pltpu...  2.38 us
  transfers between devices with their start and end apart: 24, of which 21 were waited for; matrix products, arithmetic and copies ran while one was open for 1% of the time, Pallas kernels for 11%

profile of v8, /device:TPU:0, one launch (start us, length us, event | category | flops | bytes accessed | tf_op | source)
XLA Modules:
  0.0 115.0 jit_solution(10049537995847590115)
XLA Ops:
  0.6 0.1 pad_add_fusion.place_ref
  0.7 0.8 copy-done.1
  1.6 2.4 %prepare.1 = (f32[32,32,128]{2,1,0:T(8,128)}, f32[1,128]{1,0:T(1,128)S(1)}, f32[128,128]{1,0:T(8,128)S(1)}) custom-call(s32[3]{0:T(128)S(1)} %pad_add_fusion.place_ref, f32[2048,128]{1,0:T(8,128)} %second_left_ref.1, f32[128,128]{1,0:T(8,128)S(1)} %copy-done.1, f32[1024,128]{1,0:T(8,128)} %extra_ref.1), custom_call_target="tpu_custom_call" | custom-call | flops 65536 | bytes 786432 | tf_op jit(solution)/shard_map/prepare/pallas_call | solution.py:322
  3.9 7.3 %all-to-all-start = ((f32[32,32,128]{2,1,0:T(8,128)}), f32[32,32,128]{2,1,0:T(8,128)S(1)}, u32[]{:S(2)}, u32[]{:S(2)}) async-start(f32[32,32,128]{2,1,0:T(8,128)} %get-tuple-element.13), calls=%async_computation | async-start | bytes 1048576 | tf_op jit(solution)/shard_map/all_to_all | solution.py:21
  11.3 0.0 copy-start
  11.3 1.0 copy-done
  12.3 12.6 %turn.2 = (f32[128,2048]{1,0:T(8,128)}, f32[8,136,128]{2,1,0:T(8,128)S(1)}) custom-call(f32[1024,2048]{1,0:T(8,128)} %slab_ref.3, f32[1024,128]{1,0:T(8,128)S(1)} %copy-done, f32[128,2048]{1,0:T(8,128)} %right_ref.1, f32[1024,128]{1,0:T(8,128)S(1)} %copy-done), custom_call_target="tpu_custom_call" | custom-call | flops 6442450944 | bytes 8388608 | tf_op jit(solution)/shard_map/turn/pallas_call | solution.py:257
  24.9 2.5 %all-to-all-done = f32[32,32,128]{2,1,0:T(8,128)S(1)} async-done(((f32[32,32,128]{2,1,0:T(8,128)}), f32[32,32,128]{2,1,0:T(8,128)S(1)}, u32[]{:S(2)}, u32[]{:S(2)}) %all-to-all-start) | async-done | bytes 524320 | tf_op jit(solution)/shard_map/all_to_all | solution.py:21
  27.5 0.1 collective-permute-start
  27.6 1.5 %collective-permute-done = f32[4,136,128]{2,1,0:T(8,128)S(1)} collective-permute-done((f32[4,136,128]{2,1,0:T(8,128)S(1)}, f32[4,136,128]{2,1,0:T(8,128)S(1)}, u32[]{:S(2)}, u32[]{:S(2)}) %collective-permute-start) | collective-permute-done | bytes 278560 | tf_op jit(solution)/shard_map/ppermute | solution.py:31
  29.2 0.3 collective-permute-start.1
  29.5 1.5 %collective-permute-start.2 = (f32[136,128]{1,0:T(8,128)S(1)}, f32[136,128]{1,0:T(8,128)S(1)}, u32[]{:S(2)}, u32[]{:S(2)}) collective-permute-start(f32[136,128]{1,0:T(8,128)S(1)} %get-tuple-element.36), channel_id=1, source_target_pairs={{0,2},{1,3},{2,0},{3,1},{4,6},{5,7},{6,4},{7,5},{8,10},{9,11},{10,... | collective-permute-start | bytes 208904 | tf_op jit(solution)/shard_map/ppermute | solution.py:31
  31.0 1.8 %collective-permute-start.3 = (f32[136,128]{1,0:T(8,128)S(1)}, f32[136,128]{1,0:T(8,128)S(1)}, u32[]{:S(2)}, u32[]{:S(2)}) collective-permute-start(f32[136,128]{1,0:T(8,128)S(1)} %get-tuple-element.35), channel_id=1, source_target_pairs={{0,3},{1,2},{2,1},{3,0},{4,7},{5,6},{6,5},{7,4},{8,11},{9,10},{10,... | collective-permute-start | bytes 208904 | tf_op jit(solution)/shard_map/ppermute | solution.py:31
  32.8 1.2 %collective-permute-done.1 = f32[136,128]{1,0:T(8,128)S(1)} collective-permute-done((f32[136,128]{1,0:T(8,128)S(1)}, f32[136,128]{1,0:T(8,128)S(1)}, u32[]{:S(2)}, u32[]{:S(2)}) %collective-permute-start.1) | collective-permute-done | bytes 69664 | tf_op jit(solution)/shard_map/ppermute | solution.py:31
  34.0 0.0 collective-permute-done.2
  34.0 2.2 %collective-permute-done.3 = f32[136,128]{1,0:T(8,128)S(1)} collective-permute-done((f32[136,128]{1,0:T(8,128)S(1)}, f32[136,128]{1,0:T(8,128)S(1)}, u32[]{:S(2)}, u32[]{:S(2)}) %collective-permute-start.3) | collective-permute-done | bytes 69664 | tf_op jit(solution)/shard_map/ppermute | solution.py:31
  36.2 0.5 collective-permute-start.4
  36.7 2.5 %collective-permute-start.5 = (f32[136,128]{1,0:T(8,128)S(1)}, f32[136,128]{1,0:T(8,128)S(1)}, u32[]{:S(2)}, u32[]{:S(2)}) collective-permute-start(f32[136,128]{1,0:T(8,128)S(1)} %fusion.11), channel_id=1, source_target_pairs={{0,16},{1,17},{2,18},{3,19},{4,20},{5,21},{6,22},{7,23},{8,24},{9,... | collective-permute-start | bytes 208904 | tf_op jit(solution)/shard_map/ppermute | solution.py:31
  39.2 1.5 %collective-permute-start.6 = (f32[136,128]{1,0:T(8,128)S(1)}, f32[136,128]{1,0:T(8,128)S(1)}, u32[]{:S(2)}, u32[]{:S(2)}) collective-permute-start(f32[136,128]{1,0:T(8,128)S(1)} %fusion.11), channel_id=1, source_target_pairs={{0,24},{1,25},{2,26},{3,27},{4,28},{5,29},{6,30},{7,31},{8,16},{9,... | collective-permute-start | bytes 208904 | tf_op jit(solution)/shard_map/ppermute | solution.py:31
  40.7 0.0 collective-permute-done.4
  40.7 2.8 %collective-permute-done.5 = f32[136,128]{1,0:T(8,128)S(1)} collective-permute-done((f32[136,128]{1,0:T(8,128)S(1)}, f32[136,128]{1,0:T(8,128)S(1)}, u32[]{:S(2)}, u32[]{:S(2)}) %collective-permute-start.5) | collective-permute-done | bytes 69664 | tf_op jit(solution)/shard_map/ppermute | solution.py:31
  43.4 1.9 %collective-permute-done.6 = f32[136,128]{1,0:T(8,128)S(1)} collective-permute-done((f32[136,128]{1,0:T(8,128)S(1)}, f32[136,128]{1,0:T(8,128)S(1)}, u32[]{:S(2)}, u32[]{:S(2)}) %collective-permute-start.6) | collective-permute-done | bytes 69664 | tf_op jit(solution)/shard_map/ppermute | solution.py:31
  45.4 0.6 collective-permute-start.7
  46.0 1.0 collective-permute-start.8
  47.0 1.9 %collective-permute-start.9 = (f32[128,128]{1,0:T(8,128)S(1)}, f32[128,128]{1,0:T(8,128)S(1)}, u32[]{:S(2)}, u32[]{:S(2)}) collective-permute-start(f32[128,128]{1,0:T(8,128)S(1)} %fusion.13), channel_id=1, source_target_pairs={{0,3},{1,2},{2,1},{3,0},{4,7},{5,6},{6,5},{7,4},{8,11},{9,10},{10,... | collective-permute-start | bytes 196616 | tf_op jit(solution)/shard_map/ppermute | solution.py:31
  48.9 0.8 collective-permute-done.7
  49.7 0.6 collective-permute-done.8
  50.3 1.9 %collective-permute-done.9 = f32[128,128]{1,0:T(8,128)S(1)} collective-permute-done((f32[128,128]{1,0:T(8,128)S(1)}, f32[128,128]{1,0:T(8,128)S(1)}, u32[]{:S(2)}, u32[]{:S(2)}) %collective-permute-start.9) | collective-permute-done | bytes 65568 | tf_op jit(solution)/shard_map/ppermute | solution.py:31
  52.3 0.1 collective-permute-start.10
  52.4 1.5 %collective-permute-done.10 = f32[4,128,128]{2,1,0:T(8,128)S(1)} collective-permute-done((f32[4,128,128]{2,1,0:T(8,128)S(1)}, f32[4,128,128]{2,1,0:T(8,128)S(1)}, u32[]{:S(2)}, u32[]{:S(2)}) %collective-permute-start.10) | collective-permute-done | bytes 262176 | tf_op jit(solution)/shard_map/ppermute | solution.py:31
  53.9 0.1 fusion.9
  54.0 12.0 %turn.3 = (f32[128,2048]{1,0:T(8,128)S(1)}, f32[8,136,128]{2,1,0:T(8,128)S(1)}) custom-call(f32[1024,2048]{1,0:T(8,128)} %slab_ref.3, f32[1024,128]{1,0:T(8,128)S(1)} %bitcast.82, f32[128,2048]{1,0:T(8,128)} %get-tuple-element.15.right_ref, f32[1,128]{1,0:T(1,128)S(1)} %get-tuple-element.16.extra_ref), custom_call_target="tpu_custom_call" | custom-call | flops 6442450944 | bytes 8388608 | tf_op jit(solution)/shard_map/turn/pallas_call | solution.py:257
  66.1 1.6 %second_numerator.1 = f32[4,128,128]{2,1,0:T(8,128)S(1)} custom-call(f32[128,2048]{1,0:T(8,128)S(1)} %get-tuple-element.18.right_ref, f32[512,128]{1,0:T(8,128)S(1)} %bitcast.73, f32[4,128,128]{2,1,0:T(8,128)S(1)} %bitcast.75), custom_call_target="tpu_custom_call" | custom-call | flops 402653184 | bytes 1048576 | tf_op jit(solution)/shard_map/second_numerator/pallas_call | solution.py:276
  67.7 0.2 collective-permute-start.11
  67.9 1.6 %collective-permute-done.11 = f32[4,200,128]{2,1,0:T(8,128)S(1)} collective-permute-done((f32[4,200,128]{2,1,0:T(8,128)S(1)}, f32[4,200,128]{2,1,0:T(8,128)S(1)}, u32[]{:S(2)}, u32[]{:S(2)}) %collective-permute-start.11) | collective-permute-done | bytes 409632 | tf_op jit(solution)/shard_map/ppermute | solution.py:31
  69.5 0.1 fusion.5
  69.6 1.1 collective-permute-start.12
  70.7 1.4 %collective-permute-start.13 = (f32[200,128]{1,0:T(8,128)S(1)}, f32[200,128]{1,0:T(8,128)S(1)}, u32[]{:S(2)}, u32[]{:S(2)}) collective-permute-start(f32[200,128]{1,0:T(8,128)S(1)} %get-tuple-element.27), channel_id=1, source_target_pairs={{0,2},{1,3},{2,0},{3,1},{4,6},{5,7},{6,4},{7,5},{8,10},{9,11},{10,... | collective-permute-start | bytes 307208 | tf_op jit(solution)/shard_map/ppermute | solution.py:31
  72.2 1.0 collective-permute-start.14
  73.2 1.7 %collective-permute-done.12 = f32[200,128]{1,0:T(8,128)S(1)} collective-permute-done((f32[200,128]{1,0:T(8,128)S(1)}, f32[200,128]{1,0:T(8,128)S(1)}, u32[]{:S(2)}, u32[]{:S(2)}) %collective-permute-start.12) | collective-permute-done | bytes 102432 | tf_op jit(solution)/shard_map/ppermute | solution.py:31
  74.9 1.7 %collective-permute-done.13 = f32[200,128]{1,0:T(8,128)S(1)} collective-permute-done((f32[200,128]{1,0:T(8,128)S(1)}, f32[200,128]{1,0:T(8,128)S(1)}, u32[]{:S(2)}, u32[]{:S(2)}) %collective-permute-start.13) | collective-permute-done | bytes 102432 | tf_op jit(solution)/shard_map/ppermute | solution.py:31
  76.5 1.2 %collective-permute-done.14 = f32[200,128]{1,0:T(8,128)S(1)} collective-permute-done((f32[200,128]{1,0:T(8,128)S(1)}, f32[200,128]{1,0:T(8,128)S(1)}, u32[]{:S(2)}, u32[]{:S(2)}) %collective-permute-start.14) | collective-permute-done | bytes 102432 | tf_op jit(solution)/shard_map/ppermute | solution.py:31
  77.7 0.1 collective-permute-start.15
  77.9 2.1 %collective-permute-start.16 = (f32[200,128]{1,0:T(8,128)S(1)}, f32[200,128]{1,0:T(8,128)S(1)}, u32[]{:S(2)}, u32[]{:S(2)}) collective-permute-start(f32[200,128]{1,0:T(8,128)S(1)} %fusion.10), channel_id=1, source_target_pairs={{0,16},{1,17},{2,18},{3,19},{4,20},{5,21},{6,22},{7,23},{8,24},{9,... | collective-permute-start | bytes 307208 | tf_op jit(solution)/shard_map/ppermute | solution.py:31
  79.9 2.2 %collective-permute-start.17 = (f32[200,128]{1,0:T(8,128)S(1)}, f32[200,128]{1,0:T(8,128)S(1)}, u32[]{:S(2)}, u32[]{:S(2)}) collective-permute-start(f32[200,128]{1,0:T(8,128)S(1)} %fusion.10), channel_id=1, source_target_pairs={{0,24},{1,25},{2,26},{3,27},{4,28},{5,29},{6,30},{7,31},{8,16},{9,... | collective-permute-start | bytes 307208 | tf_op jit(solution)/shard_map/ppermute | solution.py:31
  82.2 0.3 collective-permute-done.15
  82.5 5.2 %collective-permute-done.16 = f32[200,128]{1,0:T(8,128)S(1)} collective-permute-done((f32[200,128]{1,0:T(8,128)S(1)}, f32[200,128]{1,0:T(8,128)S(1)}, u32[]{:S(2)}, u32[]{:S(2)}) %collective-permute-start.16) | collective-permute-done | bytes 102432 | tf_op jit(solution)/shard_map/ppermute | solution.py:31
  87.6 0.0 collective-permute-done.17
  87.7 0.1 broadcast_divide_fusion
  87.9 1.9 %collective-permute-start.18 = (f32[192,128]{1,0:T(8,128)S(1)}, f32[192,128]{1,0:T(8,128)S(1)}, u32[]{:S(2)}, u32[]{:S(2)}) collective-permute-start(f32[192,128]{1,0:T(8,128)S(1)} %get-tuple-element.47), channel_id=1, source_target_pairs={{0,1},{1,0},{2,3},{3,2},{4,5},{5,4},{6,7},{7,6},{8,9},{9,8},{10,11... | collective-permute-start | bytes 294920 | tf_op jit(solution)/shard_map/ppermute | solution.py:31
  89.8 0.1 collective-permute-start.19
  89.9 1.5 %collective-permute-start.20 = (f32[192,128]{1,0:T(8,128)S(1)}, f32[192,128]{1,0:T(8,128)S(1)}, u32[]{:S(2)}, u32[]{:S(2)}) collective-permute-start(f32[192,128]{1,0:T(8,128)S(1)} %get-tuple-element.47), channel_id=1, source_target_pairs={{0,3},{1,2},{2,1},{3,0},{4,7},{5,6},{6,5},{7,4},{8,11},{9,10},{10,... | collective-permute-start | bytes 294920 | tf_op jit(solution)/shard_map/ppermute | solution.py:31
  91.4 1.3 %collective-permute-done.18 = f32[192,128]{1,0:T(8,128)S(1)} collective-permute-done((f32[192,128]{1,0:T(8,128)S(1)}, f32[192,128]{1,0:T(8,128)S(1)}, u32[]{:S(2)}, u32[]{:S(2)}) %collective-permute-start.18) | collective-permute-done | bytes 98336 | tf_op jit(solution)/shard_map/ppermute | solution.py:31
  92.7 1.7 %collective-permute-done.19 = f32[192,128]{1,0:T(8,128)S(1)} collective-permute-done((f32[192,128]{1,0:T(8,128)S(1)}, f32[192,128]{1,0:T(8,128)S(1)}, u32[]{:S(2)}, u32[]{:S(2)}) %collective-permute-start.19) | collective-permute-done | bytes 98336 | tf_op jit(solution)/shard_map/ppermute | solution.py:31
  94.4 1.0 collective-permute-done.20
  95.5 0.1 pad_maximum_fusion.2
  95.6 0.1 collective-permute-start.21
  95.7 1.7 %collective-permute-done.21 = f32[4,192,128]{2,1,0:T(8,128)S(1)} collective-permute-done((f32[4,192,128]{2,1,0:T(8,128)S(1)}, f32[4,192,128]{2,1,0:T(8,128)S(1)}, u32[]{:S(2)}, u32[]{:S(2)}) %collective-permute-start.21) | collective-permute-done | bytes 393248 | tf_op jit(solution)/shard_map/ppermute | solution.py:31
  97.4 0.2 fusion.6
  97.6 2.2 %second_rows.1 = f32[512,128]{1,0:T(8,128)} custom-call(f32[128,2048]{1,0:T(8,128)S(1)} %get-tuple-element.18.right_ref, f32[512,128]{1,0:T(8,128)S(1)} %bitcast.74, f32[4,128,128]{2,1,0:T(8,128)S(1)} %bitcast.81), custom_call_target="tpu_custom_call" | custom-call | flops 402653184 | bytes 1048576 | tf_op jit(solution)/shard_map/second_rows/pallas_call | solution.py:286
  99.8 3.6 %all-to-all-start.1 = ((f32[32,16,128]{2,1,0:T(8,128)}), f32[32,16,128]{2,1,0:T(8,128)S(1)}, u32[]{:S(2)}, u32[]{:S(2)}) async-start(f32[32,16,128]{2,1,0:T(8,128)} %bitcast.44), calls=%async_computation.1 | async-start | bytes 524288 | tf_op jit(solution)/shard_map/all_to_all | solution.py:21
  103.3 0.8 fusion
  104.2 10.1 %all-to-all-done.1 = f32[32,16,128]{2,1,0:T(8,128)S(1)} async-done(((f32[32,16,128]{2,1,0:T(8,128)}), f32[32,16,128]{2,1,0:T(8,128)S(1)}, u32[]{:S(2)}, u32[]{:S(2)}) %all-to-all-start.1) | async-done | bytes 262176 | tf_op jit(solution)/shard_map/all_to_all | solution.py:21
  114.3 0.7 copy.8
  (25 shorter events, 0.6 us)
Async XLA Ops:
  0.7 0.8 copy-start.1
  3.9 23.6 %all-to-all-start = ((f32[32,32,128]{2,1,0:T(8,128)}), f32[32,32,128]{2,1,0:T(8,128)S(1)}, u32[]{:S(2)}, u32[]{:S(2)}) async-start(f32[32,32,128]{2,1,0:T(8,128)} %get-tuple-element.13), calls=%async_computation | async-start | bytes 1048576 | tf_op jit(solution)/shard_map/all_to_all | solution.py:21
  11.3 1.0 copy-start
  27.5 1.6 %collective-permute-start = (f32[4,136,128]{2,1,0:T(8,128)S(1)}, f32[4,136,128]{2,1,0:T(8,128)S(1)}, u32[]{:S(2)}, u32[]{:S(2)}) collective-permute-start(f32[4,136,128]{2,1,0:T(8,128)S(1)} %dynamic-slice_bitcast_fusion), channel_id=1, source_target_pairs={{0,4},{1,5},{2,6},{3,7},{4,0},{5,1},{6,2},{7,3},{8,12},{9,13},{10,... | collective-permute-start | bytes 835592 | tf_op jit(solution)/shard_map/ppermute | solution.py:31
  29.2 4.8 %collective-permute-start.1 = (f32[136,128]{1,0:T(8,128)S(1)}, f32[136,128]{1,0:T(8,128)S(1)}, u32[]{:S(2)}, u32[]{:S(2)}) collective-permute-start(f32[136,128]{1,0:T(8,128)S(1)} %get-tuple-element.37), channel_id=1, source_target_pairs={{0,1},{1,0},{2,3},{3,2},{4,5},{5,4},{6,7},{7,6},{8,9},{9,8},{10,11... | collective-permute-start | bytes 208904 | tf_op jit(solution)/shard_map/ppermute | solution.py:31
  29.5 4.5 %collective-permute-start.2 = (f32[136,128]{1,0:T(8,128)S(1)}, f32[136,128]{1,0:T(8,128)S(1)}, u32[]{:S(2)}, u32[]{:S(2)}) collective-permute-start(f32[136,128]{1,0:T(8,128)S(1)} %get-tuple-element.36), channel_id=1, source_target_pairs={{0,2},{1,3},{2,0},{3,1},{4,6},{5,7},{6,4},{7,5},{8,10},{9,11},{10,... | collective-permute-start | bytes 208904 | tf_op jit(solution)/shard_map/ppermute | solution.py:31
  31.0 5.2 %collective-permute-start.3 = (f32[136,128]{1,0:T(8,128)S(1)}, f32[136,128]{1,0:T(8,128)S(1)}, u32[]{:S(2)}, u32[]{:S(2)}) collective-permute-start(f32[136,128]{1,0:T(8,128)S(1)} %get-tuple-element.35), channel_id=1, source_target_pairs={{0,3},{1,2},{2,1},{3,0},{4,7},{5,6},{6,5},{7,4},{8,11},{9,10},{10,... | collective-permute-start | bytes 208904 | tf_op jit(solution)/shard_map/ppermute | solution.py:31
  36.2 4.5 %collective-permute-start.4 = (f32[136,128]{1,0:T(8,128)S(1)}, f32[136,128]{1,0:T(8,128)S(1)}, u32[]{:S(2)}, u32[]{:S(2)}) collective-permute-start(f32[136,128]{1,0:T(8,128)S(1)} %fusion.11), channel_id=1, source_target_pairs={{0,8},{1,9},{2,10},{3,11},{4,12},{5,13},{6,14},{7,15},{8,0},{9,1},... | collective-permute-start | bytes 208904 | tf_op jit(solution)/shard_map/ppermute | solution.py:31
  36.7 6.7 %collective-permute-start.5 = (f32[136,128]{1,0:T(8,128)S(1)}, f32[136,128]{1,0:T(8,128)S(1)}, u32[]{:S(2)}, u32[]{:S(2)}) collective-permute-start(f32[136,128]{1,0:T(8,128)S(1)} %fusion.11), channel_id=1, source_target_pairs={{0,16},{1,17},{2,18},{3,19},{4,20},{5,21},{6,22},{7,23},{8,24},{9,... | collective-permute-start | bytes 208904 | tf_op jit(solution)/shard_map/ppermute | solution.py:31
  39.2 6.1 %collective-permute-start.6 = (f32[136,128]{1,0:T(8,128)S(1)}, f32[136,128]{1,0:T(8,128)S(1)}, u32[]{:S(2)}, u32[]{:S(2)}) collective-permute-start(f32[136,128]{1,0:T(8,128)S(1)} %fusion.11), channel_id=1, source_target_pairs={{0,24},{1,25},{2,26},{3,27},{4,28},{5,29},{6,30},{7,31},{8,16},{9,... | collective-permute-start | bytes 208904 | tf_op jit(solution)/shard_map/ppermute | solution.py:31
  45.4 4.3 %collective-permute-start.7 = (f32[128,128]{1,0:T(8,128)S(1)}, f32[128,128]{1,0:T(8,128)S(1)}, u32[]{:S(2)}, u32[]{:S(2)}) collective-permute-start(f32[128,128]{1,0:T(8,128)S(1)} %fusion.13), channel_id=1, source_target_pairs={{0,1},{1,0},{2,3},{3,2},{4,5},{5,4},{6,7},{7,6},{8,9},{9,8},{10,11... | collective-permute-start | bytes 196616 | tf_op jit(solution)/shard_map/ppermute | solution.py:31
  46.0 4.3 %collective-permute-start.8 = (f32[128,128]{1,0:T(8,128)S(1)}, f32[128,128]{1,0:T(8,128)S(1)}, u32[]{:S(2)}, u32[]{:S(2)}) collective-permute-start(f32[128,128]{1,0:T(8,128)S(1)} %fusion.13), channel_id=1, source_target_pairs={{0,2},{1,3},{2,0},{3,1},{4,6},{5,7},{6,4},{7,5},{8,10},{9,11},{10,... | collective-permute-start | bytes 196616 | tf_op jit(solution)/shard_map/ppermute | solution.py:31
  47.0 5.2 %collective-permute-start.9 = (f32[128,128]{1,0:T(8,128)S(1)}, f32[128,128]{1,0:T(8,128)S(1)}, u32[]{:S(2)}, u32[]{:S(2)}) collective-permute-start(f32[128,128]{1,0:T(8,128)S(1)} %fusion.13), channel_id=1, source_target_pairs={{0,3},{1,2},{2,1},{3,0},{4,7},{5,6},{6,5},{7,4},{8,11},{9,10},{10,... | collective-permute-start | bytes 196616 | tf_op jit(solution)/shard_map/ppermute | solution.py:31
  52.3 1.6 %collective-permute-start.10 = (f32[4,128,128]{2,1,0:T(8,128)S(1)}, f32[4,128,128]{2,1,0:T(8,128)S(1)}, u32[]{:S(2)}, u32[]{:S(2)}) collective-permute-start(f32[4,128,128]{2,1,0:T(8,128)S(1)} %get-tuple-element.38), channel_id=1, source_target_pairs={{0,4},{1,5},{2,6},{3,7},{4,0},{5,1},{6,2},{7,3},{8,12},{9,13},{10,... | collective-permute-start | bytes 786440 | tf_op jit(solution)/shard_map/ppermute | solution.py:31
  67.7 1.8 %collective-permute-start.11 = (f32[4,200,128]{2,1,0:T(8,128)S(1)}, f32[4,200,128]{2,1,0:T(8,128)S(1)}, u32[]{:S(2)}, u32[]{:S(2)}) collective-permute-start(f32[4,200,128]{2,1,0:T(8,128)S(1)} %fusion.2), channel_id=1, source_target_pairs={{0,4},{1,5},{2,6},{3,7},{4,0},{5,1},{6,2},{7,3},{8,12},{9,13},{10,... | collective-permute-start | bytes 1228808 | tf_op jit(solution)/shard_map/ppermute | solution.py:31
  69.6 5.2 %collective-permute-start.12 = (f32[200,128]{1,0:T(8,128)S(1)}, f32[200,128]{1,0:T(8,128)S(1)}, u32[]{:S(2)}, u32[]{:S(2)}) collective-permute-start(f32[200,128]{1,0:T(8,128)S(1)} %get-tuple-element.28), channel_id=1, source_target_pairs={{0,1},{1,0},{2,3},{3,2},{4,5},{5,4},{6,7},{7,6},{8,9},{9,8},{10,11... | collective-permute-start | bytes 307208 | tf_op jit(solution)/shard_map/ppermute | solution.py:31
  70.7 5.8 %collective-permute-start.13 = (f32[200,128]{1,0:T(8,128)S(1)}, f32[200,128]{1,0:T(8,128)S(1)}, u32[]{:S(2)}, u32[]{:S(2)}) collective-permute-start(f32[200,128]{1,0:T(8,128)S(1)} %get-tuple-element.27), channel_id=1, source_target_pairs={{0,2},{1,3},{2,0},{3,1},{4,6},{5,7},{6,4},{7,5},{8,10},{9,11},{10,... | collective-permute-start | bytes 307208 | tf_op jit(solution)/shard_map/ppermute | solution.py:31
  72.2 5.6 %collective-permute-start.14 = (f32[200,128]{1,0:T(8,128)S(1)}, f32[200,128]{1,0:T(8,128)S(1)}, u32[]{:S(2)}, u32[]{:S(2)}) collective-permute-start(f32[200,128]{1,0:T(8,128)S(1)} %get-tuple-element.26), channel_id=1, source_target_pairs={{0,3},{1,2},{2,1},{3,0},{4,7},{5,6},{6,5},{7,4},{8,11},{9,10},{10,... | collective-permute-start | bytes 307208 | tf_op jit(solution)/shard_map/ppermute | solution.py:31
  77.7 4.7 %collective-permute-start.15 = (f32[200,128]{1,0:T(8,128)S(1)}, f32[200,128]{1,0:T(8,128)S(1)}, u32[]{:S(2)}, u32[]{:S(2)}) collective-permute-start(f32[200,128]{1,0:T(8,128)S(1)} %fusion.10), channel_id=1, source_target_pairs={{0,8},{1,9},{2,10},{3,11},{4,12},{5,13},{6,14},{7,15},{8,0},{9,1},... | collective-permute-start | bytes 307208 | tf_op jit(solution)/shard_map/ppermute | solution.py:31
  77.9 9.8 %collective-permute-start.16 = (f32[200,128]{1,0:T(8,128)S(1)}, f32[200,128]{1,0:T(8,128)S(1)}, u32[]{:S(2)}, u32[]{:S(2)}) collective-permute-start(f32[200,128]{1,0:T(8,128)S(1)} %fusion.10), channel_id=1, source_target_pairs={{0,16},{1,17},{2,18},{3,19},{4,20},{5,21},{6,22},{7,23},{8,24},{9,... | collective-permute-start | bytes 307208 | tf_op jit(solution)/shard_map/ppermute | solution.py:31
  79.9 7.7 %collective-permute-start.17 = (f32[200,128]{1,0:T(8,128)S(1)}, f32[200,128]{1,0:T(8,128)S(1)}, u32[]{:S(2)}, u32[]{:S(2)}) collective-permute-start(f32[200,128]{1,0:T(8,128)S(1)} %fusion.10), channel_id=1, source_target_pairs={{0,24},{1,25},{2,26},{3,27},{4,28},{5,29},{6,30},{7,31},{8,16},{9,... | collective-permute-start | bytes 307208 | tf_op jit(solution)/shard_map/ppermute | solution.py:31
  87.9 4.9 %collective-permute-start.18 = (f32[192,128]{1,0:T(8,128)S(1)}, f32[192,128]{1,0:T(8,128)S(1)}, u32[]{:S(2)}, u32[]{:S(2)}) collective-permute-start(f32[192,128]{1,0:T(8,128)S(1)} %get-tuple-element.47), channel_id=1, source_target_pairs={{0,1},{1,0},{2,3},{3,2},{4,5},{5,4},{6,7},{7,6},{8,9},{9,8},{10,11... | collective-permute-start | bytes 294920 | tf_op jit(solution)/shard_map/ppermute | solution.py:31
  89.8 4.6 %collective-permute-start.19 = (f32[192,128]{1,0:T(8,128)S(1)}, f32[192,128]{1,0:T(8,128)S(1)}, u32[]{:S(2)}, u32[]{:S(2)}) collective-permute-start(f32[192,128]{1,0:T(8,128)S(1)} %get-tuple-element.47), channel_id=1, source_target_pairs={{0,2},{1,3},{2,0},{3,1},{4,6},{5,7},{6,4},{7,5},{8,10},{9,11},{10,... | collective-permute-start | bytes 294920 | tf_op jit(solution)/shard_map/ppermute | solution.py:31
  89.9 5.6 %collective-permute-start.20 = (f32[192,128]{1,0:T(8,128)S(1)}, f32[192,128]{1,0:T(8,128)S(1)}, u32[]{:S(2)}, u32[]{:S(2)}) collective-permute-start(f32[192,128]{1,0:T(8,128)S(1)} %get-tuple-element.47), channel_id=1, source_target_pairs={{0,3},{1,2},{2,1},{3,0},{4,7},{5,6},{6,5},{7,4},{8,11},{9,10},{10,... | collective-permute-start | bytes 294920 | tf_op jit(solution)/shard_map/ppermute | solution.py:31
  95.6 1.8 %collective-permute-start.21 = (f32[4,192,128]{2,1,0:T(8,128)S(1)}, f32[4,192,128]{2,1,0:T(8,128)S(1)}, u32[]{:S(2)}, u32[]{:S(2)}) collective-permute-start(f32[4,192,128]{2,1,0:T(8,128)S(1)} %get-tuple-element.29), channel_id=1, source_target_pairs={{0,4},{1,5},{2,6},{3,7},{4,0},{5,1},{6,2},{7,3},{8,12},{9,13},{10,... | collective-permute-start | bytes 1179656 | tf_op jit(solution)/shard_map/ppermute | solution.py:31
  99.8 14.5 %all-to-all-start.1 = ((f32[32,16,128]{2,1,0:T(8,128)}), f32[32,16,128]{2,1,0:T(8,128)S(1)}, u32[]{:S(2)}, u32[]{:S(2)}) async-start(f32[32,16,128]{2,1,0:T(8,128)} %bitcast.44), calls=%async_computation.1 | async-start | bytes 524288 | tf_op jit(solution)/shard_map/all_to_all | solution.py:21

commit v9 on v8

--- a/solution.py
+++ b/solution.py
@@ -10,7 +10,7 @@
 AXES = ("row", "col")
 F32, BF16 = jnp.float32, jnp.bfloat16
 PAD = 8
-ROWS = 512
+ROWS = 1024
 MIB = 1024 * 1024
 T1_MIB = 52
 PREP_KIB = 54528
@@ -257,7 +257,7 @@
     return pl.pallas_call(
         turn_kernel,
         grid=(columns // block,),
-        in_specs=[columns_spec(m), full((m, rank)), columns_spec(rank), full((min(PAD, extra.shape[0]), rank))],
+        in_specs=[columns_spec(m), full((m, rank)), columns_spec(rank), full((1, rank))],
         out_specs=[columns_spec(rank), full((parts, tall, rank))],
         out_shape=[
             jax.ShapeDtypeStruct((rank, columns), F32),
@@ -373,7 +373,7 @@
         return own * total[:rows_own] / total[rows_own][None, :]
 
     right, summed = full_turn(
-        tensor_slab, left_init, right_init, left_init, k, parts, T1_MIB * MIB
+        tensor_slab, left_init, right_init, col_part, k, parts, T1_MIB * MIB
     )
     summed, arrived = lax.optimization_barrier((summed, arrived))
     summed = summed.reshape(2, col_devices, rows_own + PAD, rank)

time: 115 us -> 116 us (level)
  no operation moved by 1% of the time
where the time goes in v9:
time: 116 us; the launch traced here: 115 us
  waiting for transfers between devices  44.4 us (38%)
  starting transfers between devices  34.3 us (30%)
  Pallas kernels  31.1 us (27%)
  local copies, waits for them, and re-layouts  2.83 us (2%)
  other arithmetic  1.72 us (1%)
    ppermute x22, waiting for transfers between devices, send(): return lax.ppermute(values, AXES, pairs)  31.9 us
    pallas_call x2, Pallas kernels, full_turn(): pl.pallas_call(turn_kernel, grid=(columns // block,), in_specs=[columns_s...  24.9 us
    ppermute x22, starting transfers between devices, send(): return lax.ppermute(values, AXES, pairs)  23.5 us
    all_to_all x2, waiting for transfers between devices, exchange(): return lax.all_to_all(parts, AXES, split_axis=0, concat_axis=0, tiled=True)  12.5 us
    all_to_all x2, starting transfers between devices, exchange(): return lax.all_to_all(parts, AXES, split_axis=0, concat_axis=0, tiled=True)  10.8 us
    pallas_call x1, Pallas kernels, prepare(): pl.pallas_call(functools.partial(prepare_kernel, slices), grid_spec=pltpu...  2.38 us
  transfers between devices with their start and end apart: 24, of which 21 were waited for; matrix products, arithmetic and copies ran while one was open for 1% of the time, Pallas kernels for 11%

profile of v9, /device:TPU:0, one launch (start us, length us, event | category | flops | bytes accessed | tf_op | source)
XLA Modules:
  0.0 115.3 jit_solution(15893493843245541028)
XLA Ops:
  0.6 0.1 pad_add_fusion.place_ref
  0.7 0.8 copy-done.1
  1.6 2.4 %prepare.1 = (f32[32,32,128]{2,1,0:T(8,128)}, f32[1,128]{1,0:T(1,128)S(1)}, f32[128,128]{1,0:T(8,128)S(1)}) custom-call(s32[3]{0:T(128)S(1)} %pad_add_fusion.place_ref, f32[2048,128]{1,0:T(8,128)} %second_left_ref.1, f32[128,128]{1,0:T(8,128)S(1)} %copy-done.1, f32[1024,128]{1,0:T(8,128)} %left_ref.3), custom_call_target="tpu_custom_call" | custom-call | flops 65536 | bytes 786432 | tf_op jit(solution)/shard_map/prepare/pallas_call | solution.py:322
  3.9 7.3 %all-to-all-start = ((f32[32,32,128]{2,1,0:T(8,128)}), f32[32,32,128]{2,1,0:T(8,128)S(1)}, u32[]{:S(2)}, u32[]{:S(2)}) async-start(f32[32,32,128]{2,1,0:T(8,128)} %get-tuple-element.14), calls=%async_computation | async-start | bytes 1048576 | tf_op jit(solution)/shard_map/all_to_all | solution.py:21
  11.3 0.0 copy-start
  11.3 1.0 copy-done
  12.3 12.8 %turn.2 = (f32[128,2048]{1,0:T(8,128)}, f32[8,136,128]{2,1,0:T(8,128)S(1)}) custom-call(f32[1024,2048]{1,0:T(8,128)} %slab_ref.3, f32[1024,128]{1,0:T(8,128)S(1)} %copy-done, f32[128,2048]{1,0:T(8,128)} %right_ref.1, f32[1,128]{1,0:T(1,128)S(1)} %get-tuple-element.12.extra_ref), custom_call_target="tpu_custom_call" | custom-call | flops 6442450944 | bytes 8388608 | tf_op jit(solution)/shard_map/turn/pallas_call | solution.py:257
  25.1 2.4 %all-to-all-done = f32[32,32,128]{2,1,0:T(8,128)S(1)} async-done(((f32[32,32,128]{2,1,0:T(8,128)}), f32[32,32,128]{2,1,0:T(8,128)S(1)}, u32[]{:S(2)}, u32[]{:S(2)}) %all-to-all-start) | async-done | bytes 524320 | tf_op jit(solution)/shard_map/all_to_all | solution.py:21
  27.5 0.1 collective-permute-start
  27.6 1.5 %collective-permute-done = f32[4,136,128]{2,1,0:T(8,128)S(1)} collective-permute-done((f32[4,136,128]{2,1,0:T(8,128)S(1)}, f32[4,136,128]{2,1,0:T(8,128)S(1)}, u32[]{:S(2)}, u32[]{:S(2)}) %collective-permute-start) | collective-permute-done | bytes 278560 | tf_op jit(solution)/shard_map/ppermute | solution.py:31
  29.2 0.3 collective-permute-start.1
  29.5 1.5 %collective-permute-start.2 = (f32[136,128]{1,0:T(8,128)S(1)}, f32[136,128]{1,0:T(8,128)S(1)}, u32[]{:S(2)}, u32[]{:S(2)}) collective-permute-start(f32[136,128]{1,0:T(8,128)S(1)} %get-tuple-element.36), channel_id=1, source_target_pairs={{0,2},{1,3},{2,0},{3,1},{4,6},{5,7},{6,4},{7,5},{8,10},{9,11},{10,... | collective-permute-start | bytes 208904 | tf_op jit(solution)/shard_map/ppermute | solution.py:31
  31.0 1.8 %collective-permute-start.3 = (f32[136,128]{1,0:T(8,128)S(1)}, f32[136,128]{1,0:T(8,128)S(1)}, u32[]{:S(2)}, u32[]{:S(2)}) collective-permute-start(f32[136,128]{1,0:T(8,128)S(1)} %get-tuple-element.35), channel_id=1, source_target_pairs={{0,3},{1,2},{2,1},{3,0},{4,7},{5,6},{6,5},{7,4},{8,11},{9,10},{10,... | collective-permute-start | bytes 208904 | tf_op jit(solution)/shard_map/ppermute | solution.py:31
  32.8 1.2 %collective-permute-done.1 = f32[136,128]{1,0:T(8,128)S(1)} collective-permute-done((f32[136,128]{1,0:T(8,128)S(1)}, f32[136,128]{1,0:T(8,128)S(1)}, u32[]{:S(2)}, u32[]{:S(2)}) %collective-permute-start.1) | collective-permute-done | bytes 69664 | tf_op jit(solution)/shard_map/ppermute | solution.py:31
  34.0 0.0 collective-permute-done.2
  34.0 2.2 %collective-permute-done.3 = f32[136,128]{1,0:T(8,128)S(1)} collective-permute-done((f32[136,128]{1,0:T(8,128)S(1)}, f32[136,128]{1,0:T(8,128)S(1)}, u32[]{:S(2)}, u32[]{:S(2)}) %collective-permute-start.3) | collective-permute-done | bytes 69664 | tf_op jit(solution)/shard_map/ppermute | solution.py:31
  36.2 0.6 collective-permute-start.4
  36.9 2.5 %collective-permute-start.5 = (f32[136,128]{1,0:T(8,128)S(1)}, f32[136,128]{1,0:T(8,128)S(1)}, u32[]{:S(2)}, u32[]{:S(2)}) collective-permute-start(f32[136,128]{1,0:T(8,128)S(1)} %fusion.11), channel_id=1, source_target_pairs={{0,16},{1,17},{2,18},{3,19},{4,20},{5,21},{6,22},{7,23},{8,24},{9,... | collective-permute-start | bytes 208904 | tf_op jit(solution)/shard_map/ppermute | solution.py:31
  39.3 1.4 %collective-permute-start.6 = (f32[136,128]{1,0:T(8,128)S(1)}, f32[136,128]{1,0:T(8,128)S(1)}, u32[]{:S(2)}, u32[]{:S(2)}) collective-permute-start(f32[136,128]{1,0:T(8,128)S(1)} %fusion.11), channel_id=1, source_target_pairs={{0,24},{1,25},{2,26},{3,27},{4,28},{5,29},{6,30},{7,31},{8,16},{9,... | collective-permute-start | bytes 208904 | tf_op jit(solution)/shard_map/ppermute | solution.py:31
  40.7 0.0 collective-permute-done.4
  40.7 2.9 %collective-permute-done.5 = f32[136,128]{1,0:T(8,128)S(1)} collective-permute-done((f32[136,128]{1,0:T(8,128)S(1)}, f32[136,128]{1,0:T(8,128)S(1)}, u32[]{:S(2)}, u32[]{:S(2)}) %collective-permute-start.5) | collective-permute-done | bytes 69664 | tf_op jit(solution)/shard_map/ppermute | solution.py:31
  43.6 1.9 %collective-permute-done.6 = f32[136,128]{1,0:T(8,128)S(1)} collective-permute-done((f32[136,128]{1,0:T(8,128)S(1)}, f32[136,128]{1,0:T(8,128)S(1)}, u32[]{:S(2)}, u32[]{:S(2)}) %collective-permute-start.6) | collective-permute-done | bytes 69664 | tf_op jit(solution)/shard_map/ppermute | solution.py:31
  45.5 0.6 collective-permute-start.7
  46.1 0.9 collective-permute-start.8
  47.0 2.0 %collective-permute-start.9 = (f32[128,128]{1,0:T(8,128)S(1)}, f32[128,128]{1,0:T(8,128)S(1)}, u32[]{:S(2)}, u32[]{:S(2)}) collective-permute-start(f32[128,128]{1,0:T(8,128)S(1)} %fusion.13), channel_id=1, source_target_pairs={{0,3},{1,2},{2,1},{3,0},{4,7},{5,6},{6,5},{7,4},{8,11},{9,10},{10,... | collective-permute-start | bytes 196616 | tf_op jit(solution)/shard_map/ppermute | solution.py:31
  49.0 0.8 collective-permute-done.7
  49.8 0.6 collective-permute-done.8
  50.4 1.8 %collective-permute-done.9 = f32[128,128]{1,0:T(8,128)S(1)} collective-permute-done((f32[128,128]{1,0:T(8,128)S(1)}, f32[128,128]{1,0:T(8,128)S(1)}, u32[]{:S(2)}, u32[]{:S(2)}) %collective-permute-start.9) | collective-permute-done | bytes 65568 | tf_op jit(solution)/shard_map/ppermute | solution.py:31
  52.3 0.1 collective-permute-start.10
  52.4 1.5 %collective-permute-done.10 = f32[4,128,128]{2,1,0:T(8,128)S(1)} collective-permute-done((f32[4,128,128]{2,1,0:T(8,128)S(1)}, f32[4,128,128]{2,1,0:T(8,128)S(1)}, u32[]{:S(2)}, u32[]{:S(2)}) %collective-permute-start.10) | collective-permute-done | bytes 262176 | tf_op jit(solution)/shard_map/ppermute | solution.py:31
  53.9 0.1 fusion.9
  54.0 12.2 %turn.3 = (f32[128,2048]{1,0:T(8,128)S(1)}, f32[8,136,128]{2,1,0:T(8,128)S(1)}) custom-call(f32[1024,2048]{1,0:T(8,128)} %slab_ref.3, f32[1024,128]{1,0:T(8,128)S(1)} %bitcast.82, f32[128,2048]{1,0:T(8,128)} %get-tuple-element.16.right_ref, f32[1,128]{1,0:T(1,128)S(1)} %get-tuple-element.12.extra_ref), custom_call_target="tpu_custom_call" | custom-call | flops 6442450944 | bytes 8388608 | tf_op jit(solution)/shard_map/turn/pallas_call | solution.py:257
  66.2 1.6 %second_numerator.1 = f32[4,128,128]{2,1,0:T(8,128)S(1)} custom-call(f32[128,2048]{1,0:T(8,128)S(1)} %get-tuple-element.18.right_ref, f32[512,128]{1,0:T(8,128)S(1)} %bitcast.73, f32[4,128,128]{2,1,0:T(8,128)S(1)} %bitcast.75), custom_call_target="tpu_custom_call" | custom-call | flops 402653184 | bytes 1048576 | tf_op jit(solution)/shard_map/second_numerator/pallas_call | solution.py:276
  67.8 0.2 collective-permute-start.11
  68.0 1.6 %collective-permute-done.11 = f32[4,200,128]{2,1,0:T(8,128)S(1)} collective-permute-done((f32[4,200,128]{2,1,0:T(8,128)S(1)}, f32[4,200,128]{2,1,0:T(8,128)S(1)}, u32[]{:S(2)}, u32[]{:S(2)}) %collective-permute-start.11) | collective-permute-done | bytes 409632 | tf_op jit(solution)/shard_map/ppermute | solution.py:31
  69.7 0.1 fusion.5
  69.7 1.2 %collective-permute-start.12 = (f32[200,128]{1,0:T(8,128)S(1)}, f32[200,128]{1,0:T(8,128)S(1)}, u32[]{:S(2)}, u32[]{:S(2)}) collective-permute-start(f32[200,128]{1,0:T(8,128)S(1)} %get-tuple-element.28), channel_id=1, source_target_pairs={{0,1},{1,0},{2,3},{3,2},{4,5},{5,4},{6,7},{7,6},{8,9},{9,8},{10,11... | collective-permute-start | bytes 307208 | tf_op jit(solution)/shard_map/ppermute | solution.py:31
  71.0 1.4 %collective-permute-start.13 = (f32[200,128]{1,0:T(8,128)S(1)}, f32[200,128]{1,0:T(8,128)S(1)}, u32[]{:S(2)}, u32[]{:S(2)}) collective-permute-start(f32[200,128]{1,0:T(8,128)S(1)} %get-tuple-element.27), channel_id=1, source_target_pairs={{0,2},{1,3},{2,0},{3,1},{4,6},{5,7},{6,4},{7,5},{8,10},{9,11},{10,... | collective-permute-start | bytes 307208 | tf_op jit(solution)/shard_map/ppermute | solution.py:31
  72.4 0.9 collective-permute-start.14
  73.3 1.5 %collective-permute-done.12 = f32[200,128]{1,0:T(8,128)S(1)} collective-permute-done((f32[200,128]{1,0:T(8,128)S(1)}, f32[200,128]{1,0:T(8,128)S(1)}, u32[]{:S(2)}, u32[]{:S(2)}) %collective-permute-start.12) | collective-permute-done | bytes 102432 | tf_op jit(solution)/shard_map/ppermute | solution.py:31
  74.8 1.9 %collective-permute-done.13 = f32[200,128]{1,0:T(8,128)S(1)} collective-permute-done((f32[200,128]{1,0:T(8,128)S(1)}, f32[200,128]{1,0:T(8,128)S(1)}, u32[]{:S(2)}, u32[]{:S(2)}) %collective-permute-start.13) | collective-permute-done | bytes 102432 | tf_op jit(solution)/shard_map/ppermute | solution.py:31
  76.8 1.2 %collective-permute-done.14 = f32[200,128]{1,0:T(8,128)S(1)} collective-permute-done((f32[200,128]{1,0:T(8,128)S(1)}, f32[200,128]{1,0:T(8,128)S(1)}, u32[]{:S(2)}, u32[]{:S(2)}) %collective-permute-start.14) | collective-permute-done | bytes 102432 | tf_op jit(solution)/shard_map/ppermute | solution.py:31
  78.0 0.1 collective-permute-start.15
  78.1 2.0 %collective-permute-start.16 = (f32[200,128]{1,0:T(8,128)S(1)}, f32[200,128]{1,0:T(8,128)S(1)}, u32[]{:S(2)}, u32[]{:S(2)}) collective-permute-start(f32[200,128]{1,0:T(8,128)S(1)} %fusion.10), channel_id=1, source_target_pairs={{0,16},{1,17},{2,18},{3,19},{4,20},{5,21},{6,22},{7,23},{8,24},{9,... | collective-permute-start | bytes 307208 | tf_op jit(solution)/shard_map/ppermute | solution.py:31
  80.1 2.4 %collective-permute-start.17 = (f32[200,128]{1,0:T(8,128)S(1)}, f32[200,128]{1,0:T(8,128)S(1)}, u32[]{:S(2)}, u32[]{:S(2)}) collective-permute-start(f32[200,128]{1,0:T(8,128)S(1)} %fusion.10), channel_id=1, source_target_pairs={{0,24},{1,25},{2,26},{3,27},{4,28},{5,29},{6,30},{7,31},{8,16},{9,... | collective-permute-start | bytes 307208 | tf_op jit(solution)/shard_map/ppermute | solution.py:31
  82.4 0.3 collective-permute-done.15
  82.7 5.2 %collective-permute-done.16 = f32[200,128]{1,0:T(8,128)S(1)} collective-permute-done((f32[200,128]{1,0:T(8,128)S(1)}, f32[200,128]{1,0:T(8,128)S(1)}, u32[]{:S(2)}, u32[]{:S(2)}) %collective-permute-start.16) | collective-permute-done | bytes 102432 | tf_op jit(solution)/shard_map/ppermute | solution.py:31
  87.9 0.0 collective-permute-done.17
  87.9 0.1 broadcast_divide_fusion
  88.1 1.9 %collective-permute-start.18 = (f32[192,128]{1,0:T(8,128)S(1)}, f32[192,128]{1,0:T(8,128)S(1)}, u32[]{:S(2)}, u32[]{:S(2)}) collective-permute-start(f32[192,128]{1,0:T(8,128)S(1)} %get-tuple-element.47), channel_id=1, source_target_pairs={{0,1},{1,0},{2,3},{3,2},{4,5},{5,4},{6,7},{7,6},{8,9},{9,8},{10,11... | collective-permute-start | bytes 294920 | tf_op jit(solution)/shard_map/ppermute | solution.py:31
  90.0 0.4 collective-permute-start.19
  90.3 1.3 %collective-permute-start.20 = (f32[192,128]{1,0:T(8,128)S(1)}, f32[192,128]{1,0:T(8,128)S(1)}, u32[]{:S(2)}, u32[]{:S(2)}) collective-permute-start(f32[192,128]{1,0:T(8,128)S(1)} %get-tuple-element.47), channel_id=1, source_target_pairs={{0,3},{1,2},{2,1},{3,0},{4,7},{5,6},{6,5},{7,4},{8,11},{9,10},{10,... | collective-permute-start | bytes 294920 | tf_op jit(solution)/shard_map/ppermute | solution.py:31
  91.7 1.3 %collective-permute-done.18 = f32[192,128]{1,0:T(8,128)S(1)} collective-permute-done((f32[192,128]{1,0:T(8,128)S(1)}, f32[192,128]{1,0:T(8,128)S(1)}, u32[]{:S(2)}, u32[]{:S(2)}) %collective-permute-start.18) | collective-permute-done | bytes 98336 | tf_op jit(solution)/shard_map/ppermute | solution.py:31
  93.0 1.6 %collective-permute-done.19 = f32[192,128]{1,0:T(8,128)S(1)} collective-permute-done((f32[192,128]{1,0:T(8,128)S(1)}, f32[192,128]{1,0:T(8,128)S(1)}, u32[]{:S(2)}, u32[]{:S(2)}) %collective-permute-start.19) | collective-permute-done | bytes 98336 | tf_op jit(solution)/shard_map/ppermute | solution.py:31
  94.6 1.3 %collective-permute-done.20 = f32[192,128]{1,0:T(8,128)S(1)} collective-permute-done((f32[192,128]{1,0:T(8,128)S(1)}, f32[192,128]{1,0:T(8,128)S(1)}, u32[]{:S(2)}, u32[]{:S(2)}) %collective-permute-start.20) | collective-permute-done | bytes 98336 | tf_op jit(solution)/shard_map/ppermute | solution.py:31
  95.9 0.1 pad_maximum_fusion.2
  96.0 0.1 collective-permute-start.21
  96.0 1.7 %collective-permute-done.21 = f32[4,192,128]{2,1,0:T(8,128)S(1)} collective-permute-done((f32[4,192,128]{2,1,0:T(8,128)S(1)}, f32[4,192,128]{2,1,0:T(8,128)S(1)}, u32[]{:S(2)}, u32[]{:S(2)}) %collective-permute-start.21) | collective-permute-done | bytes 393248 | tf_op jit(solution)/shard_map/ppermute | solution.py:31
  97.8 0.2 fusion.6
  97.9 2.2 %second_rows.1 = f32[512,128]{1,0:T(8,128)} custom-call(f32[128,2048]{1,0:T(8,128)S(1)} %get-tuple-element.18.right_ref, f32[512,128]{1,0:T(8,128)S(1)} %bitcast.74, f32[4,128,128]{2,1,0:T(8,128)S(1)} %bitcast.81), custom_call_target="tpu_custom_call" | custom-call | flops 402653184 | bytes 1048576 | tf_op jit(solution)/shard_map/second_rows/pallas_call | solution.py:286
  100.1 3.5 %all-to-all-start.1 = ((f32[32,16,128]{2,1,0:T(8,128)}), f32[32,16,128]{2,1,0:T(8,128)S(1)}, u32[]{:S(2)}, u32[]{:S(2)}) async-start(f32[32,16,128]{2,1,0:T(8,128)} %bitcast.44), calls=%async_computation.1 | async-start | bytes 524288 | tf_op jit(solution)/shard_map/all_to_all | solution.py:21
  103.6 0.8 fusion
  104.4 10.1 %all-to-all-done.1 = f32[32,16,128]{2,1,0:T(8,128)S(1)} async-done(((f32[32,16,128]{2,1,0:T(8,128)}), f32[32,16,128]{2,1,0:T(8,128)S(1)}, u32[]{:S(2)}, u32[]{:S(2)}) %all-to-all-start.1) | async-done | bytes 262176 | tf_op jit(solution)/shard_map/all_to_all | solution.py:21
  114.6 0.7 copy.8
  (25 shorter events, 0.6 us)
Async XLA Ops:
  0.7 0.8 copy-start.1
  3.9 23.6 %all-to-all-start = ((f32[32,32,128]{2,1,0:T(8,128)}), f32[32,32,128]{2,1,0:T(8,128)S(1)}, u32[]{:S(2)}, u32[]{:S(2)}) async-start(f32[32,32,128]{2,1,0:T(8,128)} %get-tuple-element.14), calls=%async_computation | async-start | bytes 1048576 | tf_op jit(solution)/shard_map/all_to_all | solution.py:21
  11.3 1.0 copy-start
  27.5 1.6 %collective-permute-start = (f32[4,136,128]{2,1,0:T(8,128)S(1)}, f32[4,136,128]{2,1,0:T(8,128)S(1)}, u32[]{:S(2)}, u32[]{:S(2)}) collective-permute-start(f32[4,136,128]{2,1,0:T(8,128)S(1)} %dynamic-slice_bitcast_fusion), channel_id=1, source_target_pairs={{0,4},{1,5},{2,6},{3,7},{4,0},{5,1},{6,2},{7,3},{8,12},{9,13},{10,... | collective-permute-start | bytes 835592 | tf_op jit(solution)/shard_map/ppermute | solution.py:31
  29.2 4.8 %collective-permute-start.1 = (f32[136,128]{1,0:T(8,128)S(1)}, f32[136,128]{1,0:T(8,128)S(1)}, u32[]{:S(2)}, u32[]{:S(2)}) collective-permute-start(f32[136,128]{1,0:T(8,128)S(1)} %get-tuple-element.37), channel_id=1, source_target_pairs={{0,1},{1,0},{2,3},{3,2},{4,5},{5,4},{6,7},{7,6},{8,9},{9,8},{10,11... | collective-permute-start | bytes 208904 | tf_op jit(solution)/shard_map/ppermute | solution.py:31
  29.5 4.5 %collective-permute-start.2 = (f32[136,128]{1,0:T(8,128)S(1)}, f32[136,128]{1,0:T(8,128)S(1)}, u32[]{:S(2)}, u32[]{:S(2)}) collective-permute-start(f32[136,128]{1,0:T(8,128)S(1)} %get-tuple-element.36), channel_id=1, source_target_pairs={{0,2},{1,3},{2,0},{3,1},{4,6},{5,7},{6,4},{7,5},{8,10},{9,11},{10,... | collective-permute-start | bytes 208904 | tf_op jit(solution)/shard_map/ppermute | solution.py:31
  31.0 5.2 %collective-permute-start.3 = (f32[136,128]{1,0:T(8,128)S(1)}, f32[136,128]{1,0:T(8,128)S(1)}, u32[]{:S(2)}, u32[]{:S(2)}) collective-permute-start(f32[136,128]{1,0:T(8,128)S(1)} %get-tuple-element.35), channel_id=1, source_target_pairs={{0,3},{1,2},{2,1},{3,0},{4,7},{5,6},{6,5},{7,4},{8,11},{9,10},{10,... | collective-permute-start | bytes 208904 | tf_op jit(solution)/shard_map/ppermute | solution.py:31
  36.2 4.5 %collective-permute-start.4 = (f32[136,128]{1,0:T(8,128)S(1)}, f32[136,128]{1,0:T(8,128)S(1)}, u32[]{:S(2)}, u32[]{:S(2)}) collective-permute-start(f32[136,128]{1,0:T(8,128)S(1)} %fusion.11), channel_id=1, source_target_pairs={{0,8},{1,9},{2,10},{3,11},{4,12},{5,13},{6,14},{7,15},{8,0},{9,1},... | collective-permute-start | bytes 208904 | tf_op jit(solution)/shard_map/ppermute | solution.py:31
  36.9 6.7 %collective-permute-start.5 = (f32[136,128]{1,0:T(8,128)S(1)}, f32[136,128]{1,0:T(8,128)S(1)}, u32[]{:S(2)}, u32[]{:S(2)}) collective-permute-start(f32[136,128]{1,0:T(8,128)S(1)} %fusion.11), channel_id=1, source_target_pairs={{0,16},{1,17},{2,18},{3,19},{4,20},{5,21},{6,22},{7,23},{8,24},{9,... | collective-permute-start | bytes 208904 | tf_op jit(solution)/shard_map/ppermute | solution.py:31
  39.3 6.1 %collective-permute-start.6 = (f32[136,128]{1,0:T(8,128)S(1)}, f32[136,128]{1,0:T(8,128)S(1)}, u32[]{:S(2)}, u32[]{:S(2)}) collective-permute-start(f32[136,128]{1,0:T(8,128)S(1)} %fusion.11), channel_id=1, source_target_pairs={{0,24},{1,25},{2,26},{3,27},{4,28},{5,29},{6,30},{7,31},{8,16},{9,... | collective-permute-start | bytes 208904 | tf_op jit(solution)/shard_map/ppermute | solution.py:31
  45.5 4.3 %collective-permute-start.7 = (f32[128,128]{1,0:T(8,128)S(1)}, f32[128,128]{1,0:T(8,128)S(1)}, u32[]{:S(2)}, u32[]{:S(2)}) collective-permute-start(f32[128,128]{1,0:T(8,128)S(1)} %fusion.13), channel_id=1, source_target_pairs={{0,1},{1,0},{2,3},{3,2},{4,5},{5,4},{6,7},{7,6},{8,9},{9,8},{10,11... | collective-permute-start | bytes 196616 | tf_op jit(solution)/shard_map/ppermute | solution.py:31
  46.1 4.3 %collective-permute-start.8 = (f32[128,128]{1,0:T(8,128)S(1)}, f32[128,128]{1,0:T(8,128)S(1)}, u32[]{:S(2)}, u32[]{:S(2)}) collective-permute-start(f32[128,128]{1,0:T(8,128)S(1)} %fusion.13), channel_id=1, source_target_pairs={{0,2},{1,3},{2,0},{3,1},{4,6},{5,7},{6,4},{7,5},{8,10},{9,11},{10,... | collective-permute-start | bytes 196616 | tf_op jit(solution)/shard_map/ppermute | solution.py:31
  47.0 5.2 %collective-permute-start.9 = (f32[128,128]{1,0:T(8,128)S(1)}, f32[128,128]{1,0:T(8,128)S(1)}, u32[]{:S(2)}, u32[]{:S(2)}) collective-permute-start(f32[128,128]{1,0:T(8,128)S(1)} %fusion.13), channel_id=1, source_target_pairs={{0,3},{1,2},{2,1},{3,0},{4,7},{5,6},{6,5},{7,4},{8,11},{9,10},{10,... | collective-permute-start | bytes 196616 | tf_op jit(solution)/shard_map/ppermute | solution.py:31
  52.3 1.6 %collective-permute-start.10 = (f32[4,128,128]{2,1,0:T(8,128)S(1)}, f32[4,128,128]{2,1,0:T(8,128)S(1)}, u32[]{:S(2)}, u32[]{:S(2)}) collective-permute-start(f32[4,128,128]{2,1,0:T(8,128)S(1)} %get-tuple-element.38), channel_id=1, source_target_pairs={{0,4},{1,5},{2,6},{3,7},{4,0},{5,1},{6,2},{7,3},{8,12},{9,13},{10,... | collective-permute-start | bytes 786440 | tf_op jit(solution)/shard_map/ppermute | solution.py:31
  67.8 1.8 %collective-permute-start.11 = (f32[4,200,128]{2,1,0:T(8,128)S(1)}, f32[4,200,128]{2,1,0:T(8,128)S(1)}, u32[]{:S(2)}, u32[]{:S(2)}) collective-permute-start(f32[4,200,128]{2,1,0:T(8,128)S(1)} %fusion.2), channel_id=1, source_target_pairs={{0,4},{1,5},{2,6},{3,7},{4,0},{5,1},{6,2},{7,3},{8,12},{9,13},{10,... | collective-permute-start | bytes 1228808 | tf_op jit(solution)/shard_map/ppermute | solution.py:31
  69.7 5.1 %collective-permute-start.12 = (f32[200,128]{1,0:T(8,128)S(1)}, f32[200,128]{1,0:T(8,128)S(1)}, u32[]{:S(2)}, u32[]{:S(2)}) collective-permute-start(f32[200,128]{1,0:T(8,128)S(1)} %get-tuple-element.28), channel_id=1, source_target_pairs={{0,1},{1,0},{2,3},{3,2},{4,5},{5,4},{6,7},{7,6},{8,9},{9,8},{10,11... | collective-permute-start | bytes 307208 | tf_op jit(solution)/shard_map/ppermute | solution.py:31
  71.0 5.8 %collective-permute-start.13 = (f32[200,128]{1,0:T(8,128)S(1)}, f32[200,128]{1,0:T(8,128)S(1)}, u32[]{:S(2)}, u32[]{:S(2)}) collective-permute-start(f32[200,128]{1,0:T(8,128)S(1)} %get-tuple-element.27), channel_id=1, source_target_pairs={{0,2},{1,3},{2,0},{3,1},{4,6},{5,7},{6,4},{7,5},{8,10},{9,11},{10,... | collective-permute-start | bytes 307208 | tf_op jit(solution)/shard_map/ppermute | solution.py:31
  72.4 5.6 %collective-permute-start.14 = (f32[200,128]{1,0:T(8,128)S(1)}, f32[200,128]{1,0:T(8,128)S(1)}, u32[]{:S(2)}, u32[]{:S(2)}) collective-permute-start(f32[200,128]{1,0:T(8,128)S(1)} %get-tuple-element.26), channel_id=1, source_target_pairs={{0,3},{1,2},{2,1},{3,0},{4,7},{5,6},{6,5},{7,4},{8,11},{9,10},{10,... | collective-permute-start | bytes 307208 | tf_op jit(solution)/shard_map/ppermute | solution.py:31
  78.0 4.7 %collective-permute-start.15 = (f32[200,128]{1,0:T(8,128)S(1)}, f32[200,128]{1,0:T(8,128)S(1)}, u32[]{:S(2)}, u32[]{:S(2)}) collective-permute-start(f32[200,128]{1,0:T(8,128)S(1)} %fusion.10), channel_id=1, source_target_pairs={{0,8},{1,9},{2,10},{3,11},{4,12},{5,13},{6,14},{7,15},{8,0},{9,1},... | collective-permute-start | bytes 307208 | tf_op jit(solution)/shard_map/ppermute | solution.py:31
  78.1 9.8 %collective-permute-start.16 = (f32[200,128]{1,0:T(8,128)S(1)}, f32[200,128]{1,0:T(8,128)S(1)}, u32[]{:S(2)}, u32[]{:S(2)}) collective-permute-start(f32[200,128]{1,0:T(8,128)S(1)} %fusion.10), channel_id=1, source_target_pairs={{0,16},{1,17},{2,18},{3,19},{4,20},{5,21},{6,22},{7,23},{8,24},{9,... | collective-permute-start | bytes 307208 | tf_op jit(solution)/shard_map/ppermute | solution.py:31
  80.1 7.8 %collective-permute-start.17 = (f32[200,128]{1,0:T(8,128)S(1)}, f32[200,128]{1,0:T(8,128)S(1)}, u32[]{:S(2)}, u32[]{:S(2)}) collective-permute-start(f32[200,128]{1,0:T(8,128)S(1)} %fusion.10), channel_id=1, source_target_pairs={{0,24},{1,25},{2,26},{3,27},{4,28},{5,29},{6,30},{7,31},{8,16},{9,... | collective-permute-start | bytes 307208 | tf_op jit(solution)/shard_map/ppermute | solution.py:31
  88.1 4.9 %collective-permute-start.18 = (f32[192,128]{1,0:T(8,128)S(1)}, f32[192,128]{1,0:T(8,128)S(1)}, u32[]{:S(2)}, u32[]{:S(2)}) collective-permute-start(f32[192,128]{1,0:T(8,128)S(1)} %get-tuple-element.47), channel_id=1, source_target_pairs={{0,1},{1,0},{2,3},{3,2},{4,5},{5,4},{6,7},{7,6},{8,9},{9,8},{10,11... | collective-permute-start | bytes 294920 | tf_op jit(solution)/shard_map/ppermute | solution.py:31
  90.0 4.6 %collective-permute-start.19 = (f32[192,128]{1,0:T(8,128)S(1)}, f32[192,128]{1,0:T(8,128)S(1)}, u32[]{:S(2)}, u32[]{:S(2)}) collective-permute-start(f32[192,128]{1,0:T(8,128)S(1)} %get-tuple-element.47), channel_id=1, source_target_pairs={{0,2},{1,3},{2,0},{3,1},{4,6},{5,7},{6,4},{7,5},{8,10},{9,11},{10,... | collective-permute-start | bytes 294920 | tf_op jit(solution)/shard_map/ppermute | solution.py:31
  90.3 5.5 %collective-permute-start.20 = (f32[192,128]{1,0:T(8,128)S(1)}, f32[192,128]{1,0:T(8,128)S(1)}, u32[]{:S(2)}, u32[]{:S(2)}) collective-permute-start(f32[192,128]{1,0:T(8,128)S(1)} %get-tuple-element.47), channel_id=1, source_target_pairs={{0,3},{1,2},{2,1},{3,0},{4,7},{5,6},{6,5},{7,4},{8,11},{9,10},{10,... | collective-permute-start | bytes 294920 | tf_op jit(solution)/shard_map/ppermute | solution.py:31
  96.0 1.8 %collective-permute-start.21 = (f32[4,192,128]{2,1,0:T(8,128)S(1)}, f32[4,192,128]{2,1,0:T(8,128)S(1)}, u32[]{:S(2)}, u32[]{:S(2)}) collective-permute-start(f32[4,192,128]{2,1,0:T(8,128)S(1)} %get-tuple-element.29), channel_id=1, source_target_pairs={{0,4},{1,5},{2,6},{3,7},{4,0},{5,1},{6,2},{7,3},{8,12},{9,13},{10,... | collective-permute-start | bytes 1179656 | tf_op jit(solution)/shard_map/ppermute | solution.py:31
  100.1 14.4 %all-to-all-start.1 = ((f32[32,16,128]{2,1,0:T(8,128)}), f32[32,16,128]{2,1,0:T(8,128)S(1)}, u32[]{:S(2)}, u32[]{:S(2)}) async-start(f32[32,16,128]{2,1,0:T(8,128)} %bitcast.44), calls=%async_computation.1 | async-start | bytes 524288 | tf_op jit(solution)/shard_map/all_to_all | solution.py:21

commit v10 on v9

--- a/solution.py
+++ b/solution.py
@@ -12,7 +12,8 @@
 PAD = 8
 ROWS = 1024
 MIB = 1024 * 1024
-T1_MIB = 52
+T1_MIB = 51
+T2_MIB = 42
 PREP_KIB = 54528
 VMEM_BYTES = 51 * MIB
 
@@ -158,26 +159,6 @@
         out_ref[part, height:, :] = stats
 
 
-def turn_kernel(
-    slab_ref, left_ref, right_ref, extra_ref, right_out, left_out,
-    pair_ref, pair_t_ref, sums_ref, total_ref, row_sums_ref,
-):
-    step = pl.program_id(0)
-
-    @pl.when(step == 0)
-    def _():
-        prepare_left(left_ref, pair_ref)
-        prepare_left_t(left_ref, pair_t_ref, sums_ref)
-
-    right = right_update(slab_ref, pair_ref, pair_t_ref, sums_ref, right_ref[...])
-    right_out[...] = right
-    left_numerator(slab_ref, pair_ref, right, total_ref, row_sums_ref, step == 0)
-
-    @pl.when(step == pl.num_programs(0) - 1)
-    def _():
-        write_left(total_ref, row_sums_ref, extra_ref, left_out)
-
-
 def second_quotient(block, second_left, pairs):
     high, low = split(second_left)
     right_high, right_low = pairs
@@ -185,20 +166,51 @@
     return split(divide(block, product))
 
 
-def numerator_kernel(slices, right_ref, second_left_ref, second_right_ref, numer_out):
-    rank = right_ref.shape[0]
-    k = right_ref.shape[1] // slices
-    pairs = split(
-        jnp.concatenate([second_right_ref[block] for block in range(k // rank)], axis=1)
-    )
-    total = 0.0
-    for index in range(slices):
-        second_left = second_left_ref[pl.ds(index, rank, stride=slices), :]
-        high, low = second_quotient(right_ref[:, pl.ds(index * k, k)], second_left, pairs)
-        left_high, left_low = split(second_left.T)
-        total = total + (dot(left_high, high) + (dot(left_low, high) + dot(left_high, low)))
+def turn_body(
+    slab_ref, left_ref, right_ref, extra_ref, right_out, left_out,
+    pair_ref, pair_t_ref, sums_ref, total_ref, row_sums_ref,
+):
+    step = pl.program_id(0)
+
+    @pl.when(step == 0)
+    def _():
+        prepare_left(left_ref, pair_ref)
+        prepare_left_t(left_ref, pair_t_ref, sums_ref)
+
+    right = right_update(slab_ref, pair_ref, pair_t_ref, sums_ref, right_ref[...])
+    right_out[...] = right
+    left_numerator(slab_ref, pair_ref, right, total_ref, row_sums_ref, step == 0)
+
+    @pl.when(step == pl.num_programs(0) - 1)
+    def _():
+        write_left(total_ref, row_sums_ref, extra_ref, left_out)
+
+    return step, right
+
+
+def turn_kernel(*refs):
+    turn_body(*refs)
+
+
+def last_turn_kernel(
+    slab_ref, left_ref, right_ref, extra_ref, second_left_ref, second_right_ref,
+    right_out, left_out, numer_out, *scratch,
+):
+    step, right = turn_body(
+        slab_ref, left_ref, right_ref, extra_ref, right_out, left_out, *scratch
+    )
+    rank, k = right.shape
+    slices = pl.num_programs(0)
+    second_left = second_left_ref[pl.ds(step, rank, stride=slices), :]
+    second_right = jnp.concatenate(
+        [second_right_ref[block] for block in range(k // rank)], axis=1
+    )
+    high, low = second_quotient(right, second_left, split(second_right))
+    left_high, left_low = split(second_left.T)
+    term = dot(left_high, high) + (dot(left_low, high) + dot(left_high, low))
     for block in range(k // rank):
-        numer_out[block] = total[:, block * rank : (block + 1) * rank]
+        part = term[:, block * rank : (block + 1) * rank]
+        numer_out[block] = jnp.where(step == 0, part, numer_out[block] + part)
 
 
 def second_kernel(slices, right_ref, second_left_ref, second_right_ref, out_ref):
@@ -250,36 +262,26 @@
     )
 
 
-def full_turn(slab, left, right, extra, block, parts, vmem_bytes):
+def full_turn(slab, left, right, extra, block, parts, vmem_bytes, second=()):
     (m, columns), rank = slab.shape, left.shape[1]
     columns_spec = lambda height: pl.BlockSpec((height, block), lambda step: (0, step))
     tall = m // parts + PAD
+    out_shapes = [(rank, columns), (parts, tall, rank)] + [factor.shape for factor in second[1:]]
+    kernel = last_turn_kernel if second else turn_kernel
     return pl.pallas_call(
-        turn_kernel,
+        kernel,
         grid=(columns // block,),
-        in_specs=[columns_spec(m), full((m, rank)), columns_spec(rank), full((1, rank))],
-        out_specs=[columns_spec(rank), full((parts, tall, rank))],
-        out_shape=[
-            jax.ShapeDtypeStruct((rank, columns), F32),
-            jax.ShapeDtypeStruct((parts, tall, rank), F32),
-        ],
+        in_specs=[columns_spec(m), full((m, rank)), columns_spec(rank), full((1, rank))]
+        + [full(factor.shape) for factor in second],
+        out_specs=[columns_spec(rank)] + [full(shape) for shape in out_shapes[1:]],
+        out_shape=[jax.ShapeDtypeStruct(shape, F32) for shape in out_shapes],
         scratch_shapes=left_scratch(m, rank)
         + right_scratch(m, rank)
         + total_scratch(m, rank),
         compiler_params=params(vmem_bytes),
         cost_estimate=cost(m, rank, columns, 4),
         name="turn",
-    )(slab, left, right, extra)
-
-
-def second_numerator(right, second_left, second_right, slices):
-    return pl.pallas_call(
-        functools.partial(numerator_kernel, slices),
-        out_shape=jax.ShapeDtypeStruct(second_right.shape, F32),
-        compiler_params=pltpu.CompilerParams(vmem_limit_bytes=VMEM_BYTES),
-        cost_estimate=cost(right.shape[0], right.shape[0], right.shape[1], 2),
-        name="second_numerator",
-    )(right, second_left, second_right)
+    )(slab, left, right, extra, *second)
 
 
 def second_rows_out(right, second_left, second_right, slices):
@@ -379,13 +381,14 @@
     summed = summed.reshape(2, col_devices, rows_own + PAD, rank)
     total = reduce_z(reduce_plane(reduce_core(summed)))
     left = spread_core(spread_plane(own_left_rows(own_init, total))).reshape(m, rank)
-    right, summed = full_turn(tensor_slab, left, right, col_part, k, parts, VMEM_BYTES)
     second_left = arrived[:, : per_owner * slices].reshape(rank * slices, rank)
     whole = arrived[:, per_owner * slices :].reshape(
         row_devices, col_devices, piece_rows // groups, groups, -1
     )
     whole = whole.transpose(0, 3, 2, 1, 4).reshape(rank, k // rank, rank).transpose(1, 0, 2)
-    numerator = second_numerator(right, second_left, whole, slices)
+    right, summed, numerator = full_turn(
+        tensor_slab, left, right, col_part, k, parts, T2_MIB * MIB, (second_left, whole)
+    )
 
     rows_part = k // parts
     summed = summed.reshape(2, col_devices, rows_own + PAD, rank)

time: 116 us -> 119 us (1.026)
  local copies, waits for them, and re-layouts: 2.83 us -> 6.21 us
    unnamed x4 -> x6, local copies, waits for them, and re-layouts: 1.88 us -> 5.25 us
    pallas_call x3 -> x2, Pallas kernels: 26.5 us -> 25.8 us  [full_turn(): pl.pallas_call(kernel, grid=(columns // block,), in_specs=[columns_spec(m...]
  transfers between devices with their start and end apart: 24 -> 24, of which waited for: 21 -> 21; matrix products, arithmetic and copies ran while one was open for 1% -> 1% of each run, Pallas kernels for 11% -> 10%
where the time goes in v10:
time: 119 us; the launch traced here: 118 us
  waiting for transfers between devices  44.8 us (38%)
  starting transfers between devices  34.4 us (29%)
  Pallas kernels  30.4 us (26%)
  local copies, waits for them, and re-layouts  6.21 us (5%)
  other arithmetic  1.73 us (1%)
    ppermute x22, waiting for transfers between devices, send(): return lax.ppermute(values, AXES, pairs)  31.6 us
    pallas_call x2, Pallas kernels, full_turn(): pl.pallas_call(kernel, grid=(columns // block,), in_specs=[columns_spec(m...  25.8 us
    ppermute x22, starting transfers between devices, send(): return lax.ppermute(values, AXES, pairs)  23.5 us
    all_to_all x2, waiting for transfers between devices, exchange(): return lax.all_to_all(parts, AXES, split_axis=0, concat_axis=0, tiled=True)  13.2 us
    all_to_all x2, starting transfers between devices, exchange(): return lax.all_to_all(parts, AXES, split_axis=0, concat_axis=0, tiled=True)  10.9 us
    unnamed x6, local copies, waits for them, and re-layouts  5.25 us
  transfers between devices with their start and end apart: 24, of which 21 were waited for; matrix products, arithmetic and copies ran while one was open for 1% of the time, Pallas kernels for 10%

profile of v10, /device:TPU:0, one launch (start us, length us, event | category | flops | bytes accessed | tf_op | source)
XLA Modules:
  0.0 118.5 jit_solution(14673499657338490492)
XLA Ops:
  0.6 0.1 pad_add_fusion.place_ref
  0.7 0.8 copy-done.1
  1.6 2.4 %prepare.1 = (f32[32,32,128]{2,1,0:T(8,128)}, f32[1,128]{1,0:T(1,128)S(1)}, f32[128,128]{1,0:T(8,128)S(1)}) custom-call(s32[3]{0:T(128)S(1)} %pad_add_fusion.place_ref, f32[2048,128]{1,0:T(8,128)} %second_left_ref.1, f32[128,128]{1,0:T(8,128)S(1)} %copy-done.1, f32[1024,128]{1,0:T(8,128)} %refs_1_.1), custom_call_target="tpu_custom_call" | custom-call | flops 65536 | bytes 786432 | tf_op jit(solution)/shard_map/prepare/pallas_call | solution.py:324
  3.9 7.3 %all-to-all-start = ((f32[32,32,128]{2,1,0:T(8,128)}), f32[32,32,128]{2,1,0:T(8,128)S(1)}, u32[]{:S(2)}, u32[]{:S(2)}) async-start(f32[32,32,128]{2,1,0:T(8,128)} %get-tuple-element.15), calls=%async_computation | async-start | bytes 1048576 | tf_op jit(solution)/shard_map/all_to_all | solution.py:22
  11.3 0.0 copy-start
  11.3 1.0 copy-done
  12.3 12.1 %turn.2 = (f32[128,2048]{1,0:T(8,128)S(1)}, f32[8,136,128]{2,1,0:T(8,128)S(1)}) custom-call(f32[1024,2048]{1,0:T(8,128)} %slab_ref.1, f32[1024,128]{1,0:T(8,128)S(1)} %copy-done, f32[128,2048]{1,0:T(8,128)} %refs_2_.1, f32[1,128]{1,0:T(1,128)S(1)} %get-tuple-element.13.refs_3_.extra_ref), custom_call_target="tpu_custom_call" | custom-call | flops 6442450944 | bytes 8388608 | tf_op jit(solution)/shard_map/turn/pallas_call | solution.py:271
  24.5 3.0 %all-to-all-done = f32[32,32,128]{2,1,0:T(8,128)S(1)} async-done(((f32[32,32,128]{2,1,0:T(8,128)}), f32[32,32,128]{2,1,0:T(8,128)S(1)}, u32[]{:S(2)}, u32[]{:S(2)}) %all-to-all-start) | async-done | bytes 524320 | tf_op jit(solution)/shard_map/all_to_all | solution.py:22
  27.5 0.1 collective-permute-start
  27.6 1.5 %collective-permute-done = f32[4,136,128]{2,1,0:T(8,128)S(1)} collective-permute-done((f32[4,136,128]{2,1,0:T(8,128)S(1)}, f32[4,136,128]{2,1,0:T(8,128)S(1)}, u32[]{:S(2)}, u32[]{:S(2)}) %collective-permute-start) | collective-permute-done | bytes 278560 | tf_op jit(solution)/shard_map/ppermute | solution.py:32
  29.2 0.3 collective-permute-start.1
  29.5 1.5 %collective-permute-start.2 = (f32[136,128]{1,0:T(8,128)S(1)}, f32[136,128]{1,0:T(8,128)S(1)}, u32[]{:S(2)}, u32[]{:S(2)}) collective-permute-start(f32[136,128]{1,0:T(8,128)S(1)} %get-tuple-element.38), channel_id=1, source_target_pairs={{0,2},{1,3},{2,0},{3,1},{4,6},{5,7},{6,4},{7,5},{8,10},{9,11},{10,... | collective-permute-start | bytes 208904 | tf_op jit(solution)/shard_map/ppermute | solution.py:32
  31.0 1.8 %collective-permute-start.3 = (f32[136,128]{1,0:T(8,128)S(1)}, f32[136,128]{1,0:T(8,128)S(1)}, u32[]{:S(2)}, u32[]{:S(2)}) collective-permute-start(f32[136,128]{1,0:T(8,128)S(1)} %get-tuple-element.37), channel_id=1, source_target_pairs={{0,3},{1,2},{2,1},{3,0},{4,7},{5,6},{6,5},{7,4},{8,11},{9,10},{10,... | collective-permute-start | bytes 208904 | tf_op jit(solution)/shard_map/ppermute | solution.py:32
  32.8 1.2 %collective-permute-done.1 = f32[136,128]{1,0:T(8,128)S(1)} collective-permute-done((f32[136,128]{1,0:T(8,128)S(1)}, f32[136,128]{1,0:T(8,128)S(1)}, u32[]{:S(2)}, u32[]{:S(2)}) %collective-permute-start.1) | collective-permute-done | bytes 69664 | tf_op jit(solution)/shard_map/ppermute | solution.py:32
  34.0 0.0 collective-permute-done.2
  34.0 2.2 %collective-permute-done.3 = f32[136,128]{1,0:T(8,128)S(1)} collective-permute-done((f32[136,128]{1,0:T(8,128)S(1)}, f32[136,128]{1,0:T(8,128)S(1)}, u32[]{:S(2)}, u32[]{:S(2)}) %collective-permute-start.3) | collective-permute-done | bytes 69664 | tf_op jit(solution)/shard_map/ppermute | solution.py:32
  36.2 0.2 collective-permute-start.4
  36.5 2.3 %collective-permute-start.5 = (f32[136,128]{1,0:T(8,128)S(1)}, f32[136,128]{1,0:T(8,128)S(1)}, u32[]{:S(2)}, u32[]{:S(2)}) collective-permute-start(f32[136,128]{1,0:T(8,128)S(1)} %fusion.11), channel_id=1, source_target_pairs={{0,16},{1,17},{2,18},{3,19},{4,20},{5,21},{6,22},{7,23},{8,24},{9,... | collective-permute-start | bytes 208904 | tf_op jit(solution)/shard_map/ppermute | solution.py:32
  38.7 2.0 %collective-permute-start.6 = (f32[136,128]{1,0:T(8,128)S(1)}, f32[136,128]{1,0:T(8,128)S(1)}, u32[]{:S(2)}, u32[]{:S(2)}) collective-permute-start(f32[136,128]{1,0:T(8,128)S(1)} %fusion.11), channel_id=1, source_target_pairs={{0,24},{1,25},{2,26},{3,27},{4,28},{5,29},{6,30},{7,31},{8,16},{9,... | collective-permute-start | bytes 208904 | tf_op jit(solution)/shard_map/ppermute | solution.py:32
  40.7 0.0 collective-permute-done.4
  40.7 2.5 %collective-permute-done.5 = f32[136,128]{1,0:T(8,128)S(1)} collective-permute-done((f32[136,128]{1,0:T(8,128)S(1)}, f32[136,128]{1,0:T(8,128)S(1)}, u32[]{:S(2)}, u32[]{:S(2)}) %collective-permute-start.5) | collective-permute-done | bytes 69664 | tf_op jit(solution)/shard_map/ppermute | solution.py:32
  43.2 1.7 %collective-permute-done.6 = f32[136,128]{1,0:T(8,128)S(1)} collective-permute-done((f32[136,128]{1,0:T(8,128)S(1)}, f32[136,128]{1,0:T(8,128)S(1)}, u32[]{:S(2)}, u32[]{:S(2)}) %collective-permute-start.6) | collective-permute-done | bytes 69664 | tf_op jit(solution)/shard_map/ppermute | solution.py:32
  44.9 0.7 collective-permute-start.7
  45.6 1.4 %collective-permute-start.8 = (f32[128,128]{1,0:T(8,128)S(1)}, f32[128,128]{1,0:T(8,128)S(1)}, u32[]{:S(2)}, u32[]{:S(2)}) collective-permute-start(f32[128,128]{1,0:T(8,128)S(1)} %fusion.13), channel_id=1, source_target_pairs={{0,2},{1,3},{2,0},{3,1},{4,6},{5,7},{6,4},{7,5},{8,10},{9,11},{10,... | collective-permute-start | bytes 196616 | tf_op jit(solution)/shard_map/ppermute | solution.py:32
  47.0 1.4 %collective-permute-start.9 = (f32[128,128]{1,0:T(8,128)S(1)}, f32[128,128]{1,0:T(8,128)S(1)}, u32[]{:S(2)}, u32[]{:S(2)}) collective-permute-start(f32[128,128]{1,0:T(8,128)S(1)} %fusion.13), channel_id=1, source_target_pairs={{0,3},{1,2},{2,1},{3,0},{4,7},{5,6},{6,5},{7,4},{8,11},{9,10},{10,... | collective-permute-start | bytes 196616 | tf_op jit(solution)/shard_map/ppermute | solution.py:32
  48.4 0.8 collective-permute-done.7
  49.2 0.7 collective-permute-done.8
  49.9 2.3 %collective-permute-done.9 = f32[128,128]{1,0:T(8,128)S(1)} collective-permute-done((f32[128,128]{1,0:T(8,128)S(1)}, f32[128,128]{1,0:T(8,128)S(1)}, u32[]{:S(2)}, u32[]{:S(2)}) %collective-permute-start.9) | collective-permute-done | bytes 65568 | tf_op jit(solution)/shard_map/ppermute | solution.py:32
  52.3 0.1 collective-permute-start.10
  52.4 1.5 %collective-permute-done.10 = f32[4,128,128]{2,1,0:T(8,128)S(1)} collective-permute-done((f32[4,128,128]{2,1,0:T(8,128)S(1)}, f32[4,128,128]{2,1,0:T(8,128)S(1)}, u32[]{:S(2)}, u32[]{:S(2)}) %collective-permute-start.10) | collective-permute-done | bytes 262176 | tf_op jit(solution)/shard_map/ppermute | solution.py:32
  53.9 0.1 fusion.9
  54.0 0.0 copy-start.2
  54.0 3.4 %copy-done.2 = f32[1024,2048]{1,0:T(8,128)S(1)} copy-done((f32[1024,2048]{1,0:T(8,128)S(1)}, f32[1024,2048]{1,0:T(8,128)}, u32[]{:S(2)}) %copy-start.2) | copy-done | bytes 8388632
  57.4 13.7 %turn.3 = (f32[128,2048]{1,0:T(8,128)S(1)}, f32[8,136,128]{2,1,0:T(8,128)S(1)}, f32[4,128,128]{2,1,0:T(8,128)S(1)}) custom-call(f32[1024,2048]{1,0:T(8,128)S(1)} %copy-done.2, f32[1024,128]{1,0:T(8,128)S(1)} %bitcast.82, f32[128,2048]{1,0:T(8,128)S(1)} %get-tuple-element.17.right_ref, f32[1,128]{1,0:T(1,128)S(1)} %get-tuple-element.13.refs_3_.extra_ref, ...), custom_call_target="tpu_custom_call" | custom-call | flops 6442450944 | bytes 8388608 | tf_op jit(solution)/shard_map/turn/pallas_call | solution.py:271
  71.1 0.2 collective-permute-start.11
  71.3 1.6 %collective-permute-done.11 = f32[4,200,128]{2,1,0:T(8,128)S(1)} collective-permute-done((f32[4,200,128]{2,1,0:T(8,128)S(1)}, f32[4,200,128]{2,1,0:T(8,128)S(1)}, u32[]{:S(2)}, u32[]{:S(2)}) %collective-permute-start.11) | collective-permute-done | bytes 409632 | tf_op jit(solution)/shard_map/ppermute | solution.py:32
  73.0 0.7 collective-permute-start.12
  73.8 1.3 %collective-permute-start.13 = (f32[200,128]{1,0:T(8,128)S(1)}, f32[200,128]{1,0:T(8,128)S(1)}, u32[]{:S(2)}, u32[]{:S(2)}) collective-permute-start(f32[200,128]{1,0:T(8,128)S(1)} %get-tuple-element.29), channel_id=1, source_target_pairs={{0,2},{1,3},{2,0},{3,1},{4,6},{5,7},{6,4},{7,5},{8,10},{9,11},{10,... | collective-permute-start | bytes 307208 | tf_op jit(solution)/shard_map/ppermute | solution.py:32
  75.1 1.5 %collective-permute-start.14 = (f32[200,128]{1,0:T(8,128)S(1)}, f32[200,128]{1,0:T(8,128)S(1)}, u32[]{:S(2)}, u32[]{:S(2)}) collective-permute-start(f32[200,128]{1,0:T(8,128)S(1)} %get-tuple-element.28), channel_id=1, source_target_pairs={{0,3},{1,2},{2,1},{3,0},{4,7},{5,6},{6,5},{7,4},{8,11},{9,10},{10,... | collective-permute-start | bytes 307208 | tf_op jit(solution)/shard_map/ppermute | solution.py:32
  76.6 2.1 %collective-permute-done.12 = f32[200,128]{1,0:T(8,128)S(1)} collective-permute-done((f32[200,128]{1,0:T(8,128)S(1)}, f32[200,128]{1,0:T(8,128)S(1)}, u32[]{:S(2)}, u32[]{:S(2)}) %collective-permute-start.12) | collective-permute-done | bytes 102432 | tf_op jit(solution)/shard_map/ppermute | solution.py:32
  78.7 0.8 collective-permute-done.13
  79.5 1.1 collective-permute-done.14
  80.7 0.9 collective-permute-start.15
  81.6 1.7 %collective-permute-start.16 = (f32[200,128]{1,0:T(8,128)S(1)}, f32[200,128]{1,0:T(8,128)S(1)}, u32[]{:S(2)}, u32[]{:S(2)}) collective-permute-start(f32[200,128]{1,0:T(8,128)S(1)} %fusion.10), channel_id=1, source_target_pairs={{0,16},{1,17},{2,18},{3,19},{4,20},{5,21},{6,22},{7,23},{8,24},{9,... | collective-permute-start | bytes 307208 | tf_op jit(solution)/shard_map/ppermute | solution.py:32
  83.3 1.9 %collective-permute-start.17 = (f32[200,128]{1,0:T(8,128)S(1)}, f32[200,128]{1,0:T(8,128)S(1)}, u32[]{:S(2)}, u32[]{:S(2)}) collective-permute-start(f32[200,128]{1,0:T(8,128)S(1)} %fusion.10), channel_id=1, source_target_pairs={{0,24},{1,25},{2,26},{3,27},{4,28},{5,29},{6,30},{7,31},{8,16},{9,... | collective-permute-start | bytes 307208 | tf_op jit(solution)/shard_map/ppermute | solution.py:32
  85.1 1.1 collective-permute-done.15
  86.3 5.1 %collective-permute-done.16 = f32[200,128]{1,0:T(8,128)S(1)} collective-permute-done((f32[200,128]{1,0:T(8,128)S(1)}, f32[200,128]{1,0:T(8,128)S(1)}, u32[]{:S(2)}, u32[]{:S(2)}) %collective-permute-start.16) | collective-permute-done | bytes 102432 | tf_op jit(solution)/shard_map/ppermute | solution.py:32
  91.3 0.0 collective-permute-done.17
  91.4 0.1 broadcast_divide_fusion
  91.5 1.1 collective-permute-start.18
  92.6 0.7 collective-permute-start.19
  93.3 1.7 %collective-permute-start.20 = (f32[192,128]{1,0:T(8,128)S(1)}, f32[192,128]{1,0:T(8,128)S(1)}, u32[]{:S(2)}, u32[]{:S(2)}) collective-permute-start(f32[192,128]{1,0:T(8,128)S(1)} %get-tuple-element.49), channel_id=1, source_target_pairs={{0,3},{1,2},{2,1},{3,0},{4,7},{5,6},{6,5},{7,4},{8,11},{9,10},{10,... | collective-permute-start | bytes 294920 | tf_op jit(solution)/shard_map/ppermute | solution.py:32
  95.1 1.1 collective-permute-done.18
  96.2 1.0 collective-permute-done.19
  97.2 1.6 %collective-permute-done.20 = f32[192,128]{1,0:T(8,128)S(1)} collective-permute-done((f32[192,128]{1,0:T(8,128)S(1)}, f32[192,128]{1,0:T(8,128)S(1)}, u32[]{:S(2)}, u32[]{:S(2)}) %collective-permute-start.20) | collective-permute-done | bytes 98336 | tf_op jit(solution)/shard_map/ppermute | solution.py:32
  98.9 0.1 pad_maximum_fusion.2
  99.0 0.1 collective-permute-start.21
  99.1 1.7 %collective-permute-done.21 = f32[4,192,128]{2,1,0:T(8,128)S(1)} collective-permute-done((f32[4,192,128]{2,1,0:T(8,128)S(1)}, f32[4,192,128]{2,1,0:T(8,128)S(1)}, u32[]{:S(2)}, u32[]{:S(2)}) %collective-permute-start.21) | collective-permute-done | bytes 393248 | tf_op jit(solution)/shard_map/ppermute | solution.py:32
  100.8 0.2 fusion.6
  101.0 2.2 %second_rows.1 = f32[512,128]{1,0:T(8,128)} custom-call(f32[128,2048]{1,0:T(8,128)S(1)} %get-tuple-element.21.right_ref, f32[512,128]{1,0:T(8,128)S(1)} %bitcast.78, f32[4,128,128]{2,1,0:T(8,128)S(1)} %bitcast.79), custom_call_target="tpu_custom_call" | custom-call | flops 402653184 | bytes 1048576 | tf_op jit(solution)/shard_map/second_rows/pallas_call | solution.py:288
  103.2 3.6 %all-to-all-start.1 = ((f32[32,16,128]{2,1,0:T(8,128)}), f32[32,16,128]{2,1,0:T(8,128)S(1)}, u32[]{:S(2)}, u32[]{:S(2)}) async-start(f32[32,16,128]{2,1,0:T(8,128)} %bitcast.44), calls=%async_computation.1 | async-start | bytes 524288 | tf_op jit(solution)/shard_map/all_to_all | solution.py:22
  106.8 0.8 fusion
  107.6 10.1 %all-to-all-done.1 = f32[32,16,128]{2,1,0:T(8,128)S(1)} async-done(((f32[32,16,128]{2,1,0:T(8,128)}), f32[32,16,128]{2,1,0:T(8,128)S(1)}, u32[]{:S(2)}, u32[]{:S(2)}) %all-to-all-start.1) | async-done | bytes 262176 | tf_op jit(solution)/shard_map/all_to_all | solution.py:22
  117.7 0.7 copy.8
  (26 shorter events, 0.6 us)
Async XLA Ops:
  0.7 0.8 copy-start.1
  3.9 23.6 %all-to-all-start = ((f32[32,32,128]{2,1,0:T(8,128)}), f32[32,32,128]{2,1,0:T(8,128)S(1)}, u32[]{:S(2)}, u32[]{:S(2)}) async-start(f32[32,32,128]{2,1,0:T(8,128)} %get-tuple-element.15), calls=%async_computation | async-start | bytes 1048576 | tf_op jit(solution)/shard_map/all_to_all | solution.py:22
  11.3 1.0 copy-start
  27.5 1.6 %collective-permute-start = (f32[4,136,128]{2,1,0:T(8,128)S(1)}, f32[4,136,128]{2,1,0:T(8,128)S(1)}, u32[]{:S(2)}, u32[]{:S(2)}) collective-permute-start(f32[4,136,128]{2,1,0:T(8,128)S(1)} %dynamic-slice_bitcast_fusion), channel_id=1, source_target_pairs={{0,4},{1,5},{2,6},{3,7},{4,0},{5,1},{6,2},{7,3},{8,12},{9,13},{10,... | collective-permute-start | bytes 835592 | tf_op jit(solution)/shard_map/ppermute | solution.py:32
  29.2 4.8 %collective-permute-start.1 = (f32[136,128]{1,0:T(8,128)S(1)}, f32[136,128]{1,0:T(8,128)S(1)}, u32[]{:S(2)}, u32[]{:S(2)}) collective-permute-start(f32[136,128]{1,0:T(8,128)S(1)} %get-tuple-element.39), channel_id=1, source_target_pairs={{0,1},{1,0},{2,3},{3,2},{4,5},{5,4},{6,7},{7,6},{8,9},{9,8},{10,11... | collective-permute-start | bytes 208904 | tf_op jit(solution)/shard_map/ppermute | solution.py:32
  29.5 4.5 %collective-permute-start.2 = (f32[136,128]{1,0:T(8,128)S(1)}, f32[136,128]{1,0:T(8,128)S(1)}, u32[]{:S(2)}, u32[]{:S(2)}) collective-permute-start(f32[136,128]{1,0:T(8,128)S(1)} %get-tuple-element.38), channel_id=1, source_target_pairs={{0,2},{1,3},{2,0},{3,1},{4,6},{5,7},{6,4},{7,5},{8,10},{9,11},{10,... | collective-permute-start | bytes 208904 | tf_op jit(solution)/shard_map/ppermute | solution.py:32
  31.0 5.2 %collective-permute-start.3 = (f32[136,128]{1,0:T(8,128)S(1)}, f32[136,128]{1,0:T(8,128)S(1)}, u32[]{:S(2)}, u32[]{:S(2)}) collective-permute-start(f32[136,128]{1,0:T(8,128)S(1)} %get-tuple-element.37), channel_id=1, source_target_pairs={{0,3},{1,2},{2,1},{3,0},{4,7},{5,6},{6,5},{7,4},{8,11},{9,10},{10,... | collective-permute-start | bytes 208904 | tf_op jit(solution)/shard_map/ppermute | solution.py:32
  36.2 4.5 %collective-permute-start.4 = (f32[136,128]{1,0:T(8,128)S(1)}, f32[136,128]{1,0:T(8,128)S(1)}, u32[]{:S(2)}, u32[]{:S(2)}) collective-permute-start(f32[136,128]{1,0:T(8,128)S(1)} %fusion.11), channel_id=1, source_target_pairs={{0,8},{1,9},{2,10},{3,11},{4,12},{5,13},{6,14},{7,15},{8,0},{9,1},... | collective-permute-start | bytes 208904 | tf_op jit(solution)/shard_map/ppermute | solution.py:32
  36.5 6.7 %collective-permute-start.5 = (f32[136,128]{1,0:T(8,128)S(1)}, f32[136,128]{1,0:T(8,128)S(1)}, u32[]{:S(2)}, u32[]{:S(2)}) collective-permute-start(f32[136,128]{1,0:T(8,128)S(1)} %fusion.11), channel_id=1, source_target_pairs={{0,16},{1,17},{2,18},{3,19},{4,20},{5,21},{6,22},{7,23},{8,24},{9,... | collective-permute-start | bytes 208904 | tf_op jit(solution)/shard_map/ppermute | solution.py:32
  38.7 6.1 %collective-permute-start.6 = (f32[136,128]{1,0:T(8,128)S(1)}, f32[136,128]{1,0:T(8,128)S(1)}, u32[]{:S(2)}, u32[]{:S(2)}) collective-permute-start(f32[136,128]{1,0:T(8,128)S(1)} %fusion.11), channel_id=1, source_target_pairs={{0,24},{1,25},{2,26},{3,27},{4,28},{5,29},{6,30},{7,31},{8,16},{9,... | collective-permute-start | bytes 208904 | tf_op jit(solution)/shard_map/ppermute | solution.py:32
  44.9 4.3 %collective-permute-start.7 = (f32[128,128]{1,0:T(8,128)S(1)}, f32[128,128]{1,0:T(8,128)S(1)}, u32[]{:S(2)}, u32[]{:S(2)}) collective-permute-start(f32[128,128]{1,0:T(8,128)S(1)} %fusion.13), channel_id=1, source_target_pairs={{0,1},{1,0},{2,3},{3,2},{4,5},{5,4},{6,7},{7,6},{8,9},{9,8},{10,11... | collective-permute-start | bytes 196616 | tf_op jit(solution)/shard_map/ppermute | solution.py:32
  45.6 4.3 %collective-permute-start.8 = (f32[128,128]{1,0:T(8,128)S(1)}, f32[128,128]{1,0:T(8,128)S(1)}, u32[]{:S(2)}, u32[]{:S(2)}) collective-permute-start(f32[128,128]{1,0:T(8,128)S(1)} %fusion.13), channel_id=1, source_target_pairs={{0,2},{1,3},{2,0},{3,1},{4,6},{5,7},{6,4},{7,5},{8,10},{9,11},{10,... | collective-permute-start | bytes 196616 | tf_op jit(solution)/shard_map/ppermute | solution.py:32
  47.0 5.2 %collective-permute-start.9 = (f32[128,128]{1,0:T(8,128)S(1)}, f32[128,128]{1,0:T(8,128)S(1)}, u32[]{:S(2)}, u32[]{:S(2)}) collective-permute-start(f32[128,128]{1,0:T(8,128)S(1)} %fusion.13), channel_id=1, source_target_pairs={{0,3},{1,2},{2,1},{3,0},{4,7},{5,6},{6,5},{7,4},{8,11},{9,10},{10,... | collective-permute-start | bytes 196616 | tf_op jit(solution)/shard_map/ppermute | solution.py:32
  52.3 1.6 %collective-permute-start.10 = (f32[4,128,128]{2,1,0:T(8,128)S(1)}, f32[4,128,128]{2,1,0:T(8,128)S(1)}, u32[]{:S(2)}, u32[]{:S(2)}) collective-permute-start(f32[4,128,128]{2,1,0:T(8,128)S(1)} %get-tuple-element.40), channel_id=1, source_target_pairs={{0,4},{1,5},{2,6},{3,7},{4,0},{5,1},{6,2},{7,3},{8,12},{9,13},{10,... | collective-permute-start | bytes 786440 | tf_op jit(solution)/shard_map/ppermute | solution.py:32
  54.0 3.4 %copy-start.2 = (f32[1024,2048]{1,0:T(8,128)S(1)}, f32[1024,2048]{1,0:T(8,128)}, u32[]{:S(2)}) copy-start(f32[1024,2048]{1,0:T(8,128)} %slab_ref.1) | copy-start | bytes 25165828
  71.1 1.8 %collective-permute-start.11 = (f32[4,200,128]{2,1,0:T(8,128)S(1)}, f32[4,200,128]{2,1,0:T(8,128)S(1)}, u32[]{:S(2)}, u32[]{:S(2)}) collective-permute-start(f32[4,200,128]{2,1,0:T(8,128)S(1)} %fusion.2), channel_id=1, source_target_pairs={{0,4},{1,5},{2,6},{3,7},{4,0},{5,1},{6,2},{7,3},{8,12},{9,13},{10,... | collective-permute-start | bytes 1228808 | tf_op jit(solution)/shard_map/ppermute | solution.py:32
  73.0 5.6 %collective-permute-start.12 = (f32[200,128]{1,0:T(8,128)S(1)}, f32[200,128]{1,0:T(8,128)S(1)}, u32[]{:S(2)}, u32[]{:S(2)}) collective-permute-start(f32[200,128]{1,0:T(8,128)S(1)} %get-tuple-element.30), channel_id=1, source_target_pairs={{0,1},{1,0},{2,3},{3,2},{4,5},{5,4},{6,7},{7,6},{8,9},{9,8},{10,11... | collective-permute-start | bytes 307208 | tf_op jit(solution)/shard_map/ppermute | solution.py:32
  73.8 5.8 %collective-permute-start.13 = (f32[200,128]{1,0:T(8,128)S(1)}, f32[200,128]{1,0:T(8,128)S(1)}, u32[]{:S(2)}, u32[]{:S(2)}) collective-permute-start(f32[200,128]{1,0:T(8,128)S(1)} %get-tuple-element.29), channel_id=1, source_target_pairs={{0,2},{1,3},{2,0},{3,1},{4,6},{5,7},{6,4},{7,5},{8,10},{9,11},{10,... | collective-permute-start | bytes 307208 | tf_op jit(solution)/shard_map/ppermute | solution.py:32
  75.1 5.6 %collective-permute-start.14 = (f32[200,128]{1,0:T(8,128)S(1)}, f32[200,128]{1,0:T(8,128)S(1)}, u32[]{:S(2)}, u32[]{:S(2)}) collective-permute-start(f32[200,128]{1,0:T(8,128)S(1)} %get-tuple-element.28), channel_id=1, source_target_pairs={{0,3},{1,2},{2,1},{3,0},{4,7},{5,6},{6,5},{7,4},{8,11},{9,10},{10,... | collective-permute-start | bytes 307208 | tf_op jit(solution)/shard_map/ppermute | solution.py:32
  80.7 5.6 %collective-permute-start.15 = (f32[200,128]{1,0:T(8,128)S(1)}, f32[200,128]{1,0:T(8,128)S(1)}, u32[]{:S(2)}, u32[]{:S(2)}) collective-permute-start(f32[200,128]{1,0:T(8,128)S(1)} %fusion.10), channel_id=1, source_target_pairs={{0,8},{1,9},{2,10},{3,11},{4,12},{5,13},{6,14},{7,15},{8,0},{9,1},... | collective-permute-start | bytes 307208 | tf_op jit(solution)/shard_map/ppermute | solution.py:32
  81.6 9.7 %collective-permute-start.16 = (f32[200,128]{1,0:T(8,128)S(1)}, f32[200,128]{1,0:T(8,128)S(1)}, u32[]{:S(2)}, u32[]{:S(2)}) collective-permute-start(f32[200,128]{1,0:T(8,128)S(1)} %fusion.10), channel_id=1, source_target_pairs={{0,16},{1,17},{2,18},{3,19},{4,20},{5,21},{6,22},{7,23},{8,24},{9,... | collective-permute-start | bytes 307208 | tf_op jit(solution)/shard_map/ppermute | solution.py:32
  83.3 8.1 %collective-permute-start.17 = (f32[200,128]{1,0:T(8,128)S(1)}, f32[200,128]{1,0:T(8,128)S(1)}, u32[]{:S(2)}, u32[]{:S(2)}) collective-permute-start(f32[200,128]{1,0:T(8,128)S(1)} %fusion.10), channel_id=1, source_target_pairs={{0,24},{1,25},{2,26},{3,27},{4,28},{5,29},{6,30},{7,31},{8,16},{9,... | collective-permute-start | bytes 307208 | tf_op jit(solution)/shard_map/ppermute | solution.py:32
  91.5 4.7 %collective-permute-start.18 = (f32[192,128]{1,0:T(8,128)S(1)}, f32[192,128]{1,0:T(8,128)S(1)}, u32[]{:S(2)}, u32[]{:S(2)}) collective-permute-start(f32[192,128]{1,0:T(8,128)S(1)} %get-tuple-element.49), channel_id=1, source_target_pairs={{0,1},{1,0},{2,3},{3,2},{4,5},{5,4},{6,7},{7,6},{8,9},{9,8},{10,11... | collective-permute-start | bytes 294920 | tf_op jit(solution)/shard_map/ppermute | solution.py:32
  92.6 4.6 %collective-permute-start.19 = (f32[192,128]{1,0:T(8,128)S(1)}, f32[192,128]{1,0:T(8,128)S(1)}, u32[]{:S(2)}, u32[]{:S(2)}) collective-permute-start(f32[192,128]{1,0:T(8,128)S(1)} %get-tuple-element.49), channel_id=1, source_target_pairs={{0,2},{1,3},{2,0},{3,1},{4,6},{5,7},{6,4},{7,5},{8,10},{9,11},{10,... | collective-permute-start | bytes 294920 | tf_op jit(solution)/shard_map/ppermute | solution.py:32
  93.3 5.5 %collective-permute-start.20 = (f32[192,128]{1,0:T(8,128)S(1)}, f32[192,128]{1,0:T(8,128)S(1)}, u32[]{:S(2)}, u32[]{:S(2)}) collective-permute-start(f32[192,128]{1,0:T(8,128)S(1)} %get-tuple-element.49), channel_id=1, source_target_pairs={{0,3},{1,2},{2,1},{3,0},{4,7},{5,6},{6,5},{7,4},{8,11},{9,10},{10,... | collective-permute-start | bytes 294920 | tf_op jit(solution)/shard_map/ppermute | solution.py:32
  99.0 1.8 %collective-permute-start.21 = (f32[4,192,128]{2,1,0:T(8,128)S(1)}, f32[4,192,128]{2,1,0:T(8,128)S(1)}, u32[]{:S(2)}, u32[]{:S(2)}) collective-permute-start(f32[4,192,128]{2,1,0:T(8,128)S(1)} %get-tuple-element.31), channel_id=1, source_target_pairs={{0,4},{1,5},{2,6},{3,7},{4,0},{5,1},{6,2},{7,3},{8,12},{9,13},{10,... | collective-permute-start | bytes 1179656 | tf_op jit(solution)/shard_map/ppermute | solution.py:32
  103.2 14.5 %all-to-all-start.1 = ((f32[32,16,128]{2,1,0:T(8,128)}), f32[32,16,128]{2,1,0:T(8,128)S(1)}, u32[]{:S(2)}, u32[]{:S(2)}) async-start(f32[32,16,128]{2,1,0:T(8,128)} %bitcast.44), calls=%async_computation.1 | async-start | bytes 524288 | tf_op jit(solution)/shard_map/all_to_all | solution.py:22

commit v11 on v7

--- a/solution.py
+++ b/solution.py
@@ -10,9 +10,10 @@
 AXES = ("row", "col")
 F32, BF16 = jnp.float32, jnp.bfloat16
 PAD = 8
-ROWS = 128
+ROWS = 1024
 MIB = 1024 * 1024
 T1_MIB = 52
+PREP_KIB = 54528
 VMEM_BYTES = 51 * MIB
 
 
@@ -55,6 +56,17 @@
     return tree_sum([pick(own, col)] + others)
 
 
+def reduce_plane_with(own, rider):
+    col, (cols, height, _) = lax.axis_index("col"), own.shape
+    others = [
+        send(jnp.concatenate([pick(own, col ^ flip), rider], axis=0), 0, flip)
+        for flip in range(1, cols)
+    ]
+    total = tree_sum([pick(own, col)] + [other[:height] for other in others])
+    riders = jnp.stack([rider] + [other[height:] for other in others])
+    return total, jnp.stack([pick(riders, index ^ col) for index in range(cols)])
+
+
 def reduce_z(own):
     return tree_sum([own] + [send(own, flip, 0) for flip in range(2, lax.axis_size("row"), 2)])
 
@@ -115,21 +127,22 @@
     return jnp.concatenate([high, high, low], axis=0)
 
 
-def quotients(slab_ref, pair_ref, right_stack, rows):
+def quotients(slab_ref, pair_ref, right_stack, rows, columns=slice(None)):
     product = dot(pair_ref[rows, :], right_stack)
-    return split(divide(slab_ref[rows, :], product))
+    return split(divide(slab_ref[rows, columns], product))
 
 
 def right_update(slab_ref, pair_ref, pair_t_ref, sums_ref, right):
-    rank = right.shape[0]
+    rank, block = right.shape
     stack = stacked(right)
-    parts = [quotients(slab_ref, pair_ref, stack, rows) for rows in chunks(slab_ref.shape[0], ROWS)]
-    both = dot(pair_t_ref[...], jnp.concatenate([high for high, _ in parts], axis=0))
-    numerator = both[:rank] + both[rank:]
-    numerator = numerator + dot(
-        pair_t_ref[:rank, :], jnp.concatenate([low for _, low in parts], axis=0)
-    )
-    return right * numerator / sums_ref[:, :1]
+    rows = pl.ds(0, slab_ref.shape[0])
+    halves = [slice(start, start + block // 2) for start in (0, block // 2)]
+    parts = [quotients(slab_ref, pair_ref, stack[:, half], rows, half) for half in halves]
+    numerators = []
+    for high, low in parts:
+        both = dot(pair_t_ref[...], high)
+        numerators.append(both[:rank] + both[rank:] + dot(pair_t_ref[:rank, :], low))
+    return right * jnp.concatenate(numerators, axis=1) / sums_ref[:, :1]
 
 
 def left_numerator(slab_ref, pair_ref, right, total_ref, sums_ref, first):
@@ -291,6 +304,41 @@
     )(right, second_left, second_right)
 
 
+def prepare_kernel(slices, place_ref, second_left_ref, out_ref, sums_out):
+    devices, tall, rank = out_ref.shape
+    second_left = second_left_ref[...]
+    sums_out[...] = jnp.sum(second_left, axis=0, keepdims=True)
+    for index in range(tall // slices):
+        for device in range(devices):
+            start = (index * devices + device) * slices
+            out_ref[device, index * slices : (index + 1) * slices, :] = second_left[
+                start : start + slices
+            ]
+
+
+def prepare(place, second_left, devices, slices, second_rows):
+    rank = second_left.shape[1]
+    shapes = [(devices, second_rows // devices, rank), (1, rank)]
+    return pl.pallas_call(
+        functools.partial(prepare_kernel, slices),
+        grid_spec=pltpu.PrefetchScalarGridSpec(
+            num_scalar_prefetch=1,
+            grid=(1,),
+            in_specs=[pl.BlockSpec((second_rows, rank), lambda step, place: (place[0], 0))],
+            out_specs=[
+                pl.BlockSpec(shapes[0], lambda step, place: (0, 0, 0)),
+                pl.BlockSpec(shapes[1], lambda step, place: (0, 0)),
+            ],
+        ),
+        out_shape=[jax.ShapeDtypeStruct(shape, F32) for shape in shapes],
+        compiler_params=params(PREP_KIB * 1024),
+        cost_estimate=pl.CostEstimate(
+            flops=second_rows * rank, bytes_accessed=8 * second_rows * rank, transcendentals=0
+        ),
+        name="prepare",
+    )(place, second_left)
+
+
 def body(tensor_slab, left_init, right_init, second_left_init, second_right_init):
     row_devices = lax.axis_size("row")
     col_devices = lax.axis_size("col")
@@ -303,38 +351,39 @@
     per_owner = rank // devices
     rows_own = m // parts
 
-    second_rows = second_left_init.shape[0] // col_devices
-    own_left = lax.dynamic_slice_in_dim(
-        second_left_init, lax.axis_index("col") * second_rows, second_rows, 0
-    )
-    col_part = jnp.sum(own_left, axis=0)[None]
-    own_left = own_left.reshape(per_owner, devices, slices, rank)
-    piece_rows = rank // row_devices
-    piece = lax.dynamic_slice_in_dim(
-        second_right_init, lax.axis_index("row") * piece_rows, piece_rows, 0
-    ).reshape(-1, rank)
-    piece = jnp.broadcast_to(piece[None], (devices,) + piece.shape)
-    second_factors = [own_left[index] for index in range(per_owner)] + [piece]
-    arrived = exchange(jnp.concatenate(second_factors, axis=1))
-
     def own_rows(left):
         return lax.dynamic_slice_in_dim(left, own_part * rows_own, rows_own, 0)
 
     def own_left_rows(own, total):
         return own * total[:rows_own] / total[rows_own][None, :]
 
-    own_init = own_rows(left_init)
     right, summed = full_turn(
-        tensor_slab, after(left_init, own_init), right_init, left_init, k, parts, T1_MIB * MIB
-    )
-    summed, arrived = lax.optimization_barrier((summed, arrived))
+        tensor_slab, left_init, right_init, left_init, k, parts, T1_MIB * MIB
+    )
+    second_left = after(second_left_init, summed)
     summed = summed.reshape(2, col_devices, rows_own + PAD, rank)
-    total = reduce_z(reduce_plane(reduce_core(summed)))
-    left = spread_core(spread_plane(own_left_rows(own_init, total))).reshape(m, rank)
+    core_sum = reduce_core(summed)
+    own_init = after(own_rows(left_init), core_sum)
+
+    half = rank // 2
+    groups = rank // second_right_init.shape[1]
+    rider = lax.dynamic_slice_in_dim(second_right_init, lax.axis_index("row") % 2 * half, half, 0)
+    rider = jnp.concatenate(jnp.split(rider, groups, axis=0), axis=1)
+    plane, riders = reduce_plane_with(core_sum, rider)
+    total = reduce_z(plane)
+    near = spread_plane(own_left_rows(own_init, total))
+    both = spread_core(jnp.concatenate([near, riders], axis=1))
+    left = both[:, :, :rows_own].reshape(m, rank)
+    whole = both[:, :, rows_own:].reshape(2, col_devices, half // groups, groups, -1)
+    whole = whole.transpose(0, 3, 2, 1, 4).reshape(rank, k // rank, rank).transpose(1, 0, 2)
+
+    second_rows = second_left_init.shape[0] // col_devices
+    place = lax.axis_index("col").astype(jnp.int32)[None]
+    second_left, col_part = prepare(place, second_left, devices, slices, second_rows)
+    arrived = exchange(after(second_left, left))
     right, summed = full_turn(tensor_slab, left, right, col_part, k, parts, VMEM_BYTES)
-    second_left = arrived[:, : per_owner * slices].reshape(rank * slices, rank)
-    whole = arrived[:, per_owner * slices :].reshape(row_devices, col_devices, piece_rows, -1)
-    whole = whole.transpose(0, 2, 1, 3).reshape(rank, k // rank, rank).transpose(1, 0, 2)
+    arrived = after(arrived, summed)
+    second_left = arrived.reshape(rank * slices, rank)
     numerator = second_numerator(right, second_left, whole, slices)
 
     rows_part = k // parts

time: 125 us -> 112 us (0.90)
  Pallas kernels: 35.7 us -> 30.4 us
  local copies, waits for them, and re-layouts: 5.92 us -> 2.87 us
  starting transfers between devices: 34.5 us -> 32.1 us
  other arithmetic: 3.52 us -> 1.76 us
    pallas_call x2, Pallas kernels: 32 us -> 24.9 us  [full_turn(): pl.pallas_call(turn_kernel, grid=(columns // block,), in_specs=[columns_s...]
    all_to_all x2, starting transfers between devices: 10.8 us -> 7.12 us  [exchange(): return lax.all_to_all(parts, AXES, split_axis=0, concat_axis=0, tiled=True)]
    concatenate x1 -> x0, local copies, waits for them, and re-layouts: 2.13 us -> none  [body(): arrived = exchange(jnp.concatenate(second_factors, axis=1))]
    pallas_call x0 -> x1, Pallas kernels: none -> 1.69 us  [prepare(): pl.pallas_call(functools.partial(prepare_kernel, slices), grid_spec=pltpu...]
  transfers between devices with their start and end apart: 24 -> 24, of which waited for: 20 -> 20; matrix products, arithmetic and copies ran while one was open for 2% -> 2% of each run, Pallas kernels for 13% -> 12%
where the time goes in v11:
time: 112 us
  waiting for transfers between devices  43.8 us (39%)
  starting transfers between devices  32.1 us (29%)
  Pallas kernels  30.4 us (27%)
  local copies, waits for them, and re-layouts  2.87 us (3%)
  other arithmetic  1.76 us (2%)
    ppermute x22, waiting for transfers between devices, send(): return lax.ppermute(values, AXES, pairs)  33.7 us
    ppermute x22, starting transfers between devices, send(): return lax.ppermute(values, AXES, pairs)  25 us
    pallas_call x2, Pallas kernels, full_turn(): pl.pallas_call(turn_kernel, grid=(columns // block,), in_specs=[columns_s...  24.9 us
    all_to_all x2, waiting for transfers between devices, exchange(): return lax.all_to_all(parts, AXES, split_axis=0, concat_axis=0, tiled=True)  10.1 us
    all_to_all x2, starting transfers between devices, exchange(): return lax.all_to_all(parts, AXES, split_axis=0, concat_axis=0, tiled=True)  7.12 us
  transfers between devices with their start and end apart: 24, of which 20 were waited for; matrix products, arithmetic and copies ran while one was open for 2% of the time, Pallas kernels for 12%

profile of v11, /device:TPU:0, one launch (start us, length us, event | category | flops | bytes accessed | tf_op | source)
XLA Modules:
  0.0 111.9 jit_solution(3460756500982858792)
XLA Ops:
  0.6 0.0 copy-start
  0.7 0.0 copy-start.1
  0.7 1.1 copy-done.1
  1.7 12.8 %turn.2 = (f32[128,2048]{1,0:T(8,128)}, f32[8,136,128]{2,1,0:T(8,128)S(1)}) custom-call(f32[1024,2048]{1,0:T(8,128)} %slab_ref.3, f32[1024,128]{1,0:T(8,128)S(1)} %copy-done.1, f32[128,2048]{1,0:T(8,128)} %right_ref.1, f32[1024,128]{1,0:T(8,128)S(1)} %copy-done.1), custom_call_target="tpu_custom_call" | custom-call | flops 6442450944 | bytes 8388608 | tf_op jit(solution)/shard_map/turn/pallas_call | solution.py:269
  14.6 0.5 collective-permute-start
  15.1 0.8 constant_dynamic-slice_fusion.13
  15.9 0.3 collective-permute-done
  16.4 2.9 %collective-permute-start.1 = (f32[200,128]{1,0:T(8,128)S(1)}, f32[200,128]{1,0:T(8,128)S(1)}, u32[]{:S(2)}, u32[]{:S(2)}) collective-permute-start(f32[200,128]{1,0:T(8,128)S(1)} %get-tuple-element.52), channel_id=1, source_target_pairs={{0,1},{1,0},{2,3},{3,2},{4,5},{5,4},{6,7},{7,6},{8,9},{9,8},{10,11... | collective-permute-start | bytes 307208 | tf_op jit(solution)/shard_map/ppermute | solution.py:31
  19.3 1.5 %collective-permute-start.2 = (f32[200,128]{1,0:T(8,128)S(1)}, f32[200,128]{1,0:T(8,128)S(1)}, u32[]{:S(2)}, u32[]{:S(2)}) collective-permute-start(f32[200,128]{1,0:T(8,128)S(1)} %get-tuple-element.53), channel_id=1, source_target_pairs={{0,2},{1,3},{2,0},{3,1},{4,6},{5,7},{6,4},{7,5},{8,10},{9,11},{10,... | collective-permute-start | bytes 307208 | tf_op jit(solution)/shard_map/ppermute | solution.py:31
  20.8 0.0 collective-permute-start.3
  20.8 1.7 %collective-permute-done.1 = f32[200,128]{1,0:T(8,128)S(1)} collective-permute-done((f32[200,128]{1,0:T(8,128)S(1)}, f32[200,128]{1,0:T(8,128)S(1)}, u32[]{:S(2)}, u32[]{:S(2)}) %collective-permute-start.1) | collective-permute-done | bytes 102432 | tf_op jit(solution)/shard_map/ppermute | solution.py:31
  22.5 2.6 %collective-permute-done.2 = f32[200,128]{1,0:T(8,128)S(1)} collective-permute-done((f32[200,128]{1,0:T(8,128)S(1)}, f32[200,128]{1,0:T(8,128)S(1)}, u32[]{:S(2)}, u32[]{:S(2)}) %collective-permute-start.2) | collective-permute-done | bytes 102432 | tf_op jit(solution)/shard_map/ppermute | solution.py:31
  25.2 1.2 %collective-permute-done.3 = f32[200,128]{1,0:T(8,128)S(1)} collective-permute-done((f32[200,128]{1,0:T(8,128)S(1)}, f32[200,128]{1,0:T(8,128)S(1)}, u32[]{:S(2)}, u32[]{:S(2)}) %collective-permute-start.3) | collective-permute-done | bytes 102432 | tf_op jit(solution)/shard_map/ppermute | solution.py:31
  26.4 3.7 %collective-permute-start.6 = (f32[136,128]{1,0:T(8,128)S(1)}, f32[136,128]{1,0:T(8,128)S(1)}, u32[]{:S(2)}, u32[]{:S(2)}) collective-permute-start(f32[136,128]{1,0:T(8,128)S(1)} %fusion.13), channel_id=1, source_target_pairs={{0,24},{1,25},{2,26},{3,27},{4,28},{5,29},{6,30},{7,31},{8,16},{9,... | collective-permute-start | bytes 208904 | tf_op jit(solution)/shard_map/ppermute | solution.py:31
  30.0 0.0 collective-permute-start.5
  30.1 0.8 collective-permute-start.4
  30.9 1.7 %collective-permute-done.6 = f32[136,128]{1,0:T(8,128)S(1)} collective-permute-done((f32[136,128]{1,0:T(8,128)S(1)}, f32[136,128]{1,0:T(8,128)S(1)}, u32[]{:S(2)}, u32[]{:S(2)}) %collective-permute-start.6) | collective-permute-done | bytes 69664 | tf_op jit(solution)/shard_map/ppermute | solution.py:31
  32.6 2.7 %collective-permute-done.5 = f32[136,128]{1,0:T(8,128)S(1)} collective-permute-done((f32[136,128]{1,0:T(8,128)S(1)}, f32[136,128]{1,0:T(8,128)S(1)}, u32[]{:S(2)}, u32[]{:S(2)}) %collective-permute-start.5) | collective-permute-done | bytes 69664 | tf_op jit(solution)/shard_map/ppermute | solution.py:31
  35.3 0.0 collective-permute-done.4
  35.3 1.6 %collective-permute-start.9 = (f32[128,128]{1,0:T(8,128)S(1)}, f32[128,128]{1,0:T(8,128)S(1)}, u32[]{:S(2)}, u32[]{:S(2)}) collective-permute-start(f32[128,128]{1,0:T(8,128)S(1)} %fusion.15), channel_id=1, source_target_pairs={{0,3},{1,2},{2,1},{3,0},{4,7},{5,6},{6,5},{7,4},{8,11},{9,10},{10,... | collective-permute-start | bytes 196616 | tf_op jit(solution)/shard_map/ppermute | solution.py:31
  36.9 1.3 %collective-permute-start.8 = (f32[128,128]{1,0:T(8,128)S(1)}, f32[128,128]{1,0:T(8,128)S(1)}, u32[]{:S(2)}, u32[]{:S(2)}) collective-permute-start(f32[128,128]{1,0:T(8,128)S(1)} %fusion.15), channel_id=1, source_target_pairs={{0,2},{1,3},{2,0},{3,1},{4,6},{5,7},{6,4},{7,5},{8,10},{9,11},{10,... | collective-permute-start | bytes 196616 | tf_op jit(solution)/shard_map/ppermute | solution.py:31
  38.2 0.7 collective-permute-start.7
  38.9 1.8 %collective-permute-done.9 = f32[128,128]{1,0:T(8,128)S(1)} collective-permute-done((f32[128,128]{1,0:T(8,128)S(1)}, f32[128,128]{1,0:T(8,128)S(1)}, u32[]{:S(2)}, u32[]{:S(2)}) %collective-permute-start.9) | collective-permute-done | bytes 65568 | tf_op jit(solution)/shard_map/ppermute | solution.py:31
  40.7 0.7 collective-permute-done.8
  41.4 1.1 collective-permute-done.7
  42.5 0.1 maximum_maximum_fusion
  42.6 0.1 collective-permute-start.10
  42.7 1.7 %prepare.1 = (f32[32,16,128]{2,1,0:T(8,128)}, f32[1,128]{1,0:T(1,128)S(1)}) custom-call(s32[1]{0:T(128)} %bitcast.19.place_ref, f32[2048,128]{1,0:T(8,128)} %second_left_ref), custom_call_target="tpu_custom_call" | custom-call | flops 65536 | bytes 524288 | tf_op jit(solution)/shard_map/prepare/pallas_call | solution.py:322
  44.4 0.0 collective-permute-done.10
  44.4 0.2 fusion.9
  44.6 3.3 %all-to-all-start = ((f32[32,16,128]{2,1,0:T(8,128)}), f32[32,16,128]{2,1,0:T(8,128)S(1)}, u32[]{:S(2)}, u32[]{:S(2)}) async-start(f32[32,16,128]{2,1,0:T(8,128)} %get-tuple-element.20), calls=%async_computation | async-start | bytes 524288 | tf_op jit(solution)/shard_map/all_to_all | solution.py:21
  48.0 12.2 %turn.3 = (f32[128,2048]{1,0:T(8,128)S(1)}, f32[8,136,128]{2,1,0:T(8,128)S(1)}) custom-call(f32[1024,2048]{1,0:T(8,128)} %slab_ref.3, f32[1024,128]{1,0:T(8,128)S(1)} %bitcast.87, f32[128,2048]{1,0:T(8,128)} %get-tuple-element.14.right_ref, f32[1,128]{1,0:T(1,128)S(1)} %get-tuple-element.16.extra_ref), custom_call_target="tpu_custom_call" | custom-call | flops 6442450944 | bytes 8388608 | tf_op jit(solution)/shard_map/turn/pallas_call | solution.py:269
  60.1 0.0 all-to-all-done
  60.1 1.6 %second_numerator.1 = f32[4,128,128]{2,1,0:T(8,128)S(1)} custom-call(f32[128,2048]{1,0:T(8,128)S(1)} %get-tuple-element.18.right_ref, f32[512,128]{1,0:T(8,128)S(1)} %bitcast.78, f32[4,128,128]{2,1,0:T(8,128)S(1)} %bitcast.80), custom_call_target="tpu_custom_call" | custom-call | flops 402653184 | bytes 1048576 | tf_op jit(solution)/shard_map/second_numerator/pallas_call | solution.py:288
  61.8 0.3 collective-permute-start.11
  62.1 1.5 %collective-permute-done.11 = f32[4,200,128]{2,1,0:T(8,128)S(1)} collective-permute-done((f32[4,200,128]{2,1,0:T(8,128)S(1)}, f32[4,200,128]{2,1,0:T(8,128)S(1)}, u32[]{:S(2)}, u32[]{:S(2)}) %collective-permute-start.11) | collective-permute-done | bytes 409632 | tf_op jit(solution)/shard_map/ppermute | solution.py:31
  63.7 2.7 %collective-permute-start.14 = (f32[200,128]{1,0:T(8,128)S(1)}, f32[200,128]{1,0:T(8,128)S(1)}, u32[]{:S(2)}, u32[]{:S(2)}) collective-permute-start(f32[200,128]{1,0:T(8,128)S(1)} %get-tuple-element.26), channel_id=1, source_target_pairs={{0,3},{1,2},{2,1},{3,0},{4,7},{5,6},{6,5},{7,4},{8,11},{9,10},{10,... | collective-permute-start | bytes 307208 | tf_op jit(solution)/shard_map/ppermute | solution.py:31
  66.4 0.6 collective-permute-start.13
  67.0 0.3 collective-permute-start.12
  67.2 2.5 %collective-permute-done.14 = f32[200,128]{1,0:T(8,128)S(1)} collective-permute-done((f32[200,128]{1,0:T(8,128)S(1)}, f32[200,128]{1,0:T(8,128)S(1)}, u32[]{:S(2)}, u32[]{:S(2)}) %collective-permute-start.14) | collective-permute-done | bytes 102432 | tf_op jit(solution)/shard_map/ppermute | solution.py:31
  69.8 2.1 %collective-permute-done.13 = f32[200,128]{1,0:T(8,128)S(1)} collective-permute-done((f32[200,128]{1,0:T(8,128)S(1)}, f32[200,128]{1,0:T(8,128)S(1)}, u32[]{:S(2)}, u32[]{:S(2)}) %collective-permute-start.13) | collective-permute-done | bytes 102432 | tf_op jit(solution)/shard_map/ppermute | solution.py:31
  71.9 0.2 collective-permute-done.12
  72.1 3.4 %collective-permute-start.17 = (f32[200,128]{1,0:T(8,128)S(1)}, f32[200,128]{1,0:T(8,128)S(1)}, u32[]{:S(2)}, u32[]{:S(2)}) collective-permute-start(f32[200,128]{1,0:T(8,128)S(1)} %fusion.12), channel_id=1, source_target_pairs={{0,24},{1,25},{2,26},{3,27},{4,28},{5,29},{6,30},{7,31},{8,16},{9,... | collective-permute-start | bytes 307208 | tf_op jit(solution)/shard_map/ppermute | solution.py:31
  75.5 0.0 collective-permute-start.16
  75.5 1.0 collective-permute-start.15
  76.6 3.0 %collective-permute-done.17 = f32[200,128]{1,0:T(8,128)S(1)} collective-permute-done((f32[200,128]{1,0:T(8,128)S(1)}, f32[200,128]{1,0:T(8,128)S(1)}, u32[]{:S(2)}, u32[]{:S(2)}) %collective-permute-start.17) | collective-permute-done | bytes 102432 | tf_op jit(solution)/shard_map/ppermute | solution.py:31
  79.5 4.9 %collective-permute-done.16 = f32[200,128]{1,0:T(8,128)S(1)} collective-permute-done((f32[200,128]{1,0:T(8,128)S(1)}, f32[200,128]{1,0:T(8,128)S(1)}, u32[]{:S(2)}, u32[]{:S(2)}) %collective-permute-start.16) | collective-permute-done | bytes 102432 | tf_op jit(solution)/shard_map/ppermute | solution.py:31
  84.5 0.0 collective-permute-done.15
  84.5 0.1 broadcast_divide_fusion
  84.7 1.5 %collective-permute-start.19 = (f32[192,128]{1,0:T(8,128)S(1)}, f32[192,128]{1,0:T(8,128)S(1)}, u32[]{:S(2)}, u32[]{:S(2)}) collective-permute-start(f32[192,128]{1,0:T(8,128)S(1)} %get-tuple-element.51), channel_id=1, source_target_pairs={{0,2},{1,3},{2,0},{3,1},{4,6},{5,7},{6,4},{7,5},{8,10},{9,11},{10,... | collective-permute-start | bytes 294920 | tf_op jit(solution)/shard_map/ppermute | solution.py:31
  86.2 0.2 collective-permute-start.18
  86.4 1.8 %collective-permute-start.20 = (f32[192,128]{1,0:T(8,128)S(1)}, f32[192,128]{1,0:T(8,128)S(1)}, u32[]{:S(2)}, u32[]{:S(2)}) collective-permute-start(f32[192,128]{1,0:T(8,128)S(1)} %get-tuple-element.51), channel_id=1, source_target_pairs={{0,3},{1,2},{2,1},{3,0},{4,7},{5,6},{6,5},{7,4},{8,11},{9,10},{10,... | collective-permute-start | bytes 294920 | tf_op jit(solution)/shard_map/ppermute | solution.py:31
  88.2 2.2 %collective-permute-done.19 = f32[192,128]{1,0:T(8,128)S(1)} collective-permute-done((f32[192,128]{1,0:T(8,128)S(1)}, f32[192,128]{1,0:T(8,128)S(1)}, u32[]{:S(2)}, u32[]{:S(2)}) %collective-permute-start.19) | collective-permute-done | bytes 98336 | tf_op jit(solution)/shard_map/ppermute | solution.py:31
  90.4 0.5 collective-permute-done.18
  90.9 1.2 %collective-permute-done.20 = f32[192,128]{1,0:T(8,128)S(1)} collective-permute-done((f32[192,128]{1,0:T(8,128)S(1)}, f32[192,128]{1,0:T(8,128)S(1)}, u32[]{:S(2)}, u32[]{:S(2)}) %collective-permute-start.20) | collective-permute-done | bytes 98336 | tf_op jit(solution)/shard_map/ppermute | solution.py:31
  92.2 0.1 pad_maximum_fusion.1
  92.3 0.1 collective-permute-start.21
  92.3 1.7 %collective-permute-done.21 = f32[4,192,128]{2,1,0:T(8,128)S(1)} collective-permute-done((f32[4,192,128]{2,1,0:T(8,128)S(1)}, f32[4,192,128]{2,1,0:T(8,128)S(1)}, u32[]{:S(2)}, u32[]{:S(2)}) %collective-permute-start.21) | collective-permute-done | bytes 393248 | tf_op jit(solution)/shard_map/ppermute | solution.py:31
  94.1 0.2 fusion.7
  94.2 2.2 %second_rows.1 = f32[512,128]{1,0:T(8,128)} custom-call(f32[128,2048]{1,0:T(8,128)S(1)} %get-tuple-element.18.right_ref, f32[512,128]{1,0:T(8,128)S(1)} %bitcast.79, f32[4,128,128]{2,1,0:T(8,128)S(1)} %bitcast.86), custom_call_target="tpu_custom_call" | custom-call | flops 402653184 | bytes 1048576 | tf_op jit(solution)/shard_map/second_rows/pallas_call | solution.py:298
  96.4 3.8 %all-to-all-start.1 = ((f32[32,16,128]{2,1,0:T(8,128)}), f32[32,16,128]{2,1,0:T(8,128)S(1)}, u32[]{:S(2)}, u32[]{:S(2)}) async-start(f32[32,16,128]{2,1,0:T(8,128)} %bitcast.45), calls=%async_computation.1 | async-start | bytes 524288 | tf_op jit(solution)/shard_map/all_to_all | solution.py:21
  100.2 0.8 fusion
  101.1 10.1 %all-to-all-done.1 = f32[32,16,128]{2,1,0:T(8,128)S(1)} async-done(((f32[32,16,128]{2,1,0:T(8,128)}), f32[32,16,128]{2,1,0:T(8,128)S(1)}, u32[]{:S(2)}, u32[]{:S(2)}) %all-to-all-start.1) | async-done | bytes 262176 | tf_op jit(solution)/shard_map/all_to_all | solution.py:21
  111.2 0.7 copy.8
  (33 shorter events, 0.6 us)
Async XLA Ops:
  0.6 14.4 %copy-start = (f32[128,128]{1,0:T(8,128)S(1)}, f32[128,128]{1,0:T(8,128)}, u32[]{:S(2)}) copy-start(f32[128,128]{1,0:T(8,128)} %param.9) | copy-start | bytes 196612
  0.7 1.1 copy-start.1
  14.6 1.7 %collective-permute-start = (f32[4,136,128]{2,1,0:T(8,128)S(1)}, f32[4,136,128]{2,1,0:T(8,128)S(1)}, u32[]{:S(2)}, u32[]{:S(2)}) collective-permute-start(f32[4,136,128]{2,1,0:T(8,128)S(1)} %dynamic-slice_bitcast_fusion), channel_id=1, source_target_pairs={{0,4},{1,5},{2,6},{3,7},{4,0},{5,1},{6,2},{7,3},{8,12},{9,13},{10,... | collective-permute-start | bytes 835592 | tf_op jit(solution)/shard_map/ppermute | solution.py:31
  16.4 6.2 %collective-permute-start.1 = (f32[200,128]{1,0:T(8,128)S(1)}, f32[200,128]{1,0:T(8,128)S(1)}, u32[]{:S(2)}, u32[]{:S(2)}) collective-permute-start(f32[200,128]{1,0:T(8,128)S(1)} %get-tuple-element.52), channel_id=1, source_target_pairs={{0,1},{1,0},{2,3},{3,2},{4,5},{5,4},{6,7},{7,6},{8,9},{9,8},{10,11... | collective-permute-start | bytes 307208 | tf_op jit(solution)/shard_map/ppermute | solution.py:31
  19.3 5.9 %collective-permute-start.2 = (f32[200,128]{1,0:T(8,128)S(1)}, f32[200,128]{1,0:T(8,128)S(1)}, u32[]{:S(2)}, u32[]{:S(2)}) collective-permute-start(f32[200,128]{1,0:T(8,128)S(1)} %get-tuple-element.53), channel_id=1, source_target_pairs={{0,2},{1,3},{2,0},{3,1},{4,6},{5,7},{6,4},{7,5},{8,10},{9,11},{10,... | collective-permute-start | bytes 307208 | tf_op jit(solution)/shard_map/ppermute | solution.py:31
  20.8 5.6 %collective-permute-start.3 = (f32[200,128]{1,0:T(8,128)S(1)}, f32[200,128]{1,0:T(8,128)S(1)}, u32[]{:S(2)}, u32[]{:S(2)}) collective-permute-start(f32[200,128]{1,0:T(8,128)S(1)} %get-tuple-element.54), channel_id=1, source_target_pairs={{0,3},{1,2},{2,1},{3,0},{4,7},{5,6},{6,5},{7,4},{8,11},{9,10},{10,... | collective-permute-start | bytes 307208 | tf_op jit(solution)/shard_map/ppermute | solution.py:31
  26.4 6.2 %collective-permute-start.6 = (f32[136,128]{1,0:T(8,128)S(1)}, f32[136,128]{1,0:T(8,128)S(1)}, u32[]{:S(2)}, u32[]{:S(2)}) collective-permute-start(f32[136,128]{1,0:T(8,128)S(1)} %fusion.13), channel_id=1, source_target_pairs={{0,24},{1,25},{2,26},{3,27},{4,28},{5,29},{6,30},{7,31},{8,16},{9,... | collective-permute-start | bytes 208904 | tf_op jit(solution)/shard_map/ppermute | solution.py:31
  30.0 5.2 %collective-permute-start.5 = (f32[136,128]{1,0:T(8,128)S(1)}, f32[136,128]{1,0:T(8,128)S(1)}, u32[]{:S(2)}, u32[]{:S(2)}) collective-permute-start(f32[136,128]{1,0:T(8,128)S(1)} %fusion.13), channel_id=1, source_target_pairs={{0,16},{1,17},{2,18},{3,19},{4,20},{5,21},{6,22},{7,23},{8,24},{9,... | collective-permute-start | bytes 208904 | tf_op jit(solution)/shard_map/ppermute | solution.py:31
  30.1 5.2 %collective-permute-start.4 = (f32[136,128]{1,0:T(8,128)S(1)}, f32[136,128]{1,0:T(8,128)S(1)}, u32[]{:S(2)}, u32[]{:S(2)}) collective-permute-start(f32[136,128]{1,0:T(8,128)S(1)} %fusion.13), channel_id=1, source_target_pairs={{0,8},{1,9},{2,10},{3,11},{4,12},{5,13},{6,14},{7,15},{8,0},{9,1},... | collective-permute-start | bytes 208904 | tf_op jit(solution)/shard_map/ppermute | solution.py:31
  35.3 5.4 %collective-permute-start.9 = (f32[128,128]{1,0:T(8,128)S(1)}, f32[128,128]{1,0:T(8,128)S(1)}, u32[]{:S(2)}, u32[]{:S(2)}) collective-permute-start(f32[128,128]{1,0:T(8,128)S(1)} %fusion.15), channel_id=1, source_target_pairs={{0,3},{1,2},{2,1},{3,0},{4,7},{5,6},{6,5},{7,4},{8,11},{9,10},{10,... | collective-permute-start | bytes 196616 | tf_op jit(solution)/shard_map/ppermute | solution.py:31
  36.9 4.5 %collective-permute-start.8 = (f32[128,128]{1,0:T(8,128)S(1)}, f32[128,128]{1,0:T(8,128)S(1)}, u32[]{:S(2)}, u32[]{:S(2)}) collective-permute-start(f32[128,128]{1,0:T(8,128)S(1)} %fusion.15), channel_id=1, source_target_pairs={{0,2},{1,3},{2,0},{3,1},{4,6},{5,7},{6,4},{7,5},{8,10},{9,11},{10,... | collective-permute-start | bytes 196616 | tf_op jit(solution)/shard_map/ppermute | solution.py:31
  38.2 4.3 %collective-permute-start.7 = (f32[128,128]{1,0:T(8,128)S(1)}, f32[128,128]{1,0:T(8,128)S(1)}, u32[]{:S(2)}, u32[]{:S(2)}) collective-permute-start(f32[128,128]{1,0:T(8,128)S(1)} %fusion.15), channel_id=1, source_target_pairs={{0,1},{1,0},{2,3},{3,2},{4,5},{5,4},{6,7},{7,6},{8,9},{9,8},{10,11... | collective-permute-start | bytes 196616 | tf_op jit(solution)/shard_map/ppermute | solution.py:31
  42.6 1.8 %collective-permute-start.10 = (f32[4,192,128]{2,1,0:T(8,128)S(1)}, f32[4,192,128]{2,1,0:T(8,128)S(1)}, u32[]{:S(2)}, u32[]{:S(2)}) collective-permute-start(f32[4,192,128]{2,1,0:T(8,128)S(1)} %get-tuple-element.35), channel_id=1, source_target_pairs={{0,4},{1,5},{2,6},{3,7},{4,0},{5,1},{6,2},{7,3},{8,12},{9,13},{10,... | collective-permute-start | bytes 1179656 | tf_op jit(solution)/shard_map/ppermute | solution.py:31
  44.6 15.5 %all-to-all-start = ((f32[32,16,128]{2,1,0:T(8,128)}), f32[32,16,128]{2,1,0:T(8,128)S(1)}, u32[]{:S(2)}, u32[]{:S(2)}) async-start(f32[32,16,128]{2,1,0:T(8,128)} %get-tuple-element.20), calls=%async_computation | async-start | bytes 524288 | tf_op jit(solution)/shard_map/all_to_all | solution.py:21
  61.8 1.8 %collective-permute-start.11 = (f32[4,200,128]{2,1,0:T(8,128)S(1)}, f32[4,200,128]{2,1,0:T(8,128)S(1)}, u32[]{:S(2)}, u32[]{:S(2)}) collective-permute-start(f32[4,200,128]{2,1,0:T(8,128)S(1)} %fusion.3), channel_id=1, source_target_pairs={{0,4},{1,5},{2,6},{3,7},{4,0},{5,1},{6,2},{7,3},{8,12},{9,13},{10,... | collective-permute-start | bytes 1228808 | tf_op jit(solution)/shard_map/ppermute | solution.py:31
  63.7 6.1 %collective-permute-start.14 = (f32[200,128]{1,0:T(8,128)S(1)}, f32[200,128]{1,0:T(8,128)S(1)}, u32[]{:S(2)}, u32[]{:S(2)}) collective-permute-start(f32[200,128]{1,0:T(8,128)S(1)} %get-tuple-element.26), channel_id=1, source_target_pairs={{0,3},{1,2},{2,1},{3,0},{4,7},{5,6},{6,5},{7,4},{8,11},{9,10},{10,... | collective-permute-start | bytes 307208 | tf_op jit(solution)/shard_map/ppermute | solution.py:31
  66.4 5.5 %collective-permute-start.13 = (f32[200,128]{1,0:T(8,128)S(1)}, f32[200,128]{1,0:T(8,128)S(1)}, u32[]{:S(2)}, u32[]{:S(2)}) collective-permute-start(f32[200,128]{1,0:T(8,128)S(1)} %get-tuple-element.27), channel_id=1, source_target_pairs={{0,2},{1,3},{2,0},{3,1},{4,6},{5,7},{6,4},{7,5},{8,10},{9,11},{10,... | collective-permute-start | bytes 307208 | tf_op jit(solution)/shard_map/ppermute | solution.py:31
  67.0 5.1 %collective-permute-start.12 = (f32[200,128]{1,0:T(8,128)S(1)}, f32[200,128]{1,0:T(8,128)S(1)}, u32[]{:S(2)}, u32[]{:S(2)}) collective-permute-start(f32[200,128]{1,0:T(8,128)S(1)} %get-tuple-element.28), channel_id=1, source_target_pairs={{0,1},{1,0},{2,3},{3,2},{4,5},{5,4},{6,7},{7,6},{8,9},{9,8},{10,11... | collective-permute-start | bytes 307208 | tf_op jit(solution)/shard_map/ppermute | solution.py:31
  72.1 7.4 %collective-permute-start.17 = (f32[200,128]{1,0:T(8,128)S(1)}, f32[200,128]{1,0:T(8,128)S(1)}, u32[]{:S(2)}, u32[]{:S(2)}) collective-permute-start(f32[200,128]{1,0:T(8,128)S(1)} %fusion.12), channel_id=1, source_target_pairs={{0,24},{1,25},{2,26},{3,27},{4,28},{5,29},{6,30},{7,31},{8,16},{9,... | collective-permute-start | bytes 307208 | tf_op jit(solution)/shard_map/ppermute | solution.py:31
  75.5 8.9 %collective-permute-start.16 = (f32[200,128]{1,0:T(8,128)S(1)}, f32[200,128]{1,0:T(8,128)S(1)}, u32[]{:S(2)}, u32[]{:S(2)}) collective-permute-start(f32[200,128]{1,0:T(8,128)S(1)} %fusion.12), channel_id=1, source_target_pairs={{0,16},{1,17},{2,18},{3,19},{4,20},{5,21},{6,22},{7,23},{8,24},{9,... | collective-permute-start | bytes 307208 | tf_op jit(solution)/shard_map/ppermute | solution.py:31
  75.5 8.9 %collective-permute-start.15 = (f32[200,128]{1,0:T(8,128)S(1)}, f32[200,128]{1,0:T(8,128)S(1)}, u32[]{:S(2)}, u32[]{:S(2)}) collective-permute-start(f32[200,128]{1,0:T(8,128)S(1)} %fusion.12), channel_id=1, source_target_pairs={{0,8},{1,9},{2,10},{3,11},{4,12},{5,13},{6,14},{7,15},{8,0},{9,1},... | collective-permute-start | bytes 307208 | tf_op jit(solution)/shard_map/ppermute | solution.py:31
  84.7 5.7 %collective-permute-start.19 = (f32[192,128]{1,0:T(8,128)S(1)}, f32[192,128]{1,0:T(8,128)S(1)}, u32[]{:S(2)}, u32[]{:S(2)}) collective-permute-start(f32[192,128]{1,0:T(8,128)S(1)} %get-tuple-element.51), channel_id=1, source_target_pairs={{0,2},{1,3},{2,0},{3,1},{4,6},{5,7},{6,4},{7,5},{8,10},{9,11},{10,... | collective-permute-start | bytes 294920 | tf_op jit(solution)/shard_map/ppermute | solution.py:31
  86.2 4.7 %collective-permute-start.18 = (f32[192,128]{1,0:T(8,128)S(1)}, f32[192,128]{1,0:T(8,128)S(1)}, u32[]{:S(2)}, u32[]{:S(2)}) collective-permute-start(f32[192,128]{1,0:T(8,128)S(1)} %get-tuple-element.51), channel_id=1, source_target_pairs={{0,1},{1,0},{2,3},{3,2},{4,5},{5,4},{6,7},{7,6},{8,9},{9,8},{10,11... | collective-permute-start | bytes 294920 | tf_op jit(solution)/shard_map/ppermute | solution.py:31
  86.4 5.7 %collective-permute-start.20 = (f32[192,128]{1,0:T(8,128)S(1)}, f32[192,128]{1,0:T(8,128)S(1)}, u32[]{:S(2)}, u32[]{:S(2)}) collective-permute-start(f32[192,128]{1,0:T(8,128)S(1)} %get-tuple-element.51), channel_id=1, source_target_pairs={{0,3},{1,2},{2,1},{3,0},{4,7},{5,6},{6,5},{7,4},{8,11},{9,10},{10,... | collective-permute-start | bytes 294920 | tf_op jit(solution)/shard_map/ppermute | solution.py:31
  92.3 1.8 %collective-permute-start.21 = (f32[4,192,128]{2,1,0:T(8,128)S(1)}, f32[4,192,128]{2,1,0:T(8,128)S(1)}, u32[]{:S(2)}, u32[]{:S(2)}) collective-permute-start(f32[4,192,128]{2,1,0:T(8,128)S(1)} %get-tuple-element.29), channel_id=1, source_target_pairs={{0,4},{1,5},{2,6},{3,7},{4,0},{5,1},{6,2},{7,3},{8,12},{9,13},{10,... | collective-permute-start | bytes 1179656 | tf_op jit(solution)/shard_map/ppermute | solution.py:31
  96.4 14.7 %all-to-all-start.1 = ((f32[32,16,128]{2,1,0:T(8,128)}), f32[32,16,128]{2,1,0:T(8,128)S(1)}, u32[]{:S(2)}, u32[]{:S(2)}) async-start(f32[32,16,128]{2,1,0:T(8,128)} %bitcast.45), calls=%async_computation.1 | async-start | bytes 524288 | tf_op jit(solution)/shard_map/all_to_all | solution.py:21

commit v12 on v11

--- a/solution.py
+++ b/solution.py
@@ -90,10 +90,6 @@
 
 def dot(a, b):
     return jnp.dot(a, b, preferred_element_type=F32)
-
-
-def dot_nt(a, b):
-    return lax.dot_general(a, b, (((1,), (1,)), ((), ())), preferred_element_type=F32)
 
 
 def divide(x, y):
@@ -148,15 +144,15 @@
 def left_numerator(slab_ref, pair_ref, right, total_ref, sums_ref, first):
     rank = right.shape[0]
     stack = stacked(right)
-    right_high, right_low = stack[:rank], stack[2 * rank :]
-    right_both = jnp.concatenate([right_high, right_low], axis=0)
-    row_sums = dot_nt(jnp.ones((16, right.shape[1]), BF16), right_both)[:PAD]
+    right_high, right_low = split(right.T)
+    right_both = jnp.concatenate([right_high, right_low], axis=1)
+    row_sums = dot(jnp.ones((16, right.shape[1]), BF16), right_both)[:PAD]
     row_sums = row_sums[:, :rank] + row_sums[:, rank:]
     sums_ref[...] = jnp.where(first, row_sums, sums_ref[...] + row_sums)
     for rows in chunks(slab_ref.shape[0], ROWS):
         high, low = quotients(slab_ref, pair_ref, stack, rows)
-        both = dot_nt(high, right_both)
-        term = both[:, :rank] + both[:, rank:] + dot_nt(low, right_high)
+        both = dot(high, right_both)
+        term = both[:, :rank] + both[:, rank:] + dot(low, right_high)
         total_ref[rows, :] = jnp.where(first, term, total_ref[rows, :] + term)
 
 
@@ -190,48 +186,48 @@
         write_left(total_ref, row_sums_ref, extra_ref, left_out)
 
 
-def second_quotient(block, second_left, pairs):
-    high, low = split(second_left)
-    right_high, right_low = pairs
-    product = dot(high, right_high) + (dot(low, right_high) + dot(high, right_low))
-    return split(divide(block, product))
-
-
-def numerator_kernel(slices, right_ref, second_left_ref, second_right_ref, numer_out):
+def second_parts(slices, right_ref, second_left_ref, second_right_ref):
     rank = right_ref.shape[0]
     k = right_ref.shape[1] // slices
-    pairs = split(
-        jnp.concatenate([second_right_ref[block] for block in range(k // rank)], axis=1)
-    )
-    total = 0.0
-    for index in range(slices):
-        second_left = second_left_ref[pl.ds(index, rank, stride=slices), :]
-        high, low = second_quotient(right_ref[:, pl.ds(index * k, k)], second_left, pairs)
-        left_high, left_low = split(second_left.T)
-        total = total + (dot(left_high, high) + (dot(left_low, high) + dot(left_high, low)))
-    for block in range(k // rank):
-        numer_out[block] = total[:, block * rank : (block + 1) * rank]
-
-
-def second_kernel(slices, right_ref, second_left_ref, second_right_ref, out_ref):
-    rank = right_ref.shape[0]
-    k = right_ref.shape[1] // slices
+    second_left = jnp.concatenate(
+        [second_left_ref[pl.ds(index, rank, stride=slices), :] for index in range(slices)], axis=0
+    )
     second_right = jnp.concatenate(
         [second_right_ref[block] for block in range(k // rank)], axis=1
     )
-    right_high, right_low = split(second_right)
-    right_both = jnp.concatenate([right_high, right_low], axis=0)
-    sums = dot_nt(jnp.ones((16, k), BF16), right_both)[:1]
-    scale = 1.0 / (sums[:, :rank] + sums[:, rank:])
+    high, low = split(second_left)
+    product = dot(jnp.concatenate([high, low, high], axis=1), stacked(second_right))
+    block = jnp.concatenate(
+        [right_ref[:, index * k : (index + 1) * k] for index in range(slices)], axis=0
+    )
+    return second_left, second_right, split(divide(block, product))
+
+
+def numerator_kernel(slices, right_ref, second_left_ref, second_right_ref, numer_out):
+    second_left, _, (high, low) = second_parts(
+        slices, right_ref, second_left_ref, second_right_ref
+    )
+    rank = second_left.shape[1]
+    left_both = jnp.concatenate(split(second_left.T), axis=0)
+    both = dot(left_both, high)
+    total = both[:rank] + both[rank:] + dot(left_both[:rank], low)
+    for block in range(total.shape[1] // rank):
+        numer_out[block] = total[:, block * rank : (block + 1) * rank]
+
+
+def second_kernel(slices, right_ref, second_left_ref, second_right_ref, out_ref):
+    second_left, second_right, (high, low) = second_parts(
+        slices, right_ref, second_left_ref, second_right_ref
+    )
+    rank = second_left.shape[1]
+    right_high, right_low = split(second_right.T)
+    right_both = jnp.concatenate([right_high, right_low], axis=1)
+    sums = dot(jnp.ones((16, right_both.shape[0]), BF16), right_both)[:1]
+    both = dot(high, right_both)
+    numer = both[:, :rank] + both[:, rank:] + dot(low, right_high)
+    rows = second_left * numer * (1.0 / (sums[:, :rank] + sums[:, rank:]))
     for index in range(slices):
-        rows = pl.ds(index, rank, stride=slices)
-        second_left = second_left_ref[rows, :]
-        high, low = second_quotient(
-            right_ref[:, pl.ds(index * k, k)], second_left, (right_high, right_low)
-        )
-        both = dot_nt(high, right_both)
-        numer = both[:, :rank] + both[:, rank:] + dot_nt(low, right_high)
-        out_ref[rows, :] = second_left * numer * scale
+        out_ref[pl.ds(index, rank, stride=slices), :] = rows[index * rank : (index + 1) * rank]
 
 
 def full(shape):

time: 112 us -> 111 us (level)
  Pallas kernels: 30.4 us -> 29.2 us
  transfers between devices with their start and end apart: 24 -> 24, of which waited for: 20 -> 20; matrix products, arithmetic and copies ran while one was open for 2% -> 2% of each run, Pallas kernels for 12% -> 13%
where the time goes in v12:
time: 111 us
  waiting for transfers between devices  43.8 us (39%)
  starting transfers between devices  32.1 us (29%)
  Pallas kernels  29.2 us (26%)
  local copies, waits for them, and re-layouts  2.87 us (3%)
  other arithmetic  1.76 us (2%)
    ppermute x22, waiting for transfers between devices, send(): return lax.ppermute(values, AXES, pairs)  33.7 us
    pallas_call x2, Pallas kernels, full_turn(): pl.pallas_call(turn_kernel, grid=(columns // block,), in_specs=[columns_s...  25.3 us
    ppermute x22, starting transfers between devices, send(): return lax.ppermute(values, AXES, pairs)  25 us
    all_to_all x2, waiting for transfers between devices, exchange(): return lax.all_to_all(parts, AXES, split_axis=0, concat_axis=0, tiled=True)  10.1 us
    all_to_all x2, starting transfers between devices, exchange(): return lax.all_to_all(parts, AXES, split_axis=0, concat_axis=0, tiled=True)  7.12 us
  transfers between devices with their start and end apart: 24, of which 20 were waited for; matrix products, arithmetic and copies ran while one was open for 2% of the time, Pallas kernels for 13%

profile of v12, /device:TPU:0, one launch (start us, length us, event | category | flops | bytes accessed | tf_op | source)
XLA Modules:
  0.0 110.7 jit_solution(7858418049402685481)
XLA Ops:
  0.6 0.0 copy-start
  0.7 0.0 copy-start.1
  0.7 1.1 copy-done.1
  1.7 13.0 %turn.2 = (f32[128,2048]{1,0:T(8,128)}, f32[8,136,128]{2,1,0:T(8,128)S(1)}) custom-call(f32[1024,2048]{1,0:T(8,128)} %slab_ref.3, f32[1024,128]{1,0:T(8,128)S(1)} %copy-done.1, f32[128,2048]{1,0:T(8,128)} %right_ref.1, f32[1024,128]{1,0:T(8,128)S(1)} %copy-done.1), custom_call_target="tpu_custom_call" | custom-call | flops 6442450944 | bytes 8388608 | tf_op jit(solution)/shard_map/turn/pallas_call | solution.py:265
  14.7 0.5 collective-permute-start
  15.2 0.8 constant_dynamic-slice_fusion.13
  16.1 0.3 collective-permute-done
  16.5 2.9 %collective-permute-start.1 = (f32[200,128]{1,0:T(8,128)S(1)}, f32[200,128]{1,0:T(8,128)S(1)}, u32[]{:S(2)}, u32[]{:S(2)}) collective-permute-start(f32[200,128]{1,0:T(8,128)S(1)} %get-tuple-element.52), channel_id=1, source_target_pairs={{0,1},{1,0},{2,3},{3,2},{4,5},{5,4},{6,7},{7,6},{8,9},{9,8},{10,11... | collective-permute-start | bytes 307208 | tf_op jit(solution)/shard_map/ppermute | solution.py:31
  19.4 1.5 %collective-permute-start.2 = (f32[200,128]{1,0:T(8,128)S(1)}, f32[200,128]{1,0:T(8,128)S(1)}, u32[]{:S(2)}, u32[]{:S(2)}) collective-permute-start(f32[200,128]{1,0:T(8,128)S(1)} %get-tuple-element.53), channel_id=1, source_target_pairs={{0,2},{1,3},{2,0},{3,1},{4,6},{5,7},{6,4},{7,5},{8,10},{9,11},{10,... | collective-permute-start | bytes 307208 | tf_op jit(solution)/shard_map/ppermute | solution.py:31
  21.0 0.0 collective-permute-start.3
  21.0 1.7 %collective-permute-done.1 = f32[200,128]{1,0:T(8,128)S(1)} collective-permute-done((f32[200,128]{1,0:T(8,128)S(1)}, f32[200,128]{1,0:T(8,128)S(1)}, u32[]{:S(2)}, u32[]{:S(2)}) %collective-permute-start.1) | collective-permute-done | bytes 102432 | tf_op jit(solution)/shard_map/ppermute | solution.py:31
  22.7 2.6 %collective-permute-done.2 = f32[200,128]{1,0:T(8,128)S(1)} collective-permute-done((f32[200,128]{1,0:T(8,128)S(1)}, f32[200,128]{1,0:T(8,128)S(1)}, u32[]{:S(2)}, u32[]{:S(2)}) %collective-permute-start.2) | collective-permute-done | bytes 102432 | tf_op jit(solution)/shard_map/ppermute | solution.py:31
  25.3 1.2 %collective-permute-done.3 = f32[200,128]{1,0:T(8,128)S(1)} collective-permute-done((f32[200,128]{1,0:T(8,128)S(1)}, f32[200,128]{1,0:T(8,128)S(1)}, u32[]{:S(2)}, u32[]{:S(2)}) %collective-permute-start.3) | collective-permute-done | bytes 102432 | tf_op jit(solution)/shard_map/ppermute | solution.py:31
  26.5 3.7 %collective-permute-start.6 = (f32[136,128]{1,0:T(8,128)S(1)}, f32[136,128]{1,0:T(8,128)S(1)}, u32[]{:S(2)}, u32[]{:S(2)}) collective-permute-start(f32[136,128]{1,0:T(8,128)S(1)} %fusion.13), channel_id=1, source_target_pairs={{0,24},{1,25},{2,26},{3,27},{4,28},{5,29},{6,30},{7,31},{8,16},{9,... | collective-permute-start | bytes 208904 | tf_op jit(solution)/shard_map/ppermute | solution.py:31
  30.2 0.0 collective-permute-start.5
  30.2 0.8 collective-permute-start.4
  31.0 1.7 %collective-permute-done.6 = f32[136,128]{1,0:T(8,128)S(1)} collective-permute-done((f32[136,128]{1,0:T(8,128)S(1)}, f32[136,128]{1,0:T(8,128)S(1)}, u32[]{:S(2)}, u32[]{:S(2)}) %collective-permute-start.6) | collective-permute-done | bytes 69664 | tf_op jit(solution)/shard_map/ppermute | solution.py:31
  32.7 2.7 %collective-permute-done.5 = f32[136,128]{1,0:T(8,128)S(1)} collective-permute-done((f32[136,128]{1,0:T(8,128)S(1)}, f32[136,128]{1,0:T(8,128)S(1)}, u32[]{:S(2)}, u32[]{:S(2)}) %collective-permute-start.5) | collective-permute-done | bytes 69664 | tf_op jit(solution)/shard_map/ppermute | solution.py:31
  35.4 0.0 collective-permute-done.4
  35.5 1.6 %collective-permute-start.9 = (f32[128,128]{1,0:T(8,128)S(1)}, f32[128,128]{1,0:T(8,128)S(1)}, u32[]{:S(2)}, u32[]{:S(2)}) collective-permute-start(f32[128,128]{1,0:T(8,128)S(1)} %fusion.15), channel_id=1, source_target_pairs={{0,3},{1,2},{2,1},{3,0},{4,7},{5,6},{6,5},{7,4},{8,11},{9,10},{10,... | collective-permute-start | bytes 196616 | tf_op jit(solution)/shard_map/ppermute | solution.py:31
  37.1 1.3 %collective-permute-start.8 = (f32[128,128]{1,0:T(8,128)S(1)}, f32[128,128]{1,0:T(8,128)S(1)}, u32[]{:S(2)}, u32[]{:S(2)}) collective-permute-start(f32[128,128]{1,0:T(8,128)S(1)} %fusion.15), channel_id=1, source_target_pairs={{0,2},{1,3},{2,0},{3,1},{4,6},{5,7},{6,4},{7,5},{8,10},{9,11},{10,... | collective-permute-start | bytes 196616 | tf_op jit(solution)/shard_map/ppermute | solution.py:31
  38.3 0.7 collective-permute-start.7
  39.0 1.8 %collective-permute-done.9 = f32[128,128]{1,0:T(8,128)S(1)} collective-permute-done((f32[128,128]{1,0:T(8,128)S(1)}, f32[128,128]{1,0:T(8,128)S(1)}, u32[]{:S(2)}, u32[]{:S(2)}) %collective-permute-start.9) | collective-permute-done | bytes 65568 | tf_op jit(solution)/shard_map/ppermute | solution.py:31
  40.9 0.7 collective-permute-done.8
  41.5 1.1 collective-permute-done.7
  42.7 0.1 maximum_maximum_fusion
  42.7 0.1 collective-permute-start.10
  42.8 1.7 %prepare.1 = (f32[32,16,128]{2,1,0:T(8,128)}, f32[1,128]{1,0:T(1,128)S(1)}) custom-call(s32[1]{0:T(128)} %bitcast.19.place_ref, f32[2048,128]{1,0:T(8,128)} %second_left_ref), custom_call_target="tpu_custom_call" | custom-call | flops 65536 | bytes 524288 | tf_op jit(solution)/shard_map/prepare/pallas_call | solution.py:318
  44.5 0.0 collective-permute-done.10
  44.5 0.2 fusion.9
  44.8 3.3 %all-to-all-start = ((f32[32,16,128]{2,1,0:T(8,128)}), f32[32,16,128]{2,1,0:T(8,128)S(1)}, u32[]{:S(2)}, u32[]{:S(2)}) async-start(f32[32,16,128]{2,1,0:T(8,128)} %get-tuple-element.20), calls=%async_computation | async-start | bytes 524288 | tf_op jit(solution)/shard_map/all_to_all | solution.py:21
  48.1 12.3 %turn.3 = (f32[128,2048]{1,0:T(8,128)S(1)}, f32[8,136,128]{2,1,0:T(8,128)S(1)}) custom-call(f32[1024,2048]{1,0:T(8,128)} %slab_ref.3, f32[1024,128]{1,0:T(8,128)S(1)} %bitcast.87, f32[128,2048]{1,0:T(8,128)} %get-tuple-element.14.right_ref, f32[1,128]{1,0:T(1,128)S(1)} %get-tuple-element.16.extra_ref), custom_call_target="tpu_custom_call" | custom-call | flops 6442450944 | bytes 8388608 | tf_op jit(solution)/shard_map/turn/pallas_call | solution.py:265
  60.4 0.0 all-to-all-done
  60.5 0.7 second_numerator.1
  61.2 0.3 collective-permute-start.11
  61.6 1.5 %collective-permute-done.11 = f32[4,200,128]{2,1,0:T(8,128)S(1)} collective-permute-done((f32[4,200,128]{2,1,0:T(8,128)S(1)}, f32[4,200,128]{2,1,0:T(8,128)S(1)}, u32[]{:S(2)}, u32[]{:S(2)}) %collective-permute-start.11) | collective-permute-done | bytes 409632 | tf_op jit(solution)/shard_map/ppermute | solution.py:31
  63.1 2.7 %collective-permute-start.14 = (f32[200,128]{1,0:T(8,128)S(1)}, f32[200,128]{1,0:T(8,128)S(1)}, u32[]{:S(2)}, u32[]{:S(2)}) collective-permute-start(f32[200,128]{1,0:T(8,128)S(1)} %get-tuple-element.26), channel_id=1, source_target_pairs={{0,3},{1,2},{2,1},{3,0},{4,7},{5,6},{6,5},{7,4},{8,11},{9,10},{10,... | collective-permute-start | bytes 307208 | tf_op jit(solution)/shard_map/ppermute | solution.py:31
  65.9 0.6 collective-permute-start.13
  66.4 0.3 collective-permute-start.12
  66.7 2.5 %collective-permute-done.14 = f32[200,128]{1,0:T(8,128)S(1)} collective-permute-done((f32[200,128]{1,0:T(8,128)S(1)}, f32[200,128]{1,0:T(8,128)S(1)}, u32[]{:S(2)}, u32[]{:S(2)}) %collective-permute-start.14) | collective-permute-done | bytes 102432 | tf_op jit(solution)/shard_map/ppermute | solution.py:31
  69.2 2.1 %collective-permute-done.13 = f32[200,128]{1,0:T(8,128)S(1)} collective-permute-done((f32[200,128]{1,0:T(8,128)S(1)}, f32[200,128]{1,0:T(8,128)S(1)}, u32[]{:S(2)}, u32[]{:S(2)}) %collective-permute-start.13) | collective-permute-done | bytes 102432 | tf_op jit(solution)/shard_map/ppermute | solution.py:31
  71.3 0.2 collective-permute-done.12
  71.6 3.4 %collective-permute-start.17 = (f32[200,128]{1,0:T(8,128)S(1)}, f32[200,128]{1,0:T(8,128)S(1)}, u32[]{:S(2)}, u32[]{:S(2)}) collective-permute-start(f32[200,128]{1,0:T(8,128)S(1)} %fusion.12), channel_id=1, source_target_pairs={{0,24},{1,25},{2,26},{3,27},{4,28},{5,29},{6,30},{7,31},{8,16},{9,... | collective-permute-start | bytes 307208 | tf_op jit(solution)/shard_map/ppermute | solution.py:31
  75.0 0.0 collective-permute-start.16
  75.0 1.0 collective-permute-start.15
  76.0 3.0 %collective-permute-done.17 = f32[200,128]{1,0:T(8,128)S(1)} collective-permute-done((f32[200,128]{1,0:T(8,128)S(1)}, f32[200,128]{1,0:T(8,128)S(1)}, u32[]{:S(2)}, u32[]{:S(2)}) %collective-permute-start.17) | collective-permute-done | bytes 102432 | tf_op jit(solution)/shard_map/ppermute | solution.py:31
  79.0 4.9 %collective-permute-done.16 = f32[200,128]{1,0:T(8,128)S(1)} collective-permute-done((f32[200,128]{1,0:T(8,128)S(1)}, f32[200,128]{1,0:T(8,128)S(1)}, u32[]{:S(2)}, u32[]{:S(2)}) %collective-permute-start.16) | collective-permute-done | bytes 102432 | tf_op jit(solution)/shard_map/ppermute | solution.py:31
  83.9 0.0 collective-permute-done.15
  84.0 0.1 broadcast_divide_fusion
  84.2 1.5 %collective-permute-start.19 = (f32[192,128]{1,0:T(8,128)S(1)}, f32[192,128]{1,0:T(8,128)S(1)}, u32[]{:S(2)}, u32[]{:S(2)}) collective-permute-start(f32[192,128]{1,0:T(8,128)S(1)} %get-tuple-element.51), channel_id=1, source_target_pairs={{0,2},{1,3},{2,0},{3,1},{4,6},{5,7},{6,4},{7,5},{8,10},{9,11},{10,... | collective-permute-start | bytes 294920 | tf_op jit(solution)/shard_map/ppermute | solution.py:31
  85.7 0.2 collective-permute-start.18
  85.9 1.8 %collective-permute-start.20 = (f32[192,128]{1,0:T(8,128)S(1)}, f32[192,128]{1,0:T(8,128)S(1)}, u32[]{:S(2)}, u32[]{:S(2)}) collective-permute-start(f32[192,128]{1,0:T(8,128)S(1)} %get-tuple-element.51), channel_id=1, source_target_pairs={{0,3},{1,2},{2,1},{3,0},{4,7},{5,6},{6,5},{7,4},{8,11},{9,10},{10,... | collective-permute-start | bytes 294920 | tf_op jit(solution)/shard_map/ppermute | solution.py:31
  87.7 2.2 %collective-permute-done.19 = f32[192,128]{1,0:T(8,128)S(1)} collective-permute-done((f32[192,128]{1,0:T(8,128)S(1)}, f32[192,128]{1,0:T(8,128)S(1)}, u32[]{:S(2)}, u32[]{:S(2)}) %collective-permute-start.19) | collective-permute-done | bytes 98336 | tf_op jit(solution)/shard_map/ppermute | solution.py:31
  89.9 0.5 collective-permute-done.18
  90.4 1.2 %collective-permute-done.20 = f32[192,128]{1,0:T(8,128)S(1)} collective-permute-done((f32[192,128]{1,0:T(8,128)S(1)}, f32[192,128]{1,0:T(8,128)S(1)}, u32[]{:S(2)}, u32[]{:S(2)}) %collective-permute-start.20) | collective-permute-done | bytes 98336 | tf_op jit(solution)/shard_map/ppermute | solution.py:31
  91.7 0.1 pad_maximum_fusion.1
  91.7 0.1 collective-permute-start.21
  91.8 1.7 %collective-permute-done.21 = f32[4,192,128]{2,1,0:T(8,128)S(1)} collective-permute-done((f32[4,192,128]{2,1,0:T(8,128)S(1)}, f32[4,192,128]{2,1,0:T(8,128)S(1)}, u32[]{:S(2)}, u32[]{:S(2)}) %collective-permute-start.21) | collective-permute-done | bytes 393248 | tf_op jit(solution)/shard_map/ppermute | solution.py:31
  93.5 0.2 fusion.7
  93.7 1.4 %second_rows.1 = f32[512,128]{1,0:T(8,128)} custom-call(f32[128,2048]{1,0:T(8,128)S(1)} %get-tuple-element.18.right_ref, f32[512,128]{1,0:T(8,128)S(1)} %bitcast.79, f32[4,128,128]{2,1,0:T(8,128)S(1)} %bitcast.86), custom_call_target="tpu_custom_call" | custom-call | flops 402653184 | bytes 1048576 | tf_op jit(solution)/shard_map/second_rows/pallas_call | solution.py:294
  95.2 3.8 %all-to-all-start.1 = ((f32[32,16,128]{2,1,0:T(8,128)}), f32[32,16,128]{2,1,0:T(8,128)S(1)}, u32[]{:S(2)}, u32[]{:S(2)}) async-start(f32[32,16,128]{2,1,0:T(8,128)} %bitcast.45), calls=%async_computation.1 | async-start | bytes 524288 | tf_op jit(solution)/shard_map/all_to_all | solution.py:21
  99.0 0.8 fusion
  99.8 10.1 %all-to-all-done.1 = f32[32,16,128]{2,1,0:T(8,128)S(1)} async-done(((f32[32,16,128]{2,1,0:T(8,128)}), f32[32,16,128]{2,1,0:T(8,128)S(1)}, u32[]{:S(2)}, u32[]{:S(2)}) %all-to-all-start.1) | async-done | bytes 262176 | tf_op jit(solution)/shard_map/all_to_all | solution.py:21
  109.9 0.7 copy.8
  (33 shorter events, 0.6 us)
Async XLA Ops:
  0.6 14.6 %copy-start = (f32[128,128]{1,0:T(8,128)S(1)}, f32[128,128]{1,0:T(8,128)}, u32[]{:S(2)}) copy-start(f32[128,128]{1,0:T(8,128)} %param.9) | copy-start | bytes 196612
  0.7 1.1 copy-start.1
  14.7 1.7 %collective-permute-start = (f32[4,136,128]{2,1,0:T(8,128)S(1)}, f32[4,136,128]{2,1,0:T(8,128)S(1)}, u32[]{:S(2)}, u32[]{:S(2)}) collective-permute-start(f32[4,136,128]{2,1,0:T(8,128)S(1)} %dynamic-slice_bitcast_fusion), channel_id=1, source_target_pairs={{0,4},{1,5},{2,6},{3,7},{4,0},{5,1},{6,2},{7,3},{8,12},{9,13},{10,... | collective-permute-start | bytes 835592 | tf_op jit(solution)/shard_map/ppermute | solution.py:31
  16.5 6.2 %collective-permute-start.1 = (f32[200,128]{1,0:T(8,128)S(1)}, f32[200,128]{1,0:T(8,128)S(1)}, u32[]{:S(2)}, u32[]{:S(2)}) collective-permute-start(f32[200,128]{1,0:T(8,128)S(1)} %get-tuple-element.52), channel_id=1, source_target_pairs={{0,1},{1,0},{2,3},{3,2},{4,5},{5,4},{6,7},{7,6},{8,9},{9,8},{10,11... | collective-permute-start | bytes 307208 | tf_op jit(solution)/shard_map/ppermute | solution.py:31
  19.4 5.9 %collective-permute-start.2 = (f32[200,128]{1,0:T(8,128)S(1)}, f32[200,128]{1,0:T(8,128)S(1)}, u32[]{:S(2)}, u32[]{:S(2)}) collective-permute-start(f32[200,128]{1,0:T(8,128)S(1)} %get-tuple-element.53), channel_id=1, source_target_pairs={{0,2},{1,3},{2,0},{3,1},{4,6},{5,7},{6,4},{7,5},{8,10},{9,11},{10,... | collective-permute-start | bytes 307208 | tf_op jit(solution)/shard_map/ppermute | solution.py:31
  21.0 5.6 %collective-permute-start.3 = (f32[200,128]{1,0:T(8,128)S(1)}, f32[200,128]{1,0:T(8,128)S(1)}, u32[]{:S(2)}, u32[]{:S(2)}) collective-permute-start(f32[200,128]{1,0:T(8,128)S(1)} %get-tuple-element.54), channel_id=1, source_target_pairs={{0,3},{1,2},{2,1},{3,0},{4,7},{5,6},{6,5},{7,4},{8,11},{9,10},{10,... | collective-permute-start | bytes 307208 | tf_op jit(solution)/shard_map/ppermute | solution.py:31
  26.5 6.2 %collective-permute-start.6 = (f32[136,128]{1,0:T(8,128)S(1)}, f32[136,128]{1,0:T(8,128)S(1)}, u32[]{:S(2)}, u32[]{:S(2)}) collective-permute-start(f32[136,128]{1,0:T(8,128)S(1)} %fusion.13), channel_id=1, source_target_pairs={{0,24},{1,25},{2,26},{3,27},{4,28},{5,29},{6,30},{7,31},{8,16},{9,... | collective-permute-start | bytes 208904 | tf_op jit(solution)/shard_map/ppermute | solution.py:31
  30.2 5.2 %collective-permute-start.5 = (f32[136,128]{1,0:T(8,128)S(1)}, f32[136,128]{1,0:T(8,128)S(1)}, u32[]{:S(2)}, u32[]{:S(2)}) collective-permute-start(f32[136,128]{1,0:T(8,128)S(1)} %fusion.13), channel_id=1, source_target_pairs={{0,16},{1,17},{2,18},{3,19},{4,20},{5,21},{6,22},{7,23},{8,24},{9,... | collective-permute-start | bytes 208904 | tf_op jit(solution)/shard_map/ppermute | solution.py:31
  30.2 5.2 %collective-permute-start.4 = (f32[136,128]{1,0:T(8,128)S(1)}, f32[136,128]{1,0:T(8,128)S(1)}, u32[]{:S(2)}, u32[]{:S(2)}) collective-permute-start(f32[136,128]{1,0:T(8,128)S(1)} %fusion.13), channel_id=1, source_target_pairs={{0,8},{1,9},{2,10},{3,11},{4,12},{5,13},{6,14},{7,15},{8,0},{9,1},... | collective-permute-start | bytes 208904 | tf_op jit(solution)/shard_map/ppermute | solution.py:31
  35.5 5.4 %collective-permute-start.9 = (f32[128,128]{1,0:T(8,128)S(1)}, f32[128,128]{1,0:T(8,128)S(1)}, u32[]{:S(2)}, u32[]{:S(2)}) collective-permute-start(f32[128,128]{1,0:T(8,128)S(1)} %fusion.15), channel_id=1, source_target_pairs={{0,3},{1,2},{2,1},{3,0},{4,7},{5,6},{6,5},{7,4},{8,11},{9,10},{10,... | collective-permute-start | bytes 196616 | tf_op jit(solution)/shard_map/ppermute | solution.py:31
  37.1 4.5 %collective-permute-start.8 = (f32[128,128]{1,0:T(8,128)S(1)}, f32[128,128]{1,0:T(8,128)S(1)}, u32[]{:S(2)}, u32[]{:S(2)}) collective-permute-start(f32[128,128]{1,0:T(8,128)S(1)} %fusion.15), channel_id=1, source_target_pairs={{0,2},{1,3},{2,0},{3,1},{4,6},{5,7},{6,4},{7,5},{8,10},{9,11},{10,... | collective-permute-start | bytes 196616 | tf_op jit(solution)/shard_map/ppermute | solution.py:31
  38.3 4.3 %collective-permute-start.7 = (f32[128,128]{1,0:T(8,128)S(1)}, f32[128,128]{1,0:T(8,128)S(1)}, u32[]{:S(2)}, u32[]{:S(2)}) collective-permute-start(f32[128,128]{1,0:T(8,128)S(1)} %fusion.15), channel_id=1, source_target_pairs={{0,1},{1,0},{2,3},{3,2},{4,5},{5,4},{6,7},{7,6},{8,9},{9,8},{10,11... | collective-permute-start | bytes 196616 | tf_op jit(solution)/shard_map/ppermute | solution.py:31
  42.7 1.8 %collective-permute-start.10 = (f32[4,192,128]{2,1,0:T(8,128)S(1)}, f32[4,192,128]{2,1,0:T(8,128)S(1)}, u32[]{:S(2)}, u32[]{:S(2)}) collective-permute-start(f32[4,192,128]{2,1,0:T(8,128)S(1)} %get-tuple-element.35), channel_id=1, source_target_pairs={{0,4},{1,5},{2,6},{3,7},{4,0},{5,1},{6,2},{7,3},{8,12},{9,13},{10,... | collective-permute-start | bytes 1179656 | tf_op jit(solution)/shard_map/ppermute | solution.py:31
  44.8 15.7 %all-to-all-start = ((f32[32,16,128]{2,1,0:T(8,128)}), f32[32,16,128]{2,1,0:T(8,128)S(1)}, u32[]{:S(2)}, u32[]{:S(2)}) async-start(f32[32,16,128]{2,1,0:T(8,128)} %get-tuple-element.20), calls=%async_computation | async-start | bytes 524288 | tf_op jit(solution)/shard_map/all_to_all | solution.py:21
  61.2 1.8 %collective-permute-start.11 = (f32[4,200,128]{2,1,0:T(8,128)S(1)}, f32[4,200,128]{2,1,0:T(8,128)S(1)}, u32[]{:S(2)}, u32[]{:S(2)}) collective-permute-start(f32[4,200,128]{2,1,0:T(8,128)S(1)} %fusion.3), channel_id=1, source_target_pairs={{0,4},{1,5},{2,6},{3,7},{4,0},{5,1},{6,2},{7,3},{8,12},{9,13},{10,... | collective-permute-start | bytes 1228808 | tf_op jit(solution)/shard_map/ppermute | solution.py:31
  63.1 6.1 %collective-permute-start.14 = (f32[200,128]{1,0:T(8,128)S(1)}, f32[200,128]{1,0:T(8,128)S(1)}, u32[]{:S(2)}, u32[]{:S(2)}) collective-permute-start(f32[200,128]{1,0:T(8,128)S(1)} %get-tuple-element.26), channel_id=1, source_target_pairs={{0,3},{1,2},{2,1},{3,0},{4,7},{5,6},{6,5},{7,4},{8,11},{9,10},{10,... | collective-permute-start | bytes 307208 | tf_op jit(solution)/shard_map/ppermute | solution.py:31
  65.9 5.5 %collective-permute-start.13 = (f32[200,128]{1,0:T(8,128)S(1)}, f32[200,128]{1,0:T(8,128)S(1)}, u32[]{:S(2)}, u32[]{:S(2)}) collective-permute-start(f32[200,128]{1,0:T(8,128)S(1)} %get-tuple-element.27), channel_id=1, source_target_pairs={{0,2},{1,3},{2,0},{3,1},{4,6},{5,7},{6,4},{7,5},{8,10},{9,11},{10,... | collective-permute-start | bytes 307208 | tf_op jit(solution)/shard_map/ppermute | solution.py:31
  66.4 5.1 %collective-permute-start.12 = (f32[200,128]{1,0:T(8,128)S(1)}, f32[200,128]{1,0:T(8,128)S(1)}, u32[]{:S(2)}, u32[]{:S(2)}) collective-permute-start(f32[200,128]{1,0:T(8,128)S(1)} %get-tuple-element.28), channel_id=1, source_target_pairs={{0,1},{1,0},{2,3},{3,2},{4,5},{5,4},{6,7},{7,6},{8,9},{9,8},{10,11... | collective-permute-start | bytes 307208 | tf_op jit(solution)/shard_map/ppermute | solution.py:31
  71.6 7.5 %collective-permute-start.17 = (f32[200,128]{1,0:T(8,128)S(1)}, f32[200,128]{1,0:T(8,128)S(1)}, u32[]{:S(2)}, u32[]{:S(2)}) collective-permute-start(f32[200,128]{1,0:T(8,128)S(1)} %fusion.12), channel_id=1, source_target_pairs={{0,24},{1,25},{2,26},{3,27},{4,28},{5,29},{6,30},{7,31},{8,16},{9,... | collective-permute-start | bytes 307208 | tf_op jit(solution)/shard_map/ppermute | solution.py:31
  75.0 8.9 %collective-permute-start.16 = (f32[200,128]{1,0:T(8,128)S(1)}, f32[200,128]{1,0:T(8,128)S(1)}, u32[]{:S(2)}, u32[]{:S(2)}) collective-permute-start(f32[200,128]{1,0:T(8,128)S(1)} %fusion.12), channel_id=1, source_target_pairs={{0,16},{1,17},{2,18},{3,19},{4,20},{5,21},{6,22},{7,23},{8,24},{9,... | collective-permute-start | bytes 307208 | tf_op jit(solution)/shard_map/ppermute | solution.py:31
  75.0 8.9 %collective-permute-start.15 = (f32[200,128]{1,0:T(8,128)S(1)}, f32[200,128]{1,0:T(8,128)S(1)}, u32[]{:S(2)}, u32[]{:S(2)}) collective-permute-start(f32[200,128]{1,0:T(8,128)S(1)} %fusion.12), channel_id=1, source_target_pairs={{0,8},{1,9},{2,10},{3,11},{4,12},{5,13},{6,14},{7,15},{8,0},{9,1},... | collective-permute-start | bytes 307208 | tf_op jit(solution)/shard_map/ppermute | solution.py:31
  84.2 5.7 %collective-permute-start.19 = (f32[192,128]{1,0:T(8,128)S(1)}, f32[192,128]{1,0:T(8,128)S(1)}, u32[]{:S(2)}, u32[]{:S(2)}) collective-permute-start(f32[192,128]{1,0:T(8,128)S(1)} %get-tuple-element.51), channel_id=1, source_target_pairs={{0,2},{1,3},{2,0},{3,1},{4,6},{5,7},{6,4},{7,5},{8,10},{9,11},{10,... | collective-permute-start | bytes 294920 | tf_op jit(solution)/shard_map/ppermute | solution.py:31
  85.7 4.7 %collective-permute-start.18 = (f32[192,128]{1,0:T(8,128)S(1)}, f32[192,128]{1,0:T(8,128)S(1)}, u32[]{:S(2)}, u32[]{:S(2)}) collective-permute-start(f32[192,128]{1,0:T(8,128)S(1)} %get-tuple-element.51), channel_id=1, source_target_pairs={{0,1},{1,0},{2,3},{3,2},{4,5},{5,4},{6,7},{7,6},{8,9},{9,8},{10,11... | collective-permute-start | bytes 294920 | tf_op jit(solution)/shard_map/ppermute | solution.py:31
  85.9 5.7 %collective-permute-start.20 = (f32[192,128]{1,0:T(8,128)S(1)}, f32[192,128]{1,0:T(8,128)S(1)}, u32[]{:S(2)}, u32[]{:S(2)}) collective-permute-start(f32[192,128]{1,0:T(8,128)S(1)} %get-tuple-element.51), channel_id=1, source_target_pairs={{0,3},{1,2},{2,1},{3,0},{4,7},{5,6},{6,5},{7,4},{8,11},{9,10},{10,... | collective-permute-start | bytes 294920 | tf_op jit(solution)/shard_map/ppermute | solution.py:31
  91.7 1.8 %collective-permute-start.21 = (f32[4,192,128]{2,1,0:T(8,128)S(1)}, f32[4,192,128]{2,1,0:T(8,128)S(1)}, u32[]{:S(2)}, u32[]{:S(2)}) collective-permute-start(f32[4,192,128]{2,1,0:T(8,128)S(1)} %get-tuple-element.29), channel_id=1, source_target_pairs={{0,4},{1,5},{2,6},{3,7},{4,0},{5,1},{6,2},{7,3},{8,12},{9,13},{10,... | collective-permute-start | bytes 1179656 | tf_op jit(solution)/shard_map/ppermute | solution.py:31
  95.2 14.7 %all-to-all-start.1 = ((f32[32,16,128]{2,1,0:T(8,128)}), f32[32,16,128]{2,1,0:T(8,128)S(1)}, u32[]{:S(2)}, u32[]{:S(2)}) async-start(f32[32,16,128]{2,1,0:T(8,128)} %bitcast.45), calls=%async_computation.1 | async-start | bytes 524288 | tf_op jit(solution)/shard_map/all_to_all | solution.py:21

commit v13 on v12

--- a/solution.py
+++ b/solution.py
@@ -10,7 +10,6 @@
 AXES = ("row", "col")
 F32, BF16 = jnp.float32, jnp.bfloat16
 PAD = 8
-ROWS = 1024
 MIB = 1024 * 1024
 T1_MIB = 52
 PREP_KIB = 54528
@@ -113,77 +112,69 @@
     sums_ref[...] = jnp.broadcast_to(jnp.sum(turned, axis=1, keepdims=True), sums_ref.shape)
 
 
-def chunks(extent, size):
-    size = min(size, extent)
-    return [pl.ds(start, size) for start in range(0, extent, size)]
-
-
 def stacked(right):
     high, low = split(right)
     return jnp.concatenate([high, high, low], axis=0)
 
 
-def quotients(slab_ref, pair_ref, right_stack, rows, columns=slice(None)):
+def quotients(slab_ref, pair_ref, right_stack, rows):
     product = dot(pair_ref[rows, :], right_stack)
-    return split(divide(slab_ref[rows, columns], product))
+    return split(divide(slab_ref[rows, :], product))
 
 
 def right_update(slab_ref, pair_ref, pair_t_ref, sums_ref, right):
-    rank, block = right.shape
-    stack = stacked(right)
-    rows = pl.ds(0, slab_ref.shape[0])
-    halves = [slice(start, start + block // 2) for start in (0, block // 2)]
-    parts = [quotients(slab_ref, pair_ref, stack[:, half], rows, half) for half in halves]
-    numerators = []
-    for high, low in parts:
-        both = dot(pair_t_ref[...], high)
-        numerators.append(both[:rank] + both[rank:] + dot(pair_t_ref[:rank, :], low))
-    return right * jnp.concatenate(numerators, axis=1) / sums_ref[:, :1]
-
-
-def left_numerator(slab_ref, pair_ref, right, total_ref, sums_ref, first):
     rank = right.shape[0]
-    stack = stacked(right)
+    high, low = quotients(slab_ref, pair_ref, stacked(right), pl.ds(0, slab_ref.shape[0]))
+    both = dot(pair_t_ref[...], high)
+    numerator = both[:rank] + both[rank:] + dot(pair_t_ref[:rank, :], low)
+    return right * numerator / sums_ref[:, :1]
+
+
+def left_numerator(slab_ref, pair_ref, right):
+    rank = right.shape[0]
     right_high, right_low = split(right.T)
     right_both = jnp.concatenate([right_high, right_low], axis=1)
     row_sums = dot(jnp.ones((16, right.shape[1]), BF16), right_both)[:PAD]
-    row_sums = row_sums[:, :rank] + row_sums[:, rank:]
-    sums_ref[...] = jnp.where(first, row_sums, sums_ref[...] + row_sums)
-    for rows in chunks(slab_ref.shape[0], ROWS):
-        high, low = quotients(slab_ref, pair_ref, stack, rows)
-        both = dot(high, right_both)
-        term = both[:, :rank] + both[:, rank:] + dot(low, right_high)
-        total_ref[rows, :] = jnp.where(first, term, total_ref[rows, :] + term)
-
-
-def write_left(total_ref, row_sums_ref, extra_ref, out_ref):
+    high, low = quotients(slab_ref, pair_ref, stacked(right), pl.ds(0, slab_ref.shape[0]))
+    both = dot(high, right_both)
+    term = both[:, :rank] + both[:, rank:] + dot(low, right_high)
+    return term, row_sums[:, :rank] + row_sums[:, rank:]
+
+
+def write_left(total, row_sums, extra_ref, out_ref):
     parts, tall, rank = out_ref.shape
     height = tall - PAD
     first = lax.broadcasted_iota(jnp.int32, (PAD, rank), 0) == 0
-    stats = jnp.where(first, row_sums_ref[...], extra_ref[:1, :])
+    stats = jnp.where(first, row_sums, extra_ref[:1, :])
     for part in range(parts):
-        out_ref[part, :height, :] = total_ref[pl.ds(part * height, height), :]
+        out_ref[part, :height, :] = total[part * height : (part + 1) * height]
         out_ref[part, height:, :] = stats
 
 
 def turn_kernel(
-    slab_ref, left_ref, right_ref, extra_ref, right_out, left_out,
-    pair_ref, pair_t_ref, sums_ref, total_ref, row_sums_ref,
+    block, slab_hbm, left_ref, right_ref, extra_ref, right_out, left_out,
+    slab_ref, pair_ref, pair_t_ref, sums_ref, arrivals,
 ):
-    step = pl.program_id(0)
-
-    @pl.when(step == 0)
-    def _():
-        prepare_left(left_ref, pair_ref)
-        prepare_left_t(left_ref, pair_t_ref, sums_ref)
-
-    right = right_update(slab_ref, pair_ref, pair_t_ref, sums_ref, right_ref[...])
-    right_out[...] = right
-    left_numerator(slab_ref, pair_ref, right, total_ref, row_sums_ref, step == 0)
-
-    @pl.when(step == pl.num_programs(0) - 1)
-    def _():
-        write_left(total_ref, row_sums_ref, extra_ref, left_out)
+    blocks = [pl.ds(start, block) for start in range(0, slab_ref.shape[1], block)]
+    copies = [
+        pltpu.make_async_copy(
+            slab_hbm.at[:, columns], slab_ref.at[:, columns], arrivals.at[index]
+        )
+        for index, columns in enumerate(blocks)
+    ]
+    for copy in copies:
+        copy.start()
+    prepare_left(left_ref, pair_ref)
+    prepare_left_t(left_ref, pair_t_ref, sums_ref)
+    total = row_sums = 0.0
+    for copy, columns in zip(copies, blocks):
+        copy.wait()
+        part_ref = slab_ref.at[:, columns]
+        right = right_update(part_ref, pair_ref, pair_t_ref, sums_ref, right_ref[:, columns])
+        right_out[:, columns] = right
+        term, sums = left_numerator(part_ref, pair_ref, right)
+        total, row_sums = total + term, row_sums + sums
+    write_left(total, row_sums, extra_ref, left_out)
 
 
 def second_parts(slices, right_ref, second_left_ref, second_right_ref):
@@ -248,10 +239,6 @@
     return [pltpu.VMEM((2 * rank, m), BF16), pltpu.VMEM((rank, rank), F32)]
 
 
-def total_scratch(m, rank):
-    return [pltpu.VMEM((m, rank), F32), pltpu.VMEM((PAD, rank), F32)]
-
-
 def cost(m, rank, columns, dots):
     return pl.CostEstimate(
         flops=6 * dots * m * rank * columns, bytes_accessed=4 * m * columns, transcendentals=0
@@ -260,20 +247,25 @@
 
 def full_turn(slab, left, right, extra, block, parts, vmem_bytes):
     (m, columns), rank = slab.shape, left.shape[1]
-    columns_spec = lambda height: pl.BlockSpec((height, block), lambda step: (0, step))
     tall = m // parts + PAD
     return pl.pallas_call(
-        turn_kernel,
-        grid=(columns // block,),
-        in_specs=[columns_spec(m), full((m, rank)), columns_spec(rank), full((min(PAD, extra.shape[0]), rank))],
-        out_specs=[columns_spec(rank), full((parts, tall, rank))],
+        functools.partial(turn_kernel, block),
+        grid=(1,),
+        in_specs=[
+            pl.BlockSpec(memory_space=pl.ANY),
+            full((m, rank)),
+            full((rank, columns)),
+            full((min(PAD, extra.shape[0]), rank)),
+        ],
+        out_specs=[full((rank, columns)), full((parts, tall, rank))],
         out_shape=[
             jax.ShapeDtypeStruct((rank, columns), F32),
             jax.ShapeDtypeStruct((parts, tall, rank), F32),
         ],
-        scratch_shapes=left_scratch(m, rank)
+        scratch_shapes=[pltpu.VMEM((m, columns), F32)]
+        + left_scratch(m, rank)
         + right_scratch(m, rank)
-        + total_scratch(m, rank),
+        + [pltpu.SemaphoreType.DMA((columns // block,))],
         compiler_params=params(vmem_bytes),
         cost_estimate=cost(m, rank, columns, 4),
         name="turn",

time: 111 us -> 116 us (1.045)
  Pallas kernels: 29.2 us -> 33.5 us
    pallas_call x2, Pallas kernels: 25.3 us -> 29.6 us  [full_turn(): pl.pallas_call(functools.partial(turn_kernel, block), grid=(1,), in_specs...]
  transfers between devices with their start and end apart: 24 -> 24, of which waited for: 20 -> 20; matrix products, arithmetic and copies ran while one was open for 2% -> 1% of each run, Pallas kernels for 13% -> 14%
where the time goes in v13:
time: 116 us; the launch traced here: 115 us
  waiting for transfers between devices  43.8 us (38%)
  Pallas kernels  33.5 us (29%)
  starting transfers between devices  32.3 us (28%)
  local copies, waits for them, and re-layouts  2.87 us (2%)
  other arithmetic  1.76 us (2%)
    ppermute x22, waiting for transfers between devices, send(): return lax.ppermute(values, AXES, pairs)  33.7 us
    pallas_call x2, Pallas kernels, full_turn(): pl.pallas_call(functools.partial(turn_kernel, block), grid=(1,), in_specs...  29.6 us
    ppermute x22, starting transfers between devices, send(): return lax.ppermute(values, AXES, pairs)  25 us
    all_to_all x2, waiting for transfers between devices, exchange(): return lax.all_to_all(parts, AXES, split_axis=0, concat_axis=0, tiled=True)  10.1 us
    all_to_all x2, starting transfers between devices, exchange(): return lax.all_to_all(parts, AXES, split_axis=0, concat_axis=0, tiled=True)  7.33 us
  transfers between devices with their start and end apart: 24, of which 20 were waited for; matrix products, arithmetic and copies ran while one was open for 1% of the time, Pallas kernels for 14%

profile of v13, /device:TPU:0, one launch (start us, length us, event | category | flops | bytes accessed | tf_op | source)
XLA Modules:
  0.0 115.2 jit_solution(9749800955733703185)
XLA Ops:
  0.6 0.0 copy-start
  0.7 0.0 copy-start.1
  0.7 1.1 copy-done.1
  1.7 14.8 %turn.2 = (f32[128,2048]{1,0:T(8,128)}, f32[8,136,128]{2,1,0:T(8,128)S(1)}) custom-call(f32[1024,2048]{1,0:T(8,128)} %slab_hbm.3, f32[1024,128]{1,0:T(8,128)S(1)} %copy-done.1, f32[128,2048]{1,0:T(8,128)} %right_ref.1, f32[1024,128]{1,0:T(8,128)S(1)} %copy-done.1), custom_call_target="tpu_custom_call" | custom-call | flops 6442450944 | bytes 8388608 | tf_op jit(solution)/shard_map/turn/pallas_call | solution.py:251
  16.6 0.5 collective-permute-start
  17.1 0.8 constant_dynamic-slice_fusion.13
  17.9 0.3 collective-permute-done
  18.4 2.9 %collective-permute-start.1 = (f32[200,128]{1,0:T(8,128)S(1)}, f32[200,128]{1,0:T(8,128)S(1)}, u32[]{:S(2)}, u32[]{:S(2)}) collective-permute-start(f32[200,128]{1,0:T(8,128)S(1)} %get-tuple-element.52), channel_id=1, source_target_pairs={{0,1},{1,0},{2,3},{3,2},{4,5},{5,4},{6,7},{7,6},{8,9},{9,8},{10,11... | collective-permute-start | bytes 307208 | tf_op jit(solution)/shard_map/ppermute | solution.py:30
  21.3 1.5 %collective-permute-start.2 = (f32[200,128]{1,0:T(8,128)S(1)}, f32[200,128]{1,0:T(8,128)S(1)}, u32[]{:S(2)}, u32[]{:S(2)}) collective-permute-start(f32[200,128]{1,0:T(8,128)S(1)} %get-tuple-element.53), channel_id=1, source_target_pairs={{0,2},{1,3},{2,0},{3,1},{4,6},{5,7},{6,4},{7,5},{8,10},{9,11},{10,... | collective-permute-start | bytes 307208 | tf_op jit(solution)/shard_map/ppermute | solution.py:30
  22.8 0.0 collective-permute-start.3
  22.9 1.7 %collective-permute-done.1 = f32[200,128]{1,0:T(8,128)S(1)} collective-permute-done((f32[200,128]{1,0:T(8,128)S(1)}, f32[200,128]{1,0:T(8,128)S(1)}, u32[]{:S(2)}, u32[]{:S(2)}) %collective-permute-start.1) | collective-permute-done | bytes 102432 | tf_op jit(solution)/shard_map/ppermute | solution.py:30
  24.6 2.6 %collective-permute-done.2 = f32[200,128]{1,0:T(8,128)S(1)} collective-permute-done((f32[200,128]{1,0:T(8,128)S(1)}, f32[200,128]{1,0:T(8,128)S(1)}, u32[]{:S(2)}, u32[]{:S(2)}) %collective-permute-start.2) | collective-permute-done | bytes 102432 | tf_op jit(solution)/shard_map/ppermute | solution.py:30
  27.2 1.2 %collective-permute-done.3 = f32[200,128]{1,0:T(8,128)S(1)} collective-permute-done((f32[200,128]{1,0:T(8,128)S(1)}, f32[200,128]{1,0:T(8,128)S(1)}, u32[]{:S(2)}, u32[]{:S(2)}) %collective-permute-start.3) | collective-permute-done | bytes 102432 | tf_op jit(solution)/shard_map/ppermute | solution.py:30
  28.4 3.7 %collective-permute-start.6 = (f32[136,128]{1,0:T(8,128)S(1)}, f32[136,128]{1,0:T(8,128)S(1)}, u32[]{:S(2)}, u32[]{:S(2)}) collective-permute-start(f32[136,128]{1,0:T(8,128)S(1)} %fusion.13), channel_id=1, source_target_pairs={{0,24},{1,25},{2,26},{3,27},{4,28},{5,29},{6,30},{7,31},{8,16},{9,... | collective-permute-start | bytes 208904 | tf_op jit(solution)/shard_map/ppermute | solution.py:30
  32.1 0.0 collective-permute-start.5
  32.1 0.8 collective-permute-start.4
  32.9 1.7 %collective-permute-done.6 = f32[136,128]{1,0:T(8,128)S(1)} collective-permute-done((f32[136,128]{1,0:T(8,128)S(1)}, f32[136,128]{1,0:T(8,128)S(1)}, u32[]{:S(2)}, u32[]{:S(2)}) %collective-permute-start.6) | collective-permute-done | bytes 69664 | tf_op jit(solution)/shard_map/ppermute | solution.py:30
  34.6 2.7 %collective-permute-done.5 = f32[136,128]{1,0:T(8,128)S(1)} collective-permute-done((f32[136,128]{1,0:T(8,128)S(1)}, f32[136,128]{1,0:T(8,128)S(1)}, u32[]{:S(2)}, u32[]{:S(2)}) %collective-permute-start.5) | collective-permute-done | bytes 69664 | tf_op jit(solution)/shard_map/ppermute | solution.py:30
  37.3 0.0 collective-permute-done.4
  37.3 1.6 %collective-permute-start.9 = (f32[128,128]{1,0:T(8,128)S(1)}, f32[128,128]{1,0:T(8,128)S(1)}, u32[]{:S(2)}, u32[]{:S(2)}) collective-permute-start(f32[128,128]{1,0:T(8,128)S(1)} %fusion.15), channel_id=1, source_target_pairs={{0,3},{1,2},{2,1},{3,0},{4,7},{5,6},{6,5},{7,4},{8,11},{9,10},{10,... | collective-permute-start | bytes 196616 | tf_op jit(solution)/shard_map/ppermute | solution.py:30
  38.9 1.3 %collective-permute-start.8 = (f32[128,128]{1,0:T(8,128)S(1)}, f32[128,128]{1,0:T(8,128)S(1)}, u32[]{:S(2)}, u32[]{:S(2)}) collective-permute-start(f32[128,128]{1,0:T(8,128)S(1)} %fusion.15), channel_id=1, source_target_pairs={{0,2},{1,3},{2,0},{3,1},{4,6},{5,7},{6,4},{7,5},{8,10},{9,11},{10,... | collective-permute-start | bytes 196616 | tf_op jit(solution)/shard_map/ppermute | solution.py:30
  40.2 0.7 collective-permute-start.7
  40.9 1.8 %collective-permute-done.9 = f32[128,128]{1,0:T(8,128)S(1)} collective-permute-done((f32[128,128]{1,0:T(8,128)S(1)}, f32[128,128]{1,0:T(8,128)S(1)}, u32[]{:S(2)}, u32[]{:S(2)}) %collective-permute-start.9) | collective-permute-done | bytes 65568 | tf_op jit(solution)/shard_map/ppermute | solution.py:30
  42.7 0.7 collective-permute-done.8
  43.4 1.1 collective-permute-done.7
  44.5 0.1 maximum_maximum_fusion
  44.6 0.1 collective-permute-start.10
  44.7 1.7 %prepare.1 = (f32[32,16,128]{2,1,0:T(8,128)}, f32[1,128]{1,0:T(1,128)S(1)}) custom-call(s32[1]{0:T(128)} %bitcast.19.place_ref, f32[2048,128]{1,0:T(8,128)} %second_left_ref), custom_call_target="tpu_custom_call" | custom-call | flops 65536 | bytes 524288 | tf_op jit(solution)/shard_map/prepare/pallas_call | solution.py:310
  46.4 0.0 collective-permute-done.10
  46.4 0.2 fusion.9
  46.6 3.5 %all-to-all-start = ((f32[32,16,128]{2,1,0:T(8,128)}), f32[32,16,128]{2,1,0:T(8,128)S(1)}, u32[]{:S(2)}, u32[]{:S(2)}) async-start(f32[32,16,128]{2,1,0:T(8,128)} %get-tuple-element.20), calls=%async_computation | async-start | bytes 524288 | tf_op jit(solution)/shard_map/all_to_all | solution.py:20
  50.2 14.8 %turn.3 = (f32[128,2048]{1,0:T(8,128)S(1)}, f32[8,136,128]{2,1,0:T(8,128)S(1)}) custom-call(f32[1024,2048]{1,0:T(8,128)} %slab_hbm.3, f32[1024,128]{1,0:T(8,128)S(1)} %bitcast.87, f32[128,2048]{1,0:T(8,128)} %get-tuple-element.14.right_ref, f32[1,128]{1,0:T(1,128)S(1)} %get-tuple-element.16.extra_ref), custom_call_target="tpu_custom_call" | custom-call | flops 6442450944 | bytes 8388608 | tf_op jit(solution)/shard_map/turn/pallas_call | solution.py:251
  65.0 0.0 all-to-all-done
  65.0 0.7 second_numerator.1
  65.8 0.3 collective-permute-start.11
  66.1 1.5 %collective-permute-done.11 = f32[4,200,128]{2,1,0:T(8,128)S(1)} collective-permute-done((f32[4,200,128]{2,1,0:T(8,128)S(1)}, f32[4,200,128]{2,1,0:T(8,128)S(1)}, u32[]{:S(2)}, u32[]{:S(2)}) %collective-permute-start.11) | collective-permute-done | bytes 409632 | tf_op jit(solution)/shard_map/ppermute | solution.py:30
  67.7 2.7 %collective-permute-start.14 = (f32[200,128]{1,0:T(8,128)S(1)}, f32[200,128]{1,0:T(8,128)S(1)}, u32[]{:S(2)}, u32[]{:S(2)}) collective-permute-start(f32[200,128]{1,0:T(8,128)S(1)} %get-tuple-element.26), channel_id=1, source_target_pairs={{0,3},{1,2},{2,1},{3,0},{4,7},{5,6},{6,5},{7,4},{8,11},{9,10},{10,... | collective-permute-start | bytes 307208 | tf_op jit(solution)/shard_map/ppermute | solution.py:30
  70.4 0.6 collective-permute-start.13
  71.0 0.3 collective-permute-start.12
  71.2 2.5 %collective-permute-done.14 = f32[200,128]{1,0:T(8,128)S(1)} collective-permute-done((f32[200,128]{1,0:T(8,128)S(1)}, f32[200,128]{1,0:T(8,128)S(1)}, u32[]{:S(2)}, u32[]{:S(2)}) %collective-permute-start.14) | collective-permute-done | bytes 102432 | tf_op jit(solution)/shard_map/ppermute | solution.py:30
  73.8 2.1 %collective-permute-done.13 = f32[200,128]{1,0:T(8,128)S(1)} collective-permute-done((f32[200,128]{1,0:T(8,128)S(1)}, f32[200,128]{1,0:T(8,128)S(1)}, u32[]{:S(2)}, u32[]{:S(2)}) %collective-permute-start.13) | collective-permute-done | bytes 102432 | tf_op jit(solution)/shard_map/ppermute | solution.py:30
  75.9 0.2 collective-permute-done.12
  76.1 3.4 %collective-permute-start.17 = (f32[200,128]{1,0:T(8,128)S(1)}, f32[200,128]{1,0:T(8,128)S(1)}, u32[]{:S(2)}, u32[]{:S(2)}) collective-permute-start(f32[200,128]{1,0:T(8,128)S(1)} %fusion.12), channel_id=1, source_target_pairs={{0,24},{1,25},{2,26},{3,27},{4,28},{5,29},{6,30},{7,31},{8,16},{9,... | collective-permute-start | bytes 307208 | tf_op jit(solution)/shard_map/ppermute | solution.py:30
  79.5 0.0 collective-permute-start.16
  79.5 1.0 collective-permute-start.15
  80.6 3.0 %collective-permute-done.17 = f32[200,128]{1,0:T(8,128)S(1)} collective-permute-done((f32[200,128]{1,0:T(8,128)S(1)}, f32[200,128]{1,0:T(8,128)S(1)}, u32[]{:S(2)}, u32[]{:S(2)}) %collective-permute-start.17) | collective-permute-done | bytes 102432 | tf_op jit(solution)/shard_map/ppermute | solution.py:30
  83.5 4.9 %collective-permute-done.16 = f32[200,128]{1,0:T(8,128)S(1)} collective-permute-done((f32[200,128]{1,0:T(8,128)S(1)}, f32[200,128]{1,0:T(8,128)S(1)}, u32[]{:S(2)}, u32[]{:S(2)}) %collective-permute-start.16) | collective-permute-done | bytes 102432 | tf_op jit(solution)/shard_map/ppermute | solution.py:30
  88.5 0.0 collective-permute-done.15
  88.5 0.1 broadcast_divide_fusion
  88.7 1.5 %collective-permute-start.19 = (f32[192,128]{1,0:T(8,128)S(1)}, f32[192,128]{1,0:T(8,128)S(1)}, u32[]{:S(2)}, u32[]{:S(2)}) collective-permute-start(f32[192,128]{1,0:T(8,128)S(1)} %get-tuple-element.51), channel_id=1, source_target_pairs={{0,2},{1,3},{2,0},{3,1},{4,6},{5,7},{6,4},{7,5},{8,10},{9,11},{10,... | collective-permute-start | bytes 294920 | tf_op jit(solution)/shard_map/ppermute | solution.py:30
  90.2 0.2 collective-permute-start.18
  90.4 1.8 %collective-permute-start.20 = (f32[192,128]{1,0:T(8,128)S(1)}, f32[192,128]{1,0:T(8,128)S(1)}, u32[]{:S(2)}, u32[]{:S(2)}) collective-permute-start(f32[192,128]{1,0:T(8,128)S(1)} %get-tuple-element.51), channel_id=1, source_target_pairs={{0,3},{1,2},{2,1},{3,0},{4,7},{5,6},{6,5},{7,4},{8,11},{9,10},{10,... | collective-permute-start | bytes 294920 | tf_op jit(solution)/shard_map/ppermute | solution.py:30
  92.2 2.2 %collective-permute-done.19 = f32[192,128]{1,0:T(8,128)S(1)} collective-permute-done((f32[192,128]{1,0:T(8,128)S(1)}, f32[192,128]{1,0:T(8,128)S(1)}, u32[]{:S(2)}, u32[]{:S(2)}) %collective-permute-start.19) | collective-permute-done | bytes 98336 | tf_op jit(solution)/shard_map/ppermute | solution.py:30
  94.4 0.5 collective-permute-done.18
  94.9 1.2 %collective-permute-done.20 = f32[192,128]{1,0:T(8,128)S(1)} collective-permute-done((f32[192,128]{1,0:T(8,128)S(1)}, f32[192,128]{1,0:T(8,128)S(1)}, u32[]{:S(2)}, u32[]{:S(2)}) %collective-permute-start.20) | collective-permute-done | bytes 98336 | tf_op jit(solution)/shard_map/ppermute | solution.py:30
  96.2 0.1 pad_maximum_fusion.1
  96.3 0.1 collective-permute-start.21
  96.3 1.7 %collective-permute-done.21 = f32[4,192,128]{2,1,0:T(8,128)S(1)} collective-permute-done((f32[4,192,128]{2,1,0:T(8,128)S(1)}, f32[4,192,128]{2,1,0:T(8,128)S(1)}, u32[]{:S(2)}, u32[]{:S(2)}) %collective-permute-start.21) | collective-permute-done | bytes 393248 | tf_op jit(solution)/shard_map/ppermute | solution.py:30
  98.0 0.2 fusion.7
  98.2 1.4 %second_rows.1 = f32[512,128]{1,0:T(8,128)} custom-call(f32[128,2048]{1,0:T(8,128)S(1)} %get-tuple-element.18.right_ref, f32[512,128]{1,0:T(8,128)S(1)} %bitcast.79, f32[4,128,128]{2,1,0:T(8,128)S(1)} %bitcast.86), custom_call_target="tpu_custom_call" | custom-call | flops 402653184 | bytes 1048576 | tf_op jit(solution)/shard_map/second_rows/pallas_call | solution.py:286
  99.7 3.8 %all-to-all-start.1 = ((f32[32,16,128]{2,1,0:T(8,128)}), f32[32,16,128]{2,1,0:T(8,128)S(1)}, u32[]{:S(2)}, u32[]{:S(2)}) async-start(f32[32,16,128]{2,1,0:T(8,128)} %bitcast.45), calls=%async_computation.1 | async-start | bytes 524288 | tf_op jit(solution)/shard_map/all_to_all | solution.py:20
  103.5 0.8 fusion
  104.3 10.1 %all-to-all-done.1 = f32[32,16,128]{2,1,0:T(8,128)S(1)} async-done(((f32[32,16,128]{2,1,0:T(8,128)}), f32[32,16,128]{2,1,0:T(8,128)S(1)}, u32[]{:S(2)}, u32[]{:S(2)}) %all-to-all-start.1) | async-done | bytes 262176 | tf_op jit(solution)/shard_map/all_to_all | solution.py:20
  114.4 0.7 copy.8
  (33 shorter events, 0.6 us)
Async XLA Ops:
  0.6 16.5 %copy-start = (f32[128,128]{1,0:T(8,128)S(1)}, f32[128,128]{1,0:T(8,128)}, u32[]{:S(2)}) copy-start(f32[128,128]{1,0:T(8,128)} %param.9) | copy-start | bytes 196612
  0.7 1.1 copy-start.1
  16.6 1.7 %collective-permute-start = (f32[4,136,128]{2,1,0:T(8,128)S(1)}, f32[4,136,128]{2,1,0:T(8,128)S(1)}, u32[]{:S(2)}, u32[]{:S(2)}) collective-permute-start(f32[4,136,128]{2,1,0:T(8,128)S(1)} %dynamic-slice_bitcast_fusion), channel_id=1, source_target_pairs={{0,4},{1,5},{2,6},{3,7},{4,0},{5,1},{6,2},{7,3},{8,12},{9,13},{10,... | collective-permute-start | bytes 835592 | tf_op jit(solution)/shard_map/ppermute | solution.py:30
  18.4 6.2 %collective-permute-start.1 = (f32[200,128]{1,0:T(8,128)S(1)}, f32[200,128]{1,0:T(8,128)S(1)}, u32[]{:S(2)}, u32[]{:S(2)}) collective-permute-start(f32[200,128]{1,0:T(8,128)S(1)} %get-tuple-element.52), channel_id=1, source_target_pairs={{0,1},{1,0},{2,3},{3,2},{4,5},{5,4},{6,7},{7,6},{8,9},{9,8},{10,11... | collective-permute-start | bytes 307208 | tf_op jit(solution)/shard_map/ppermute | solution.py:30
  21.3 5.9 %collective-permute-start.2 = (f32[200,128]{1,0:T(8,128)S(1)}, f32[200,128]{1,0:T(8,128)S(1)}, u32[]{:S(2)}, u32[]{:S(2)}) collective-permute-start(f32[200,128]{1,0:T(8,128)S(1)} %get-tuple-element.53), channel_id=1, source_target_pairs={{0,2},{1,3},{2,0},{3,1},{4,6},{5,7},{6,4},{7,5},{8,10},{9,11},{10,... | collective-permute-start | bytes 307208 | tf_op jit(solution)/shard_map/ppermute | solution.py:30
  22.8 5.6 %collective-permute-start.3 = (f32[200,128]{1,0:T(8,128)S(1)}, f32[200,128]{1,0:T(8,128)S(1)}, u32[]{:S(2)}, u32[]{:S(2)}) collective-permute-start(f32[200,128]{1,0:T(8,128)S(1)} %get-tuple-element.54), channel_id=1, source_target_pairs={{0,3},{1,2},{2,1},{3,0},{4,7},{5,6},{6,5},{7,4},{8,11},{9,10},{10,... | collective-permute-start | bytes 307208 | tf_op jit(solution)/shard_map/ppermute | solution.py:30
  28.4 6.2 %collective-permute-start.6 = (f32[136,128]{1,0:T(8,128)S(1)}, f32[136,128]{1,0:T(8,128)S(1)}, u32[]{:S(2)}, u32[]{:S(2)}) collective-permute-start(f32[136,128]{1,0:T(8,128)S(1)} %fusion.13), channel_id=1, source_target_pairs={{0,24},{1,25},{2,26},{3,27},{4,28},{5,29},{6,30},{7,31},{8,16},{9,... | collective-permute-start | bytes 208904 | tf_op jit(solution)/shard_map/ppermute | solution.py:30
  32.1 5.2 %collective-permute-start.5 = (f32[136,128]{1,0:T(8,128)S(1)}, f32[136,128]{1,0:T(8,128)S(1)}, u32[]{:S(2)}, u32[]{:S(2)}) collective-permute-start(f32[136,128]{1,0:T(8,128)S(1)} %fusion.13), channel_id=1, source_target_pairs={{0,16},{1,17},{2,18},{3,19},{4,20},{5,21},{6,22},{7,23},{8,24},{9,... | collective-permute-start | bytes 208904 | tf_op jit(solution)/shard_map/ppermute | solution.py:30
  32.1 5.2 %collective-permute-start.4 = (f32[136,128]{1,0:T(8,128)S(1)}, f32[136,128]{1,0:T(8,128)S(1)}, u32[]{:S(2)}, u32[]{:S(2)}) collective-permute-start(f32[136,128]{1,0:T(8,128)S(1)} %fusion.13), channel_id=1, source_target_pairs={{0,8},{1,9},{2,10},{3,11},{4,12},{5,13},{6,14},{7,15},{8,0},{9,1},... | collective-permute-start | bytes 208904 | tf_op jit(solution)/shard_map/ppermute | solution.py:30
  37.3 5.4 %collective-permute-start.9 = (f32[128,128]{1,0:T(8,128)S(1)}, f32[128,128]{1,0:T(8,128)S(1)}, u32[]{:S(2)}, u32[]{:S(2)}) collective-permute-start(f32[128,128]{1,0:T(8,128)S(1)} %fusion.15), channel_id=1, source_target_pairs={{0,3},{1,2},{2,1},{3,0},{4,7},{5,6},{6,5},{7,4},{8,11},{9,10},{10,... | collective-permute-start | bytes 196616 | tf_op jit(solution)/shard_map/ppermute | solution.py:30
  38.9 4.5 %collective-permute-start.8 = (f32[128,128]{1,0:T(8,128)S(1)}, f32[128,128]{1,0:T(8,128)S(1)}, u32[]{:S(2)}, u32[]{:S(2)}) collective-permute-start(f32[128,128]{1,0:T(8,128)S(1)} %fusion.15), channel_id=1, source_target_pairs={{0,2},{1,3},{2,0},{3,1},{4,6},{5,7},{6,4},{7,5},{8,10},{9,11},{10,... | collective-permute-start | bytes 196616 | tf_op jit(solution)/shard_map/ppermute | solution.py:30
  40.2 4.3 %collective-permute-start.7 = (f32[128,128]{1,0:T(8,128)S(1)}, f32[128,128]{1,0:T(8,128)S(1)}, u32[]{:S(2)}, u32[]{:S(2)}) collective-permute-start(f32[128,128]{1,0:T(8,128)S(1)} %fusion.15), channel_id=1, source_target_pairs={{0,1},{1,0},{2,3},{3,2},{4,5},{5,4},{6,7},{7,6},{8,9},{9,8},{10,11... | collective-permute-start | bytes 196616 | tf_op jit(solution)/shard_map/ppermute | solution.py:30
  44.6 1.8 %collective-permute-start.10 = (f32[4,192,128]{2,1,0:T(8,128)S(1)}, f32[4,192,128]{2,1,0:T(8,128)S(1)}, u32[]{:S(2)}, u32[]{:S(2)}) collective-permute-start(f32[4,192,128]{2,1,0:T(8,128)S(1)} %get-tuple-element.35), channel_id=1, source_target_pairs={{0,4},{1,5},{2,6},{3,7},{4,0},{5,1},{6,2},{7,3},{8,12},{9,13},{10,... | collective-permute-start | bytes 1179656 | tf_op jit(solution)/shard_map/ppermute | solution.py:30
  46.6 18.3 %all-to-all-start = ((f32[32,16,128]{2,1,0:T(8,128)}), f32[32,16,128]{2,1,0:T(8,128)S(1)}, u32[]{:S(2)}, u32[]{:S(2)}) async-start(f32[32,16,128]{2,1,0:T(8,128)} %get-tuple-element.20), calls=%async_computation | async-start | bytes 524288 | tf_op jit(solution)/shard_map/all_to_all | solution.py:20
  65.8 1.8 %collective-permute-start.11 = (f32[4,200,128]{2,1,0:T(8,128)S(1)}, f32[4,200,128]{2,1,0:T(8,128)S(1)}, u32[]{:S(2)}, u32[]{:S(2)}) collective-permute-start(f32[4,200,128]{2,1,0:T(8,128)S(1)} %fusion.3), channel_id=1, source_target_pairs={{0,4},{1,5},{2,6},{3,7},{4,0},{5,1},{6,2},{7,3},{8,12},{9,13},{10,... | collective-permute-start | bytes 1228808 | tf_op jit(solution)/shard_map/ppermute | solution.py:30
  67.7 6.1 %collective-permute-start.14 = (f32[200,128]{1,0:T(8,128)S(1)}, f32[200,128]{1,0:T(8,128)S(1)}, u32[]{:S(2)}, u32[]{:S(2)}) collective-permute-start(f32[200,128]{1,0:T(8,128)S(1)} %get-tuple-element.26), channel_id=1, source_target_pairs={{0,3},{1,2},{2,1},{3,0},{4,7},{5,6},{6,5},{7,4},{8,11},{9,10},{10,... | collective-permute-start | bytes 307208 | tf_op jit(solution)/shard_map/ppermute | solution.py:30
  70.4 5.5 %collective-permute-start.13 = (f32[200,128]{1,0:T(8,128)S(1)}, f32[200,128]{1,0:T(8,128)S(1)}, u32[]{:S(2)}, u32[]{:S(2)}) collective-permute-start(f32[200,128]{1,0:T(8,128)S(1)} %get-tuple-element.27), channel_id=1, source_target_pairs={{0,2},{1,3},{2,0},{3,1},{4,6},{5,7},{6,4},{7,5},{8,10},{9,11},{10,... | collective-permute-start | bytes 307208 | tf_op jit(solution)/shard_map/ppermute | solution.py:30
  71.0 5.1 %collective-permute-start.12 = (f32[200,128]{1,0:T(8,128)S(1)}, f32[200,128]{1,0:T(8,128)S(1)}, u32[]{:S(2)}, u32[]{:S(2)}) collective-permute-start(f32[200,128]{1,0:T(8,128)S(1)} %get-tuple-element.28), channel_id=1, source_target_pairs={{0,1},{1,0},{2,3},{3,2},{4,5},{5,4},{6,7},{7,6},{8,9},{9,8},{10,11... | collective-permute-start | bytes 307208 | tf_op jit(solution)/shard_map/ppermute | solution.py:30
  76.1 7.4 %collective-permute-start.17 = (f32[200,128]{1,0:T(8,128)S(1)}, f32[200,128]{1,0:T(8,128)S(1)}, u32[]{:S(2)}, u32[]{:S(2)}) collective-permute-start(f32[200,128]{1,0:T(8,128)S(1)} %fusion.12), channel_id=1, source_target_pairs={{0,24},{1,25},{2,26},{3,27},{4,28},{5,29},{6,30},{7,31},{8,16},{9,... | collective-permute-start | bytes 307208 | tf_op jit(solution)/shard_map/ppermute | solution.py:30
  79.5 8.9 %collective-permute-start.16 = (f32[200,128]{1,0:T(8,128)S(1)}, f32[200,128]{1,0:T(8,128)S(1)}, u32[]{:S(2)}, u32[]{:S(2)}) collective-permute-start(f32[200,128]{1,0:T(8,128)S(1)} %fusion.12), channel_id=1, source_target_pairs={{0,16},{1,17},{2,18},{3,19},{4,20},{5,21},{6,22},{7,23},{8,24},{9,... | collective-permute-start | bytes 307208 | tf_op jit(solution)/shard_map/ppermute | solution.py:30
  79.5 8.9 %collective-permute-start.15 = (f32[200,128]{1,0:T(8,128)S(1)}, f32[200,128]{1,0:T(8,128)S(1)}, u32[]{:S(2)}, u32[]{:S(2)}) collective-permute-start(f32[200,128]{1,0:T(8,128)S(1)} %fusion.12), channel_id=1, source_target_pairs={{0,8},{1,9},{2,10},{3,11},{4,12},{5,13},{6,14},{7,15},{8,0},{9,1},... | collective-permute-start | bytes 307208 | tf_op jit(solution)/shard_map/ppermute | solution.py:30
  88.7 5.7 %collective-permute-start.19 = (f32[192,128]{1,0:T(8,128)S(1)}, f32[192,128]{1,0:T(8,128)S(1)}, u32[]{:S(2)}, u32[]{:S(2)}) collective-permute-start(f32[192,128]{1,0:T(8,128)S(1)} %get-tuple-element.51), channel_id=1, source_target_pairs={{0,2},{1,3},{2,0},{3,1},{4,6},{5,7},{6,4},{7,5},{8,10},{9,11},{10,... | collective-permute-start | bytes 294920 | tf_op jit(solution)/shard_map/ppermute | solution.py:30
  90.2 4.7 %collective-permute-start.18 = (f32[192,128]{1,0:T(8,128)S(1)}, f32[192,128]{1,0:T(8,128)S(1)}, u32[]{:S(2)}, u32[]{:S(2)}) collective-permute-start(f32[192,128]{1,0:T(8,128)S(1)} %get-tuple-element.51), channel_id=1, source_target_pairs={{0,1},{1,0},{2,3},{3,2},{4,5},{5,4},{6,7},{7,6},{8,9},{9,8},{10,11... | collective-permute-start | bytes 294920 | tf_op jit(solution)/shard_map/ppermute | solution.py:30
  90.4 5.7 %collective-permute-start.20 = (f32[192,128]{1,0:T(8,128)S(1)}, f32[192,128]{1,0:T(8,128)S(1)}, u32[]{:S(2)}, u32[]{:S(2)}) collective-permute-start(f32[192,128]{1,0:T(8,128)S(1)} %get-tuple-element.51), channel_id=1, source_target_pairs={{0,3},{1,2},{2,1},{3,0},{4,7},{5,6},{6,5},{7,4},{8,11},{9,10},{10,... | collective-permute-start | bytes 294920 | tf_op jit(solution)/shard_map/ppermute | solution.py:30
  96.3 1.8 %collective-permute-start.21 = (f32[4,192,128]{2,1,0:T(8,128)S(1)}, f32[4,192,128]{2,1,0:T(8,128)S(1)}, u32[]{:S(2)}, u32[]{:S(2)}) collective-permute-start(f32[4,192,128]{2,1,0:T(8,128)S(1)} %get-tuple-element.29), channel_id=1, source_target_pairs={{0,4},{1,5},{2,6},{3,7},{4,0},{5,1},{6,2},{7,3},{8,12},{9,13},{10,... | collective-permute-start | bytes 1179656 | tf_op jit(solution)/shard_map/ppermute | solution.py:30
  99.7 14.8 %all-to-all-start.1 = ((f32[32,16,128]{2,1,0:T(8,128)}), f32[32,16,128]{2,1,0:T(8,128)S(1)}, u32[]{:S(2)}, u32[]{:S(2)}) async-start(f32[32,16,128]{2,1,0:T(8,128)} %bitcast.45), calls=%async_computation.1 | async-start | bytes 524288 | tf_op jit(solution)/shard_map/all_to_all | solution.py:20

commit v14 on v12

--- a/solution.py
+++ b/solution.py
@@ -123,22 +123,17 @@
     return jnp.concatenate([high, high, low], axis=0)
 
 
-def quotients(slab_ref, pair_ref, right_stack, rows, columns=slice(None)):
+def quotients(slab_ref, pair_ref, right_stack, rows):
     product = dot(pair_ref[rows, :], right_stack)
-    return split(divide(slab_ref[rows, columns], product))
+    return split(divide(slab_ref[rows, :], product))
 
 
 def right_update(slab_ref, pair_ref, pair_t_ref, sums_ref, right):
-    rank, block = right.shape
-    stack = stacked(right)
-    rows = pl.ds(0, slab_ref.shape[0])
-    halves = [slice(start, start + block // 2) for start in (0, block // 2)]
-    parts = [quotients(slab_ref, pair_ref, stack[:, half], rows, half) for half in halves]
-    numerators = []
-    for high, low in parts:
-        both = dot(pair_t_ref[...], high)
-        numerators.append(both[:rank] + both[rank:] + dot(pair_t_ref[:rank, :], low))
-    return right * jnp.concatenate(numerators, axis=1) / sums_ref[:, :1]
+    rank = right.shape[0]
+    high, low = quotients(slab_ref, pair_ref, stacked(right), pl.ds(0, slab_ref.shape[0]))
+    both = dot(pair_t_ref[...], high)
+    numerator = both[:rank] + both[rank:] + dot(pair_t_ref[:rank, :], low)
+    return right * numerator / sums_ref[:, :1]
 
 
 def left_numerator(slab_ref, pair_ref, right, total_ref, sums_ref, first):
@@ -354,7 +349,7 @@
         return own * total[:rows_own] / total[rows_own][None, :]
 
     right, summed = full_turn(
-        tensor_slab, left_init, right_init, left_init, k, parts, T1_MIB * MIB
+        tensor_slab, left_init, right_init, left_init, k // 2, parts, T1_MIB * MIB
     )
     second_left = after(second_left_init, summed)
     summed = summed.reshape(2, col_devices, rows_own + PAD, rank)
@@ -377,7 +372,7 @@
     place = lax.axis_index("col").astype(jnp.int32)[None]
     second_left, col_part = prepare(place, second_left, devices, slices, second_rows)
     arrived = exchange(after(second_left, left))
-    right, summed = full_turn(tensor_slab, left, right, col_part, k, parts, VMEM_BYTES)
+    right, summed = full_turn(tensor_slab, left, right, col_part, k // 2, parts, VMEM_BYTES)
     arrived = after(arrived, summed)
     second_left = arrived.reshape(rank * slices, rank)
     numerator = second_numerator(right, second_left, whole, slices)

time: 111 us -> 126 us (1.14)
  Pallas kernels: 29.2 us -> 43.6 us
    pallas_call x2, Pallas kernels: 25.3 us -> 39.7 us  [full_turn(): pl.pallas_call(turn_kernel, grid=(columns // block,), in_specs=[columns_s...]
  transfers between devices with their start and end apart: 24 -> 24, of which waited for: 20 -> 20; matrix products, arithmetic and copies ran while one was open for 2% -> 1% of each run, Pallas kernels for 13% -> 17%
where the time goes in v14:
time: 126 us; the launch traced here: 125 us
  waiting for transfers between devices  43.8 us (35%)
  Pallas kernels  43.6 us (35%)
  starting transfers between devices  32.1 us (25%)
  local copies, waits for them, and re-layouts  2.87 us (2%)
  other arithmetic  1.76 us (1%)
    pallas_call x2, Pallas kernels, full_turn(): pl.pallas_call(turn_kernel, grid=(columns // block,), in_specs=[columns_s...  39.7 us
    ppermute x22, waiting for transfers between devices, send(): return lax.ppermute(values, AXES, pairs)  33.7 us
    ppermute x22, starting transfers between devices, send(): return lax.ppermute(values, AXES, pairs)  25 us
    all_to_all x2, waiting for transfers between devices, exchange(): return lax.all_to_all(parts, AXES, split_axis=0, concat_axis=0, tiled=True)  10.1 us
    all_to_all x2, starting transfers between devices, exchange(): return lax.all_to_all(parts, AXES, split_axis=0, concat_axis=0, tiled=True)  7.14 us
  transfers between devices with their start and end apart: 24, of which 20 were waited for; matrix products, arithmetic and copies ran while one was open for 1% of the time, Pallas kernels for 17%

profile of v14, /device:TPU:0, one launch (start us, length us, event | category | flops | bytes accessed | tf_op | source)
XLA Modules:
  0.0 125.1 jit_solution(18366347002408699508)
XLA Ops:
  0.6 0.0 copy-start
  0.7 0.0 copy-start.1
  0.7 1.1 copy-done.1
  1.7 20.2 %turn.2 = (f32[128,2048]{1,0:T(8,128)}, f32[8,136,128]{2,1,0:T(8,128)S(1)}) custom-call(f32[1024,2048]{1,0:T(8,128)} %slab_ref.3, f32[1024,128]{1,0:T(8,128)S(1)} %copy-done.1, f32[128,2048]{1,0:T(8,128)} %right_ref.1, f32[1024,128]{1,0:T(8,128)S(1)} %copy-done.1), custom_call_target="tpu_custom_call" | custom-call | flops 6442450944 | bytes 8388608 | tf_op jit(solution)/shard_map/turn/pallas_call | solution.py:260
  21.9 0.5 collective-permute-start
  22.4 0.8 constant_dynamic-slice_fusion.13
  23.3 0.3 collective-permute-done
  23.7 2.9 %collective-permute-start.1 = (f32[200,128]{1,0:T(8,128)S(1)}, f32[200,128]{1,0:T(8,128)S(1)}, u32[]{:S(2)}, u32[]{:S(2)}) collective-permute-start(f32[200,128]{1,0:T(8,128)S(1)} %get-tuple-element.52), channel_id=1, source_target_pairs={{0,1},{1,0},{2,3},{3,2},{4,5},{5,4},{6,7},{7,6},{8,9},{9,8},{10,11... | collective-permute-start | bytes 307208 | tf_op jit(solution)/shard_map/ppermute | solution.py:31
  26.6 1.5 %collective-permute-start.2 = (f32[200,128]{1,0:T(8,128)S(1)}, f32[200,128]{1,0:T(8,128)S(1)}, u32[]{:S(2)}, u32[]{:S(2)}) collective-permute-start(f32[200,128]{1,0:T(8,128)S(1)} %get-tuple-element.53), channel_id=1, source_target_pairs={{0,2},{1,3},{2,0},{3,1},{4,6},{5,7},{6,4},{7,5},{8,10},{9,11},{10,... | collective-permute-start | bytes 307208 | tf_op jit(solution)/shard_map/ppermute | solution.py:31
  28.2 0.0 collective-permute-start.3
  28.2 1.7 %collective-permute-done.1 = f32[200,128]{1,0:T(8,128)S(1)} collective-permute-done((f32[200,128]{1,0:T(8,128)S(1)}, f32[200,128]{1,0:T(8,128)S(1)}, u32[]{:S(2)}, u32[]{:S(2)}) %collective-permute-start.1) | collective-permute-done | bytes 102432 | tf_op jit(solution)/shard_map/ppermute | solution.py:31
  29.9 2.6 %collective-permute-done.2 = f32[200,128]{1,0:T(8,128)S(1)} collective-permute-done((f32[200,128]{1,0:T(8,128)S(1)}, f32[200,128]{1,0:T(8,128)S(1)}, u32[]{:S(2)}, u32[]{:S(2)}) %collective-permute-start.2) | collective-permute-done | bytes 102432 | tf_op jit(solution)/shard_map/ppermute | solution.py:31
  32.5 1.2 collective-permute-done.3
  33.7 3.7 %collective-permute-start.6 = (f32[136,128]{1,0:T(8,128)S(1)}, f32[136,128]{1,0:T(8,128)S(1)}, u32[]{:S(2)}, u32[]{:S(2)}) collective-permute-start(f32[136,128]{1,0:T(8,128)S(1)} %fusion.13), channel_id=1, source_target_pairs={{0,24},{1,25},{2,26},{3,27},{4,28},{5,29},{6,30},{7,31},{8,16},{9,... | collective-permute-start | bytes 208904 | tf_op jit(solution)/shard_map/ppermute | solution.py:31
  37.4 0.0 collective-permute-start.5
  37.4 0.8 collective-permute-start.4
  38.2 1.7 %collective-permute-done.6 = f32[136,128]{1,0:T(8,128)S(1)} collective-permute-done((f32[136,128]{1,0:T(8,128)S(1)}, f32[136,128]{1,0:T(8,128)S(1)}, u32[]{:S(2)}, u32[]{:S(2)}) %collective-permute-start.6) | collective-permute-done | bytes 69664 | tf_op jit(solution)/shard_map/ppermute | solution.py:31
  39.9 2.7 %collective-permute-done.5 = f32[136,128]{1,0:T(8,128)S(1)} collective-permute-done((f32[136,128]{1,0:T(8,128)S(1)}, f32[136,128]{1,0:T(8,128)S(1)}, u32[]{:S(2)}, u32[]{:S(2)}) %collective-permute-start.5) | collective-permute-done | bytes 69664 | tf_op jit(solution)/shard_map/ppermute | solution.py:31
  42.6 0.0 collective-permute-done.4
  42.7 1.6 %collective-permute-start.9 = (f32[128,128]{1,0:T(8,128)S(1)}, f32[128,128]{1,0:T(8,128)S(1)}, u32[]{:S(2)}, u32[]{:S(2)}) collective-permute-start(f32[128,128]{1,0:T(8,128)S(1)} %fusion.15), channel_id=1, source_target_pairs={{0,3},{1,2},{2,1},{3,0},{4,7},{5,6},{6,5},{7,4},{8,11},{9,10},{10,... | collective-permute-start | bytes 196616 | tf_op jit(solution)/shard_map/ppermute | solution.py:31
  44.3 1.3 %collective-permute-start.8 = (f32[128,128]{1,0:T(8,128)S(1)}, f32[128,128]{1,0:T(8,128)S(1)}, u32[]{:S(2)}, u32[]{:S(2)}) collective-permute-start(f32[128,128]{1,0:T(8,128)S(1)} %fusion.15), channel_id=1, source_target_pairs={{0,2},{1,3},{2,0},{3,1},{4,6},{5,7},{6,4},{7,5},{8,10},{9,11},{10,... | collective-permute-start | bytes 196616 | tf_op jit(solution)/shard_map/ppermute | solution.py:31
  45.6 0.7 collective-permute-start.7
  46.2 1.8 %collective-permute-done.9 = f32[128,128]{1,0:T(8,128)S(1)} collective-permute-done((f32[128,128]{1,0:T(8,128)S(1)}, f32[128,128]{1,0:T(8,128)S(1)}, u32[]{:S(2)}, u32[]{:S(2)}) %collective-permute-start.9) | collective-permute-done | bytes 65568 | tf_op jit(solution)/shard_map/ppermute | solution.py:31
  48.1 0.7 collective-permute-done.8
  48.8 1.1 collective-permute-done.7
  49.9 0.1 maximum_maximum_fusion
  49.9 0.1 collective-permute-start.10
  50.0 1.7 %prepare.1 = (f32[32,16,128]{2,1,0:T(8,128)}, f32[1,128]{1,0:T(1,128)S(1)}) custom-call(s32[1]{0:T(128)} %bitcast.19.place_ref, f32[2048,128]{1,0:T(8,128)} %second_left_ref), custom_call_target="tpu_custom_call" | custom-call | flops 65536 | bytes 524288 | tf_op jit(solution)/shard_map/prepare/pallas_call | solution.py:313
  51.7 0.0 collective-permute-done.10
  51.7 0.2 fusion.9
  52.0 3.3 %all-to-all-start = ((f32[32,16,128]{2,1,0:T(8,128)}), f32[32,16,128]{2,1,0:T(8,128)S(1)}, u32[]{:S(2)}, u32[]{:S(2)}) async-start(f32[32,16,128]{2,1,0:T(8,128)} %get-tuple-element.20), calls=%async_computation | async-start | bytes 524288 | tf_op jit(solution)/shard_map/all_to_all | solution.py:21
  55.3 19.6 %turn.3 = (f32[128,2048]{1,0:T(8,128)S(1)}, f32[8,136,128]{2,1,0:T(8,128)S(1)}) custom-call(f32[1024,2048]{1,0:T(8,128)} %slab_ref.3, f32[1024,128]{1,0:T(8,128)S(1)} %bitcast.87, f32[128,2048]{1,0:T(8,128)} %get-tuple-element.14.right_ref, f32[1,128]{1,0:T(1,128)S(1)} %get-tuple-element.16.extra_ref), custom_call_target="tpu_custom_call" | custom-call | flops 6442450944 | bytes 8388608 | tf_op jit(solution)/shard_map/turn/pallas_call | solution.py:260
  74.9 0.0 all-to-all-done
  74.9 0.7 second_numerator.1
  75.7 0.3 collective-permute-start.11
  76.0 1.5 %collective-permute-done.11 = f32[4,200,128]{2,1,0:T(8,128)S(1)} collective-permute-done((f32[4,200,128]{2,1,0:T(8,128)S(1)}, f32[4,200,128]{2,1,0:T(8,128)S(1)}, u32[]{:S(2)}, u32[]{:S(2)}) %collective-permute-start.11) | collective-permute-done | bytes 409632 | tf_op jit(solution)/shard_map/ppermute | solution.py:31
  77.6 2.7 %collective-permute-start.14 = (f32[200,128]{1,0:T(8,128)S(1)}, f32[200,128]{1,0:T(8,128)S(1)}, u32[]{:S(2)}, u32[]{:S(2)}) collective-permute-start(f32[200,128]{1,0:T(8,128)S(1)} %get-tuple-element.26), channel_id=1, source_target_pairs={{0,3},{1,2},{2,1},{3,0},{4,7},{5,6},{6,5},{7,4},{8,11},{9,10},{10,... | collective-permute-start | bytes 307208 | tf_op jit(solution)/shard_map/ppermute | solution.py:31
  80.3 0.6 collective-permute-start.13
  80.9 0.3 collective-permute-start.12
  81.2 2.5 %collective-permute-done.14 = f32[200,128]{1,0:T(8,128)S(1)} collective-permute-done((f32[200,128]{1,0:T(8,128)S(1)}, f32[200,128]{1,0:T(8,128)S(1)}, u32[]{:S(2)}, u32[]{:S(2)}) %collective-permute-start.14) | collective-permute-done | bytes 102432 | tf_op jit(solution)/shard_map/ppermute | solution.py:31
  83.7 2.1 %collective-permute-done.13 = f32[200,128]{1,0:T(8,128)S(1)} collective-permute-done((f32[200,128]{1,0:T(8,128)S(1)}, f32[200,128]{1,0:T(8,128)S(1)}, u32[]{:S(2)}, u32[]{:S(2)}) %collective-permute-start.13) | collective-permute-done | bytes 102432 | tf_op jit(solution)/shard_map/ppermute | solution.py:31
  85.8 0.2 collective-permute-done.12
  86.0 3.4 %collective-permute-start.17 = (f32[200,128]{1,0:T(8,128)S(1)}, f32[200,128]{1,0:T(8,128)S(1)}, u32[]{:S(2)}, u32[]{:S(2)}) collective-permute-start(f32[200,128]{1,0:T(8,128)S(1)} %fusion.12), channel_id=1, source_target_pairs={{0,24},{1,25},{2,26},{3,27},{4,28},{5,29},{6,30},{7,31},{8,16},{9,... | collective-permute-start | bytes 307208 | tf_op jit(solution)/shard_map/ppermute | solution.py:31
  89.4 0.0 collective-permute-start.16
  89.4 1.0 collective-permute-start.15
  90.5 3.0 %collective-permute-done.17 = f32[200,128]{1,0:T(8,128)S(1)} collective-permute-done((f32[200,128]{1,0:T(8,128)S(1)}, f32[200,128]{1,0:T(8,128)S(1)}, u32[]{:S(2)}, u32[]{:S(2)}) %collective-permute-start.17) | collective-permute-done | bytes 102432 | tf_op jit(solution)/shard_map/ppermute | solution.py:31
  93.5 4.9 %collective-permute-done.16 = f32[200,128]{1,0:T(8,128)S(1)} collective-permute-done((f32[200,128]{1,0:T(8,128)S(1)}, f32[200,128]{1,0:T(8,128)S(1)}, u32[]{:S(2)}, u32[]{:S(2)}) %collective-permute-start.16) | collective-permute-done | bytes 102432 | tf_op jit(solution)/shard_map/ppermute | solution.py:31
  98.4 0.0 collective-permute-done.15
  98.5 0.1 broadcast_divide_fusion
  98.6 1.5 %collective-permute-start.19 = (f32[192,128]{1,0:T(8,128)S(1)}, f32[192,128]{1,0:T(8,128)S(1)}, u32[]{:S(2)}, u32[]{:S(2)}) collective-permute-start(f32[192,128]{1,0:T(8,128)S(1)} %get-tuple-element.51), channel_id=1, source_target_pairs={{0,2},{1,3},{2,0},{3,1},{4,6},{5,7},{6,4},{7,5},{8,10},{9,11},{10,... | collective-permute-start | bytes 294920 | tf_op jit(solution)/shard_map/ppermute | solution.py:31
  100.1 0.2 collective-permute-start.18
  100.3 1.8 %collective-permute-start.20 = (f32[192,128]{1,0:T(8,128)S(1)}, f32[192,128]{1,0:T(8,128)S(1)}, u32[]{:S(2)}, u32[]{:S(2)}) collective-permute-start(f32[192,128]{1,0:T(8,128)S(1)} %get-tuple-element.51), channel_id=1, source_target_pairs={{0,3},{1,2},{2,1},{3,0},{4,7},{5,6},{6,5},{7,4},{8,11},{9,10},{10,... | collective-permute-start | bytes 294920 | tf_op jit(solution)/shard_map/ppermute | solution.py:31
  102.2 2.2 %collective-permute-done.19 = f32[192,128]{1,0:T(8,128)S(1)} collective-permute-done((f32[192,128]{1,0:T(8,128)S(1)}, f32[192,128]{1,0:T(8,128)S(1)}, u32[]{:S(2)}, u32[]{:S(2)}) %collective-permute-start.19) | collective-permute-done | bytes 98336 | tf_op jit(solution)/shard_map/ppermute | solution.py:31
  104.3 0.5 collective-permute-done.18
  104.9 1.2 collective-permute-done.20
  106.1 0.1 pad_maximum_fusion.1
  106.2 0.1 collective-permute-start.21
  106.3 1.7 %collective-permute-done.21 = f32[4,192,128]{2,1,0:T(8,128)S(1)} collective-permute-done((f32[4,192,128]{2,1,0:T(8,128)S(1)}, f32[4,192,128]{2,1,0:T(8,128)S(1)}, u32[]{:S(2)}, u32[]{:S(2)}) %collective-permute-start.21) | collective-permute-done | bytes 393248 | tf_op jit(solution)/shard_map/ppermute | solution.py:31
  108.0 0.2 fusion.7
  108.1 1.4 %second_rows.1 = f32[512,128]{1,0:T(8,128)} custom-call(f32[128,2048]{1,0:T(8,128)S(1)} %get-tuple-element.18.right_ref, f32[512,128]{1,0:T(8,128)S(1)} %bitcast.79, f32[4,128,128]{2,1,0:T(8,128)S(1)} %bitcast.86), custom_call_target="tpu_custom_call" | custom-call | flops 402653184 | bytes 1048576 | tf_op jit(solution)/shard_map/second_rows/pallas_call | solution.py:289
  109.6 3.8 %all-to-all-start.1 = ((f32[32,16,128]{2,1,0:T(8,128)}), f32[32,16,128]{2,1,0:T(8,128)S(1)}, u32[]{:S(2)}, u32[]{:S(2)}) async-start(f32[32,16,128]{2,1,0:T(8,128)} %bitcast.45), calls=%async_computation.1 | async-start | bytes 524288 | tf_op jit(solution)/shard_map/all_to_all | solution.py:21
  113.4 0.8 fusion
  114.2 10.1 %all-to-all-done.1 = f32[32,16,128]{2,1,0:T(8,128)S(1)} async-done(((f32[32,16,128]{2,1,0:T(8,128)}), f32[32,16,128]{2,1,0:T(8,128)S(1)}, u32[]{:S(2)}, u32[]{:S(2)}) %all-to-all-start.1) | async-done | bytes 262176 | tf_op jit(solution)/shard_map/all_to_all | solution.py:21
  124.4 0.7 copy.8
  (33 shorter events, 0.6 us)
Async XLA Ops:
  0.6 21.8 %copy-start = (f32[128,128]{1,0:T(8,128)S(1)}, f32[128,128]{1,0:T(8,128)}, u32[]{:S(2)}) copy-start(f32[128,128]{1,0:T(8,128)} %param.9) | copy-start | bytes 196612
  0.7 1.1 copy-start.1
  21.9 1.7 %collective-permute-start = (f32[4,136,128]{2,1,0:T(8,128)S(1)}, f32[4,136,128]{2,1,0:T(8,128)S(1)}, u32[]{:S(2)}, u32[]{:S(2)}) collective-permute-start(f32[4,136,128]{2,1,0:T(8,128)S(1)} %dynamic-slice_bitcast_fusion), channel_id=1, source_target_pairs={{0,4},{1,5},{2,6},{3,7},{4,0},{5,1},{6,2},{7,3},{8,12},{9,13},{10,... | collective-permute-start | bytes 835592 | tf_op jit(solution)/shard_map/ppermute | solution.py:31
  23.7 6.2 %collective-permute-start.1 = (f32[200,128]{1,0:T(8,128)S(1)}, f32[200,128]{1,0:T(8,128)S(1)}, u32[]{:S(2)}, u32[]{:S(2)}) collective-permute-start(f32[200,128]{1,0:T(8,128)S(1)} %get-tuple-element.52), channel_id=1, source_target_pairs={{0,1},{1,0},{2,3},{3,2},{4,5},{5,4},{6,7},{7,6},{8,9},{9,8},{10,11... | collective-permute-start | bytes 307208 | tf_op jit(solution)/shard_map/ppermute | solution.py:31
  26.6 5.9 %collective-permute-start.2 = (f32[200,128]{1,0:T(8,128)S(1)}, f32[200,128]{1,0:T(8,128)S(1)}, u32[]{:S(2)}, u32[]{:S(2)}) collective-permute-start(f32[200,128]{1,0:T(8,128)S(1)} %get-tuple-element.53), channel_id=1, source_target_pairs={{0,2},{1,3},{2,0},{3,1},{4,6},{5,7},{6,4},{7,5},{8,10},{9,11},{10,... | collective-permute-start | bytes 307208 | tf_op jit(solution)/shard_map/ppermute | solution.py:31
  28.2 5.6 %collective-permute-start.3 = (f32[200,128]{1,0:T(8,128)S(1)}, f32[200,128]{1,0:T(8,128)S(1)}, u32[]{:S(2)}, u32[]{:S(2)}) collective-permute-start(f32[200,128]{1,0:T(8,128)S(1)} %get-tuple-element.54), channel_id=1, source_target_pairs={{0,3},{1,2},{2,1},{3,0},{4,7},{5,6},{6,5},{7,4},{8,11},{9,10},{10,... | collective-permute-start | bytes 307208 | tf_op jit(solution)/shard_map/ppermute | solution.py:31
  33.7 6.2 %collective-permute-start.6 = (f32[136,128]{1,0:T(8,128)S(1)}, f32[136,128]{1,0:T(8,128)S(1)}, u32[]{:S(2)}, u32[]{:S(2)}) collective-permute-start(f32[136,128]{1,0:T(8,128)S(1)} %fusion.13), channel_id=1, source_target_pairs={{0,24},{1,25},{2,26},{3,27},{4,28},{5,29},{6,30},{7,31},{8,16},{9,... | collective-permute-start | bytes 208904 | tf_op jit(solution)/shard_map/ppermute | solution.py:31
  37.4 5.2 %collective-permute-start.5 = (f32[136,128]{1,0:T(8,128)S(1)}, f32[136,128]{1,0:T(8,128)S(1)}, u32[]{:S(2)}, u32[]{:S(2)}) collective-permute-start(f32[136,128]{1,0:T(8,128)S(1)} %fusion.13), channel_id=1, source_target_pairs={{0,16},{1,17},{2,18},{3,19},{4,20},{5,21},{6,22},{7,23},{8,24},{9,... | collective-permute-start | bytes 208904 | tf_op jit(solution)/shard_map/ppermute | solution.py:31
  37.4 5.2 %collective-permute-start.4 = (f32[136,128]{1,0:T(8,128)S(1)}, f32[136,128]{1,0:T(8,128)S(1)}, u32[]{:S(2)}, u32[]{:S(2)}) collective-permute-start(f32[136,128]{1,0:T(8,128)S(1)} %fusion.13), channel_id=1, source_target_pairs={{0,8},{1,9},{2,10},{3,11},{4,12},{5,13},{6,14},{7,15},{8,0},{9,1},... | collective-permute-start | bytes 208904 | tf_op jit(solution)/shard_map/ppermute | solution.py:31
  42.7 5.4 %collective-permute-start.9 = (f32[128,128]{1,0:T(8,128)S(1)}, f32[128,128]{1,0:T(8,128)S(1)}, u32[]{:S(2)}, u32[]{:S(2)}) collective-permute-start(f32[128,128]{1,0:T(8,128)S(1)} %fusion.15), channel_id=1, source_target_pairs={{0,3},{1,2},{2,1},{3,0},{4,7},{5,6},{6,5},{7,4},{8,11},{9,10},{10,... | collective-permute-start | bytes 196616 | tf_op jit(solution)/shard_map/ppermute | solution.py:31
  44.3 4.5 %collective-permute-start.8 = (f32[128,128]{1,0:T(8,128)S(1)}, f32[128,128]{1,0:T(8,128)S(1)}, u32[]{:S(2)}, u32[]{:S(2)}) collective-permute-start(f32[128,128]{1,0:T(8,128)S(1)} %fusion.15), channel_id=1, source_target_pairs={{0,2},{1,3},{2,0},{3,1},{4,6},{5,7},{6,4},{7,5},{8,10},{9,11},{10,... | collective-permute-start | bytes 196616 | tf_op jit(solution)/shard_map/ppermute | solution.py:31
  45.6 4.3 %collective-permute-start.7 = (f32[128,128]{1,0:T(8,128)S(1)}, f32[128,128]{1,0:T(8,128)S(1)}, u32[]{:S(2)}, u32[]{:S(2)}) collective-permute-start(f32[128,128]{1,0:T(8,128)S(1)} %fusion.15), channel_id=1, source_target_pairs={{0,1},{1,0},{2,3},{3,2},{4,5},{5,4},{6,7},{7,6},{8,9},{9,8},{10,11... | collective-permute-start | bytes 196616 | tf_op jit(solution)/shard_map/ppermute | solution.py:31
  49.9 1.8 %collective-permute-start.10 = (f32[4,192,128]{2,1,0:T(8,128)S(1)}, f32[4,192,128]{2,1,0:T(8,128)S(1)}, u32[]{:S(2)}, u32[]{:S(2)}) collective-permute-start(f32[4,192,128]{2,1,0:T(8,128)S(1)} %get-tuple-element.35), channel_id=1, source_target_pairs={{0,4},{1,5},{2,6},{3,7},{4,0},{5,1},{6,2},{7,3},{8,12},{9,13},{10,... | collective-permute-start | bytes 1179656 | tf_op jit(solution)/shard_map/ppermute | solution.py:31
  52.0 22.9 %all-to-all-start = ((f32[32,16,128]{2,1,0:T(8,128)}), f32[32,16,128]{2,1,0:T(8,128)S(1)}, u32[]{:S(2)}, u32[]{:S(2)}) async-start(f32[32,16,128]{2,1,0:T(8,128)} %get-tuple-element.20), calls=%async_computation | async-start | bytes 524288 | tf_op jit(solution)/shard_map/all_to_all | solution.py:21
  75.7 1.8 %collective-permute-start.11 = (f32[4,200,128]{2,1,0:T(8,128)S(1)}, f32[4,200,128]{2,1,0:T(8,128)S(1)}, u32[]{:S(2)}, u32[]{:S(2)}) collective-permute-start(f32[4,200,128]{2,1,0:T(8,128)S(1)} %fusion.3), channel_id=1, source_target_pairs={{0,4},{1,5},{2,6},{3,7},{4,0},{5,1},{6,2},{7,3},{8,12},{9,13},{10,... | collective-permute-start | bytes 1228808 | tf_op jit(solution)/shard_map/ppermute | solution.py:31
  77.6 6.1 %collective-permute-start.14 = (f32[200,128]{1,0:T(8,128)S(1)}, f32[200,128]{1,0:T(8,128)S(1)}, u32[]{:S(2)}, u32[]{:S(2)}) collective-permute-start(f32[200,128]{1,0:T(8,128)S(1)} %get-tuple-element.26), channel_id=1, source_target_pairs={{0,3},{1,2},{2,1},{3,0},{4,7},{5,6},{6,5},{7,4},{8,11},{9,10},{10,... | collective-permute-start | bytes 307208 | tf_op jit(solution)/shard_map/ppermute | solution.py:31
  80.3 5.5 %collective-permute-start.13 = (f32[200,128]{1,0:T(8,128)S(1)}, f32[200,128]{1,0:T(8,128)S(1)}, u32[]{:S(2)}, u32[]{:S(2)}) collective-permute-start(f32[200,128]{1,0:T(8,128)S(1)} %get-tuple-element.27), channel_id=1, source_target_pairs={{0,2},{1,3},{2,0},{3,1},{4,6},{5,7},{6,4},{7,5},{8,10},{9,11},{10,... | collective-permute-start | bytes 307208 | tf_op jit(solution)/shard_map/ppermute | solution.py:31
  80.9 5.1 %collective-permute-start.12 = (f32[200,128]{1,0:T(8,128)S(1)}, f32[200,128]{1,0:T(8,128)S(1)}, u32[]{:S(2)}, u32[]{:S(2)}) collective-permute-start(f32[200,128]{1,0:T(8,128)S(1)} %get-tuple-element.28), channel_id=1, source_target_pairs={{0,1},{1,0},{2,3},{3,2},{4,5},{5,4},{6,7},{7,6},{8,9},{9,8},{10,11... | collective-permute-start | bytes 307208 | tf_op jit(solution)/shard_map/ppermute | solution.py:31
  86.0 7.5 %collective-permute-start.17 = (f32[200,128]{1,0:T(8,128)S(1)}, f32[200,128]{1,0:T(8,128)S(1)}, u32[]{:S(2)}, u32[]{:S(2)}) collective-permute-start(f32[200,128]{1,0:T(8,128)S(1)} %fusion.12), channel_id=1, source_target_pairs={{0,24},{1,25},{2,26},{3,27},{4,28},{5,29},{6,30},{7,31},{8,16},{9,... | collective-permute-start | bytes 307208 | tf_op jit(solution)/shard_map/ppermute | solution.py:31
  89.4 8.9 %collective-permute-start.16 = (f32[200,128]{1,0:T(8,128)S(1)}, f32[200,128]{1,0:T(8,128)S(1)}, u32[]{:S(2)}, u32[]{:S(2)}) collective-permute-start(f32[200,128]{1,0:T(8,128)S(1)} %fusion.12), channel_id=1, source_target_pairs={{0,16},{1,17},{2,18},{3,19},{4,20},{5,21},{6,22},{7,23},{8,24},{9,... | collective-permute-start | bytes 307208 | tf_op jit(solution)/shard_map/ppermute | solution.py:31
  89.4 8.9 %collective-permute-start.15 = (f32[200,128]{1,0:T(8,128)S(1)}, f32[200,128]{1,0:T(8,128)S(1)}, u32[]{:S(2)}, u32[]{:S(2)}) collective-permute-start(f32[200,128]{1,0:T(8,128)S(1)} %fusion.12), channel_id=1, source_target_pairs={{0,8},{1,9},{2,10},{3,11},{4,12},{5,13},{6,14},{7,15},{8,0},{9,1},... | collective-permute-start | bytes 307208 | tf_op jit(solution)/shard_map/ppermute | solution.py:31
  98.6 5.7 %collective-permute-start.19 = (f32[192,128]{1,0:T(8,128)S(1)}, f32[192,128]{1,0:T(8,128)S(1)}, u32[]{:S(2)}, u32[]{:S(2)}) collective-permute-start(f32[192,128]{1,0:T(8,128)S(1)} %get-tuple-element.51), channel_id=1, source_target_pairs={{0,2},{1,3},{2,0},{3,1},{4,6},{5,7},{6,4},{7,5},{8,10},{9,11},{10,... | collective-permute-start | bytes 294920 | tf_op jit(solution)/shard_map/ppermute | solution.py:31
  100.1 4.7 %collective-permute-start.18 = (f32[192,128]{1,0:T(8,128)S(1)}, f32[192,128]{1,0:T(8,128)S(1)}, u32[]{:S(2)}, u32[]{:S(2)}) collective-permute-start(f32[192,128]{1,0:T(8,128)S(1)} %get-tuple-element.51), channel_id=1, source_target_pairs={{0,1},{1,0},{2,3},{3,2},{4,5},{5,4},{6,7},{7,6},{8,9},{9,8},{10,11... | collective-permute-start | bytes 294920 | tf_op jit(solution)/shard_map/ppermute | solution.py:31
  100.3 5.7 %collective-permute-start.20 = (f32[192,128]{1,0:T(8,128)S(1)}, f32[192,128]{1,0:T(8,128)S(1)}, u32[]{:S(2)}, u32[]{:S(2)}) collective-permute-start(f32[192,128]{1,0:T(8,128)S(1)} %get-tuple-element.51), channel_id=1, source_target_pairs={{0,3},{1,2},{2,1},{3,0},{4,7},{5,6},{6,5},{7,4},{8,11},{9,10},{10,... | collective-permute-start | bytes 294920 | tf_op jit(solution)/shard_map/ppermute | solution.py:31
  106.2 1.8 %collective-permute-start.21 = (f32[4,192,128]{2,1,0:T(8,128)S(1)}, f32[4,192,128]{2,1,0:T(8,128)S(1)}, u32[]{:S(2)}, u32[]{:S(2)}) collective-permute-start(f32[4,192,128]{2,1,0:T(8,128)S(1)} %get-tuple-element.29), channel_id=1, source_target_pairs={{0,4},{1,5},{2,6},{3,7},{4,0},{5,1},{6,2},{7,3},{8,12},{9,13},{10,... | collective-permute-start | bytes 1179656 | tf_op jit(solution)/shard_map/ppermute | solution.py:31
  109.6 14.8 %all-to-all-start.1 = ((f32[32,16,128]{2,1,0:T(8,128)}), f32[32,16,128]{2,1,0:T(8,128)S(1)}, u32[]{:S(2)}, u32[]{:S(2)}) async-start(f32[32,16,128]{2,1,0:T(8,128)} %bitcast.45), calls=%async_computation.1 | async-start | bytes 524288 | tf_op jit(solution)/shard_map/all_to_all | solution.py:21

commit v15 on v14

--- a/solution.py
+++ b/solution.py
@@ -10,7 +10,6 @@
 AXES = ("row", "col")
 F32, BF16 = jnp.float32, jnp.bfloat16
 PAD = 8
-ROWS = 1024
 MIB = 1024 * 1024
 T1_MIB = 52
 PREP_KIB = 54528
@@ -92,6 +91,10 @@
     return jnp.dot(a, b, preferred_element_type=F32)
 
 
+def dot_nt(a, b):
+    return lax.dot_general(a, b, (((1,), (1,)), ((), ())), preferred_element_type=F32)
+
+
 def divide(x, y):
     return x * pl.reciprocal(y, approx=True)
 
@@ -113,11 +116,6 @@
     sums_ref[...] = jnp.broadcast_to(jnp.sum(turned, axis=1, keepdims=True), sums_ref.shape)
 
 
-def chunks(extent, size):
-    size = min(size, extent)
-    return [pl.ds(start, size) for start in range(0, extent, size)]
-
-
 def stacked(right):
     high, low = split(right)
     return jnp.concatenate([high, high, low], axis=0)
@@ -139,16 +137,14 @@
 def left_numerator(slab_ref, pair_ref, right, total_ref, sums_ref, first):
     rank = right.shape[0]
     stack = stacked(right)
-    right_high, right_low = split(right.T)
-    right_both = jnp.concatenate([right_high, right_low], axis=1)
-    row_sums = dot(jnp.ones((16, right.shape[1]), BF16), right_both)[:PAD]
+    right_both = jnp.concatenate([stack[:rank], stack[2 * rank :]], axis=0)
+    row_sums = dot_nt(jnp.ones((16, right.shape[1]), BF16), right_both)[:PAD]
     row_sums = row_sums[:, :rank] + row_sums[:, rank:]
     sums_ref[...] = jnp.where(first, row_sums, sums_ref[...] + row_sums)
-    for rows in chunks(slab_ref.shape[0], ROWS):
-        high, low = quotients(slab_ref, pair_ref, stack, rows)
-        both = dot(high, right_both)
-        term = both[:, :rank] + both[:, rank:] + dot(low, right_high)
-        total_ref[rows, :] = jnp.where(first, term, total_ref[rows, :] + term)
+    high, low = quotients(slab_ref, pair_ref, stack, pl.ds(0, slab_ref.shape[0]))
+    both = dot_nt(right_both, high)
+    term = both[:rank] + both[rank:] + dot_nt(stack[:rank], low)
+    total_ref[...] = jnp.where(first, term, total_ref[...] + term)
 
 
 def write_left(total_ref, row_sums_ref, extra_ref, out_ref):
@@ -156,8 +152,9 @@
     height = tall - PAD
     first = lax.broadcasted_iota(jnp.int32, (PAD, rank), 0) == 0
     stats = jnp.where(first, row_sums_ref[...], extra_ref[:1, :])
+    total = total_ref[...].T
     for part in range(parts):
-        out_ref[part, :height, :] = total_ref[pl.ds(part * height, height), :]
+        out_ref[part, :height, :] = total[part * height : (part + 1) * height]
         out_ref[part, height:, :] = stats
 
 
@@ -244,7 +241,7 @@
 
 
 def total_scratch(m, rank):
-    return [pltpu.VMEM((m, rank), F32), pltpu.VMEM((PAD, rank), F32)]
+    return [pltpu.VMEM((rank, m), F32), pltpu.VMEM((PAD, rank), F32)]
 
 
 def cost(m, rank, columns, dots):
@@ -349,7 +346,7 @@
         return own * total[:rows_own] / total[rows_own][None, :]
 
     right, summed = full_turn(
-        tensor_slab, left_init, right_init, left_init, k // 2, parts, T1_MIB * MIB
+        tensor_slab, left_init, right_init, left_init, k, parts, T1_MIB * MIB
     )
     second_left = after(second_left_init, summed)
     summed = summed.reshape(2, col_devices, rows_own + PAD, rank)
@@ -372,7 +369,7 @@
     place = lax.axis_index("col").astype(jnp.int32)[None]
     second_left, col_part = prepare(place, second_left, devices, slices, second_rows)
     arrived = exchange(after(second_left, left))
-    right, summed = full_turn(tensor_slab, left, right, col_part, k // 2, parts, VMEM_BYTES)
+    right, summed = full_turn(tensor_slab, left, right, col_part, k, parts, VMEM_BYTES)
     arrived = after(arrived, summed)
     second_left = arrived.reshape(rank * slices, rank)
     numerator = second_numerator(right, second_left, whole, slices)

time: 126 us -> 111 us (0.88)
  Pallas kernels: 43.6 us -> 29 us
    pallas_call x2, Pallas kernels: 39.7 us -> 25.2 us  [full_turn(): pl.pallas_call(turn_kernel, grid=(columns // block,), in_specs=[columns_s...]
  transfers between devices with their start and end apart: 24 -> 24, of which waited for: 20 -> 20; matrix products, arithmetic and copies ran while one was open for 1% -> 2% of each run, Pallas kernels for 17% -> 13%
where the time goes in v15:
time: 111 us
  waiting for transfers between devices  43.8 us (39%)
  starting transfers between devices  32.1 us (29%)
  Pallas kernels  29 us (26%)
  local copies, waits for them, and re-layouts  2.87 us (3%)
  other arithmetic  1.76 us (2%)
    ppermute x22, waiting for transfers between devices, send(): return lax.ppermute(values, AXES, pairs)  33.7 us
    pallas_call x2, Pallas kernels, full_turn(): pl.pallas_call(turn_kernel, grid=(columns // block,), in_specs=[columns_s...  25.2 us
    ppermute x22, starting transfers between devices, send(): return lax.ppermute(values, AXES, pairs)  25 us
    all_to_all x2, waiting for transfers between devices, exchange(): return lax.all_to_all(parts, AXES, split_axis=0, concat_axis=0, tiled=True)  10.1 us
    all_to_all x2, starting transfers between devices, exchange(): return lax.all_to_all(parts, AXES, split_axis=0, concat_axis=0, tiled=True)  7.11 us
  transfers between devices with their start and end apart: 24, of which 20 were waited for; matrix products, arithmetic and copies ran while one was open for 2% of the time, Pallas kernels for 13%

profile of v15, /device:TPU:0, one launch (start us, length us, event | category | flops | bytes accessed | tf_op | source)
XLA Modules:
  0.0 110.5 jit_solution(4008897244711104324)
XLA Ops:
  0.6 0.0 copy-start
  0.7 0.0 copy-start.1
  0.7 1.1 copy-done.1
  1.7 12.9 %turn.2 = (f32[128,2048]{1,0:T(8,128)}, f32[8,136,128]{2,1,0:T(8,128)S(1)}) custom-call(f32[1024,2048]{1,0:T(8,128)} %slab_ref.3, f32[1024,128]{1,0:T(8,128)S(1)} %copy-done.1, f32[128,2048]{1,0:T(8,128)} %right_ref.1, f32[1024,128]{1,0:T(8,128)S(1)} %copy-done.1), custom_call_target="tpu_custom_call" | custom-call | flops 6442450944 | bytes 8388608 | tf_op jit(solution)/shard_map/turn/pallas_call | solution.py:257
  14.7 0.5 collective-permute-start
  15.2 0.8 constant_dynamic-slice_fusion.13
  16.0 0.3 collective-permute-done
  16.5 2.9 %collective-permute-start.1 = (f32[200,128]{1,0:T(8,128)S(1)}, f32[200,128]{1,0:T(8,128)S(1)}, u32[]{:S(2)}, u32[]{:S(2)}) collective-permute-start(f32[200,128]{1,0:T(8,128)S(1)} %get-tuple-element.52), channel_id=1, source_target_pairs={{0,1},{1,0},{2,3},{3,2},{4,5},{5,4},{6,7},{7,6},{8,9},{9,8},{10,11... | collective-permute-start | bytes 307208 | tf_op jit(solution)/shard_map/ppermute | solution.py:30
  19.4 1.5 %collective-permute-start.2 = (f32[200,128]{1,0:T(8,128)S(1)}, f32[200,128]{1,0:T(8,128)S(1)}, u32[]{:S(2)}, u32[]{:S(2)}) collective-permute-start(f32[200,128]{1,0:T(8,128)S(1)} %get-tuple-element.53), channel_id=1, source_target_pairs={{0,2},{1,3},{2,0},{3,1},{4,6},{5,7},{6,4},{7,5},{8,10},{9,11},{10,... | collective-permute-start | bytes 307208 | tf_op jit(solution)/shard_map/ppermute | solution.py:30
  20.9 0.0 collective-permute-start.3
  20.9 1.7 %collective-permute-done.1 = f32[200,128]{1,0:T(8,128)S(1)} collective-permute-done((f32[200,128]{1,0:T(8,128)S(1)}, f32[200,128]{1,0:T(8,128)S(1)}, u32[]{:S(2)}, u32[]{:S(2)}) %collective-permute-start.1) | collective-permute-done | bytes 102432 | tf_op jit(solution)/shard_map/ppermute | solution.py:30
  22.6 2.6 %collective-permute-done.2 = f32[200,128]{1,0:T(8,128)S(1)} collective-permute-done((f32[200,128]{1,0:T(8,128)S(1)}, f32[200,128]{1,0:T(8,128)S(1)}, u32[]{:S(2)}, u32[]{:S(2)}) %collective-permute-start.2) | collective-permute-done | bytes 102432 | tf_op jit(solution)/shard_map/ppermute | solution.py:30
  25.3 1.2 %collective-permute-done.3 = f32[200,128]{1,0:T(8,128)S(1)} collective-permute-done((f32[200,128]{1,0:T(8,128)S(1)}, f32[200,128]{1,0:T(8,128)S(1)}, u32[]{:S(2)}, u32[]{:S(2)}) %collective-permute-start.3) | collective-permute-done | bytes 102432 | tf_op jit(solution)/shard_map/ppermute | solution.py:30
  26.5 3.7 %collective-permute-start.6 = (f32[136,128]{1,0:T(8,128)S(1)}, f32[136,128]{1,0:T(8,128)S(1)}, u32[]{:S(2)}, u32[]{:S(2)}) collective-permute-start(f32[136,128]{1,0:T(8,128)S(1)} %fusion.13), channel_id=1, source_target_pairs={{0,24},{1,25},{2,26},{3,27},{4,28},{5,29},{6,30},{7,31},{8,16},{9,... | collective-permute-start | bytes 208904 | tf_op jit(solution)/shard_map/ppermute | solution.py:30
  30.2 0.0 collective-permute-start.5
  30.2 0.8 collective-permute-start.4
  31.0 1.7 %collective-permute-done.6 = f32[136,128]{1,0:T(8,128)S(1)} collective-permute-done((f32[136,128]{1,0:T(8,128)S(1)}, f32[136,128]{1,0:T(8,128)S(1)}, u32[]{:S(2)}, u32[]{:S(2)}) %collective-permute-start.6) | collective-permute-done | bytes 69664 | tf_op jit(solution)/shard_map/ppermute | solution.py:30
  32.7 2.7 %collective-permute-done.5 = f32[136,128]{1,0:T(8,128)S(1)} collective-permute-done((f32[136,128]{1,0:T(8,128)S(1)}, f32[136,128]{1,0:T(8,128)S(1)}, u32[]{:S(2)}, u32[]{:S(2)}) %collective-permute-start.5) | collective-permute-done | bytes 69664 | tf_op jit(solution)/shard_map/ppermute | solution.py:30
  35.4 0.0 collective-permute-done.4
  35.4 1.6 %collective-permute-start.9 = (f32[128,128]{1,0:T(8,128)S(1)}, f32[128,128]{1,0:T(8,128)S(1)}, u32[]{:S(2)}, u32[]{:S(2)}) collective-permute-start(f32[128,128]{1,0:T(8,128)S(1)} %fusion.15), channel_id=1, source_target_pairs={{0,3},{1,2},{2,1},{3,0},{4,7},{5,6},{6,5},{7,4},{8,11},{9,10},{10,... | collective-permute-start | bytes 196616 | tf_op jit(solution)/shard_map/ppermute | solution.py:30
  37.0 1.3 %collective-permute-start.8 = (f32[128,128]{1,0:T(8,128)S(1)}, f32[128,128]{1,0:T(8,128)S(1)}, u32[]{:S(2)}, u32[]{:S(2)}) collective-permute-start(f32[128,128]{1,0:T(8,128)S(1)} %fusion.15), channel_id=1, source_target_pairs={{0,2},{1,3},{2,0},{3,1},{4,6},{5,7},{6,4},{7,5},{8,10},{9,11},{10,... | collective-permute-start | bytes 196616 | tf_op jit(solution)/shard_map/ppermute | solution.py:30
  38.3 0.7 collective-permute-start.7
  39.0 1.8 %collective-permute-done.9 = f32[128,128]{1,0:T(8,128)S(1)} collective-permute-done((f32[128,128]{1,0:T(8,128)S(1)}, f32[128,128]{1,0:T(8,128)S(1)}, u32[]{:S(2)}, u32[]{:S(2)}) %collective-permute-start.9) | collective-permute-done | bytes 65568 | tf_op jit(solution)/shard_map/ppermute | solution.py:30
  40.8 0.7 collective-permute-done.8
  41.5 1.1 collective-permute-done.7
  42.6 0.1 maximum_maximum_fusion
  42.7 0.1 collective-permute-start.10
  42.8 1.7 %prepare.1 = (f32[32,16,128]{2,1,0:T(8,128)}, f32[1,128]{1,0:T(1,128)S(1)}) custom-call(s32[1]{0:T(128)} %bitcast.19.place_ref, f32[2048,128]{1,0:T(8,128)} %second_left_ref), custom_call_target="tpu_custom_call" | custom-call | flops 65536 | bytes 524288 | tf_op jit(solution)/shard_map/prepare/pallas_call | solution.py:310
  44.5 0.0 collective-permute-done.10
  44.5 0.2 fusion.9
  44.7 3.3 %all-to-all-start = ((f32[32,16,128]{2,1,0:T(8,128)}), f32[32,16,128]{2,1,0:T(8,128)S(1)}, u32[]{:S(2)}, u32[]{:S(2)}) async-start(f32[32,16,128]{2,1,0:T(8,128)} %get-tuple-element.20), calls=%async_computation | async-start | bytes 524288 | tf_op jit(solution)/shard_map/all_to_all | solution.py:20
  48.1 12.3 %turn.3 = (f32[128,2048]{1,0:T(8,128)S(1)}, f32[8,136,128]{2,1,0:T(8,128)S(1)}) custom-call(f32[1024,2048]{1,0:T(8,128)} %slab_ref.3, f32[1024,128]{1,0:T(8,128)S(1)} %bitcast.87, f32[128,2048]{1,0:T(8,128)} %get-tuple-element.14.right_ref, f32[1,128]{1,0:T(1,128)S(1)} %get-tuple-element.16.extra_ref), custom_call_target="tpu_custom_call" | custom-call | flops 6442450944 | bytes 8388608 | tf_op jit(solution)/shard_map/turn/pallas_call | solution.py:257
  60.3 0.0 all-to-all-done
  60.3 0.7 second_numerator.1
  61.1 0.3 collective-permute-start.11
  61.5 1.5 %collective-permute-done.11 = f32[4,200,128]{2,1,0:T(8,128)S(1)} collective-permute-done((f32[4,200,128]{2,1,0:T(8,128)S(1)}, f32[4,200,128]{2,1,0:T(8,128)S(1)}, u32[]{:S(2)}, u32[]{:S(2)}) %collective-permute-start.11) | collective-permute-done | bytes 409632 | tf_op jit(solution)/shard_map/ppermute | solution.py:30
  63.0 2.7 %collective-permute-start.14 = (f32[200,128]{1,0:T(8,128)S(1)}, f32[200,128]{1,0:T(8,128)S(1)}, u32[]{:S(2)}, u32[]{:S(2)}) collective-permute-start(f32[200,128]{1,0:T(8,128)S(1)} %get-tuple-element.26), channel_id=1, source_target_pairs={{0,3},{1,2},{2,1},{3,0},{4,7},{5,6},{6,5},{7,4},{8,11},{9,10},{10,... | collective-permute-start | bytes 307208 | tf_op jit(solution)/shard_map/ppermute | solution.py:30
  65.8 0.6 collective-permute-start.13
  66.3 0.3 collective-permute-start.12
  66.6 2.5 %collective-permute-done.14 = f32[200,128]{1,0:T(8,128)S(1)} collective-permute-done((f32[200,128]{1,0:T(8,128)S(1)}, f32[200,128]{1,0:T(8,128)S(1)}, u32[]{:S(2)}, u32[]{:S(2)}) %collective-permute-start.14) | collective-permute-done | bytes 102432 | tf_op jit(solution)/shard_map/ppermute | solution.py:30
  69.1 2.1 %collective-permute-done.13 = f32[200,128]{1,0:T(8,128)S(1)} collective-permute-done((f32[200,128]{1,0:T(8,128)S(1)}, f32[200,128]{1,0:T(8,128)S(1)}, u32[]{:S(2)}, u32[]{:S(2)}) %collective-permute-start.13) | collective-permute-done | bytes 102432 | tf_op jit(solution)/shard_map/ppermute | solution.py:30
  71.2 0.2 collective-permute-done.12
  71.5 3.4 %collective-permute-start.17 = (f32[200,128]{1,0:T(8,128)S(1)}, f32[200,128]{1,0:T(8,128)S(1)}, u32[]{:S(2)}, u32[]{:S(2)}) collective-permute-start(f32[200,128]{1,0:T(8,128)S(1)} %fusion.12), channel_id=1, source_target_pairs={{0,24},{1,25},{2,26},{3,27},{4,28},{5,29},{6,30},{7,31},{8,16},{9,... | collective-permute-start | bytes 307208 | tf_op jit(solution)/shard_map/ppermute | solution.py:30
  74.9 0.0 collective-permute-start.16
  74.9 1.0 collective-permute-start.15
  75.9 3.0 %collective-permute-done.17 = f32[200,128]{1,0:T(8,128)S(1)} collective-permute-done((f32[200,128]{1,0:T(8,128)S(1)}, f32[200,128]{1,0:T(8,128)S(1)}, u32[]{:S(2)}, u32[]{:S(2)}) %collective-permute-start.17) | collective-permute-done | bytes 102432 | tf_op jit(solution)/shard_map/ppermute | solution.py:30
  78.9 4.9 %collective-permute-done.16 = f32[200,128]{1,0:T(8,128)S(1)} collective-permute-done((f32[200,128]{1,0:T(8,128)S(1)}, f32[200,128]{1,0:T(8,128)S(1)}, u32[]{:S(2)}, u32[]{:S(2)}) %collective-permute-start.16) | collective-permute-done | bytes 102432 | tf_op jit(solution)/shard_map/ppermute | solution.py:30
  83.8 0.0 collective-permute-done.15
  83.9 0.1 broadcast_divide_fusion
  84.0 1.5 %collective-permute-start.19 = (f32[192,128]{1,0:T(8,128)S(1)}, f32[192,128]{1,0:T(8,128)S(1)}, u32[]{:S(2)}, u32[]{:S(2)}) collective-permute-start(f32[192,128]{1,0:T(8,128)S(1)} %get-tuple-element.51), channel_id=1, source_target_pairs={{0,2},{1,3},{2,0},{3,1},{4,6},{5,7},{6,4},{7,5},{8,10},{9,11},{10,... | collective-permute-start | bytes 294920 | tf_op jit(solution)/shard_map/ppermute | solution.py:30
  85.6 0.2 collective-permute-start.18
  85.8 1.8 %collective-permute-start.20 = (f32[192,128]{1,0:T(8,128)S(1)}, f32[192,128]{1,0:T(8,128)S(1)}, u32[]{:S(2)}, u32[]{:S(2)}) collective-permute-start(f32[192,128]{1,0:T(8,128)S(1)} %get-tuple-element.51), channel_id=1, source_target_pairs={{0,3},{1,2},{2,1},{3,0},{4,7},{5,6},{6,5},{7,4},{8,11},{9,10},{10,... | collective-permute-start | bytes 294920 | tf_op jit(solution)/shard_map/ppermute | solution.py:30
  87.6 2.2 %collective-permute-done.19 = f32[192,128]{1,0:T(8,128)S(1)} collective-permute-done((f32[192,128]{1,0:T(8,128)S(1)}, f32[192,128]{1,0:T(8,128)S(1)}, u32[]{:S(2)}, u32[]{:S(2)}) %collective-permute-start.19) | collective-permute-done | bytes 98336 | tf_op jit(solution)/shard_map/ppermute | solution.py:30
  89.8 0.5 collective-permute-done.18
  90.3 1.2 %collective-permute-done.20 = f32[192,128]{1,0:T(8,128)S(1)} collective-permute-done((f32[192,128]{1,0:T(8,128)S(1)}, f32[192,128]{1,0:T(8,128)S(1)}, u32[]{:S(2)}, u32[]{:S(2)}) %collective-permute-start.20) | collective-permute-done | bytes 98336 | tf_op jit(solution)/shard_map/ppermute | solution.py:30
  91.6 0.1 pad_maximum_fusion.1
  91.6 0.1 collective-permute-start.21
  91.7 1.7 %collective-permute-done.21 = f32[4,192,128]{2,1,0:T(8,128)S(1)} collective-permute-done((f32[4,192,128]{2,1,0:T(8,128)S(1)}, f32[4,192,128]{2,1,0:T(8,128)S(1)}, u32[]{:S(2)}, u32[]{:S(2)}) %collective-permute-start.21) | collective-permute-done | bytes 393248 | tf_op jit(solution)/shard_map/ppermute | solution.py:30
  93.4 0.2 fusion.7
  93.6 1.4 %second_rows.1 = f32[512,128]{1,0:T(8,128)} custom-call(f32[128,2048]{1,0:T(8,128)S(1)} %get-tuple-element.18.right_ref, f32[512,128]{1,0:T(8,128)S(1)} %bitcast.79, f32[4,128,128]{2,1,0:T(8,128)S(1)} %bitcast.86), custom_call_target="tpu_custom_call" | custom-call | flops 402653184 | bytes 1048576 | tf_op jit(solution)/shard_map/second_rows/pallas_call | solution.py:286
  95.0 3.8 %all-to-all-start.1 = ((f32[32,16,128]{2,1,0:T(8,128)}), f32[32,16,128]{2,1,0:T(8,128)S(1)}, u32[]{:S(2)}, u32[]{:S(2)}) async-start(f32[32,16,128]{2,1,0:T(8,128)} %bitcast.45), calls=%async_computation.1 | async-start | bytes 524288 | tf_op jit(solution)/shard_map/all_to_all | solution.py:20
  98.8 0.8 fusion
  99.7 10.1 %all-to-all-done.1 = f32[32,16,128]{2,1,0:T(8,128)S(1)} async-done(((f32[32,16,128]{2,1,0:T(8,128)}), f32[32,16,128]{2,1,0:T(8,128)S(1)}, u32[]{:S(2)}, u32[]{:S(2)}) %all-to-all-start.1) | async-done | bytes 262176 | tf_op jit(solution)/shard_map/all_to_all | solution.py:20
  109.8 0.7 copy.8
  (33 shorter events, 0.6 us)
Async XLA Ops:
  0.6 14.6 %copy-start = (f32[128,128]{1,0:T(8,128)S(1)}, f32[128,128]{1,0:T(8,128)}, u32[]{:S(2)}) copy-start(f32[128,128]{1,0:T(8,128)} %param.9) | copy-start | bytes 196612
  0.7 1.1 copy-start.1
  14.7 1.7 %collective-permute-start = (f32[4,136,128]{2,1,0:T(8,128)S(1)}, f32[4,136,128]{2,1,0:T(8,128)S(1)}, u32[]{:S(2)}, u32[]{:S(2)}) collective-permute-start(f32[4,136,128]{2,1,0:T(8,128)S(1)} %dynamic-slice_bitcast_fusion), channel_id=1, source_target_pairs={{0,4},{1,5},{2,6},{3,7},{4,0},{5,1},{6,2},{7,3},{8,12},{9,13},{10,... | collective-permute-start | bytes 835592 | tf_op jit(solution)/shard_map/ppermute | solution.py:30
  16.5 6.2 %collective-permute-start.1 = (f32[200,128]{1,0:T(8,128)S(1)}, f32[200,128]{1,0:T(8,128)S(1)}, u32[]{:S(2)}, u32[]{:S(2)}) collective-permute-start(f32[200,128]{1,0:T(8,128)S(1)} %get-tuple-element.52), channel_id=1, source_target_pairs={{0,1},{1,0},{2,3},{3,2},{4,5},{5,4},{6,7},{7,6},{8,9},{9,8},{10,11... | collective-permute-start | bytes 307208 | tf_op jit(solution)/shard_map/ppermute | solution.py:30
  19.4 5.9 %collective-permute-start.2 = (f32[200,128]{1,0:T(8,128)S(1)}, f32[200,128]{1,0:T(8,128)S(1)}, u32[]{:S(2)}, u32[]{:S(2)}) collective-permute-start(f32[200,128]{1,0:T(8,128)S(1)} %get-tuple-element.53), channel_id=1, source_target_pairs={{0,2},{1,3},{2,0},{3,1},{4,6},{5,7},{6,4},{7,5},{8,10},{9,11},{10,... | collective-permute-start | bytes 307208 | tf_op jit(solution)/shard_map/ppermute | solution.py:30
  20.9 5.6 %collective-permute-start.3 = (f32[200,128]{1,0:T(8,128)S(1)}, f32[200,128]{1,0:T(8,128)S(1)}, u32[]{:S(2)}, u32[]{:S(2)}) collective-permute-start(f32[200,128]{1,0:T(8,128)S(1)} %get-tuple-element.54), channel_id=1, source_target_pairs={{0,3},{1,2},{2,1},{3,0},{4,7},{5,6},{6,5},{7,4},{8,11},{9,10},{10,... | collective-permute-start | bytes 307208 | tf_op jit(solution)/shard_map/ppermute | solution.py:30
  26.5 6.2 %collective-permute-start.6 = (f32[136,128]{1,0:T(8,128)S(1)}, f32[136,128]{1,0:T(8,128)S(1)}, u32[]{:S(2)}, u32[]{:S(2)}) collective-permute-start(f32[136,128]{1,0:T(8,128)S(1)} %fusion.13), channel_id=1, source_target_pairs={{0,24},{1,25},{2,26},{3,27},{4,28},{5,29},{6,30},{7,31},{8,16},{9,... | collective-permute-start | bytes 208904 | tf_op jit(solution)/shard_map/ppermute | solution.py:30
  30.2 5.2 %collective-permute-start.5 = (f32[136,128]{1,0:T(8,128)S(1)}, f32[136,128]{1,0:T(8,128)S(1)}, u32[]{:S(2)}, u32[]{:S(2)}) collective-permute-start(f32[136,128]{1,0:T(8,128)S(1)} %fusion.13), channel_id=1, source_target_pairs={{0,16},{1,17},{2,18},{3,19},{4,20},{5,21},{6,22},{7,23},{8,24},{9,... | collective-permute-start | bytes 208904 | tf_op jit(solution)/shard_map/ppermute | solution.py:30
  30.2 5.2 %collective-permute-start.4 = (f32[136,128]{1,0:T(8,128)S(1)}, f32[136,128]{1,0:T(8,128)S(1)}, u32[]{:S(2)}, u32[]{:S(2)}) collective-permute-start(f32[136,128]{1,0:T(8,128)S(1)} %fusion.13), channel_id=1, source_target_pairs={{0,8},{1,9},{2,10},{3,11},{4,12},{5,13},{6,14},{7,15},{8,0},{9,1},... | collective-permute-start | bytes 208904 | tf_op jit(solution)/shard_map/ppermute | solution.py:30
  35.4 5.4 %collective-permute-start.9 = (f32[128,128]{1,0:T(8,128)S(1)}, f32[128,128]{1,0:T(8,128)S(1)}, u32[]{:S(2)}, u32[]{:S(2)}) collective-permute-start(f32[128,128]{1,0:T(8,128)S(1)} %fusion.15), channel_id=1, source_target_pairs={{0,3},{1,2},{2,1},{3,0},{4,7},{5,6},{6,5},{7,4},{8,11},{9,10},{10,... | collective-permute-start | bytes 196616 | tf_op jit(solution)/shard_map/ppermute | solution.py:30
  37.0 4.5 %collective-permute-start.8 = (f32[128,128]{1,0:T(8,128)S(1)}, f32[128,128]{1,0:T(8,128)S(1)}, u32[]{:S(2)}, u32[]{:S(2)}) collective-permute-start(f32[128,128]{1,0:T(8,128)S(1)} %fusion.15), channel_id=1, source_target_pairs={{0,2},{1,3},{2,0},{3,1},{4,6},{5,7},{6,4},{7,5},{8,10},{9,11},{10,... | collective-permute-start | bytes 196616 | tf_op jit(solution)/shard_map/ppermute | solution.py:30
  38.3 4.3 %collective-permute-start.7 = (f32[128,128]{1,0:T(8,128)S(1)}, f32[128,128]{1,0:T(8,128)S(1)}, u32[]{:S(2)}, u32[]{:S(2)}) collective-permute-start(f32[128,128]{1,0:T(8,128)S(1)} %fusion.15), channel_id=1, source_target_pairs={{0,1},{1,0},{2,3},{3,2},{4,5},{5,4},{6,7},{7,6},{8,9},{9,8},{10,11... | collective-permute-start | bytes 196616 | tf_op jit(solution)/shard_map/ppermute | solution.py:30
  42.7 1.8 %collective-permute-start.10 = (f32[4,192,128]{2,1,0:T(8,128)S(1)}, f32[4,192,128]{2,1,0:T(8,128)S(1)}, u32[]{:S(2)}, u32[]{:S(2)}) collective-permute-start(f32[4,192,128]{2,1,0:T(8,128)S(1)} %get-tuple-element.35), channel_id=1, source_target_pairs={{0,4},{1,5},{2,6},{3,7},{4,0},{5,1},{6,2},{7,3},{8,12},{9,13},{10,... | collective-permute-start | bytes 1179656 | tf_op jit(solution)/shard_map/ppermute | solution.py:30
  44.7 15.6 %all-to-all-start = ((f32[32,16,128]{2,1,0:T(8,128)}), f32[32,16,128]{2,1,0:T(8,128)S(1)}, u32[]{:S(2)}, u32[]{:S(2)}) async-start(f32[32,16,128]{2,1,0:T(8,128)} %get-tuple-element.20), calls=%async_computation | async-start | bytes 524288 | tf_op jit(solution)/shard_map/all_to_all | solution.py:20
  61.1 1.8 %collective-permute-start.11 = (f32[4,200,128]{2,1,0:T(8,128)S(1)}, f32[4,200,128]{2,1,0:T(8,128)S(1)}, u32[]{:S(2)}, u32[]{:S(2)}) collective-permute-start(f32[4,200,128]{2,1,0:T(8,128)S(1)} %fusion.3), channel_id=1, source_target_pairs={{0,4},{1,5},{2,6},{3,7},{4,0},{5,1},{6,2},{7,3},{8,12},{9,13},{10,... | collective-permute-start | bytes 1228808 | tf_op jit(solution)/shard_map/ppermute | solution.py:30
  63.0 6.1 %collective-permute-start.14 = (f32[200,128]{1,0:T(8,128)S(1)}, f32[200,128]{1,0:T(8,128)S(1)}, u32[]{:S(2)}, u32[]{:S(2)}) collective-permute-start(f32[200,128]{1,0:T(8,128)S(1)} %get-tuple-element.26), channel_id=1, source_target_pairs={{0,3},{1,2},{2,1},{3,0},{4,7},{5,6},{6,5},{7,4},{8,11},{9,10},{10,... | collective-permute-start | bytes 307208 | tf_op jit(solution)/shard_map/ppermute | solution.py:30
  65.8 5.5 %collective-permute-start.13 = (f32[200,128]{1,0:T(8,128)S(1)}, f32[200,128]{1,0:T(8,128)S(1)}, u32[]{:S(2)}, u32[]{:S(2)}) collective-permute-start(f32[200,128]{1,0:T(8,128)S(1)} %get-tuple-element.27), channel_id=1, source_target_pairs={{0,2},{1,3},{2,0},{3,1},{4,6},{5,7},{6,4},{7,5},{8,10},{9,11},{10,... | collective-permute-start | bytes 307208 | tf_op jit(solution)/shard_map/ppermute | solution.py:30
  66.3 5.1 %collective-permute-start.12 = (f32[200,128]{1,0:T(8,128)S(1)}, f32[200,128]{1,0:T(8,128)S(1)}, u32[]{:S(2)}, u32[]{:S(2)}) collective-permute-start(f32[200,128]{1,0:T(8,128)S(1)} %get-tuple-element.28), channel_id=1, source_target_pairs={{0,1},{1,0},{2,3},{3,2},{4,5},{5,4},{6,7},{7,6},{8,9},{9,8},{10,11... | collective-permute-start | bytes 307208 | tf_op jit(solution)/shard_map/ppermute | solution.py:30
  71.5 7.4 %collective-permute-start.17 = (f32[200,128]{1,0:T(8,128)S(1)}, f32[200,128]{1,0:T(8,128)S(1)}, u32[]{:S(2)}, u32[]{:S(2)}) collective-permute-start(f32[200,128]{1,0:T(8,128)S(1)} %fusion.12), channel_id=1, source_target_pairs={{0,24},{1,25},{2,26},{3,27},{4,28},{5,29},{6,30},{7,31},{8,16},{9,... | collective-permute-start | bytes 307208 | tf_op jit(solution)/shard_map/ppermute | solution.py:30
  74.9 8.9 %collective-permute-start.16 = (f32[200,128]{1,0:T(8,128)S(1)}, f32[200,128]{1,0:T(8,128)S(1)}, u32[]{:S(2)}, u32[]{:S(2)}) collective-permute-start(f32[200,128]{1,0:T(8,128)S(1)} %fusion.12), channel_id=1, source_target_pairs={{0,16},{1,17},{2,18},{3,19},{4,20},{5,21},{6,22},{7,23},{8,24},{9,... | collective-permute-start | bytes 307208 | tf_op jit(solution)/shard_map/ppermute | solution.py:30
  74.9 8.9 %collective-permute-start.15 = (f32[200,128]{1,0:T(8,128)S(1)}, f32[200,128]{1,0:T(8,128)S(1)}, u32[]{:S(2)}, u32[]{:S(2)}) collective-permute-start(f32[200,128]{1,0:T(8,128)S(1)} %fusion.12), channel_id=1, source_target_pairs={{0,8},{1,9},{2,10},{3,11},{4,12},{5,13},{6,14},{7,15},{8,0},{9,1},... | collective-permute-start | bytes 307208 | tf_op jit(solution)/shard_map/ppermute | solution.py:30
  84.0 5.7 %collective-permute-start.19 = (f32[192,128]{1,0:T(8,128)S(1)}, f32[192,128]{1,0:T(8,128)S(1)}, u32[]{:S(2)}, u32[]{:S(2)}) collective-permute-start(f32[192,128]{1,0:T(8,128)S(1)} %get-tuple-element.51), channel_id=1, source_target_pairs={{0,2},{1,3},{2,0},{3,1},{4,6},{5,7},{6,4},{7,5},{8,10},{9,11},{10,... | collective-permute-start | bytes 294920 | tf_op jit(solution)/shard_map/ppermute | solution.py:30
  85.6 4.7 %collective-permute-start.18 = (f32[192,128]{1,0:T(8,128)S(1)}, f32[192,128]{1,0:T(8,128)S(1)}, u32[]{:S(2)}, u32[]{:S(2)}) collective-permute-start(f32[192,128]{1,0:T(8,128)S(1)} %get-tuple-element.51), channel_id=1, source_target_pairs={{0,1},{1,0},{2,3},{3,2},{4,5},{5,4},{6,7},{7,6},{8,9},{9,8},{10,11... | collective-permute-start | bytes 294920 | tf_op jit(solution)/shard_map/ppermute | solution.py:30
  85.8 5.7 %collective-permute-start.20 = (f32[192,128]{1,0:T(8,128)S(1)}, f32[192,128]{1,0:T(8,128)S(1)}, u32[]{:S(2)}, u32[]{:S(2)}) collective-permute-start(f32[192,128]{1,0:T(8,128)S(1)} %get-tuple-element.51), channel_id=1, source_target_pairs={{0,3},{1,2},{2,1},{3,0},{4,7},{5,6},{6,5},{7,4},{8,11},{9,10},{10,... | collective-permute-start | bytes 294920 | tf_op jit(solution)/shard_map/ppermute | solution.py:30
  91.6 1.8 %collective-permute-start.21 = (f32[4,192,128]{2,1,0:T(8,128)S(1)}, f32[4,192,128]{2,1,0:T(8,128)S(1)}, u32[]{:S(2)}, u32[]{:S(2)}) collective-permute-start(f32[4,192,128]{2,1,0:T(8,128)S(1)} %get-tuple-element.29), channel_id=1, source_target_pairs={{0,4},{1,5},{2,6},{3,7},{4,0},{5,1},{6,2},{7,3},{8,12},{9,13},{10,... | collective-permute-start | bytes 1179656 | tf_op jit(solution)/shard_map/ppermute | solution.py:30
  95.0 14.7 %all-to-all-start.1 = ((f32[32,16,128]{2,1,0:T(8,128)}), f32[32,16,128]{2,1,0:T(8,128)S(1)}, u32[]{:S(2)}, u32[]{:S(2)}) async-start(f32[32,16,128]{2,1,0:T(8,128)} %bitcast.45), calls=%async_computation.1 | async-start | bytes 524288 | tf_op jit(solution)/shard_map/all_to_all | solution.py:20

commit v16 on v15

--- a/solution.py
+++ b/solution.py
@@ -346,7 +346,7 @@
         return own * total[:rows_own] / total[rows_own][None, :]
 
     right, summed = full_turn(
-        tensor_slab, left_init, right_init, left_init, k, parts, T1_MIB * MIB
+        tensor_slab, left_init, right_init, left_init, 2 * k, parts, T1_MIB * MIB
     )
     second_left = after(second_left_init, summed)
     summed = summed.reshape(2, col_devices, rows_own + PAD, rank)
@@ -369,7 +369,7 @@
     place = lax.axis_index("col").astype(jnp.int32)[None]
     second_left, col_part = prepare(place, second_left, devices, slices, second_rows)
     arrived = exchange(after(second_left, left))
-    right, summed = full_turn(tensor_slab, left, right, col_part, k, parts, VMEM_BYTES)
+    right, summed = full_turn(tensor_slab, left, right, col_part, 2 * k, parts, VMEM_BYTES)
     arrived = after(arrived, summed)
     second_left = arrived.reshape(rank * slices, rank)
     numerator = second_numerator(right, second_left, whole, slices)

time: 111 us -> 111 us (level)
  no operation moved by 1% of the time
where the time goes in v16:
time: 111 us; the launch traced here: 110 us
  waiting for transfers between devices  43.8 us (39%)
  starting transfers between devices  32.2 us (29%)
  Pallas kernels  28.9 us (26%)
  local copies, waits for them, and re-layouts  2.87 us (3%)
  other arithmetic  1.76 us (2%)
    ppermute x22, waiting for transfers between devices, send(): return lax.ppermute(values, AXES, pairs)  33.7 us
    pallas_call x2, Pallas kernels, full_turn(): pl.pallas_call(turn_kernel, grid=(columns // block,), in_specs=[columns_s...  25 us
    ppermute x22, starting transfers between devices, send(): return lax.ppermute(values, AXES, pairs)  24.8 us
    all_to_all x2, waiting for transfers between devices, exchange(): return lax.all_to_all(parts, AXES, split_axis=0, concat_axis=0, tiled=True)  10.1 us
    all_to_all x2, starting transfers between devices, exchange(): return lax.all_to_all(parts, AXES, split_axis=0, concat_axis=0, tiled=True)  7.32 us
  transfers between devices with their start and end apart: 24, of which 20 were waited for; matrix products, arithmetic and copies ran while one was open for 2% of the time, Pallas kernels for 13%

profile of v16, /device:TPU:0, one launch (start us, length us, event | category | flops | bytes accessed | tf_op | source)
XLA Modules:
  0.0 110.4 jit_solution(15356779546541426003)
XLA Ops:
  0.6 0.0 copy-start
  0.7 0.0 copy-start.1
  0.7 1.1 copy-done.1
  1.7 12.9 %turn.2 = (f32[128,2048]{1,0:T(8,128)}, f32[8,136,128]{2,1,0:T(8,128)S(1)}) custom-call(f32[1024,2048]{1,0:T(8,128)} %slab_ref.3, f32[1024,128]{1,0:T(8,128)S(1)} %copy-done.1, f32[128,2048]{1,0:T(8,128)} %right_ref.1, f32[1024,128]{1,0:T(8,128)S(1)} %copy-done.1), custom_call_target="tpu_custom_call" | custom-call | flops 6442450944 | bytes 8388608 | tf_op jit(solution)/shard_map/turn/pallas_call | solution.py:257
  14.6 0.5 collective-permute-start
  15.2 0.8 constant_dynamic-slice_fusion.13
  16.0 0.3 collective-permute-done
  16.4 2.9 %collective-permute-start.1 = (f32[200,128]{1,0:T(8,128)S(1)}, f32[200,128]{1,0:T(8,128)S(1)}, u32[]{:S(2)}, u32[]{:S(2)}) collective-permute-start(f32[200,128]{1,0:T(8,128)S(1)} %get-tuple-element.52), channel_id=1, source_target_pairs={{0,1},{1,0},{2,3},{3,2},{4,5},{5,4},{6,7},{7,6},{8,9},{9,8},{10,11... | collective-permute-start | bytes 307208 | tf_op jit(solution)/shard_map/ppermute | solution.py:30
  19.4 1.5 %collective-permute-start.2 = (f32[200,128]{1,0:T(8,128)S(1)}, f32[200,128]{1,0:T(8,128)S(1)}, u32[]{:S(2)}, u32[]{:S(2)}) collective-permute-start(f32[200,128]{1,0:T(8,128)S(1)} %get-tuple-element.53), channel_id=1, source_target_pairs={{0,2},{1,3},{2,0},{3,1},{4,6},{5,7},{6,4},{7,5},{8,10},{9,11},{10,... | collective-permute-start | bytes 307208 | tf_op jit(solution)/shard_map/ppermute | solution.py:30
  20.9 0.0 collective-permute-start.3
  20.9 1.7 %collective-permute-done.1 = f32[200,128]{1,0:T(8,128)S(1)} collective-permute-done((f32[200,128]{1,0:T(8,128)S(1)}, f32[200,128]{1,0:T(8,128)S(1)}, u32[]{:S(2)}, u32[]{:S(2)}) %collective-permute-start.1) | collective-permute-done | bytes 102432 | tf_op jit(solution)/shard_map/ppermute | solution.py:30
  22.6 2.7 %collective-permute-done.2 = f32[200,128]{1,0:T(8,128)S(1)} collective-permute-done((f32[200,128]{1,0:T(8,128)S(1)}, f32[200,128]{1,0:T(8,128)S(1)}, u32[]{:S(2)}, u32[]{:S(2)}) %collective-permute-start.2) | collective-permute-done | bytes 102432 | tf_op jit(solution)/shard_map/ppermute | solution.py:30
  25.3 1.2 %collective-permute-done.3 = f32[200,128]{1,0:T(8,128)S(1)} collective-permute-done((f32[200,128]{1,0:T(8,128)S(1)}, f32[200,128]{1,0:T(8,128)S(1)}, u32[]{:S(2)}, u32[]{:S(2)}) %collective-permute-start.3) | collective-permute-done | bytes 102432 | tf_op jit(solution)/shard_map/ppermute | solution.py:30
  26.5 3.7 %collective-permute-start.6 = (f32[136,128]{1,0:T(8,128)S(1)}, f32[136,128]{1,0:T(8,128)S(1)}, u32[]{:S(2)}, u32[]{:S(2)}) collective-permute-start(f32[136,128]{1,0:T(8,128)S(1)} %fusion.13), channel_id=1, source_target_pairs={{0,24},{1,25},{2,26},{3,27},{4,28},{5,29},{6,30},{7,31},{8,16},{9,... | collective-permute-start | bytes 208904 | tf_op jit(solution)/shard_map/ppermute | solution.py:30
  30.1 0.0 collective-permute-start.5
  30.1 0.8 collective-permute-start.4
  30.9 1.7 %collective-permute-done.6 = f32[136,128]{1,0:T(8,128)S(1)} collective-permute-done((f32[136,128]{1,0:T(8,128)S(1)}, f32[136,128]{1,0:T(8,128)S(1)}, u32[]{:S(2)}, u32[]{:S(2)}) %collective-permute-start.6) | collective-permute-done | bytes 69664 | tf_op jit(solution)/shard_map/ppermute | solution.py:30
  32.6 2.7 %collective-permute-done.5 = f32[136,128]{1,0:T(8,128)S(1)} collective-permute-done((f32[136,128]{1,0:T(8,128)S(1)}, f32[136,128]{1,0:T(8,128)S(1)}, u32[]{:S(2)}, u32[]{:S(2)}) %collective-permute-start.5) | collective-permute-done | bytes 69664 | tf_op jit(solution)/shard_map/ppermute | solution.py:30
  35.3 0.0 collective-permute-done.4
  35.4 1.6 %collective-permute-start.9 = (f32[128,128]{1,0:T(8,128)S(1)}, f32[128,128]{1,0:T(8,128)S(1)}, u32[]{:S(2)}, u32[]{:S(2)}) collective-permute-start(f32[128,128]{1,0:T(8,128)S(1)} %fusion.15), channel_id=1, source_target_pairs={{0,3},{1,2},{2,1},{3,0},{4,7},{5,6},{6,5},{7,4},{8,11},{9,10},{10,... | collective-permute-start | bytes 196616 | tf_op jit(solution)/shard_map/ppermute | solution.py:30
  37.0 1.3 %collective-permute-start.8 = (f32[128,128]{1,0:T(8,128)S(1)}, f32[128,128]{1,0:T(8,128)S(1)}, u32[]{:S(2)}, u32[]{:S(2)}) collective-permute-start(f32[128,128]{1,0:T(8,128)S(1)} %fusion.15), channel_id=1, source_target_pairs={{0,2},{1,3},{2,0},{3,1},{4,6},{5,7},{6,4},{7,5},{8,10},{9,11},{10,... | collective-permute-start | bytes 196616 | tf_op jit(solution)/shard_map/ppermute | solution.py:30
  38.3 0.7 collective-permute-start.7
  39.0 1.8 %collective-permute-done.9 = f32[128,128]{1,0:T(8,128)S(1)} collective-permute-done((f32[128,128]{1,0:T(8,128)S(1)}, f32[128,128]{1,0:T(8,128)S(1)}, u32[]{:S(2)}, u32[]{:S(2)}) %collective-permute-start.9) | collective-permute-done | bytes 65568 | tf_op jit(solution)/shard_map/ppermute | solution.py:30
  40.8 0.7 collective-permute-done.8
  41.5 1.1 collective-permute-done.7
  42.6 0.1 maximum_maximum_fusion
  42.7 0.1 collective-permute-start.10
  42.7 1.7 %prepare.1 = (f32[32,16,128]{2,1,0:T(8,128)}, f32[1,128]{1,0:T(1,128)S(1)}) custom-call(s32[1]{0:T(128)} %bitcast.19.place_ref, f32[2048,128]{1,0:T(8,128)} %second_left_ref), custom_call_target="tpu_custom_call" | custom-call | flops 65536 | bytes 524288 | tf_op jit(solution)/shard_map/prepare/pallas_call | solution.py:310
  44.4 0.0 collective-permute-done.10
  44.4 0.2 fusion.9
  44.7 3.5 %all-to-all-start = ((f32[32,16,128]{2,1,0:T(8,128)}), f32[32,16,128]{2,1,0:T(8,128)S(1)}, u32[]{:S(2)}, u32[]{:S(2)}) async-start(f32[32,16,128]{2,1,0:T(8,128)} %get-tuple-element.20), calls=%async_computation | async-start | bytes 524288 | tf_op jit(solution)/shard_map/all_to_all | solution.py:20
  48.2 12.1 %turn.3 = (f32[128,2048]{1,0:T(8,128)S(1)}, f32[8,136,128]{2,1,0:T(8,128)S(1)}) custom-call(f32[1024,2048]{1,0:T(8,128)} %slab_ref.3, f32[1024,128]{1,0:T(8,128)S(1)} %bitcast.87, f32[128,2048]{1,0:T(8,128)} %get-tuple-element.14.right_ref, f32[1,128]{1,0:T(1,128)S(1)} %get-tuple-element.16.extra_ref), custom_call_target="tpu_custom_call" | custom-call | flops 6442450944 | bytes 8388608 | tf_op jit(solution)/shard_map/turn/pallas_call | solution.py:257
  60.4 0.0 all-to-all-done
  60.4 0.7 second_numerator.1
  61.2 0.1 collective-permute-start.11
  61.3 1.7 %collective-permute-done.11 = f32[4,200,128]{2,1,0:T(8,128)S(1)} collective-permute-done((f32[4,200,128]{2,1,0:T(8,128)S(1)}, f32[4,200,128]{2,1,0:T(8,128)S(1)}, u32[]{:S(2)}, u32[]{:S(2)}) %collective-permute-start.11) | collective-permute-done | bytes 409632 | tf_op jit(solution)/shard_map/ppermute | solution.py:30
  63.1 2.6 %collective-permute-start.14 = (f32[200,128]{1,0:T(8,128)S(1)}, f32[200,128]{1,0:T(8,128)S(1)}, u32[]{:S(2)}, u32[]{:S(2)}) collective-permute-start(f32[200,128]{1,0:T(8,128)S(1)} %get-tuple-element.26), channel_id=1, source_target_pairs={{0,3},{1,2},{2,1},{3,0},{4,7},{5,6},{6,5},{7,4},{8,11},{9,10},{10,... | collective-permute-start | bytes 307208 | tf_op jit(solution)/shard_map/ppermute | solution.py:30
  65.6 0.6 collective-permute-start.13
  66.2 0.4 collective-permute-start.12
  66.6 2.4 %collective-permute-done.14 = f32[200,128]{1,0:T(8,128)S(1)} collective-permute-done((f32[200,128]{1,0:T(8,128)S(1)}, f32[200,128]{1,0:T(8,128)S(1)}, u32[]{:S(2)}, u32[]{:S(2)}) %collective-permute-start.14) | collective-permute-done | bytes 102432 | tf_op jit(solution)/shard_map/ppermute | solution.py:30
  69.0 2.1 %collective-permute-done.13 = f32[200,128]{1,0:T(8,128)S(1)} collective-permute-done((f32[200,128]{1,0:T(8,128)S(1)}, f32[200,128]{1,0:T(8,128)S(1)}, u32[]{:S(2)}, u32[]{:S(2)}) %collective-permute-start.13) | collective-permute-done | bytes 102432 | tf_op jit(solution)/shard_map/ppermute | solution.py:30
  71.1 0.1 collective-permute-done.12
  71.3 3.4 %collective-permute-start.17 = (f32[200,128]{1,0:T(8,128)S(1)}, f32[200,128]{1,0:T(8,128)S(1)}, u32[]{:S(2)}, u32[]{:S(2)}) collective-permute-start(f32[200,128]{1,0:T(8,128)S(1)} %fusion.12), channel_id=1, source_target_pairs={{0,24},{1,25},{2,26},{3,27},{4,28},{5,29},{6,30},{7,31},{8,16},{9,... | collective-permute-start | bytes 307208 | tf_op jit(solution)/shard_map/ppermute | solution.py:30
  74.7 0.0 collective-permute-start.16
  74.7 1.0 collective-permute-start.15
  75.8 3.0 %collective-permute-done.17 = f32[200,128]{1,0:T(8,128)S(1)} collective-permute-done((f32[200,128]{1,0:T(8,128)S(1)}, f32[200,128]{1,0:T(8,128)S(1)}, u32[]{:S(2)}, u32[]{:S(2)}) %collective-permute-start.17) | collective-permute-done | bytes 102432 | tf_op jit(solution)/shard_map/ppermute | solution.py:30
  78.8 4.9 %collective-permute-done.16 = f32[200,128]{1,0:T(8,128)S(1)} collective-permute-done((f32[200,128]{1,0:T(8,128)S(1)}, f32[200,128]{1,0:T(8,128)S(1)}, u32[]{:S(2)}, u32[]{:S(2)}) %collective-permute-start.16) | collective-permute-done | bytes 102432 | tf_op jit(solution)/shard_map/ppermute | solution.py:30
  83.7 0.0 collective-permute-done.15
  83.7 0.1 broadcast_divide_fusion
  83.9 1.5 %collective-permute-start.19 = (f32[192,128]{1,0:T(8,128)S(1)}, f32[192,128]{1,0:T(8,128)S(1)}, u32[]{:S(2)}, u32[]{:S(2)}) collective-permute-start(f32[192,128]{1,0:T(8,128)S(1)} %get-tuple-element.51), channel_id=1, source_target_pairs={{0,2},{1,3},{2,0},{3,1},{4,6},{5,7},{6,4},{7,5},{8,10},{9,11},{10,... | collective-permute-start | bytes 294920 | tf_op jit(solution)/shard_map/ppermute | solution.py:30
  85.4 0.2 collective-permute-start.18
  85.6 1.8 %collective-permute-start.20 = (f32[192,128]{1,0:T(8,128)S(1)}, f32[192,128]{1,0:T(8,128)S(1)}, u32[]{:S(2)}, u32[]{:S(2)}) collective-permute-start(f32[192,128]{1,0:T(8,128)S(1)} %get-tuple-element.51), channel_id=1, source_target_pairs={{0,3},{1,2},{2,1},{3,0},{4,7},{5,6},{6,5},{7,4},{8,11},{9,10},{10,... | collective-permute-start | bytes 294920 | tf_op jit(solution)/shard_map/ppermute | solution.py:30
  87.4 2.2 %collective-permute-done.19 = f32[192,128]{1,0:T(8,128)S(1)} collective-permute-done((f32[192,128]{1,0:T(8,128)S(1)}, f32[192,128]{1,0:T(8,128)S(1)}, u32[]{:S(2)}, u32[]{:S(2)}) %collective-permute-start.19) | collective-permute-done | bytes 98336 | tf_op jit(solution)/shard_map/ppermute | solution.py:30
  89.6 0.5 collective-permute-done.18
  90.2 1.2 %collective-permute-done.20 = f32[192,128]{1,0:T(8,128)S(1)} collective-permute-done((f32[192,128]{1,0:T(8,128)S(1)}, f32[192,128]{1,0:T(8,128)S(1)}, u32[]{:S(2)}, u32[]{:S(2)}) %collective-permute-start.20) | collective-permute-done | bytes 98336 | tf_op jit(solution)/shard_map/ppermute | solution.py:30
  91.4 0.1 pad_maximum_fusion.1
  91.5 0.1 collective-permute-start.21
  91.5 1.7 %collective-permute-done.21 = f32[4,192,128]{2,1,0:T(8,128)S(1)} collective-permute-done((f32[4,192,128]{2,1,0:T(8,128)S(1)}, f32[4,192,128]{2,1,0:T(8,128)S(1)}, u32[]{:S(2)}, u32[]{:S(2)}) %collective-permute-start.21) | collective-permute-done | bytes 393248 | tf_op jit(solution)/shard_map/ppermute | solution.py:30
  93.2 0.2 fusion.7
  93.4 1.4 %second_rows.1 = f32[512,128]{1,0:T(8,128)} custom-call(f32[128,2048]{1,0:T(8,128)S(1)} %get-tuple-element.18.right_ref, f32[512,128]{1,0:T(8,128)S(1)} %bitcast.79, f32[4,128,128]{2,1,0:T(8,128)S(1)} %bitcast.86), custom_call_target="tpu_custom_call" | custom-call | flops 402653184 | bytes 1048576 | tf_op jit(solution)/shard_map/second_rows/pallas_call | solution.py:286
  94.9 3.8 %all-to-all-start.1 = ((f32[32,16,128]{2,1,0:T(8,128)}), f32[32,16,128]{2,1,0:T(8,128)S(1)}, u32[]{:S(2)}, u32[]{:S(2)}) async-start(f32[32,16,128]{2,1,0:T(8,128)} %bitcast.45), calls=%async_computation.1 | async-start | bytes 524288 | tf_op jit(solution)/shard_map/all_to_all | solution.py:20
  98.7 0.8 fusion
  99.5 10.1 %all-to-all-done.1 = f32[32,16,128]{2,1,0:T(8,128)S(1)} async-done(((f32[32,16,128]{2,1,0:T(8,128)}), f32[32,16,128]{2,1,0:T(8,128)S(1)}, u32[]{:S(2)}, u32[]{:S(2)}) %all-to-all-start.1) | async-done | bytes 262176 | tf_op jit(solution)/shard_map/all_to_all | solution.py:20
  109.6 0.7 copy.8
  (33 shorter events, 0.6 us)
Async XLA Ops:
  0.6 14.5 %copy-start = (f32[128,128]{1,0:T(8,128)S(1)}, f32[128,128]{1,0:T(8,128)}, u32[]{:S(2)}) copy-start(f32[128,128]{1,0:T(8,128)} %param.9) | copy-start | bytes 196612
  0.7 1.1 copy-start.1
  14.6 1.7 %collective-permute-start = (f32[4,136,128]{2,1,0:T(8,128)S(1)}, f32[4,136,128]{2,1,0:T(8,128)S(1)}, u32[]{:S(2)}, u32[]{:S(2)}) collective-permute-start(f32[4,136,128]{2,1,0:T(8,128)S(1)} %dynamic-slice_bitcast_fusion), channel_id=1, source_target_pairs={{0,4},{1,5},{2,6},{3,7},{4,0},{5,1},{6,2},{7,3},{8,12},{9,13},{10,... | collective-permute-start | bytes 835592 | tf_op jit(solution)/shard_map/ppermute | solution.py:30
  16.4 6.2 %collective-permute-start.1 = (f32[200,128]{1,0:T(8,128)S(1)}, f32[200,128]{1,0:T(8,128)S(1)}, u32[]{:S(2)}, u32[]{:S(2)}) collective-permute-start(f32[200,128]{1,0:T(8,128)S(1)} %get-tuple-element.52), channel_id=1, source_target_pairs={{0,1},{1,0},{2,3},{3,2},{4,5},{5,4},{6,7},{7,6},{8,9},{9,8},{10,11... | collective-permute-start | bytes 307208 | tf_op jit(solution)/shard_map/ppermute | solution.py:30
  19.4 5.9 %collective-permute-start.2 = (f32[200,128]{1,0:T(8,128)S(1)}, f32[200,128]{1,0:T(8,128)S(1)}, u32[]{:S(2)}, u32[]{:S(2)}) collective-permute-start(f32[200,128]{1,0:T(8,128)S(1)} %get-tuple-element.53), channel_id=1, source_target_pairs={{0,2},{1,3},{2,0},{3,1},{4,6},{5,7},{6,4},{7,5},{8,10},{9,11},{10,... | collective-permute-start | bytes 307208 | tf_op jit(solution)/shard_map/ppermute | solution.py:30
  20.9 5.6 %collective-permute-start.3 = (f32[200,128]{1,0:T(8,128)S(1)}, f32[200,128]{1,0:T(8,128)S(1)}, u32[]{:S(2)}, u32[]{:S(2)}) collective-permute-start(f32[200,128]{1,0:T(8,128)S(1)} %get-tuple-element.54), channel_id=1, source_target_pairs={{0,3},{1,2},{2,1},{3,0},{4,7},{5,6},{6,5},{7,4},{8,11},{9,10},{10,... | collective-permute-start | bytes 307208 | tf_op jit(solution)/shard_map/ppermute | solution.py:30
  26.5 6.2 %collective-permute-start.6 = (f32[136,128]{1,0:T(8,128)S(1)}, f32[136,128]{1,0:T(8,128)S(1)}, u32[]{:S(2)}, u32[]{:S(2)}) collective-permute-start(f32[136,128]{1,0:T(8,128)S(1)} %fusion.13), channel_id=1, source_target_pairs={{0,24},{1,25},{2,26},{3,27},{4,28},{5,29},{6,30},{7,31},{8,16},{9,... | collective-permute-start | bytes 208904 | tf_op jit(solution)/shard_map/ppermute | solution.py:30
  30.1 5.2 %collective-permute-start.5 = (f32[136,128]{1,0:T(8,128)S(1)}, f32[136,128]{1,0:T(8,128)S(1)}, u32[]{:S(2)}, u32[]{:S(2)}) collective-permute-start(f32[136,128]{1,0:T(8,128)S(1)} %fusion.13), channel_id=1, source_target_pairs={{0,16},{1,17},{2,18},{3,19},{4,20},{5,21},{6,22},{7,23},{8,24},{9,... | collective-permute-start | bytes 208904 | tf_op jit(solution)/shard_map/ppermute | solution.py:30
  30.1 5.2 %collective-permute-start.4 = (f32[136,128]{1,0:T(8,128)S(1)}, f32[136,128]{1,0:T(8,128)S(1)}, u32[]{:S(2)}, u32[]{:S(2)}) collective-permute-start(f32[136,128]{1,0:T(8,128)S(1)} %fusion.13), channel_id=1, source_target_pairs={{0,8},{1,9},{2,10},{3,11},{4,12},{5,13},{6,14},{7,15},{8,0},{9,1},... | collective-permute-start | bytes 208904 | tf_op jit(solution)/shard_map/ppermute | solution.py:30
  35.4 5.4 %collective-permute-start.9 = (f32[128,128]{1,0:T(8,128)S(1)}, f32[128,128]{1,0:T(8,128)S(1)}, u32[]{:S(2)}, u32[]{:S(2)}) collective-permute-start(f32[128,128]{1,0:T(8,128)S(1)} %fusion.15), channel_id=1, source_target_pairs={{0,3},{1,2},{2,1},{3,0},{4,7},{5,6},{6,5},{7,4},{8,11},{9,10},{10,... | collective-permute-start | bytes 196616 | tf_op jit(solution)/shard_map/ppermute | solution.py:30
  37.0 4.5 %collective-permute-start.8 = (f32[128,128]{1,0:T(8,128)S(1)}, f32[128,128]{1,0:T(8,128)S(1)}, u32[]{:S(2)}, u32[]{:S(2)}) collective-permute-start(f32[128,128]{1,0:T(8,128)S(1)} %fusion.15), channel_id=1, source_target_pairs={{0,2},{1,3},{2,0},{3,1},{4,6},{5,7},{6,4},{7,5},{8,10},{9,11},{10,... | collective-permute-start | bytes 196616 | tf_op jit(solution)/shard_map/ppermute | solution.py:30
  38.3 4.3 %collective-permute-start.7 = (f32[128,128]{1,0:T(8,128)S(1)}, f32[128,128]{1,0:T(8,128)S(1)}, u32[]{:S(2)}, u32[]{:S(2)}) collective-permute-start(f32[128,128]{1,0:T(8,128)S(1)} %fusion.15), channel_id=1, source_target_pairs={{0,1},{1,0},{2,3},{3,2},{4,5},{5,4},{6,7},{7,6},{8,9},{9,8},{10,11... | collective-permute-start | bytes 196616 | tf_op jit(solution)/shard_map/ppermute | solution.py:30
  42.7 1.8 %collective-permute-start.10 = (f32[4,192,128]{2,1,0:T(8,128)S(1)}, f32[4,192,128]{2,1,0:T(8,128)S(1)}, u32[]{:S(2)}, u32[]{:S(2)}) collective-permute-start(f32[4,192,128]{2,1,0:T(8,128)S(1)} %get-tuple-element.35), channel_id=1, source_target_pairs={{0,4},{1,5},{2,6},{3,7},{4,0},{5,1},{6,2},{7,3},{8,12},{9,13},{10,... | collective-permute-start | bytes 1179656 | tf_op jit(solution)/shard_map/ppermute | solution.py:30
  44.7 15.7 %all-to-all-start = ((f32[32,16,128]{2,1,0:T(8,128)}), f32[32,16,128]{2,1,0:T(8,128)S(1)}, u32[]{:S(2)}, u32[]{:S(2)}) async-start(f32[32,16,128]{2,1,0:T(8,128)} %get-tuple-element.20), calls=%async_computation | async-start | bytes 524288 | tf_op jit(solution)/shard_map/all_to_all | solution.py:20
  61.2 1.8 %collective-permute-start.11 = (f32[4,200,128]{2,1,0:T(8,128)S(1)}, f32[4,200,128]{2,1,0:T(8,128)S(1)}, u32[]{:S(2)}, u32[]{:S(2)}) collective-permute-start(f32[4,200,128]{2,1,0:T(8,128)S(1)} %fusion.3), channel_id=1, source_target_pairs={{0,4},{1,5},{2,6},{3,7},{4,0},{5,1},{6,2},{7,3},{8,12},{9,13},{10,... | collective-permute-start | bytes 1228808 | tf_op jit(solution)/shard_map/ppermute | solution.py:30
  63.1 6.0 %collective-permute-start.14 = (f32[200,128]{1,0:T(8,128)S(1)}, f32[200,128]{1,0:T(8,128)S(1)}, u32[]{:S(2)}, u32[]{:S(2)}) collective-permute-start(f32[200,128]{1,0:T(8,128)S(1)} %get-tuple-element.26), channel_id=1, source_target_pairs={{0,3},{1,2},{2,1},{3,0},{4,7},{5,6},{6,5},{7,4},{8,11},{9,10},{10,... | collective-permute-start | bytes 307208 | tf_op jit(solution)/shard_map/ppermute | solution.py:30
  65.6 5.5 %collective-permute-start.13 = (f32[200,128]{1,0:T(8,128)S(1)}, f32[200,128]{1,0:T(8,128)S(1)}, u32[]{:S(2)}, u32[]{:S(2)}) collective-permute-start(f32[200,128]{1,0:T(8,128)S(1)} %get-tuple-element.27), channel_id=1, source_target_pairs={{0,2},{1,3},{2,0},{3,1},{4,6},{5,7},{6,4},{7,5},{8,10},{9,11},{10,... | collective-permute-start | bytes 307208 | tf_op jit(solution)/shard_map/ppermute | solution.py:30
  66.2 5.1 %collective-permute-start.12 = (f32[200,128]{1,0:T(8,128)S(1)}, f32[200,128]{1,0:T(8,128)S(1)}, u32[]{:S(2)}, u32[]{:S(2)}) collective-permute-start(f32[200,128]{1,0:T(8,128)S(1)} %get-tuple-element.28), channel_id=1, source_target_pairs={{0,1},{1,0},{2,3},{3,2},{4,5},{5,4},{6,7},{7,6},{8,9},{9,8},{10,11... | collective-permute-start | bytes 307208 | tf_op jit(solution)/shard_map/ppermute | solution.py:30
  71.3 7.4 %collective-permute-start.17 = (f32[200,128]{1,0:T(8,128)S(1)}, f32[200,128]{1,0:T(8,128)S(1)}, u32[]{:S(2)}, u32[]{:S(2)}) collective-permute-start(f32[200,128]{1,0:T(8,128)S(1)} %fusion.12), channel_id=1, source_target_pairs={{0,24},{1,25},{2,26},{3,27},{4,28},{5,29},{6,30},{7,31},{8,16},{9,... | collective-permute-start | bytes 307208 | tf_op jit(solution)/shard_map/ppermute | solution.py:30
  74.7 8.9 %collective-permute-start.16 = (f32[200,128]{1,0:T(8,128)S(1)}, f32[200,128]{1,0:T(8,128)S(1)}, u32[]{:S(2)}, u32[]{:S(2)}) collective-permute-start(f32[200,128]{1,0:T(8,128)S(1)} %fusion.12), channel_id=1, source_target_pairs={{0,16},{1,17},{2,18},{3,19},{4,20},{5,21},{6,22},{7,23},{8,24},{9,... | collective-permute-start | bytes 307208 | tf_op jit(solution)/shard_map/ppermute | solution.py:30
  74.7 8.9 %collective-permute-start.15 = (f32[200,128]{1,0:T(8,128)S(1)}, f32[200,128]{1,0:T(8,128)S(1)}, u32[]{:S(2)}, u32[]{:S(2)}) collective-permute-start(f32[200,128]{1,0:T(8,128)S(1)} %fusion.12), channel_id=1, source_target_pairs={{0,8},{1,9},{2,10},{3,11},{4,12},{5,13},{6,14},{7,15},{8,0},{9,1},... | collective-permute-start | bytes 307208 | tf_op jit(solution)/shard_map/ppermute | solution.py:30
  83.9 5.7 %collective-permute-start.19 = (f32[192,128]{1,0:T(8,128)S(1)}, f32[192,128]{1,0:T(8,128)S(1)}, u32[]{:S(2)}, u32[]{:S(2)}) collective-permute-start(f32[192,128]{1,0:T(8,128)S(1)} %get-tuple-element.51), channel_id=1, source_target_pairs={{0,2},{1,3},{2,0},{3,1},{4,6},{5,7},{6,4},{7,5},{8,10},{9,11},{10,... | collective-permute-start | bytes 294920 | tf_op jit(solution)/shard_map/ppermute | solution.py:30
  85.4 4.7 %collective-permute-start.18 = (f32[192,128]{1,0:T(8,128)S(1)}, f32[192,128]{1,0:T(8,128)S(1)}, u32[]{:S(2)}, u32[]{:S(2)}) collective-permute-start(f32[192,128]{1,0:T(8,128)S(1)} %get-tuple-element.51), channel_id=1, source_target_pairs={{0,1},{1,0},{2,3},{3,2},{4,5},{5,4},{6,7},{7,6},{8,9},{9,8},{10,11... | collective-permute-start | bytes 294920 | tf_op jit(solution)/shard_map/ppermute | solution.py:30
  85.6 5.7 %collective-permute-start.20 = (f32[192,128]{1,0:T(8,128)S(1)}, f32[192,128]{1,0:T(8,128)S(1)}, u32[]{:S(2)}, u32[]{:S(2)}) collective-permute-start(f32[192,128]{1,0:T(8,128)S(1)} %get-tuple-element.51), channel_id=1, source_target_pairs={{0,3},{1,2},{2,1},{3,0},{4,7},{5,6},{6,5},{7,4},{8,11},{9,10},{10,... | collective-permute-start | bytes 294920 | tf_op jit(solution)/shard_map/ppermute | solution.py:30
  91.5 1.8 %collective-permute-start.21 = (f32[4,192,128]{2,1,0:T(8,128)S(1)}, f32[4,192,128]{2,1,0:T(8,128)S(1)}, u32[]{:S(2)}, u32[]{:S(2)}) collective-permute-start(f32[4,192,128]{2,1,0:T(8,128)S(1)} %get-tuple-element.29), channel_id=1, source_target_pairs={{0,4},{1,5},{2,6},{3,7},{4,0},{5,1},{6,2},{7,3},{8,12},{9,13},{10,... | collective-permute-start | bytes 1179656 | tf_op jit(solution)/shard_map/ppermute | solution.py:30
  94.9 14.8 %all-to-all-start.1 = ((f32[32,16,128]{2,1,0:T(8,128)}), f32[32,16,128]{2,1,0:T(8,128)S(1)}, u32[]{:S(2)}, u32[]{:S(2)}) async-start(f32[32,16,128]{2,1,0:T(8,128)} %bitcast.45), calls=%async_computation.1 | async-start | bytes 524288 | tf_op jit(solution)/shard_map/all_to_all | solution.py:20
